TPU v7x, 256 devices: a whole 4x4x8 slice. The times are simulated.
256 devices in a mesh: sec: 4 (over x_lo, core), tile: 64 (over z, y, x_hi).
Axes of the slice: x: 4 (x_hi: 2, x_lo: 2; x = x_hi * 2 + x_lo), y: 4, z: 8, core: 2. Of those that a mesh axis runs over, the one named last changes fastest.
Arguments:
- flow_field: float32 [4, 32, 1024, 512], P(None, 'sec', 'tile'), may hold values from -6 to 6
- viscosity: float32 [32, 1024, 512], P('sec', 'tile'), may hold values from 0.05 to 0.16
- port_plane: float32 [4, 8192], P(None, ('sec', 'tile')), may hold values from -8 to 8
- port_match: int32 [8192], P(('sec', 'tile')), may hold values from 0 to 8191, each once
- inlet_cell: int32 [8192], P(('sec', 'tile')), may hold values from 0 to 65535
- inclusion_state: float32 [4, 4, 64, 64, 128], P(None, 'sec', 'tile'), may hold values from -6 to 6
- response_rate: float32 [4, 64, 64, 128], P('sec', 'tile'), may hold values from 0.1 to 0.9
- inclusion_mass: float32 [4, 64, 64, 128], P('sec', 'tile'), may hold values from 0.1 to 1
- anchor_cell: int32 [4, 64, 64, 128], P('sec', 'tile'), may hold values from 0 to 65535
- live_counts: int32 [4, 64, 64], P('sec', 'tile'), may hold values from 0 to 128, as said below
- arrival_cell: int32 [4, 64, 64, 128], P('sec', 'tile'), may hold values from 0 to 65535
Outputs:
- flow_next: float32 [4, 32, 1024, 512], P(None, 'sec', 'tile')
- arrived_state: float32 [4, 4, 64, 64, 128], P(None, 'sec', 'tile')
Inputs may be any that keep to these rules, and one draw needn't show every extreme that they name: `live_counts`: in each sender's row one partner gets exactly 128 live inclusions; live slots come first.
All inputs are finite; a program needn't handle non-finite values.
Results may differ from a plain program's by a relative error of at most 0.00002.
Values sent between devices are 32-bit elements; how exact they have to be, the bound alone decides.
No kernel may reach another device: no remote copies, remote signals or barrier semaphores. Data moves between devices by JAX's collectives and lax.ppermute only.
A program may use at most 128 MiB of HBM per device.

v0:
```python
import jax
import jax.numpy as jnp
from jax import lax
from jax.sharding import PartitionSpec as P

time_step = 0.5
relaxation = 0.5


def with_halo(cells, sides, width):
    for axis, dim in sides:
        count = lax.axis_size(axis)
        ends = count - 1
        head = lax.slice_in_dim(cells, 0, width, axis=dim)
        tail = lax.slice_in_dim(cells, cells.shape[dim] - width, cells.shape[dim], axis=dim)
        cells = jnp.concatenate(
            [
                lax.ppermute(tail, axis, [(i, (i + 1) % count) for i in range(ends)]),
                cells,
                lax.ppermute(head, axis, [((i + 1) % count, i) for i in range(ends)]),
            ],
            axis=dim,
        )
    return cells


def tendency(padded, viscosity):
    center = padded[:, 1:-1, 1:-1, :]
    upper_z = padded[:, 2:, 1:-1, :]
    lower_z = padded[:, :-2, 1:-1, :]
    upper_x = padded[:, 1:-1, 2:, :]
    lower_x = padded[:, 1:-1, :-2, :]
    zeros_row = jnp.zeros(center.shape[:-1] + (1,), center.dtype)
    upper_y = jnp.concatenate([center[..., 1:], zeros_row], axis=-1)
    lower_y = jnp.concatenate([zeros_row, center[..., :-1]], axis=-1)
    laplace = upper_z + lower_z + upper_x + lower_x + upper_y + lower_y - 6.0 * center
    grad_z = 0.5 * (upper_z - lower_z)
    grad_x = 0.5 * (upper_x - lower_x)
    grad_y = 0.5 * (upper_y - lower_y)
    strain = jnp.sum(
        grad_z[:3] * grad_z[:3] + grad_x[:3] * grad_x[:3] + grad_y[:3] * grad_y[:3], axis=0
    )
    eddy = viscosity * (1.0 + strain / (1.0 + strain))
    carried = center[0:1] * grad_z + center[1:2] * grad_x + center[2:3] * grad_y
    return eddy * laplace - carried


def margins(state):
    return with_halo(state, (("sec", 1), ("tile", 2)), 1)


def on_device(
    flow_field,
    viscosity,
    port_plane,
    port_match,
    inlet_cell,
    inclusion_state,
    response_rate,
    inclusion_mass,
    anchor_cell,
    live_counts,
    arrival_cell,
):
    components = flow_field.shape[0]
    flat_start = flow_field.reshape(components, -1)
    sampled = flat_start[:, anchor_cell.reshape(-1)].reshape(inclusion_state.shape)
    slot = lax.broadcasted_iota(jnp.int32, anchor_cell.shape, 3)
    live = (slot < live_counts[..., None]).astype(jnp.float32)
    moved = live * (inclusion_state + response_rate * (sampled - inclusion_state))
    deposit = live * inclusion_mass * response_rate * (inclusion_state - sampled)
    outgoing = jnp.concatenate([moved, deposit], axis=0)
    incoming = lax.all_to_all(outgoing, "tile", split_axis=3, concat_axis=2, tiled=True)
    incoming = incoming.reshape(outgoing.shape)
    first = flow_field + time_step * tendency(margins(flow_field), viscosity)
    second = 0.5 * flow_field + 0.5 * (first + time_step * tendency(margins(first), viscosity))
    whole_plane = lax.all_gather(port_plane, ("sec", "tile"), axis=1, tiled=True)
    target = whole_plane[:, port_match]
    flat = second.reshape(components, -1)
    flat = flat.at[:, inlet_cell].add(relaxation * (target - flat[:, inlet_cell]))
    flat = flat.at[:, arrival_cell.reshape(-1)].add(incoming[components:].reshape(components, -1))
    return (flat.reshape(flow_field.shape), incoming[:components])


def solution(mesh):
    return jax.shard_map(
        on_device,
        mesh=mesh,
        in_specs=(
            P(None, "sec", "tile", None),
            P("sec", "tile", None),
            P(None, ("sec", "tile")),
            P(("sec", "tile")),
            P(("sec", "tile")),
            P(None, "sec", "tile", None, None),
            P("sec", "tile", None, None),
            P("sec", "tile", None, None),
            P("sec", "tile", None, None),
            P("sec", "tile", None),
            P("sec", "tile", None, None),
        ),
        out_specs=(P(None, "sec", "tile", None), P(None, "sec", "tile", None, None)),
        check_vma=False,
    )
```

profile of v0, /device:TPU:126, one launch (start us, length us, event | category | flops | bytes accessed | tf_op | source)
XLA Modules:
  0.0 1008.2 jit_solution(16917316252090790031)
XLA Ops:
  2.5 1.9 collective-permute-start.1
  4.5 3.6 collective-permute-start
  8.1 17.7 %copy.97 = f32[4,8,16,512]{0,3,2,1:T(8,128)} copy(f32[4,8,16,512]{3,2,1,0:T(8,128)} %param.11) | data formatting | bytes 2097152 | tf_op args[0]
  25.9 38.4 %gather_fusion = f32[8192,4]{1,0:T(8,128)} fusion(f32[4,65536]{0,1:T(8,128)} %bitcast.38, s32[8192]{0:T(1024)S(1)} %broadcast_clamp_fusion), kind=kCustom, calls=%fused_computation.2 | custom fusion | bytes 294912 | tf_op jit(solution)/shard_map/gather | solution.py:67
  64.3 2.9 copy.98
  68.2 13.2 %all-to-all-start = ((f32[8,1,1,64,128]{4,0,2,1,3:T(8,128)}), f32[8,1,1,64,128]{4,0,2,1,3:T(8,128)}, u32[]{:S(2)}, u32[]{:S(2)}) async-start(f32[8,1,1,64,128]{4,0,2,1,3:T(8,128)} %copy.100), calls=%async_computation | async-start | bytes 524288 | tf_op jit(solution)/shard_map/all_to_all | solution.py:73
  84.4 736.1 %all-gather = f32[256,32,4]{1,2,0:T(4,128)} all-gather(f32[1,32,4]{1,2,0:T(4,128)S(1)} %bitcast.46), channel_id=1, replica_groups=mesh['sec'=4,'tile'=64] {'sec','tile'}, dimensions={0}, use_global_device_ids=true | all-gather | bytes 131584 | tf_op jit(solution)/shard_map/all_gather | solution.py:77
  820.5 4.0 copy.96
  826.7 10.0 collective-permute-start.3
  836.7 1.9 collective-permute-start.2
  839.2 10.1 %collective-permute-done.2 = f32[4,10,1,512]{3,1,2,0:T(8,128)S(1)} collective-permute-done((f32[4,10,1,512]{3,1,2,0:T(8,128)S(1)}, f32[4,10,1,512]{3,1,2,0:T(8,128)S(1)}, u32[]{:S(2)}, u32[]{:S(2)}) %collective-permute-start.2) | collective-permute-done | bytes 81952 | tf_op jit(solution)/shard_map/ppermute | solution.py:20
  851.6 2.9 multiply_add_fusion
  854.7 1.9 collective-permute-start.4
  856.7 2.4 collective-permute-start.5
  859.6 3.3 collective-permute-done.5
  863.1 3.2 collective-permute-start.7
  866.3 4.2 collective-permute-start.6
  871.5 7.4 collective-permute-done.6
  880.0 2.0 add_multiply_fusion
  882.0 16.1 %copy.95 = f32[4,8,16,512]{0,3,2,1:T(8,128)} copy(f32[4,8,16,512]{3,1,2,0:T(8,128)S(1)} %add_multiply_fusion) | data formatting | bytes 2097152 | tf_op jit(solution)/shard_map/add | solution.py:76
  898.1 23.9 %scatter_custom_fusion = f32[4,65536]{0,1:T(8,128)} fusion(f32[4,65536]{0,1:T(8,128)} %bitcast.36, s32[32]{0:T(128)S(1)} %compare_select_fusion.3, f32[]{:T(128)} %constant.7.clone.1, s32[1024]{0:T(1024)S(1)} %get-tuple-element.36, f32[4,8192]{0,1:T(8,128)} %bitcast.39, s32[1024]{0:T(1024)S(1)} %get-tuple-element.37), kind=kCustom, calls=%fused_computation.86 | custom fusion | flops 384 | bytes 2236420 | tf_op jit(solution)/shard_map/scatter-add | solution.py:80
  923.8 2.7 copy.101
  926.5 61.4 %scatter_fusion = f32[4,65536]{0,1:T(8,128)} fusion(f32[4,65536]{0,1:T(8,128)} %scatter_custom_fusion, s32[8192]{0:T(1024)S(1)} %bitcast.41, f32[8192,4]{1,0:T(8,128)} %copy.101), kind=kCustom, calls=%fused_computation.4 | custom fusion | flops 32768 | bytes 425984 | tf_op jit(solution)/shard_map/scatter-add | solution.py:81
  987.9 20.3 %copy.102 = f32[4,8,16,512]{3,2,1,0:T(8,128)} copy(f32[4,8,16,512]{0,3,2,1:T(8,128)} %bitcast.37) | data formatting | bytes 2097152
  (62 shorter events, 15.6 us)
Async XLA Ops:
  0.6 80.8 %copy-start = (f32[4,8,16,512]{3,2,1,0:T(8,128)S(1)}, f32[4,8,16,512]{3,2,1,0:T(8,128)}, u32[]{:S(2)}) copy-start(f32[4,8,16,512]{3,2,1,0:T(8,128)} %param.11) | copy-start | bytes 3145732
  0.6 25.1 %copy-start.5 = (s32[1,1,64,128]{3,2,1,0:T(8,128)S(1)}, s32[1,1,64,128]{3,2,1,0:T(8,128)}, u32[]{:S(2)}) copy-start(s32[1,1,64,128]{3,2,1,0:T(8,128)} %param.19) | copy-start | bytes 98308
  0.7 25.2 %copy-start.8 = (s32[1,1,64]{2,1,0:T(1,128)S(1)}, s32[1,1,64]{2,1,0:T(1,128)}, u32[]{:S(2)}) copy-start(s32[1,1,64]{2,1,0:T(1,128)} %param.20) | copy-start | bytes 772
  0.7 66.5 %copy-start.3 = (f32[1,1,64,128]{3,2,1,0:T(8,128)S(1)}, f32[1,1,64,128]{3,2,1,0:T(8,128)}, u32[]{:S(2)}) copy-start(f32[1,1,64,128]{3,2,1,0:T(8,128)} %param.17) | copy-start | bytes 98308
  0.7 66.5 %copy-start.4 = (f32[1,1,64,128]{3,2,1,0:T(8,128)S(1)}, f32[1,1,64,128]{3,2,1,0:T(8,128)}, u32[]{:S(2)}) copy-start(f32[1,1,64,128]{3,2,1,0:T(8,128)} %param.18) | copy-start | bytes 98308
  0.7 66.6 %copy-start.2 = (f32[4,1,1,64,128]{4,3,2,1,0:T(8,128)S(1)}, f32[4,1,1,64,128]{4,3,2,1,0:T(8,128)}, u32[]{:S(2)}) copy-start(f32[4,1,1,64,128]{4,3,2,1,0:T(8,128)} %param.16) | copy-start | bytes 393220
  0.7 83.6 %copy-start.9 = (s32[32]{0:T(128)S(1)}, s32[32]{0:T(128)}, u32[]{:S(2)}) copy-start(s32[32]{0:T(128)} %param.15) | copy-start | bytes 388
  0.7 83.6 %copy-start.6 = (s32[1,1,64,128]{3,2,1,0:T(8,128)S(1)}, s32[1,1,64,128]{3,2,1,0:T(8,128)}, u32[]{:S(2)}) copy-start(s32[1,1,64,128]{3,2,1,0:T(8,128)} %param.21) | copy-start | bytes 98308
  0.7 83.6 %copy-start.7 = (f32[4,32]{1,0:T(4,128)S(1)}, f32[4,32]{1,0:T(4,128)}, u32[]{:S(2)}) copy-start(f32[4,32]{1,0:T(4,128)} %param.13) | copy-start | bytes 1540
  0.7 823.8 %copy-start.10 = (s32[32]{0:T(128)S(1)}, s32[32]{0:T(128)}, u32[]{:S(2)}) copy-start(s32[32]{0:T(128)} %param.14) | copy-start | bytes 388
  0.7 850.6 %copy-start.1 = (f32[8,16,512]{2,1,0:T(8,128)S(1)}, f32[8,16,512]{2,1,0:T(8,128)}, u32[]{:S(2)}) copy-start(f32[8,16,512]{2,1,0:T(8,128)} %param.12) | copy-start | bytes 786436
  2.5 822.0 %collective-permute-start.1 = (f32[4,1,16,512]{3,2,1,0:T(8,128)}, f32[4,1,16,512]{3,2,1,0:T(8,128)}, u32[]{:S(2)}, u32[]{:S(2)}) collective-permute-start(f32[4,1,16,512]{3,2,1,0:T(8,128)} %get-tuple-element.28), channel_id=1, source_target_pairs={{0,64},{64,128},{128,192},{1,65},{65,129},{129,193},{2,66},{66,130... | collective-permute-start | bytes 393224 | tf_op jit(solution)/shard_map/ppermute | solution.py:18
  4.5 821.1 %collective-permute-start = (f32[4,1,16,512]{3,2,1,0:T(8,128)}, f32[4,1,16,512]{3,2,1,0:T(8,128)}, u32[]{:S(2)}, u32[]{:S(2)}) collective-permute-start(f32[4,1,16,512]{3,2,1,0:T(8,128)} %get-tuple-element.29), channel_id=1, source_target_pairs={{64,0},{128,64},{192,128},{65,1},{129,65},{193,129},{66,2},{130,66... | collective-permute-start | bytes 393224 | tf_op jit(solution)/shard_map/ppermute | solution.py:20
  68.2 853.8 %all-to-all-start = ((f32[8,1,1,64,128]{4,0,2,1,3:T(8,128)}), f32[8,1,1,64,128]{4,0,2,1,3:T(8,128)}, u32[]{:S(2)}, u32[]{:S(2)}) async-start(f32[8,1,1,64,128]{4,0,2,1,3:T(8,128)} %copy.100), calls=%async_computation | async-start | bytes 524288 | tf_op jit(solution)/shard_map/all_to_all | solution.py:73
  826.7 12.5 %collective-permute-start.3 = (f32[4,10,1,512]{3,1,2,0:T(8,128)S(1)}, f32[4,10,1,512]{3,1,2,0:T(8,128)S(1)}, u32[]{:S(2)}, u32[]{:S(2)}) collective-permute-start(f32[4,10,1,512]{3,1,2,0:T(8,128)S(1)} %get-tuple-element.16), channel_id=1, source_target_pairs={{0,1},{1,2},{2,3},{3,4},{4,5},{5,6},{6,7},{7,8},{8,9},{9,10},{10,1... | collective-permute-start | bytes 245768 | tf_op jit(solution)/shard_map/ppermute | solution.py:18
  836.7 12.6 %collective-permute-start.2 = (f32[4,10,1,512]{3,1,2,0:T(8,128)S(1)}, f32[4,10,1,512]{3,1,2,0:T(8,128)S(1)}, u32[]{:S(2)}, u32[]{:S(2)}) collective-permute-start(f32[4,10,1,512]{3,1,2,0:T(8,128)S(1)} %get-tuple-element.17), channel_id=1, source_target_pairs={{1,0},{2,1},{3,2},{4,3},{5,4},{6,5},{7,6},{8,7},{9,8},{10,9},{11,1... | collective-permute-start | bytes 245768 | tf_op jit(solution)/shard_map/ppermute | solution.py:20
  854.7 4.7 collective-permute-start.4
  856.7 6.3 collective-permute-start.5
  863.1 8.4 collective-permute-start.7
  866.3 12.6 %collective-permute-start.6 = (f32[4,10,1,512]{3,1,2,0:T(8,128)S(1)}, f32[4,10,1,512]{3,1,2,0:T(8,128)S(1)}, u32[]{:S(2)}, u32[]{:S(2)}) collective-permute-start(f32[4,10,1,512]{3,1,2,0:T(8,128)S(1)} %get-tuple-element.13), channel_id=1, source_target_pairs={{1,0},{2,1},{3,2},{4,3},{5,4},{6,5},{7,6},{8,7},{9,8},{10,9},{11,1... | collective-permute-start | bytes 245768 | tf_op jit(solution)/shard_map/ppermute | solution.py:20
where the time goes:
time: 1010 us
  blocking collectives  736 us (73%)
  local copies, waits for them, and re-layouts  111 us (11%)
  other arithmetic  95 us (9%)
  starting transfers between devices  42.4 us (4%)
  waiting for transfers between devices  22.3 us (2%)
    all_gather x1, blocking collectives, on_device(): lax.all_gather(port_plane, ('sec', 'tile'), axis=1, tiled=True)  736 us
    scatter-add x1, other arithmetic, on_device(): flat.at[:, arrival_cell.reshape(-1)]  61.4 us
    unnamed x26, local copies, waits for them, and re-layouts  39.3 us
    gather x1, local copies, waits for them, and re-layouts, on_device(): flat_start[:, anchor_cell.reshape(-1)].reshape(inclusion_state.shape)  38.4 us
    scatter-add x1, other arithmetic, on_device(): flat.at[:, inlet_cell].add(relaxation * (target - flat[:, inlet_cell]))  23.9 us
  transfers between devices with their start and end apart: 9, of which 5 were waited for; matrix products, arithmetic and copies ran while one was open for 12% of the time, Pallas kernels for 0%

commit v1 on v0

--- a/solution.py
+++ b/solution.py
@@ -69,16 +69,19 @@
     live = (slot < live_counts[..., None]).astype(jnp.float32)
     moved = live * (inclusion_state + response_rate * (sampled - inclusion_state))
     deposit = live * inclusion_mass * response_rate * (inclusion_state - sampled)
-    outgoing = jnp.concatenate([moved, deposit], axis=0)
+    section_ports = lax.all_gather(port_plane.reshape(1, -1), "sec", axis=0, tiled=True)
+    port_rows = jnp.broadcast_to(section_ports[:, None, None, None, :], moved.shape)
+    outgoing = jnp.concatenate([moved, deposit, port_rows], axis=0)
     incoming = lax.all_to_all(outgoing, "tile", split_axis=3, concat_axis=2, tiled=True)
     incoming = incoming.reshape(outgoing.shape)
     first = flow_field + time_step * tendency(margins(flow_field), viscosity)
     second = 0.5 * flow_field + 0.5 * (first + time_step * tendency(margins(first), viscosity))
-    whole_plane = lax.all_gather(port_plane, ("sec", "tile"), axis=1, tiled=True)
+    gathered = incoming[2 * components :].reshape(lax.axis_size("sec"), -1, components, port_plane.shape[1])
+    whole_plane = jnp.transpose(gathered, (2, 0, 1, 3)).reshape(components, -1)
     target = whole_plane[:, port_match]
     flat = second.reshape(components, -1)
     flat = flat.at[:, inlet_cell].add(relaxation * (target - flat[:, inlet_cell]))
-    flat = flat.at[:, arrival_cell.reshape(-1)].add(incoming[components:].reshape(components, -1))
+    flat = flat.at[:, arrival_cell.reshape(-1)].add(incoming[components : 2 * components].reshape(components, -1))
     return (flat.reshape(flow_field.shape), incoming[:components])
 
 

time: 1010 us -> 265 us (0.26)
  the two profiles are of different devices: /device:TPU:126 before, /device:TPU:130 now
where the time goes in v1:
time: 265 us; the launch traced here: 264 us
  local copies, waits for them, and re-layouts  108 us (41%)
  other arithmetic  91.7 us (35%)
  starting transfers between devices  37.1 us (14%)
  waiting for transfers between devices  20.9 us (8%)
  blocking collectives  5.03 us (2%)
    scatter-add x1, other arithmetic, on_device(): flat.at[:, arrival_cell.reshape(-1)]  61.4 us
    unnamed x28, local copies, waits for them, and re-layouts  39.5 us
    gather x1, local copies, waits for them, and re-layouts, on_device(): flat_start[:, anchor_cell.reshape(-1)].reshape(inclusion_state.shape)  38.4 us
    scatter-add x1, other arithmetic, on_device(): flat.at[:, inlet_cell].add(relaxation * (target - flat[:, inlet_cell]))  23.9 us
    ppermute x4, waiting for transfers between devices, with_halo(): lax.ppermute(tail, axis, [(i, (i + 1) % count) for i in range(ends)])  18.7 us
    add x1, local copies, waits for them, and re-layouts, on_device(): 0.5 * flow_field  16.1 us
    ppermute x4, starting transfers between devices, with_halo(): lax.ppermute(head, axis, [((i + 1) % count, i) for i in range(ends)])  12.7 us
    ppermute x4, starting transfers between devices, with_halo(): lax.ppermute(tail, axis, [(i, (i + 1) % count) for i in range(ends)])  12.3 us
  transfers between devices with their start and end apart: 9, of which 5 were waited for; matrix products, arithmetic and copies ran while one was open for 32% of the time, Pallas kernels for 0%

profile of v1, /device:TPU:130, one launch (start us, length us, event | category | flops | bytes accessed | tf_op | source)
XLA Modules:
  0.0 264.0 jit_solution(17851343762656524174)
XLA Ops:
  1.9 1.9 collective-permute-start
  3.8 2.4 collective-permute-start.1
  6.2 17.7 %copy.134 = f32[4,8,16,512]{0,3,2,1:T(8,128)} copy(f32[4,8,16,512]{3,2,1,0:T(8,128)} %param.11) | data formatting | bytes 2097152 | tf_op args[0]
  24.0 38.4 %gather_fusion = f32[8192,4]{1,0:T(8,128)} fusion(f32[4,65536]{0,1:T(8,128)} %bitcast.36, s32[8192]{0:T(1024)S(1)} %broadcast_clamp_fusion), kind=kCustom, calls=%fused_computation | custom fusion | bytes 294912 | tf_op jit(solution)/shard_map/gather | solution.py:67
  62.4 2.9 %copy.143 = f32[4,1,1,64,128]{4,3,2,1,0:T(8,128)S(1)} copy(f32[4,1,1,64,128]{0,4,3,2,1:T(8,128)} %bitcast.38) | data formatting | bytes 262144 | tf_op jit(solution)/shard_map/reshape | solution.py:67
  65.4 5.0 %all-gather = f32[4,1,128]{2,1,0:T(1,128)S(1)} all-gather(f32[1,1,128]{2,1,0:T(1,128)S(1)} %reshape.233), channel_id=1, replica_groups=mesh['sec'=4,'tile'=64] {'sec'}, dimensions={0}, use_global_device_ids=true | all-gather | bytes 2560 | tf_op jit(solution)/shard_map/all_gather | solution.py:72
  71.7 12.1 %all-to-all-start = ((f32[12,1,1,64,128]{4,2,1,0,3:T(1,128)}), f32[12,1,1,64,128]{4,2,1,0,3:T(1,128)S(1)}, u32[]{:S(2)}, u32[]{:S(2)}) async-start(f32[12,1,1,64,128]{4,2,1,0,3:T(1,128)} %copy.136), calls=%async_computation | async-start | bytes 786432 | tf_op jit(solution)/shard_map/all_to_all | solution.py:75
  85.4 7.0 %collective-permute-start.2 = (f32[4,10,1,512]{3,1,2,0:T(8,128)S(1)}, f32[4,10,1,512]{3,1,2,0:T(8,128)S(1)}, u32[]{:S(2)}, u32[]{:S(2)}) collective-permute-start(f32[4,10,1,512]{3,1,2,0:T(8,128)S(1)} %get-tuple-element.21), channel_id=1, source_target_pairs={{1,0},{2,1},{3,2},{4,3},{5,4},{6,5},{7,6},{8,7},{9,8},{10,9},{11,1... | collective-permute-start | bytes 245768 | tf_op jit(solution)/shard_map/ppermute | solution.py:20
  92.3 1.9 collective-permute-start.3
  95.7 9.2 %collective-permute-done.3 = f32[4,10,1,512]{3,1,2,0:T(8,128)S(1)} collective-permute-done((f32[4,10,1,512]{3,1,2,0:T(8,128)S(1)}, f32[4,10,1,512]{3,1,2,0:T(8,128)S(1)}, u32[]{:S(2)}, u32[]{:S(2)}) %collective-permute-start.3) | collective-permute-done | bytes 81952 | tf_op jit(solution)/shard_map/ppermute | solution.py:18
  106.1 1.6 multiply_add_fusion
  107.8 1.9 collective-permute-start.4
  109.8 2.4 collective-permute-start.5
  112.7 3.3 %collective-permute-done.5 = f32[4,1,16,512]{3,2,1,0:T(8,128)S(1)} collective-permute-done((f32[4,1,16,512]{3,2,1,0:T(8,128)S(1)}, f32[4,1,16,512]{3,2,1,0:T(8,128)S(1)}, u32[]{:S(2)}, u32[]{:S(2)}) %collective-permute-start.5) | collective-permute-done | bytes 131104 | tf_op jit(solution)/shard_map/ppermute | solution.py:18
  116.2 1.9 collective-permute-start.6
  118.2 5.6 %collective-permute-start.7 = (f32[4,10,1,512]{3,1,2,0:T(8,128)S(1)}, f32[4,10,1,512]{3,1,2,0:T(8,128)S(1)}, u32[]{:S(2)}, u32[]{:S(2)}) collective-permute-start(f32[4,10,1,512]{3,1,2,0:T(8,128)S(1)} %get-tuple-element.16), channel_id=1, source_target_pairs={{0,1},{1,2},{2,3},{3,4},{4,5},{5,6},{6,7},{7,8},{8,9},{9,10},{10,1... | collective-permute-start | bytes 245768 | tf_op jit(solution)/shard_map/ppermute | solution.py:18
  124.6 6.1 %collective-permute-done.7 = f32[4,10,1,512]{3,1,2,0:T(8,128)S(1)} collective-permute-done((f32[4,10,1,512]{3,1,2,0:T(8,128)S(1)}, f32[4,10,1,512]{3,1,2,0:T(8,128)S(1)}, u32[]{:S(2)}, u32[]{:S(2)}) %collective-permute-start.7) | collective-permute-done | bytes 81952 | tf_op jit(solution)/shard_map/ppermute | solution.py:18
  131.9 2.0 add_multiply_fusion
  133.9 16.1 %copy.133 = f32[4,8,16,512]{0,3,2,1:T(8,128)} copy(f32[4,8,16,512]{3,1,2,0:T(8,128)S(1)} %add_multiply_fusion) | data formatting | bytes 2097152 | tf_op jit(solution)/shard_map/add | solution.py:78
  150.4 4.5 %copy.138 = f32[4,4,64,32]{0,3,2,1:T(8,128)} copy(f32[4,4,64,32]{2,3,0,1:T(8,128)S(1)} %bitcast.39) | data formatting | bytes 262144 | tf_op jit(solution)/shard_map/transpose | solution.py:80
  154.9 2.7 %copy.140 = f32[8192,4]{1,0:T(8,128)} copy(f32[8192,4]{0,1:T(4,128)S(1)} %bitcast.40) | data formatting | bytes 262144 | tf_op jit(solution)/shard_map/reshape | solution.py:84
  157.7 23.9 %scatter_custom_fusion = f32[4,65536]{0,1:T(8,128)} fusion(f32[4,65536]{0,1:T(8,128)} %bitcast.34, s32[32]{0:T(128)S(1)} %compare_select_fusion.3, f32[]{:T(128)} %constant.7.clone.1, s32[1024]{0:T(1024)S(1)} %get-tuple-element.41, f32[4,8192]{0,1:T(8,128)} %bitcast.37, s32[1024]{0:T(1024)S(1)} %get-tuple-element.42), kind=kCustom, calls=%fused_computation.85 | custom fusion | flops 384 | bytes 2236420 | tf_op jit(solution)/shard_map/scatter-add | solution.py:83
  181.6 61.4 %scatter_fusion = f32[4,65536]{0,1:T(8,128)} fusion(f32[4,65536]{0,1:T(8,128)} %scatter_custom_fusion, s32[8192]{0:T(1024)S(1)} %bitcast.41, f32[8192,4]{1,0:T(8,128)} %copy.140), kind=kCustom, calls=%fused_computation.4 | custom fusion | flops 32768 | bytes 425984 | tf_op jit(solution)/shard_map/scatter-add | solution.py:84
  243.0 20.3 %copy.141 = f32[4,8,16,512]{3,2,1,0:T(8,128)} copy(f32[4,8,16,512]{0,3,2,1:T(8,128)} %bitcast.35) | data formatting | bytes 2097152
  (65 shorter events, 10.5 us)
Async XLA Ops:
  0.6 83.2 %copy-start = (f32[4,8,16,512]{3,2,1,0:T(8,128)S(1)}, f32[4,8,16,512]{3,2,1,0:T(8,128)}, u32[]{:S(2)}) copy-start(f32[4,8,16,512]{3,2,1,0:T(8,128)} %param.11) | copy-start | bytes 3145732
  0.6 23.2 %copy-start.7 = (s32[1,1,64]{2,1,0:T(1,128)S(1)}, s32[1,1,64]{2,1,0:T(1,128)}, u32[]{:S(2)}) copy-start(s32[1,1,64]{2,1,0:T(1,128)} %param.20) | copy-start | bytes 772
  0.7 23.3 %copy-start.5 = (s32[1,1,64,128]{3,2,1,0:T(8,128)S(1)}, s32[1,1,64,128]{3,2,1,0:T(8,128)}, u32[]{:S(2)}) copy-start(s32[1,1,64,128]{3,2,1,0:T(8,128)} %param.19) | copy-start | bytes 98308
  0.7 64.6 %copy-start.8 = (f32[4,32]{1,0:T(4,128)S(1)}, f32[4,32]{1,0:T(4,128)}, u32[]{:S(2)}) copy-start(f32[4,32]{1,0:T(4,128)} %param.13) | copy-start | bytes 1540
  0.7 69.7 %copy-start.3 = (f32[1,1,64,128]{3,2,1,0:T(8,128)S(1)}, f32[1,1,64,128]{3,2,1,0:T(8,128)}, u32[]{:S(2)}) copy-start(f32[1,1,64,128]{3,2,1,0:T(8,128)} %param.17) | copy-start | bytes 98308
  0.7 69.7 %copy-start.4 = (f32[1,1,64,128]{3,2,1,0:T(8,128)S(1)}, f32[1,1,64,128]{3,2,1,0:T(8,128)}, u32[]{:S(2)}) copy-start(f32[1,1,64,128]{3,2,1,0:T(8,128)} %param.18) | copy-start | bytes 98308
  0.7 69.8 %copy-start.2 = (f32[4,1,1,64,128]{4,3,2,1,0:T(8,128)S(1)}, f32[4,1,1,64,128]{4,3,2,1,0:T(8,128)}, u32[]{:S(2)}) copy-start(f32[4,1,1,64,128]{4,3,2,1,0:T(8,128)} %param.16) | copy-start | bytes 393220
  0.7 84.2 %copy-start.9 = (s32[32]{0:T(128)S(1)}, s32[32]{0:T(128)}, u32[]{:S(2)}) copy-start(s32[32]{0:T(128)} %param.15) | copy-start | bytes 388
  0.7 84.2 %copy-start.6 = (s32[1,1,64,128]{3,2,1,0:T(8,128)S(1)}, s32[1,1,64,128]{3,2,1,0:T(8,128)}, u32[]{:S(2)}) copy-start(s32[1,1,64,128]{3,2,1,0:T(8,128)} %param.21) | copy-start | bytes 98308
  0.7 84.2 %copy-start.10 = (s32[32]{0:T(128)S(1)}, s32[32]{0:T(128)}, u32[]{:S(2)}) copy-start(s32[32]{0:T(128)} %param.14) | copy-start | bytes 388
  0.7 105.1 %copy-start.1 = (f32[8,16,512]{2,1,0:T(8,128)S(1)}, f32[8,16,512]{2,1,0:T(8,128)}, u32[]{:S(2)}) copy-start(f32[8,16,512]{2,1,0:T(8,128)} %param.12) | copy-start | bytes 786436
  1.9 83.1 %collective-permute-start = (f32[4,1,16,512]{3,2,1,0:T(8,128)S(1)}, f32[4,1,16,512]{3,2,1,0:T(8,128)S(1)}, u32[]{:S(2)}, u32[]{:S(2)}) collective-permute-start(f32[4,1,16,512]{3,2,1,0:T(8,128)S(1)} %get-tuple-element.33), channel_id=1, source_target_pairs={{64,0},{128,64},{192,128},{65,1},{129,65},{193,129},{66,2},{130,66... | collective-permute-start | bytes 393224 | tf_op jit(solution)/shard_map/ppermute | solution.py:20
  3.8 81.3 %collective-permute-start.1 = (f32[4,1,16,512]{3,2,1,0:T(8,128)S(1)}, f32[4,1,16,512]{3,2,1,0:T(8,128)S(1)}, u32[]{:S(2)}, u32[]{:S(2)}) collective-permute-start(f32[4,1,16,512]{3,2,1,0:T(8,128)S(1)} %get-tuple-element.32), channel_id=1, source_target_pairs={{0,64},{64,128},{128,192},{1,65},{65,129},{129,193},{2,66},{66,130... | collective-permute-start | bytes 393224 | tf_op jit(solution)/shard_map/ppermute | solution.py:18
  71.7 78.2 %all-to-all-start = ((f32[12,1,1,64,128]{4,2,1,0,3:T(1,128)}), f32[12,1,1,64,128]{4,2,1,0,3:T(1,128)S(1)}, u32[]{:S(2)}, u32[]{:S(2)}) async-start(f32[12,1,1,64,128]{4,2,1,0,3:T(1,128)} %copy.136), calls=%async_computation | async-start | bytes 786432 | tf_op jit(solution)/shard_map/all_to_all | solution.py:75
  85.4 10.3 %collective-permute-start.2 = (f32[4,10,1,512]{3,1,2,0:T(8,128)S(1)}, f32[4,10,1,512]{3,1,2,0:T(8,128)S(1)}, u32[]{:S(2)}, u32[]{:S(2)}) collective-permute-start(f32[4,10,1,512]{3,1,2,0:T(8,128)S(1)} %get-tuple-element.21), channel_id=1, source_target_pairs={{1,0},{2,1},{3,2},{4,3},{5,4},{6,5},{7,6},{8,7},{9,8},{10,9},{11,1... | collective-permute-start | bytes 245768 | tf_op jit(solution)/shard_map/ppermute | solution.py:20
  92.3 12.6 %collective-permute-start.3 = (f32[4,10,1,512]{3,1,2,0:T(8,128)S(1)}, f32[4,10,1,512]{3,1,2,0:T(8,128)S(1)}, u32[]{:S(2)}, u32[]{:S(2)}) collective-permute-start(f32[4,10,1,512]{3,1,2,0:T(8,128)S(1)} %get-tuple-element.20), channel_id=1, source_target_pairs={{0,1},{1,2},{2,3},{3,4},{4,5},{5,6},{6,7},{7,8},{8,9},{9,10},{10,1... | collective-permute-start | bytes 245768 | tf_op jit(solution)/shard_map/ppermute | solution.py:18
  107.8 4.7 %collective-permute-start.4 = (f32[4,1,16,512]{3,2,1,0:T(8,128)S(1)}, f32[4,1,16,512]{3,2,1,0:T(8,128)S(1)}, u32[]{:S(2)}, u32[]{:S(2)}) collective-permute-start(f32[4,1,16,512]{3,2,1,0:T(8,128)S(1)} %copy.125), channel_id=1, source_target_pairs={{64,0},{128,64},{192,128},{65,1},{129,65},{193,129},{66,2},{130,66... | collective-permute-start | bytes 393224 | tf_op jit(solution)/shard_map/ppermute | solution.py:20
  109.8 6.3 %collective-permute-start.5 = (f32[4,1,16,512]{3,2,1,0:T(8,128)S(1)}, f32[4,1,16,512]{3,2,1,0:T(8,128)S(1)}, u32[]{:S(2)}, u32[]{:S(2)}) collective-permute-start(f32[4,1,16,512]{3,2,1,0:T(8,128)S(1)} %copy.127), channel_id=1, source_target_pairs={{0,64},{64,128},{128,192},{1,65},{65,129},{129,193},{2,66},{66,130... | collective-permute-start | bytes 393224 | tf_op jit(solution)/shard_map/ppermute | solution.py:18
  116.2 8.4 %collective-permute-start.6 = (f32[4,10,1,512]{3,1,2,0:T(8,128)S(1)}, f32[4,10,1,512]{3,1,2,0:T(8,128)S(1)}, u32[]{:S(2)}, u32[]{:S(2)}) collective-permute-start(f32[4,10,1,512]{3,1,2,0:T(8,128)S(1)} %get-tuple-element.17), channel_id=1, source_target_pairs={{1,0},{2,1},{3,2},{4,3},{5,4},{6,5},{7,6},{8,7},{9,8},{10,9},{11,1... | collective-permute-start | bytes 245768 | tf_op jit(solution)/shard_map/ppermute | solution.py:20
  118.2 12.6 %collective-permute-start.7 = (f32[4,10,1,512]{3,1,2,0:T(8,128)S(1)}, f32[4,10,1,512]{3,1,2,0:T(8,128)S(1)}, u32[]{:S(2)}, u32[]{:S(2)}) collective-permute-start(f32[4,10,1,512]{3,1,2,0:T(8,128)S(1)} %get-tuple-element.16), channel_id=1, source_target_pairs={{0,1},{1,2},{2,3},{3,4},{4,5},{5,6},{6,7},{7,8},{8,9},{9,10},{10,1... | collective-permute-start | bytes 245768 | tf_op jit(solution)/shard_map/ppermute | solution.py:18

commit v2 on v0

v2 whole, which is shorter than its diff:
```python
import functools

import jax
import jax.numpy as jnp
from jax import lax
from jax.experimental import pallas as pl
from jax.experimental.pallas import tpu as pltpu

from jax.sharding import PartitionSpec as P

VM = pl.BlockSpec(memory_space=pltpu.VMEM)
SM = pl.BlockSpec(memory_space=pltpu.SMEM)


def halves(value):
    high = value.astype(jnp.bfloat16)
    low = (value - high.astype(jnp.float32)).astype(jnp.bfloat16)
    return high, low


def column_hot(cells, depth):
    at = lax.broadcasted_iota(jnp.int32, (depth, cells.shape[1]), 0)
    return jnp.where(at == (cells & (depth - 1)), 1.0, 0.0).astype(jnp.bfloat16)


def slip_kernel(GP, counts, flow, anchor, state, rate, mass, ports, out, table):
    comps, partners, cap = state.shape
    total, depth = flow.shape
    rows = total // comps
    shift = depth.bit_length() - 1
    high, low = halves(flow[...])
    table[0:total] = high
    table[total:] = low
    lane = lax.broadcasted_iota(jnp.int32, (1, cap), 1)

    def group(g, carry):
        first = g * GP
        cells = jnp.concatenate([anchor[pl.ds(first + i, 1), :] for i in range(GP)], axis=1)
        hot = column_hot(cells, depth)
        picked = jnp.dot(table[...], hot, preferred_element_type=jnp.float32)
        row = lax.broadcasted_iota(jnp.int32, (rows, cells.shape[1]), 0) == (cells >> shift)
        parts = []
        for c in range(comps):
            both = picked[c * rows : (c + 1) * rows] + picked[total + c * rows : total + (c + 1) * rows]
            parts.append(jnp.sum(jnp.where(row, both, 0.0), axis=0, keepdims=True))
        sampled = jnp.concatenate(parts, axis=0)
        for i in range(GP):
            p = first + i
            live = jnp.where(lane < counts[p], 1.0, 0.0)
            own = jnp.concatenate([state[c, pl.ds(p, 1), :] for c in range(comps)], axis=0)
            r = rate[pl.ds(p, 1), :]
            slip = own - sampled[:, i * cap : (i + 1) * cap]
            out[3 * p] = live * (own - r * slip)
            out[3 * p + 1] = (live * mass[pl.ds(p, 1), :] * r) * slip
            out[3 * p + 2] = ports[...]
        return carry

    lax.fori_loop(0, partners // GP, group, 0)


def slip(counts, flow, anchor, state, rate, mass, ports, GP=4):
    comps, partners, cap = state.shape
    return pl.pallas_call(
        functools.partial(slip_kernel, GP),
        out_shape=jax.ShapeDtypeStruct((partners * 3, comps, cap), jnp.float32),
        in_specs=[SM] + [VM] * 6,
        out_specs=VM,
        scratch_shapes=[pltpu.VMEM((2 * flow.shape[0], flow.shape[1]), jnp.bfloat16)],
        compiler_params=pltpu.CompilerParams(vmem_limit_bytes=48 * 1024 * 1024),
        cost_estimate=pl.CostEstimate(flops=2 * 8192 * 512 * 1024, bytes_accessed=2**21, transcendentals=0),
        name="slip",
    )(counts, flow, anchor, state, rate, mass, ports)


def land_kernel(GP, match, second, inlet_now, inlet, arrival, arrived, flow_out, state_out, rows_ref, total_ref):
    comps, partners, cap = state_out.shape
    total, depth = second.shape
    rows = total // comps
    shift = depth.bit_length() - 1
    entries = match.shape[0]
    per = cap // comps
    nt = (((1,), (1,)), ((), ()))

    def spread(cells, values):
        row = lax.broadcasted_iota(jnp.int32, (rows, cells.shape[1]), 0) == (cells >> shift)
        high, low = halves(values)
        parts = []
        for part in (high.astype(jnp.float32), low.astype(jnp.float32)):
            for c in range(comps):
                parts.append(jnp.where(row, part[c : c + 1], 0.0).astype(jnp.bfloat16))
        return jnp.concatenate(parts, axis=0)

    def product(cells, values):
        both = lax.dot_general(spread(cells, values), column_hot(cells, depth), nt, preferred_element_type=jnp.float32)
        return both[:total] + both[total:]

    rows_ref[...] = jnp.zeros_like(rows_ref)
    for k in range(entries):
        port = match[k]
        device = port // entries
        rows_ref[k : k + 1, :] = arrived[3 * (device % partners) + 2, pl.ds(device // partners, 1), :]
    turned = rows_ref[...].T
    slot = lax.broadcasted_iota(jnp.int32, (1, cap), 1)
    which = inlet[1:2, :] % entries
    pick = lax.broadcasted_iota(jnp.int32, (per, cap), 0) == which
    target = jnp.concatenate(
        [jnp.sum(jnp.where(pick, turned[c * per : (c + 1) * per], 0.0), axis=0, keepdims=True) for c in range(comps)], axis=0
    )
    change = jnp.where(slot < entries, 0.5 * (target - inlet_now[...]), 0.0)
    flow_out[...] = second[...] + product(inlet[0:1, :], change)

    def group(g, carry):
        first = g * GP
        cells = jnp.concatenate([arrival[pl.ds(first + i, 1), :] for i in range(GP)], axis=1)
        values = jnp.concatenate([arrived[3 * (first + i) + 1] for i in range(GP)], axis=1)
        flow_out[...] += product(cells, values)
        for i in range(GP):
            p = first + i
            moved = arrived[3 * p]
            for c in range(comps):
                state_out[c, pl.ds(p, 1), :] = moved[c : c + 1]
        return carry

    lax.fori_loop(0, partners // GP, group, 0)


def land(match, second, inlet_now, inlet, arrival, arrived, GP=8):
    partners, cap = arrival.shape
    comps = arrived.shape[1]
    return pl.pallas_call(
        functools.partial(land_kernel, GP),
        out_shape=(
            jax.ShapeDtypeStruct(second.shape, jnp.float32),
            jax.ShapeDtypeStruct((comps, partners, cap), jnp.float32),
        ),
        in_specs=[SM] + [VM] * 5,
        out_specs=(VM, VM),
        scratch_shapes=[pltpu.VMEM((cap, cap), jnp.float32), pltpu.VMEM((8, 128), jnp.float32)],
        compiler_params=pltpu.CompilerParams(vmem_limit_bytes=48 * 1024 * 1024),
        cost_estimate=pl.CostEstimate(flops=2 * 8192 * 512 * 1024, bytes_accessed=2**21, transcendentals=0),
        name="land",
    )(match, second, inlet_now, inlet, arrival, arrived)


def edge_kernel(comps, depth_z, width, flow, viscosity, low_out, high_out):
    for k in range(comps * depth_z):
        low_out[2 * k : 2 * k + 2, :] = flow[k * width : k * width + 2, :]
        high_out[2 * k : 2 * k + 2, :] = flow[(k + 1) * width - 2 : (k + 1) * width, :]
    base = 2 * comps * depth_z
    for z in range(depth_z):
        low_out[base + z : base + z + 1, :] = viscosity[z * width : z * width + 1, :]
        high_out[base + z : base + z + 1, :] = viscosity[(z + 1) * width - 1 : (z + 1) * width, :]


def edges(comps, depth_z, width, flow, viscosity):
    shape = jax.ShapeDtypeStruct(((2 * comps + 1) * depth_z, flow.shape[1]), jnp.float32)
    return pl.pallas_call(
        functools.partial(edge_kernel, comps, depth_z, width),
        out_shape=(shape, shape),
        in_specs=[VM] * 2,
        out_specs=(VM, VM),
        name="edges",
    )(flow, viscosity)


def side_tile(tile, left, right, k, reach):
    tile[...] = jnp.zeros_like(tile)
    tile[0:reach, :] = right[2 * k : 2 * k + reach, :]
    tile[8 - reach : 8, :] = left[2 * k + 2 - reach : 2 * k + 2, :]


def cap_kernel(comps, depth_z, width, flow, viscosity, left, right, low_out, high_out, tile):
    per = 2 * width + 8
    for c in range(comps):
        for out, near, far in ((low_out, 0, 1), (high_out, depth_z - 1, depth_z - 2)):
            k = c * depth_z + near
            out[c * per : c * per + width, :] = flow[k * width : (k + 1) * width, :]
            side_tile(tile, left, right, k, 1)
            out[c * per + width : c * per + width + 8, :] = tile[...]
            k = c * depth_z + far
            out[c * per + width + 8 : (c + 1) * per, :] = flow[k * width : (k + 1) * width, :]
    low_out[comps * per :, :] = viscosity[0:width, :]
    high_out[comps * per :, :] = viscosity[(depth_z - 1) * width : depth_z * width, :]


def caps(comps, depth_z, width, flow, viscosity, left, right):
    shape = jax.ShapeDtypeStruct((comps * (2 * width + 8) + width, flow.shape[1]), jnp.float32)
    return pl.pallas_call(
        functools.partial(cap_kernel, comps, depth_z, width),
        out_shape=(shape, shape),
        in_specs=[VM] * 4,
        out_specs=(VM, VM),
        scratch_shapes=[pltpu.VMEM((8, flow.shape[1]), jnp.float32)],
        name="caps",
    )(flow, viscosity, left, right)


def stencil_kernel(comps, depth_z, width, flow, viscosity, left, right, below, above, inlet, second_out, inlet_now, state, first, visc, table):
    depth = flow.shape[1]
    per = 2 * width + 8
    total = comps * depth_z * width
    rows = depth_z * width
    wide = width + 8
    base = 2 * comps * depth_z
    blank = jnp.zeros((8, depth), jnp.float32)
    for c in range(comps):
        for z in range(depth_z):
            k = c * depth_z + z
            state[c, z + 2, 0:width, :] = flow[k * width : (k + 1) * width, :]
            state[c, z + 2, width:wide, :] = blank
            state[c, z + 2, width : width + 2, :] = right[2 * k : 2 * k + 2, :]
            state[c, z + 2, wide - 2 : wide, :] = left[2 * k : 2 * k + 2, :]
        for near, far, source in ((1, 0, below), (depth_z + 2, depth_z + 3, above)):
            state[c, near] = source[c * per : c * per + wide, :]
            state[c, far, 0:width, :] = source[c * per + wide : (c + 1) * per, :]
            state[c, far, width:wide, :] = blank
    for z in range(depth_z):
        visc[z + 1, 0:width, :] = viscosity[z * width : (z + 1) * width, :]
        visc[z + 1, width:wide, :] = blank
        visc[z + 1, width : width + 1, :] = right[base + z : base + z + 1, :]
        visc[z + 1, wide - 1 : wide, :] = left[base + z : base + z + 1, :]
    for z, source in ((0, below), (depth_z + 1, above)):
        visc[z, 0:width, :] = source[comps * per :, :]
        visc[z, width:wide, :] = blank

    place = lax.broadcasted_iota(jnp.int32, (1, depth), 1)

    def tendency(ref, z, eddy_base, keep):
        centers, laps, dz, dx, dy = [], [], [], [], []
        for c in range(comps):
            plane = ref[c, z]
            center = plane[:keep]
            up_x = pltpu.roll(plane, wide - 1, 0)[:keep]
            low_x = pltpu.roll(plane, 1, 0)[:keep]
            up_y = jnp.where(place == depth - 1, 0.0, pltpu.roll(center, depth - 1, 1))
            low_y = jnp.where(place == 0, 0.0, pltpu.roll(center, 1, 1))
            up_z = ref[c, z + 1, 0:keep, :]
            low_z = ref[c, z - 1, 0:keep, :]
            centers.append(center)
            laps.append((up_z + low_z) + (up_x + low_x) + (up_y + low_y) - 6.0 * center)
            dz.append(up_z - low_z)
            dx.append(up_x - low_x)
            dy.append(up_y - low_y)
        strain = sum(d[c] * d[c] for c in range(3) for d in (dz, dx, dy)) * 0.25
        eddy = eddy_base * (1.0 + strain / (1.0 + strain))
        out = []
        for c in range(comps):
            carried = centers[0] * dz[c] + centers[1] * dx[c] + centers[2] * dy[c]
            out.append(0.5 * (eddy * laps[c]) - 0.25 * carried)
        return centers, out

    def one(z, carry):
        centers, change = tendency(state, z + 1, visc[z], wide)
        for c in range(comps):
            first[c, z] = centers[c] + change[c]
        return carry

    lax.fori_loop(0, depth_z + 2, one, 0)

    def two(z, carry):
        centers, change = tendency(first, z + 1, visc[z + 1, 0:width, :], width)
        for c in range(comps):
            value = 0.5 * state[c, z + 2, 0:width, :] + 0.5 * (centers[c] + change[c])
            spot = pl.multiple_of((c * depth_z + z) * width, width)
            second_out[pl.ds(spot, width), :] = value
            high, low = halves(value)
            table[pl.ds(spot, width), :] = high
            table[pl.ds(total + spot, width), :] = low
        return carry

    lax.fori_loop(0, depth_z, two, 0)

    cells = inlet[0:1, :]
    picked = jnp.dot(table[...], column_hot(cells, depth), preferred_element_type=jnp.float32)
    row = lax.broadcasted_iota(jnp.int32, (rows, cells.shape[1]), 0) == (cells >> (depth.bit_length() - 1))
    for c in range(comps):
        both = picked[c * rows : (c + 1) * rows] + picked[total + c * rows : total + (c + 1) * rows]
        inlet_now[c : c + 1, :] = jnp.sum(jnp.where(row, both, 0.0), axis=0, keepdims=True)


def stencil(comps, depth_z, width, flow, viscosity, left, right, below, above, inlet):
    depth = flow.shape[1]
    wide = width + 8
    return pl.pallas_call(
        functools.partial(stencil_kernel, comps, depth_z, width),
        out_shape=(
            jax.ShapeDtypeStruct(flow.shape, jnp.float32),
            jax.ShapeDtypeStruct((comps, inlet.shape[1]), jnp.float32),
        ),
        in_specs=[VM] * 7,
        out_specs=(VM, VM),
        scratch_shapes=[
            pltpu.VMEM((comps, depth_z + 4, wide, depth), jnp.float32),
            pltpu.VMEM((comps, depth_z + 2, wide, depth), jnp.float32),
            pltpu.VMEM((depth_z + 2, wide, depth), jnp.float32),
            pltpu.VMEM((2 * flow.shape[0], depth), jnp.bfloat16),
        ],
        compiler_params=pltpu.CompilerParams(vmem_limit_bytes=48 * 1024 * 1024),
        cost_estimate=pl.CostEstimate(flops=2 * 10**7, bytes_accessed=2**22, transcendentals=0),
        name="stencil",
    )(flow, viscosity, left, right, below, above, inlet)


def on_device(
    flow_field,
    viscosity,
    port_plane,
    port_match,
    inlet_cell,
    inclusion_state,
    response_rate,
    inclusion_mass,
    anchor_cell,
    live_counts,
    arrival_cell,
):
    comps, depth_z, width, depth = flow_field.shape
    partners, cap = anchor_cell.shape[2:]
    sizes = (comps, depth_z, width)
    flow = flow_field.reshape(-1, depth)
    visc = viscosity.reshape(-1, depth)
    count = lax.axis_size("tile")
    forth = [(i, i + 1) for i in range(count - 1)]
    back = [(i + 1, i) for i in range(count - 1)]
    levels = lax.axis_size("sec")
    up = [(i, i + 1) for i in range(levels - 1)]
    down = [(i + 1, i) for i in range(levels - 1)]

    ports = lax.all_gather(port_plane.reshape(1, -1), "sec", axis=0, tiled=True)
    low_edge, high_edge = edges(*sizes, flow, visc)
    left = lax.ppermute(high_edge, "tile", forth)
    right = lax.ppermute(low_edge, "tile", back)
    outgoing = slip(
        live_counts.reshape(-1),
        flow,
        anchor_cell.reshape(partners, cap),
        inclusion_state.reshape(comps, partners, cap),
        response_rate.reshape(partners, cap),
        inclusion_mass.reshape(partners, cap),
        ports,
    )
    arrived = lax.all_to_all(outgoing, "tile", split_axis=0, concat_axis=0, tiled=True)
    low_cap, high_cap = caps(*sizes, flow, visc, left, right)
    below = lax.ppermute(high_cap, "sec", up)
    above = lax.ppermute(low_cap, "sec", down)
    inlet = jnp.pad(jnp.stack([inlet_cell, port_match]), ((0, 0), (0, cap - inlet_cell.shape[0])))
    second, inlet_now = stencil(*sizes, flow, visc, left, right, below, above, inlet)
    flow_next, arrived_state = land(
        port_match, second, inlet_now, inlet, arrival_cell.reshape(partners, cap), arrived
    )
    return flow_next.reshape(flow_field.shape), arrived_state.reshape(inclusion_state.shape)


def solution(mesh):
    return jax.shard_map(
        on_device,
        mesh=mesh,
        in_specs=(
            P(None, "sec", "tile", None),
            P("sec", "tile", None),
            P(None, ("sec", "tile")),
            P(("sec", "tile")),
            P(("sec", "tile")),
            P(None, "sec", "tile", None, None),
            P("sec", "tile", None, None),
            P("sec", "tile", None, None),
            P("sec", "tile", None, None),
            P("sec", "tile", None),
            P("sec", "tile", None, None),
        ),
        out_specs=(P(None, "sec", "tile", None), P(None, "sec", "tile", None, None)),
        check_vma=False,
    )
```

time: 1010 us -> 92.8 us (0.09)
  the two profiles are of different devices: /device:TPU:126 before, /device:TPU:1 now
where the time goes in v2:
time: 92.8 us; the launch traced here: 91.5 us
  Pallas kernels  34.9 us (38%)
  starting transfers between devices  23.6 us (25%)
  waiting for transfers between devices  15.2 us (16%)
  local copies, waits for them, and re-layouts  8.99 us (10%)
  blocking collectives  8.06 us (9%)
    pallas_call x1, Pallas kernels, slip(): pl.pallas_call(functools.partial(slip_kernel, GP), out_shape=jax.ShapeDty...  13 us
    pallas_call x1, Pallas kernels, land(): pl.pallas_call(functools.partial(land_kernel, GP), out_shape=(jax.ShapeDt...  12.7 us
    all_to_all x1, starting transfers between devices, on_device(): lax.all_to_all(outgoing, 'tile', split_axis=0, concat_axis=0, tiled=True)  12.6 us
    unnamed x31, local copies, waits for them, and re-layouts  8.98 us
    all_gather x1, blocking collectives, on_device(): ports = lax.all_gather(port_plane.reshape(1, -1), 'sec', axis=0, tiled=True)  8.06 us
    ppermute x1, waiting for transfers between devices, on_device(): right = lax.ppermute(low_edge, 'tile', back)  5.92 us
    pallas_call x1, Pallas kernels, stencil(): pl.pallas_call(functools.partial(stencil_kernel, comps, depth_z, width),...  4.78 us
    ppermute x1, starting transfers between devices, on_device(): left = lax.ppermute(high_edge, 'tile', forth)  4.55 us
  transfers between devices with their start and end apart: 5, of which 4 were waited for; matrix products, arithmetic and copies ran while one was open for 0% of the time, Pallas kernels for 10%

profile of v2, /device:TPU:1, one launch (start us, length us, event | category | flops | bytes accessed | tf_op | source)
XLA Modules:
  0.0 91.5 jit_solution(13222080890206326516)
XLA Ops:
  0.6 0.8 reshape.48
  1.4 8.1 %all-gather = f32[4,1,128]{2,1,0:T(1,128)S(1)} all-gather(f32[1,1,128]{2,1,0:T(1,128)S(1)} %reshape.48), channel_id=1, replica_groups=mesh['sec'=4,'tile'=64] {'sec'}, dimensions={0}, use_global_device_ids=true | all-gather | bytes 2560 | tf_op jit(solution)/shard_map/all_gather | solution.py:329
  10.1 1.2 %copy-done = f32[4,8,16,512]{3,2,1,0:T(8,128)S(1)} copy-done((f32[4,8,16,512]{3,2,1,0:T(8,128)S(1)}, f32[4,8,16,512]{3,2,1,0:T(8,128)}, u32[]{:S(2)}) %copy-start) | copy-done | bytes 1048600
  11.3 0.9 copy-done.8
  12.2 0.8 copy-done.9
  13.0 0.8 copy-done.10
  13.8 0.8 copy-done.11
  14.5 13.0 %slip.1 = f32[192,4,128]{2,1,0:T(4,128)} custom-call(s32[64]{0:T(128)S(1)} %bitcast.29, f32[512,512]{1,0:T(8,128)S(1)} %bitcast.17, s32[64,128]{1,0:T(8,128)S(1)} %bitcast.25, f32[4,64,128]{2,1,0:T(8,128)S(1)} %bitcast.24, f32[64,128]{1,0:T(8,128)S(1)} %bitcast.26, f32[64,128]{1,0:T(8,128)S(1)} %bitcast.27, f32[4,128]{1,0:T(4,128)S(1)} %bitcast.22), custom_call_target="tpu_custom_call" | custom-call | flops 8589934592 | bytes 2097152 | tf_op jit(solution)/shard_map/slip/pallas_call | solution.py:63
  27.5 12.6 %all-to-all-start = ((f32[192,4,128]{2,1,0:T(4,128)}), f32[192,4,128]{2,1,0:T(4,128)S(1)}, u32[]{:S(2)}, u32[]{:S(2)}) async-start(f32[192,4,128]{2,1,0:T(4,128)} %slip.1), calls=%async_computation | async-start | bytes 786432 | tf_op jit(solution)/shard_map/all_to_all | solution.py:342
  40.1 2.1 %edges.1 = (f32[72,512]{1,0:T(8,128)}, f32[72,512]{1,0:T(8,128)}) custom-call(f32[512,512]{1,0:T(8,128)} %bitcast.15, f32[128,512]{1,0:T(8,128)} %bitcast.19), custom_call_target="tpu_custom_call" | custom-call | tf_op jit(solution)/shard_map/edges/pallas_call | solution.py:157
  42.2 4.5 %collective-permute-start = (f32[72,512]{1,0:T(8,128)}, f32[72,512]{1,0:T(8,128)S(1)}, u32[]{:S(2)}, u32[]{:S(2)}) collective-permute-start(f32[72,512]{1,0:T(8,128)} %get-tuple-element.10), channel_id=1, source_target_pairs={{0,1},{1,2},{2,3},{3,4},{4,5},{5,6},{6,7},{7,8},{8,9},{9,10},{10,1... | collective-permute-start | bytes 442376 | tf_op jit(solution)/shard_map/ppermute | solution.py:331
  46.8 1.4 %collective-permute-start.1 = (f32[72,512]{1,0:T(8,128)}, f32[72,512]{1,0:T(8,128)S(1)}, u32[]{:S(2)}, u32[]{:S(2)}) collective-permute-start(f32[72,512]{1,0:T(8,128)} %get-tuple-element.11), channel_id=1, source_target_pairs={{1,0},{2,1},{3,2},{4,3},{5,4},{6,5},{7,6},{8,7},{9,8},{10,9},{11,1... | collective-permute-start | bytes 442376 | tf_op jit(solution)/shard_map/ppermute | solution.py:332
  48.2 2.9 %collective-permute-done.left = f32[72,512]{1,0:T(8,128)S(1)} collective-permute-done((f32[72,512]{1,0:T(8,128)}, f32[72,512]{1,0:T(8,128)S(1)}, u32[]{:S(2)}, u32[]{:S(2)}) %collective-permute-start) | collective-permute-done | bytes 147488 | tf_op jit(solution)/shard_map/ppermute | solution.py:331
  51.1 5.9 %collective-permute-done.1.right = f32[72,512]{1,0:T(8,128)S(1)} collective-permute-done((f32[72,512]{1,0:T(8,128)}, f32[72,512]{1,0:T(8,128)S(1)}, u32[]{:S(2)}, u32[]{:S(2)}) %collective-permute-start.1) | collective-permute-done | bytes 147488 | tf_op jit(solution)/shard_map/ppermute | solution.py:332
  57.0 0.7 copy-done.5
  57.7 2.3 %caps.1 = (f32[176,512]{1,0:T(8,128)}, f32[176,512]{1,0:T(8,128)}) custom-call(f32[512,512]{1,0:T(8,128)} %bitcast.16, f32[128,512]{1,0:T(8,128)} %bitcast.20, f32[72,512]{1,0:T(8,128)} %copy-done.3, f32[72,512]{1,0:T(8,128)} %copy-done.5), custom_call_target="tpu_custom_call" | custom-call | tf_op jit(solution)/shard_map/caps/pallas_call | solution.py:188
  60.0 3.2 %collective-permute-start.2 = (f32[176,512]{1,0:T(8,128)}, f32[176,512]{1,0:T(8,128)S(1)}, u32[]{:S(2)}, u32[]{:S(2)}) collective-permute-start(f32[176,512]{1,0:T(8,128)} %get-tuple-element.12), channel_id=1, source_target_pairs={{0,64},{64,128},{128,192},{1,65},{65,129},{129,193},{2,66},{66,130... | collective-permute-start | bytes 1081352 | tf_op jit(solution)/shard_map/ppermute | solution.py:344
  63.2 1.9 %collective-permute-start.3 = (f32[176,512]{1,0:T(8,128)}, f32[176,512]{1,0:T(8,128)S(1)}, u32[]{:S(2)}, u32[]{:S(2)}) collective-permute-start(f32[176,512]{1,0:T(8,128)} %get-tuple-element.13), channel_id=1, source_target_pairs={{64,0},{128,64},{192,128},{65,1},{129,65},{193,129},{66,2},{130,66... | collective-permute-start | bytes 1081352 | tf_op jit(solution)/shard_map/ppermute | solution.py:345
  65.8 2.0 %collective-permute-done.2.below = f32[176,512]{1,0:T(8,128)S(1)} collective-permute-done((f32[176,512]{1,0:T(8,128)}, f32[176,512]{1,0:T(8,128)S(1)}, u32[]{:S(2)}, u32[]{:S(2)}) %collective-permute-start.2) | collective-permute-done | bytes 360480 | tf_op jit(solution)/shard_map/ppermute | solution.py:344
  67.8 4.3 %collective-permute-done.3.above = f32[176,512]{1,0:T(8,128)S(1)} collective-permute-done((f32[176,512]{1,0:T(8,128)}, f32[176,512]{1,0:T(8,128)S(1)}, u32[]{:S(2)}, u32[]{:S(2)}) %collective-permute-start.3) | collective-permute-done | bytes 360480 | tf_op jit(solution)/shard_map/ppermute | solution.py:345
  72.1 0.9 copy-done.4
  73.1 0.9 copy-done.6
  74.0 4.8 %stencil.1 = (f32[512,512]{1,0:T(8,128)S(1)}, f32[4,128]{1,0:T(4,128)S(1)}) custom-call(f32[512,512]{1,0:T(8,128)S(1)} %bitcast.18, f32[128,512]{1,0:T(8,128)S(1)} %bitcast.21, f32[72,512]{1,0:T(8,128)S(1)} %copy-done.4, f32[72,512]{1,0:T(8,128)S(1)} %copy-done.6, f32[176,512]{1,0:T(8,128)S(1)} %collective-permute-done.2.below, ...), custom_call_target="tpu_custom_call" | custom-call | flops 20000000 | bytes 4194304 | tf_op jit(solution)/shard_map/stencil/pallas_call | solution.py:284
  78.8 12.7 %land.1 = (f32[512,512]{1,0:T(8,128)}, f32[4,64,128]{2,1,0:T(8,128)}) custom-call(s32[32]{0:T(128)S(1)} %copy-done.7, f32[512,512]{1,0:T(8,128)S(1)} %get-tuple-element.14.second, f32[4,128]{1,0:T(4,128)S(1)} %get-tuple-element.15.inlet_now, s32[2,128]{1,0:T(2,128)S(1)} %pad.4.inlet, s32[64,128]{1,0:T(8,128)S(1)} %bitcast.28, ...), custom_call_target="tpu_custom_call" | custom-call | flops 8589934592 | bytes 2097152 | tf_op jit(solution)/shard_map/land/pallas_call | solution.py:130
  (25 shorter events, 1.4 us)
Async XLA Ops:
  9.5 0.7 copy-start.13
  10.1 1.2 %copy-start = (f32[4,8,16,512]{3,2,1,0:T(8,128)S(1)}, f32[4,8,16,512]{3,2,1,0:T(8,128)}, u32[]{:S(2)}) copy-start(f32[4,8,16,512]{3,2,1,0:T(8,128)} %param.11) | copy-start | bytes 3145732
  11.3 0.9 copy-start.8
  12.2 0.8 copy-start.9
  13.0 0.8 copy-start.10
  13.8 0.8 copy-start.11
  27.5 51.2 %all-to-all-start = ((f32[192,4,128]{2,1,0:T(4,128)}), f32[192,4,128]{2,1,0:T(4,128)S(1)}, u32[]{:S(2)}, u32[]{:S(2)}) async-start(f32[192,4,128]{2,1,0:T(4,128)} %slip.1), calls=%async_computation | async-start | bytes 786432 | tf_op jit(solution)/shard_map/all_to_all | solution.py:342
  42.2 29.9 %copy-start.1 = (f32[4,8,16,512]{3,2,1,0:T(8,128)S(1)}, f32[4,8,16,512]{3,2,1,0:T(8,128)}, u32[]{:S(2)}) copy-start(f32[4,8,16,512]{3,2,1,0:T(8,128)} %param.11) | copy-start | bytes 3145732
  42.2 8.9 %collective-permute-start = (f32[72,512]{1,0:T(8,128)}, f32[72,512]{1,0:T(8,128)S(1)}, u32[]{:S(2)}, u32[]{:S(2)}) collective-permute-start(f32[72,512]{1,0:T(8,128)} %get-tuple-element.10), channel_id=1, source_target_pairs={{0,1},{1,2},{2,3},{3,4},{4,5},{5,6},{6,7},{7,8},{8,9},{9,10},{10,1... | collective-permute-start | bytes 442376 | tf_op jit(solution)/shard_map/ppermute | solution.py:331
  46.8 25.4 %copy-start.2 = (f32[8,16,512]{2,1,0:T(8,128)S(1)}, f32[8,16,512]{2,1,0:T(8,128)}, u32[]{:S(2)}) copy-start(f32[8,16,512]{2,1,0:T(8,128)} %param.12) | copy-start | bytes 786436
  46.8 10.3 %collective-permute-start.1 = (f32[72,512]{1,0:T(8,128)}, f32[72,512]{1,0:T(8,128)S(1)}, u32[]{:S(2)}, u32[]{:S(2)}) collective-permute-start(f32[72,512]{1,0:T(8,128)} %get-tuple-element.11), channel_id=1, source_target_pairs={{1,0},{2,1},{3,2},{4,3},{5,4},{6,5},{7,6},{8,7},{9,8},{10,9},{11,1... | collective-permute-start | bytes 442376 | tf_op jit(solution)/shard_map/ppermute | solution.py:332
  51.1 5.9 %copy-start.3 = (f32[72,512]{1,0:T(8,128)}, f32[72,512]{1,0:T(8,128)S(1)}, u32[]{:S(2)}) copy-start(f32[72,512]{1,0:T(8,128)S(1)} %collective-permute-done.left) | copy-start | bytes 442372
  57.0 0.7 copy-start.5
  60.0 7.9 %collective-permute-start.2 = (f32[176,512]{1,0:T(8,128)}, f32[176,512]{1,0:T(8,128)S(1)}, u32[]{:S(2)}, u32[]{:S(2)}) collective-permute-start(f32[176,512]{1,0:T(8,128)} %get-tuple-element.12), channel_id=1, source_target_pairs={{0,64},{64,128},{128,192},{1,65},{65,129},{129,193},{2,66},{66,130... | collective-permute-start | bytes 1081352 | tf_op jit(solution)/shard_map/ppermute | solution.py:344
  63.2 9.0 %collective-permute-start.3 = (f32[176,512]{1,0:T(8,128)}, f32[176,512]{1,0:T(8,128)S(1)}, u32[]{:S(2)}, u32[]{:S(2)}) collective-permute-start(f32[176,512]{1,0:T(8,128)} %get-tuple-element.13), channel_id=1, source_target_pairs={{64,0},{128,64},{192,128},{65,1},{129,65},{193,129},{66,2},{130,66... | collective-permute-start | bytes 1081352 | tf_op jit(solution)/shard_map/ppermute | solution.py:345
  65.1 0.7 copy-start.7
  65.1 0.7 copy-start.14
  72.1 0.9 copy-start.4
  73.1 0.9 copy-start.6
  74.0 4.8 %copy-start.12 = (s32[1,1,64,128]{3,2,1,0:T(8,128)S(1)}, s32[1,1,64,128]{3,2,1,0:T(8,128)}, u32[]{:S(2)}) copy-start(s32[1,1,64,128]{3,2,1,0:T(8,128)} %param.21) | copy-start | bytes 98308

commit v3 on v2

--- a/solution.py
+++ b/solution.py
@@ -5,11 +5,11 @@
 from jax import lax
 from jax.experimental import pallas as pl
 from jax.experimental.pallas import tpu as pltpu
-
 from jax.sharding import PartitionSpec as P
 
 VM = pl.BlockSpec(memory_space=pltpu.VMEM)
 SM = pl.BlockSpec(memory_space=pltpu.SMEM)
+HB = pl.BlockSpec(memory_space=pltpu.HBM)
 
 
 def halves(value):
@@ -23,19 +23,37 @@
     return jnp.where(at == (cells & (depth - 1)), 1.0, 0.0).astype(jnp.bfloat16)
 
 
-def slip_kernel(GP, counts, flow, anchor, state, rate, mass, ports, out, table):
+def slip_kernel(GP, counts, flow_far, anchor_far, state_far, rate_far, mass_far, ports, out, flow, anchor, state, rate, mass, table, packed, sampled, sems):
     comps, partners, cap = state.shape
     total, depth = flow.shape
     rows = total // comps
     shift = depth.bit_length() - 1
+    cap_shift = cap.bit_length() - 1
+    pairs = ((anchor_far, anchor), (flow_far, flow), (state_far, state), (rate_far, rate), (mass_far, mass))
+    copies = [pltpu.make_async_copy(far, near, sems.at[i]) for i, (far, near) in enumerate(pairs)]
+    for copy in copies:
+        copy.start()
+    lane = lax.broadcasted_iota(jnp.int32, (1, cap), 1)
+    packed[...] = jnp.zeros_like(packed)
+    copies[0].wait()
+
+    def pack(p, base):
+        begin = base & (cap - 1)
+        spot = base >> cap_shift
+        turned = pltpu.roll(anchor[pl.ds(p, 1), :], begin, 1)
+        pltpu.store(packed.at[pl.ds(spot, 1), :], turned, mask=lane >= begin)
+        pltpu.store(packed.at[pl.ds(spot + 1, 1), :], turned, mask=lane < begin)
+        return base + counts[p]
+
+    used = lax.fori_loop(0, partners, pack, 0, unroll=8)
+    copies[1].wait()
     high, low = halves(flow[...])
     table[0:total] = high
     table[total:] = low
-    lane = lax.broadcasted_iota(jnp.int32, (1, cap), 1)
 
     def group(g, carry):
         first = g * GP
-        cells = jnp.concatenate([anchor[pl.ds(first + i, 1), :] for i in range(GP)], axis=1)
+        cells = jnp.concatenate([packed[pl.ds(first + i, 1), :] for i in range(GP)], axis=1)
         hot = column_hot(cells, depth)
         picked = jnp.dot(table[...], hot, preferred_element_type=jnp.float32)
         row = lax.broadcasted_iota(jnp.int32, (rows, cells.shape[1]), 0) == (cells >> shift)
@@ -43,43 +61,80 @@
         for c in range(comps):
             both = picked[c * rows : (c + 1) * rows] + picked[total + c * rows : total + (c + 1) * rows]
             parts.append(jnp.sum(jnp.where(row, both, 0.0), axis=0, keepdims=True))
-        sampled = jnp.concatenate(parts, axis=0)
+        found = jnp.concatenate(parts, axis=0)
         for i in range(GP):
-            p = first + i
-            live = jnp.where(lane < counts[p], 1.0, 0.0)
-            own = jnp.concatenate([state[c, pl.ds(p, 1), :] for c in range(comps)], axis=0)
-            r = rate[pl.ds(p, 1), :]
-            slip = own - sampled[:, i * cap : (i + 1) * cap]
-            out[3 * p] = live * (own - r * slip)
-            out[3 * p + 1] = (live * mass[pl.ds(p, 1), :] * r) * slip
-            out[3 * p + 2] = ports[...]
+            sampled[first + i] = found[:, i * cap : (i + 1) * cap]
         return carry
 
-    lax.fori_loop(0, partners // GP, group, 0)
+    lax.fori_loop(0, (used + GP * cap - 1) // (GP * cap), group, 0)
+    for copy in copies[2:]:
+        copy.wait()
+
+    def finish(p, base):
+        n = counts[p]
+        begin = base & (cap - 1)
+        spot = base >> cap_shift
+        both = jnp.where(lane >= begin, sampled[spot], sampled[spot + 1])
+        value = pltpu.roll(both, (cap - begin) & (cap - 1), 1)
+        own = jnp.concatenate([state[c, pl.ds(p, 1), :] for c in range(comps)], axis=0)
+        r = rate[pl.ds(p, 1), :]
+        drop = r * (own - value)
+        live = lane < n
+        out[3 * p] = jnp.where(live, own - drop, 0.0)
+        out[3 * p + 1] = jnp.where(live, mass[pl.ds(p, 1), :] * drop, 0.0)
+        out[3 * p + 2] = ports[...]
+        return base + n
+
+    lax.fori_loop(0, partners, finish, 0, unroll=8)
 
 
 def slip(counts, flow, anchor, state, rate, mass, ports, GP=4):
     comps, partners, cap = state.shape
+    near = [pltpu.VMEM(x.shape, x.dtype) for x in (flow, anchor, state, rate, mass)]
     return pl.pallas_call(
         functools.partial(slip_kernel, GP),
         out_shape=jax.ShapeDtypeStruct((partners * 3, comps, cap), jnp.float32),
-        in_specs=[SM] + [VM] * 6,
+        in_specs=[SM] + [HB] * 5 + [VM],
         out_specs=VM,
-        scratch_shapes=[pltpu.VMEM((2 * flow.shape[0], flow.shape[1]), jnp.bfloat16)],
-        compiler_params=pltpu.CompilerParams(vmem_limit_bytes=48 * 1024 * 1024),
+        scratch_shapes=near
+        + [
+            pltpu.VMEM((2 * flow.shape[0], flow.shape[1]), jnp.bfloat16),
+            pltpu.VMEM((partners + 8, cap), jnp.int32),
+            pltpu.VMEM((partners + 8, comps, cap), jnp.float32),
+            pltpu.SemaphoreType.DMA((5,)),
+        ],
+        compiler_params=pltpu.CompilerParams(vmem_limit_bytes=60 * 1024 * 1024),
         cost_estimate=pl.CostEstimate(flops=2 * 8192 * 512 * 1024, bytes_accessed=2**21, transcendentals=0),
         name="slip",
     )(counts, flow, anchor, state, rate, mass, ports)
 
 
-def land_kernel(GP, match, second, inlet_now, inlet, arrival, arrived, flow_out, state_out, rows_ref, total_ref):
+def land_kernel(GP, match, second, inlet_now, inlet, arrival, arrived, flow_out, state_out, rows_ref, last_ref, last, packed, sem):
     comps, partners, cap = state_out.shape
     total, depth = second.shape
     rows = total // comps
     shift = depth.bit_length() - 1
+    cap_shift = cap.bit_length() - 1
     entries = match.shape[0]
     per = cap // comps
     nt = (((1,), (1,)), ((), ()))
+    slot = lax.broadcasted_iota(jnp.int32, (1, cap), 1)
+
+    def ends(p, carry):
+        moved = arrived[3 * p]
+        gift = arrived[3 * p + 1]
+        for c in range(comps):
+            state_out[c, pl.ds(p, 1), :] = moved[c : c + 1]
+        biggest = jnp.max(jnp.abs(gift), axis=0, keepdims=True)
+        last_ref[pl.ds(p, 1), :] = jnp.where(biggest > 0.0, slot + 1, 0)
+        return carry
+
+    lax.fori_loop(0, partners, ends, 0, unroll=8)
+    last_ref[partners:, :] = jnp.zeros_like(last_ref[partners:, :])
+    top = jnp.max(last_ref[...].T, axis=0, keepdims=True)
+    last_ref[0:1, :] = top
+    fetch = pltpu.make_async_copy(last_ref.at[0:1, :], last, sem)
+    fetch.start()
 
     def spread(cells, values):
         row = lax.broadcasted_iota(jnp.int32, (rows, cells.shape[1]), 0) == (cells >> shift)
@@ -100,7 +155,6 @@
         device = port // entries
         rows_ref[k : k + 1, :] = arrived[3 * (device % partners) + 2, pl.ds(device // partners, 1), :]
     turned = rows_ref[...].T
-    slot = lax.broadcasted_iota(jnp.int32, (1, cap), 1)
     which = inlet[1:2, :] % entries
     pick = lax.broadcasted_iota(jnp.int32, (per, cap), 0) == which
     target = jnp.concatenate(
@@ -108,23 +162,32 @@
     )
     change = jnp.where(slot < entries, 0.5 * (target - inlet_now[...]), 0.0)
     flow_out[...] = second[...] + product(inlet[0:1, :], change)
+    packed[...] = jnp.zeros_like(packed)
+    fetch.wait()
+
+    def pack(p, base):
+        begin = base & (cap - 1)
+        spot = base >> cap_shift
+        cells = arrival[pl.ds(p, 1), :].astype(jnp.float32)
+        both = jnp.concatenate([arrived[3 * p + 1], jnp.broadcast_to(cells, (8 - comps, cap))], axis=0)
+        turned = pltpu.roll(both, begin, 1)
+        wide = lax.broadcasted_iota(jnp.int32, (8, cap), 1)
+        pltpu.store(packed.at[spot], turned, mask=wide >= begin)
+        pltpu.store(packed.at[spot + 1], turned, mask=wide < begin)
+        return base + last[0, p]
+
+    used = lax.fori_loop(0, partners, pack, 0, unroll=8)
 
     def group(g, carry):
         first = g * GP
-        cells = jnp.concatenate([arrival[pl.ds(first + i, 1), :] for i in range(GP)], axis=1)
-        values = jnp.concatenate([arrived[3 * (first + i) + 1] for i in range(GP)], axis=1)
-        flow_out[...] += product(cells, values)
-        for i in range(GP):
-            p = first + i
-            moved = arrived[3 * p]
-            for c in range(comps):
-                state_out[c, pl.ds(p, 1), :] = moved[c : c + 1]
+        both = jnp.concatenate([packed[first + i] for i in range(GP)], axis=1)
+        flow_out[...] += product(both[comps : comps + 1].astype(jnp.int32), both[:comps])
         return carry
 
-    lax.fori_loop(0, partners // GP, group, 0)
-
-
-def land(match, second, inlet_now, inlet, arrival, arrived, GP=8):
+    lax.fori_loop(0, (used + GP * cap - 1) // (GP * cap), group, 0)
+
+
+def land(match, second, inlet_now, inlet, arrival, arrived, GP=4):
     partners, cap = arrival.shape
     comps = arrived.shape[1]
     return pl.pallas_call(
@@ -135,8 +198,14 @@
         ),
         in_specs=[SM] + [VM] * 5,
         out_specs=(VM, VM),
-        scratch_shapes=[pltpu.VMEM((cap, cap), jnp.float32), pltpu.VMEM((8, 128), jnp.float32)],
-        compiler_params=pltpu.CompilerParams(vmem_limit_bytes=48 * 1024 * 1024),
+        scratch_shapes=[
+            pltpu.VMEM((cap, cap), jnp.float32),
+            pltpu.VMEM((cap, cap), jnp.int32),
+            pltpu.SMEM((1, cap), jnp.int32),
+            pltpu.VMEM((partners + 8, 8, cap), jnp.float32),
+            pltpu.SemaphoreType.DMA,
+        ],
+        compiler_params=pltpu.CompilerParams(vmem_limit_bytes=32 * 1024 * 1024),
         cost_estimate=pl.CostEstimate(flops=2 * 8192 * 512 * 1024, bytes_accessed=2**21, transcendentals=0),
         name="land",
     )(match, second, inlet_now, inlet, arrival, arrived)
@@ -159,6 +228,7 @@
         out_shape=(shape, shape),
         in_specs=[VM] * 2,
         out_specs=(VM, VM),
+        compiler_params=pltpu.CompilerParams(vmem_limit_bytes=60 * 1024 * 1024),
         name="edges",
     )(flow, viscosity)
 
@@ -191,6 +261,7 @@
         in_specs=[VM] * 4,
         out_specs=(VM, VM),
         scratch_shapes=[pltpu.VMEM((8, flow.shape[1]), jnp.float32)],
+        compiler_params=pltpu.CompilerParams(vmem_limit_bytes=24 * 1024 * 1024),
         name="caps",
     )(flow, viscosity, left, right)
 
@@ -295,7 +366,7 @@
             pltpu.VMEM((depth_z + 2, wide, depth), jnp.float32),
             pltpu.VMEM((2 * flow.shape[0], depth), jnp.bfloat16),
         ],
-        compiler_params=pltpu.CompilerParams(vmem_limit_bytes=48 * 1024 * 1024),
+        compiler_params=pltpu.CompilerParams(vmem_limit_bytes=32 * 1024 * 1024),
         cost_estimate=pl.CostEstimate(flops=2 * 10**7, bytes_accessed=2**22, transcendentals=0),
         name="stencil",
     )(flow, viscosity, left, right, below, above, inlet)
@@ -330,8 +401,9 @@
     low_edge, high_edge = edges(*sizes, flow, visc)
     left = lax.ppermute(high_edge, "tile", forth)
     right = lax.ppermute(low_edge, "tile", back)
+    counts, low_edge, high_edge = lax.optimization_barrier((live_counts.reshape(-1), low_edge, high_edge))
     outgoing = slip(
-        live_counts.reshape(-1),
+        counts,
         flow,
         anchor_cell.reshape(partners, cap),
         inclusion_state.reshape(comps, partners, cap),
@@ -339,6 +411,7 @@
         inclusion_mass.reshape(partners, cap),
         ports,
     )
+    left, right, outgoing = lax.optimization_barrier((left, right, outgoing))
     arrived = lax.all_to_all(outgoing, "tile", split_axis=0, concat_axis=0, tiled=True)
     low_cap, high_cap = caps(*sizes, flow, visc, left, right)
     below = lax.ppermute(high_cap, "sec", up)

time: 92.8 us -> 64.8 us (0.70)
  Pallas kernels: 34.9 us -> 21.8 us
  local copies, waits for them, and re-layouts: 8.99 us -> 0.77 us
  waiting for transfers between devices: 15.2 us -> 7.01 us
  starting transfers between devices: 23.6 us -> 28.1 us
  blocking collectives: 8.06 us -> 5.77 us
    unnamed x31 -> x13, local copies, waits for them, and re-layouts: 8.98 us -> 0.76 us
    ppermute x1, waiting for transfers between devices: 5.92 us -> 0.01 us  [on_device(): right = lax.ppermute(low_edge, 'tile', back)]
    pallas_call x1, Pallas kernels: 13 us -> 7.45 us  [slip(): pl.pallas_call(functools.partial(slip_kernel, GP), out_shape=jax.ShapeDty...]
    pallas_call x1, Pallas kernels: 12.7 us -> 7.43 us  [land(): pl.pallas_call(functools.partial(land_kernel, GP), out_shape=(jax.ShapeDt...]
    all_to_all x1, starting transfers between devices: 12.6 us -> 16.9 us  [on_device(): lax.all_to_all(outgoing, 'tile', split_axis=0, concat_axis=0, tiled=True)]
    ppermute x1, waiting for transfers between devices: 2.91 us -> 0.01 us  [on_device(): left = lax.ppermute(high_edge, 'tile', forth)]
    all_gather x1, blocking collectives: 8.06 us -> 5.77 us  [on_device(): ports = lax.all_gather(port_plane.reshape(1, -1), 'sec', axis=0, tiled=True)]
    pallas_call x1, Pallas kernels: 2.29 us -> 0.08 us  [caps(): pl.pallas_call(functools.partial(cap_kernel, comps, depth_z, width), out_...]
  transfers between devices with their start and end apart: 5 -> 5, of which waited for: 4 -> 2; matrix products, arithmetic and copies ran while one was open for 0% -> 0% of each run, Pallas kernels for 10% -> 19%
where the time goes in v3:
time: 64.8 us; the launch traced here: 64.3 us
  starting transfers between devices  28.1 us (43%)
  Pallas kernels  21.8 us (34%)
  waiting for transfers between devices  7.01 us (11%)
  blocking collectives  5.77 us (9%)
  local copies, waits for them, and re-layouts  0.77 us (1%)
  between operations  0.77 us (1%)
    all_to_all x1, starting transfers between devices, on_device(): lax.all_to_all(outgoing, 'tile', split_axis=0, concat_axis=0, tiled=True)  16.9 us
    pallas_call x1, Pallas kernels, slip(): pl.pallas_call(functools.partial(slip_kernel, GP), out_shape=jax.ShapeDty...  7.45 us
    pallas_call x1, Pallas kernels, land(): pl.pallas_call(functools.partial(land_kernel, GP), out_shape=(jax.ShapeDt...  7.43 us
    all_gather x1, blocking collectives, on_device(): ports = lax.all_gather(port_plane.reshape(1, -1), 'sec', axis=0, tiled=True)  5.77 us
    ppermute x1, starting transfers between devices, on_device(): left = lax.ppermute(high_edge, 'tile', forth)  5.6 us
    pallas_call x1, Pallas kernels, stencil(): pl.pallas_call(functools.partial(stencil_kernel, comps, depth_z, width),...  4.79 us
    ppermute x1, waiting for transfers between devices, on_device(): below = lax.ppermute(high_cap, 'sec', up)  4.12 us
    ppermute x1, waiting for transfers between devices, on_device(): above = lax.ppermute(low_cap, 'sec', down)  2.88 us
  transfers between devices with their start and end apart: 5, of which 2 were waited for; matrix products, arithmetic and copies ran while one was open for 0% of the time, Pallas kernels for 19%

profile of v3, /device:TPU:1, one launch (start us, length us, event | category | flops | bytes accessed | tf_op | source)
XLA Modules:
  0.0 64.3 jit_solution(5020619379694234225)
XLA Ops:
  0.6 2.1 %edges.1 = (f32[72,512]{1,0:T(8,128)}, f32[72,512]{1,0:T(8,128)}) custom-call(f32[512,512]{1,0:T(8,128)} %bitcast.15, f32[128,512]{1,0:T(8,128)} %bitcast.19), custom_call_target="tpu_custom_call" | custom-call | tf_op jit(solution)/shard_map/edges/pallas_call | solution.py:226
  2.7 5.6 %collective-permute-start = (f32[72,512]{1,0:T(8,128)}, f32[72,512]{1,0:T(8,128)S(1)}, u32[]{:S(2)}, u32[]{:S(2)}) collective-permute-start(f32[72,512]{1,0:T(8,128)} %get-tuple-element.14), channel_id=1, source_target_pairs={{0,1},{1,2},{2,3},{3,4},{4,5},{5,6},{6,7},{7,8},{8,9},{9,10},{10,1... | collective-permute-start | bytes 442376 | tf_op jit(solution)/shard_map/ppermute | solution.py:402
  8.3 1.3 %collective-permute-start.1 = (f32[72,512]{1,0:T(8,128)}, f32[72,512]{1,0:T(8,128)S(1)}, u32[]{:S(2)}, u32[]{:S(2)}) collective-permute-start(f32[72,512]{1,0:T(8,128)} %get-tuple-element.15), channel_id=1, source_target_pairs={{1,0},{2,1},{3,2},{4,3},{5,4},{6,5},{7,6},{8,7},{9,8},{10,9},{11,1... | collective-permute-start | bytes 442376 | tf_op jit(solution)/shard_map/ppermute | solution.py:403
  9.6 0.0 copy-done.4
  9.6 0.1 reshape.48
  9.7 5.8 %all-gather = f32[4,1,128]{2,1,0:T(1,128)} all-gather(f32[1,1,128]{2,1,0:T(1,128)S(1)} %reshape.48), channel_id=1, replica_groups=mesh['sec'=4,'tile'=64] {'sec'}, dimensions={0}, use_global_device_ids=true | all-gather | bytes 2560 | tf_op jit(solution)/shard_map/all_gather | solution.py:400
  15.5 7.5 %slip.1 = f32[192,4,128]{2,1,0:T(4,128)} custom-call(s32[64]{0:T(128)} %bitcast.30, f32[512,512]{1,0:T(8,128)} %bitcast.16, s32[64,128]{1,0:T(8,128)} %bitcast.27, f32[4,64,128]{2,1,0:T(8,128)} %bitcast.26, f32[64,128]{1,0:T(8,128)} %bitcast.28, f32[64,128]{1,0:T(8,128)} %bitcast.29, f32[4,128]{1,0:T(4,128)} %bitcast.24), custom_call_target="tpu_custom_call" | custom-call | flops 8589934592 | bytes 2097152 | tf_op jit(solution)/shard_map/slip/pallas_call | solution.py:94
  22.9 0.0 copy-start.1
  23.0 0.0 collective-permute-done.left
  23.0 0.0 collective-permute-done.1.right
  23.0 16.9 %all-to-all-start = ((f32[192,4,128]{2,1,0:T(4,128)}), f32[192,4,128]{2,1,0:T(4,128)S(1)}, u32[]{:S(2)}, u32[]{:S(2)}) async-start(f32[192,4,128]{2,1,0:T(4,128)} %slip.1), calls=%async_computation | async-start | bytes 786432 | tf_op jit(solution)/shard_map/all_to_all | solution.py:415
  39.9 0.1 caps.1
  40.0 1.9 %collective-permute-start.2 = (f32[176,512]{1,0:T(8,128)S(1)}, f32[176,512]{1,0:T(8,128)S(1)}, u32[]{:S(2)}, u32[]{:S(2)}) collective-permute-start(f32[176,512]{1,0:T(8,128)S(1)} %get-tuple-element.19), channel_id=1, source_target_pairs={{0,64},{64,128},{128,192},{1,65},{65,129},{129,193},{2,66},{66,130... | collective-permute-start | bytes 1081352 | tf_op jit(solution)/shard_map/ppermute | solution.py:417
  41.9 2.4 %collective-permute-start.3 = (f32[176,512]{1,0:T(8,128)S(1)}, f32[176,512]{1,0:T(8,128)S(1)}, u32[]{:S(2)}, u32[]{:S(2)}) collective-permute-start(f32[176,512]{1,0:T(8,128)S(1)} %get-tuple-element.20), channel_id=1, source_target_pairs={{64,0},{128,64},{192,128},{65,1},{129,65},{193,129},{66,2},{130,66... | collective-permute-start | bytes 1081352 | tf_op jit(solution)/shard_map/ppermute | solution.py:418
  44.3 0.0 copy-start.2
  44.3 0.0 copy-start.5
  44.4 0.6 copy-done.2
  45.0 0.0 copy-done.5
  45.0 4.1 %collective-permute-done.2.below = f32[176,512]{1,0:T(8,128)S(1)} collective-permute-done((f32[176,512]{1,0:T(8,128)S(1)}, f32[176,512]{1,0:T(8,128)S(1)}, u32[]{:S(2)}, u32[]{:S(2)}) %collective-permute-start.2) | collective-permute-done | bytes 360480 | tf_op jit(solution)/shard_map/ppermute | solution.py:417
  49.2 2.9 %collective-permute-done.3.above = f32[176,512]{1,0:T(8,128)S(1)} collective-permute-done((f32[176,512]{1,0:T(8,128)S(1)}, f32[176,512]{1,0:T(8,128)S(1)}, u32[]{:S(2)}, u32[]{:S(2)}) %collective-permute-start.3) | collective-permute-done | bytes 360480 | tf_op jit(solution)/shard_map/ppermute | solution.py:418
  52.0 4.8 %stencil.1 = (f32[512,512]{1,0:T(8,128)S(1)}, f32[4,128]{1,0:T(4,128)S(1)}) custom-call(f32[512,512]{1,0:T(8,128)S(1)} %bitcast.18, f32[128,512]{1,0:T(8,128)S(1)} %bitcast.21, f32[72,512]{1,0:T(8,128)S(1)} %collective-permute-done.left, f32[72,512]{1,0:T(8,128)S(1)} %collective-permute-done.1.right, f32[176,512]{1,0:T(8,128)S(1)} %collective-permute-done.2.below, ...), custom_call_target="tpu_custom_call" | custom-call | flops 20000000 | bytes 4194304 | tf_op jit(solution)/shard_map/stencil/pallas_call | solution.py:355
  56.8 0.0 all-to-all-done.arrived
  56.8 0.0 copy-done.3
  56.8 7.4 %land.1 = (f32[512,512]{1,0:T(8,128)}, f32[4,64,128]{2,1,0:T(8,128)}) custom-call(s32[32]{0:T(128)S(1)} %copy-done.2, f32[512,512]{1,0:T(8,128)S(1)} %get-tuple-element.21.second, f32[4,128]{1,0:T(4,128)S(1)} %get-tuple-element.22.inlet_now, s32[2,128]{1,0:T(2,128)S(1)} %pad.4.inlet, s32[64,128]{1,0:T(8,128)S(1)} %bitcast.23, ...), custom_call_target="tpu_custom_call" | custom-call | flops 8589934592 | bytes 2097152 | tf_op jit(solution)/shard_map/land/pallas_call | solution.py:193
  (7 shorter events, 0.0 us)
Async XLA Ops:
  2.7 6.9 %copy-start.4 = (f32[4,32]{1,0:T(4,128)S(1)}, f32[4,32]{1,0:T(4,128)}, u32[]{:S(2)}) copy-start(f32[4,32]{1,0:T(4,128)} %param.13) | copy-start | bytes 1540
  2.7 20.2 %collective-permute-start = (f32[72,512]{1,0:T(8,128)}, f32[72,512]{1,0:T(8,128)S(1)}, u32[]{:S(2)}, u32[]{:S(2)}) collective-permute-start(f32[72,512]{1,0:T(8,128)} %get-tuple-element.14), channel_id=1, source_target_pairs={{0,1},{1,2},{2,3},{3,4},{4,5},{5,6},{6,7},{7,8},{8,9},{9,10},{10,1... | collective-permute-start | bytes 442376 | tf_op jit(solution)/shard_map/ppermute | solution.py:402
  8.3 14.6 %collective-permute-start.1 = (f32[72,512]{1,0:T(8,128)}, f32[72,512]{1,0:T(8,128)S(1)}, u32[]{:S(2)}, u32[]{:S(2)}) collective-permute-start(f32[72,512]{1,0:T(8,128)} %get-tuple-element.15), channel_id=1, source_target_pairs={{1,0},{2,1},{3,2},{4,3},{5,4},{6,5},{7,6},{8,7},{9,8},{10,9},{11,1... | collective-permute-start | bytes 442376 | tf_op jit(solution)/shard_map/ppermute | solution.py:403
  15.5 24.4 %copy-start = (f32[4,8,16,512]{3,2,1,0:T(8,128)S(1)}, f32[4,8,16,512]{3,2,1,0:T(8,128)}, u32[]{:S(2)}) copy-start(f32[4,8,16,512]{3,2,1,0:T(8,128)} %param.11) | copy-start | bytes 3145732
  22.9 16.9 %copy-start.1 = (f32[8,16,512]{2,1,0:T(8,128)S(1)}, f32[8,16,512]{2,1,0:T(8,128)}, u32[]{:S(2)}) copy-start(f32[8,16,512]{2,1,0:T(8,128)} %param.12) | copy-start | bytes 786436
  23.0 33.8 %all-to-all-start = ((f32[192,4,128]{2,1,0:T(4,128)}), f32[192,4,128]{2,1,0:T(4,128)S(1)}, u32[]{:S(2)}, u32[]{:S(2)}) async-start(f32[192,4,128]{2,1,0:T(4,128)} %slip.1), calls=%async_computation | async-start | bytes 786432 | tf_op jit(solution)/shard_map/all_to_all | solution.py:415
  40.0 9.2 %collective-permute-start.2 = (f32[176,512]{1,0:T(8,128)S(1)}, f32[176,512]{1,0:T(8,128)S(1)}, u32[]{:S(2)}, u32[]{:S(2)}) collective-permute-start(f32[176,512]{1,0:T(8,128)S(1)} %get-tuple-element.19), channel_id=1, source_target_pairs={{0,64},{64,128},{128,192},{1,65},{65,129},{129,193},{2,66},{66,130... | collective-permute-start | bytes 1081352 | tf_op jit(solution)/shard_map/ppermute | solution.py:417
  41.9 10.1 %collective-permute-start.3 = (f32[176,512]{1,0:T(8,128)S(1)}, f32[176,512]{1,0:T(8,128)S(1)}, u32[]{:S(2)}, u32[]{:S(2)}) collective-permute-start(f32[176,512]{1,0:T(8,128)S(1)} %get-tuple-element.20), channel_id=1, source_target_pairs={{64,0},{128,64},{192,128},{65,1},{129,65},{193,129},{66,2},{130,66... | collective-permute-start | bytes 1081352 | tf_op jit(solution)/shard_map/ppermute | solution.py:418
  44.3 0.7 %copy-start.2 = (s32[32]{0:T(128)S(1)}, s32[32]{0:T(128)}, u32[]{:S(2)}) copy-start(s32[32]{0:T(128)} %match.1) | copy-start | bytes 388
  44.3 0.7 %copy-start.5 = (s32[32]{0:T(128)S(1)}, s32[32]{0:T(128)}, u32[]{:S(2)}) copy-start(s32[32]{0:T(128)} %param.15) | copy-start | bytes 388
  45.0 11.8 %copy-start.3 = (s32[1,1,64,128]{3,2,1,0:T(8,128)S(1)}, s32[1,1,64,128]{3,2,1,0:T(8,128)}, u32[]{:S(2)}) copy-start(s32[1,1,64,128]{3,2,1,0:T(8,128)} %param.21) | copy-start | bytes 98308

commit v4 on v3

--- a/solution.py
+++ b/solution.py
@@ -23,14 +23,17 @@
     return jnp.where(at == (cells & (depth - 1)), 1.0, 0.0).astype(jnp.bfloat16)
 
 
-def slip_kernel(GP, counts, flow_far, anchor_far, state_far, rate_far, mass_far, ports, out, flow, anchor, state, rate, mass, table, packed, sampled, sems):
+chunks = 4
+
+
+def slip_kernel(GP, counts, flow_far, anchor_far, state_far, rate_far, mass_far, ports, far, out, flow, anchor, state, rate, mass, table, packed, sampled, sems, out_sems):
     comps, partners, cap = state.shape
     total, depth = flow.shape
     rows = total // comps
     shift = depth.bit_length() - 1
     cap_shift = cap.bit_length() - 1
     pairs = ((anchor_far, anchor), (flow_far, flow), (state_far, state), (rate_far, rate), (mass_far, mass))
-    copies = [pltpu.make_async_copy(far, near, sems.at[i]) for i, (far, near) in enumerate(pairs)]
+    copies = [pltpu.make_async_copy(source, target, sems.at[i]) for i, (source, target) in enumerate(pairs)]
     for copy in copies:
         copy.start()
     lane = lax.broadcasted_iota(jnp.int32, (1, cap), 1)
@@ -85,23 +88,33 @@
         out[3 * p + 2] = ports[...]
         return base + n
 
-    lax.fori_loop(0, partners, finish, 0, unroll=8)
-
-
-def slip(counts, flow, anchor, state, rate, mass, ports, GP=4):
+    block = partners // chunks
+    base = 0
+    copies = []
+    for i in range(chunks):
+        base = lax.fori_loop(i * block, (i + 1) * block, finish, base, unroll=8)
+        part = pl.ds(3 * i * block, 3 * block)
+        copies.append(pltpu.make_async_copy(out.at[part], far.at[part], out_sems.at[i]))
+        copies[i].start()
+    for copy in copies:
+        copy.wait()
+
+
+def slip(counts, flow, anchor, state, rate, mass, ports, GP=8):
     comps, partners, cap = state.shape
     near = [pltpu.VMEM(x.shape, x.dtype) for x in (flow, anchor, state, rate, mass)]
     return pl.pallas_call(
         functools.partial(slip_kernel, GP),
         out_shape=jax.ShapeDtypeStruct((partners * 3, comps, cap), jnp.float32),
         in_specs=[SM] + [HB] * 5 + [VM],
-        out_specs=VM,
-        scratch_shapes=near
+        out_specs=HB,
+        scratch_shapes=[pltpu.VMEM((partners * 3, comps, cap), jnp.float32)] + near
         + [
             pltpu.VMEM((2 * flow.shape[0], flow.shape[1]), jnp.bfloat16),
             pltpu.VMEM((partners + 8, cap), jnp.int32),
             pltpu.VMEM((partners + 8, comps, cap), jnp.float32),
             pltpu.SemaphoreType.DMA((5,)),
+            pltpu.SemaphoreType.DMA((chunks,)),
         ],
         compiler_params=pltpu.CompilerParams(vmem_limit_bytes=60 * 1024 * 1024),
         cost_estimate=pl.CostEstimate(flops=2 * 8192 * 512 * 1024, bytes_accessed=2**21, transcendentals=0),
@@ -187,7 +200,7 @@
     lax.fori_loop(0, (used + GP * cap - 1) // (GP * cap), group, 0)
 
 
-def land(match, second, inlet_now, inlet, arrival, arrived, GP=4):
+def land(match, second, inlet_now, inlet, arrival, arrived, GP=8):
     partners, cap = arrival.shape
     comps = arrived.shape[1]
     return pl.pallas_call(
@@ -205,7 +218,7 @@
             pltpu.VMEM((partners + 8, 8, cap), jnp.float32),
             pltpu.SemaphoreType.DMA,
         ],
-        compiler_params=pltpu.CompilerParams(vmem_limit_bytes=32 * 1024 * 1024),
+        compiler_params=pltpu.CompilerParams(vmem_limit_bytes=24 * 1024 * 1024),
         cost_estimate=pl.CostEstimate(flops=2 * 8192 * 512 * 1024, bytes_accessed=2**21, transcendentals=0),
         name="land",
     )(match, second, inlet_now, inlet, arrival, arrived)
@@ -266,80 +279,133 @@
     )(flow, viscosity, left, right)
 
 
-def stencil_kernel(comps, depth_z, width, flow, viscosity, left, right, below, above, inlet, second_out, inlet_now, state, first, visc, table):
+def tendency(plane, upper, lower, viscosity, keep):
+    place = lax.broadcasted_iota(jnp.int32, (1, viscosity.shape[1]), 1)
+    depth = viscosity.shape[1]
+    centers, laps, dz, dx, dy = [], [], [], [], []
+    for c in range(len(plane)):
+        whole = plane[c]
+        center = whole[:keep]
+        up_x = pltpu.roll(whole, whole.shape[0] - 1, 0)[:keep]
+        low_x = pltpu.roll(whole, 1, 0)[:keep]
+        up_y = jnp.where(place == depth - 1, 0.0, pltpu.roll(center, depth - 1, 1))
+        low_y = jnp.where(place == 0, 0.0, pltpu.roll(center, 1, 1))
+        centers.append(center)
+        laps.append((upper[c] + lower[c]) + (up_x + low_x) + (up_y + low_y) - 6.0 * center)
+        dz.append(upper[c] - lower[c])
+        dx.append(up_x - low_x)
+        dy.append(up_y - low_y)
+    strain = sum(d[c] * d[c] for c in range(3) for d in (dz, dx, dy)) * 0.25
+    eddy = viscosity * (1.0 + strain / (1.0 + strain))
+    out = []
+    for c in range(len(plane)):
+        carried = centers[0] * dz[c] + centers[1] * dx[c] + centers[2] * dy[c]
+        out.append(0.5 * (eddy * laps[c]) - 0.25 * carried)
+    return centers, out
+
+
+def inner_kernel(comps, depth_z, width, flow, viscosity, left, right, state, visc, first, second):
     depth = flow.shape[1]
-    per = 2 * width + 8
-    total = comps * depth_z * width
-    rows = depth_z * width
     wide = width + 8
     base = 2 * comps * depth_z
     blank = jnp.zeros((8, depth), jnp.float32)
+    for z in range(depth_z):
+        for c in range(comps):
+            k = c * depth_z + z
+            state[c, z, 0:width, :] = flow[k * width : (k + 1) * width, :]
+            state[c, z, width:wide, :] = blank
+            state[c, z, width : width + 2, :] = right[2 * k : 2 * k + 2, :]
+            state[c, z, wide - 2 : wide, :] = left[2 * k : 2 * k + 2, :]
+        visc[z, 0:width, :] = viscosity[z * width : (z + 1) * width, :]
+        visc[z, width:wide, :] = blank
+        visc[z, width : width + 1, :] = right[base + z : base + z + 1, :]
+        visc[z, wide - 1 : wide, :] = left[base + z : base + z + 1, :]
+
+    def one(z, carry):
+        plane, upper, lower = ([state[c, z + d] for c in range(comps)] for d in (0, 1, -1))
+        centers, change = tendency(plane, upper, lower, visc[z], wide)
+        for c in range(comps):
+            first[c, z - 1] = centers[c] + change[c]
+        return carry
+
+    lax.fori_loop(1, depth_z - 1, one, 0)
+
+    def two(z, carry):
+        plane = [first[c, z - 1] for c in range(comps)]
+        upper, lower = ([first[c, z - 1 + d, 0:width, :] for c in range(comps)] for d in (1, -1))
+        centers, change = tendency(plane, upper, lower, visc[z, 0:width, :], width)
+        for c in range(comps):
+            second[c, z - 2] = 0.5 * state[c, z, 0:width, :] + 0.5 * (centers[c] + change[c])
+        return carry
+
+    lax.fori_loop(2, depth_z - 2, two, 0)
+
+
+def inner(comps, depth_z, width, flow, viscosity, left, right):
+    depth = flow.shape[1]
+    wide = width + 8
+    shapes = ((comps, depth_z, wide), (depth_z, wide), (comps, depth_z - 2, wide), (comps, depth_z - 4, width))
+    return pl.pallas_call(
+        functools.partial(inner_kernel, comps, depth_z, width),
+        out_shape=tuple(jax.ShapeDtypeStruct(shape + (depth,), jnp.float32) for shape in shapes),
+        in_specs=[VM] * 4,
+        out_specs=(VM,) * 4,
+        compiler_params=pltpu.CompilerParams(vmem_limit_bytes=24 * 1024 * 1024),
+        cost_estimate=pl.CostEstimate(flops=10**7, bytes_accessed=2**22, transcendentals=0),
+        name="inner",
+    )(flow, viscosity, left, right)
+
+
+def outer_kernel(state, visc, first, second, below, above, inlet, second_out, inlet_now, rim, table):
+    comps, depth_z, wide, depth = state.shape
+    width = second.shape[2]
+    per = width + wide
+    rows = depth_z * width
+    total = comps * rows
+    last = depth_z - 1
+
+    def near(source):
+        return [source[c * per : c * per + wide, :] for c in range(comps)]
+
+    def far(source):
+        return [source[c * per + wide : (c + 1) * per, :] for c in range(comps)]
+
+    def own(z, keep):
+        return [state[c, z, 0:keep, :] for c in range(comps)]
+
+    def put(slot, keep, plane, upper, lower, viscosity):
+        centers, change = tendency(plane, upper, lower, viscosity, keep)
+        for c in range(comps):
+            rim[c, slot, 0:keep, :] = centers[c] + change[c]
+
+    put(0, width, near(below), own(0, width), far(below), below[comps * per :, :])
+    put(1, wide, own(0, wide), own(1, wide), near(below), visc[0])
+    put(2, wide, own(last, wide), near(above), own(last - 1, wide), visc[last])
+    put(3, width, near(above), far(above), own(last, width), above[comps * per :, :])
+
+    def started(z, keep):
+        if z < 1 or z > last - 1:
+            slot = {-1: 0, 0: 1, last: 2, last + 1: 3}[z]
+            return [rim[c, slot, 0:keep, :] for c in range(comps)]
+        return [first[c, z - 1, 0:keep, :] for c in range(comps)]
+
+    def keep_value(c, z, value):
+        spot = (c * depth_z + z) * width
+        count = value.shape[0]
+        second_out[spot : spot + count, :] = value
+        high, low = halves(value)
+        table[spot : spot + count] = high
+        table[total + spot : total + spot + count] = low
+
+    for z in (0, 1, last - 1, last):
+        centers, change = tendency(
+            started(z, wide), started(z + 1, width), started(z - 1, width), visc[z, 0:width, :], width
+        )
+        for c in range(comps):
+            keep_value(c, z, 0.5 * state[c, z, 0:width, :] + 0.5 * (centers[c] + change[c]))
     for c in range(comps):
-        for z in range(depth_z):
-            k = c * depth_z + z
-            state[c, z + 2, 0:width, :] = flow[k * width : (k + 1) * width, :]
-            state[c, z + 2, width:wide, :] = blank
-            state[c, z + 2, width : width + 2, :] = right[2 * k : 2 * k + 2, :]
-            state[c, z + 2, wide - 2 : wide, :] = left[2 * k : 2 * k + 2, :]
-        for near, far, source in ((1, 0, below), (depth_z + 2, depth_z + 3, above)):
-            state[c, near] = source[c * per : c * per + wide, :]
-            state[c, far, 0:width, :] = source[c * per + wide : (c + 1) * per, :]
-            state[c, far, width:wide, :] = blank
-    for z in range(depth_z):
-        visc[z + 1, 0:width, :] = viscosity[z * width : (z + 1) * width, :]
-        visc[z + 1, width:wide, :] = blank
-        visc[z + 1, width : width + 1, :] = right[base + z : base + z + 1, :]
-        visc[z + 1, wide - 1 : wide, :] = left[base + z : base + z + 1, :]
-    for z, source in ((0, below), (depth_z + 1, above)):
-        visc[z, 0:width, :] = source[comps * per :, :]
-        visc[z, width:wide, :] = blank
-
-    place = lax.broadcasted_iota(jnp.int32, (1, depth), 1)
-
-    def tendency(ref, z, eddy_base, keep):
-        centers, laps, dz, dx, dy = [], [], [], [], []
-        for c in range(comps):
-            plane = ref[c, z]
-            center = plane[:keep]
-            up_x = pltpu.roll(plane, wide - 1, 0)[:keep]
-            low_x = pltpu.roll(plane, 1, 0)[:keep]
-            up_y = jnp.where(place == depth - 1, 0.0, pltpu.roll(center, depth - 1, 1))
-            low_y = jnp.where(place == 0, 0.0, pltpu.roll(center, 1, 1))
-            up_z = ref[c, z + 1, 0:keep, :]
-            low_z = ref[c, z - 1, 0:keep, :]
-            centers.append(center)
-            laps.append((up_z + low_z) + (up_x + low_x) + (up_y + low_y) - 6.0 * center)
-            dz.append(up_z - low_z)
-            dx.append(up_x - low_x)
-            dy.append(up_y - low_y)
-        strain = sum(d[c] * d[c] for c in range(3) for d in (dz, dx, dy)) * 0.25
-        eddy = eddy_base * (1.0 + strain / (1.0 + strain))
-        out = []
-        for c in range(comps):
-            carried = centers[0] * dz[c] + centers[1] * dx[c] + centers[2] * dy[c]
-            out.append(0.5 * (eddy * laps[c]) - 0.25 * carried)
-        return centers, out
-
-    def one(z, carry):
-        centers, change = tendency(state, z + 1, visc[z], wide)
-        for c in range(comps):
-            first[c, z] = centers[c] + change[c]
-        return carry
-
-    lax.fori_loop(0, depth_z + 2, one, 0)
-
-    def two(z, carry):
-        centers, change = tendency(first, z + 1, visc[z + 1, 0:width, :], width)
-        for c in range(comps):
-            value = 0.5 * state[c, z + 2, 0:width, :] + 0.5 * (centers[c] + change[c])
-            spot = pl.multiple_of((c * depth_z + z) * width, width)
-            second_out[pl.ds(spot, width), :] = value
-            high, low = halves(value)
-            table[pl.ds(spot, width), :] = high
-            table[pl.ds(total + spot, width), :] = low
-        return carry
-
-    lax.fori_loop(0, depth_z, two, 0)
+        for z in range(2, last - 1):
+            keep_value(c, z, second[c, z - 2])
 
     cells = inlet[0:1, :]
     picked = jnp.dot(table[...], column_hot(cells, depth), preferred_element_type=jnp.float32)
@@ -349,27 +415,25 @@
         inlet_now[c : c + 1, :] = jnp.sum(jnp.where(row, both, 0.0), axis=0, keepdims=True)
 
 
-def stencil(comps, depth_z, width, flow, viscosity, left, right, below, above, inlet):
-    depth = flow.shape[1]
-    wide = width + 8
+def outer(state, visc, first, second, below, above, inlet):
+    comps, depth_z, wide, depth = state.shape
+    total = comps * depth_z * second.shape[2]
     return pl.pallas_call(
-        functools.partial(stencil_kernel, comps, depth_z, width),
+        outer_kernel,
         out_shape=(
-            jax.ShapeDtypeStruct(flow.shape, jnp.float32),
+            jax.ShapeDtypeStruct((total, depth), jnp.float32),
             jax.ShapeDtypeStruct((comps, inlet.shape[1]), jnp.float32),
         ),
         in_specs=[VM] * 7,
         out_specs=(VM, VM),
         scratch_shapes=[
-            pltpu.VMEM((comps, depth_z + 4, wide, depth), jnp.float32),
-            pltpu.VMEM((comps, depth_z + 2, wide, depth), jnp.float32),
-            pltpu.VMEM((depth_z + 2, wide, depth), jnp.float32),
-            pltpu.VMEM((2 * flow.shape[0], depth), jnp.bfloat16),
+            pltpu.VMEM((comps, 4, wide, depth), jnp.float32),
+            pltpu.VMEM((2 * total, depth), jnp.bfloat16),
         ],
-        compiler_params=pltpu.CompilerParams(vmem_limit_bytes=32 * 1024 * 1024),
-        cost_estimate=pl.CostEstimate(flops=2 * 10**7, bytes_accessed=2**22, transcendentals=0),
-        name="stencil",
-    )(flow, viscosity, left, right, below, above, inlet)
+        compiler_params=pltpu.CompilerParams(vmem_limit_bytes=24 * 1024 * 1024),
+        cost_estimate=pl.CostEstimate(flops=10**7, bytes_accessed=2**22, transcendentals=0),
+        name="outer",
+    )(state, visc, first, second, below, above, inlet)
 
 
 def on_device(
@@ -417,7 +481,8 @@
     below = lax.ppermute(high_cap, "sec", up)
     above = lax.ppermute(low_cap, "sec", down)
     inlet = jnp.pad(jnp.stack([inlet_cell, port_match]), ((0, 0), (0, cap - inlet_cell.shape[0])))
-    second, inlet_now = stencil(*sizes, flow, visc, left, right, below, above, inlet)
+    middle = inner(*sizes, flow, visc, left, right)
+    second, inlet_now = outer(*middle, below, above, inlet)
     flow_next, arrived_state = land(
         port_match, second, inlet_now, inlet, arrival_cell.reshape(partners, cap), arrived
     )

time: 64.8 us -> 62.7 us (0.968)
  the two profiles are of different devices: /device:TPU:1 before, /device:TPU:2 now
where the time goes in v4:
time: 62.7 us; the launch traced here: 61.9 us
  starting transfers between devices  27.9 us (44%)
  Pallas kernels  20.5 us (33%)
  waiting for transfers between devices  6.92 us (11%)
  blocking collectives  5.04 us (8%)
  local copies, waits for them, and re-layouts  0.79 us (1%)
  between operations  0.77 us (1%)
    all_to_all x1, starting transfers between devices, on_device(): lax.all_to_all(outgoing, 'tile', split_axis=0, concat_axis=0, tiled=True)  17 us
    pallas_call x1, Pallas kernels, land(): pl.pallas_call(functools.partial(land_kernel, GP), out_shape=(jax.ShapeDt...  7.54 us
    pallas_call x1, Pallas kernels, slip(): pl.pallas_call(functools.partial(slip_kernel, GP), out_shape=jax.ShapeDty...  6.37 us
    all_gather x1, blocking collectives, on_device(): ports = lax.all_gather(port_plane.reshape(1, -1), 'sec', axis=0, tiled=True)  5.04 us
    ppermute x1, starting transfers between devices, on_device(): left = lax.ppermute(high_edge, 'tile', forth)  4.02 us
    ppermute x1, starting transfers between devices, on_device(): above = lax.ppermute(low_cap, 'sec', down)  3.64 us
    ppermute x1, waiting for transfers between devices, on_device(): below = lax.ppermute(high_cap, 'sec', up)  3.2 us
    all_to_all x1, waiting for transfers between devices, on_device(): lax.all_to_all(outgoing, 'tile', split_axis=0, concat_axis=0, tiled=True)  2.95 us
  transfers between devices with their start and end apart: 5, of which 3 were waited for; matrix products, arithmetic and copies ran while one was open for 1% of the time, Pallas kernels for 18%

profile of v4, /device:TPU:2, one launch (start us, length us, event | category | flops | bytes accessed | tf_op | source)
XLA Modules:
  0.0 61.9 jit_solution(15656550385474137349)
XLA Ops:
  0.6 2.1 %edges.1 = (f32[72,512]{1,0:T(8,128)}, f32[72,512]{1,0:T(8,128)}) custom-call(f32[512,512]{1,0:T(8,128)} %bitcast.15, f32[128,512]{1,0:T(8,128)} %bitcast.19), custom_call_target="tpu_custom_call" | custom-call | tf_op jit(solution)/shard_map/edges/pallas_call | solution.py:239
  2.7 4.0 %collective-permute-start = (f32[72,512]{1,0:T(8,128)}, f32[72,512]{1,0:T(8,128)S(1)}, u32[]{:S(2)}, u32[]{:S(2)}) collective-permute-start(f32[72,512]{1,0:T(8,128)} %get-tuple-element.18), channel_id=1, source_target_pairs={{0,1},{1,2},{2,3},{3,4},{4,5},{5,6},{6,7},{7,8},{8,9},{9,10},{10,1... | collective-permute-start | bytes 442376 | tf_op jit(solution)/shard_map/ppermute | solution.py:466
  6.7 1.3 %collective-permute-start.1 = (f32[72,512]{1,0:T(8,128)}, f32[72,512]{1,0:T(8,128)S(1)}, u32[]{:S(2)}, u32[]{:S(2)}) collective-permute-start(f32[72,512]{1,0:T(8,128)} %get-tuple-element.19), channel_id=1, source_target_pairs={{1,0},{2,1},{3,2},{4,3},{5,4},{6,5},{7,6},{8,7},{9,8},{10,9},{11,1... | collective-permute-start | bytes 442376 | tf_op jit(solution)/shard_map/ppermute | solution.py:467
  8.0 0.8 %reshape.48 = f32[1,1,128]{2,1,0:T(1,128)S(1)} reshape(f32[4,32]{1,0:T(4,128)} %param.13) | data formatting | bytes 1024
  8.8 5.0 %all-gather = f32[4,1,128]{2,1,0:T(1,128)} all-gather(f32[1,1,128]{2,1,0:T(1,128)S(1)} %reshape.48), channel_id=1, replica_groups=mesh['sec'=4,'tile'=64] {'sec'}, dimensions={0}, use_global_device_ids=true | all-gather | bytes 2560 | tf_op jit(solution)/shard_map/all_gather | solution.py:464
  13.9 6.4 %slip.1 = f32[192,4,128]{2,1,0:T(4,128)} custom-call(s32[64]{0:T(128)} %bitcast.30, f32[512,512]{1,0:T(8,128)} %bitcast.16, s32[64,128]{1,0:T(8,128)} %bitcast.27, f32[4,64,128]{2,1,0:T(8,128)} %bitcast.26, f32[64,128]{1,0:T(8,128)} %bitcast.28, f32[64,128]{1,0:T(8,128)} %bitcast.29, f32[4,128]{1,0:T(4,128)} %bitcast.24), custom_call_target="tpu_custom_call" | custom-call | flops 8589934592 | bytes 2097152 | tf_op jit(solution)/shard_map/slip/pallas_call | solution.py:106
  20.2 0.0 copy-start.2
  20.2 0.0 copy-start.4
  20.3 0.0 collective-permute-done.left
  20.3 0.0 collective-permute-done.1.right
  20.3 17.0 %all-to-all-start = ((f32[192,4,128]{2,1,0:T(4,128)}), f32[192,4,128]{2,1,0:T(4,128)S(1)}, u32[]{:S(2)}, u32[]{:S(2)}) async-start(f32[192,4,128]{2,1,0:T(4,128)} %slip.1), calls=%async_computation | async-start | bytes 786432 | tf_op jit(solution)/shard_map/all_to_all | solution.py:479
  37.3 0.0 copy-done
  37.3 0.0 copy-done.1
  37.3 0.1 caps.1
  37.4 1.9 %collective-permute-start.2 = (f32[176,512]{1,0:T(8,128)S(1)}, f32[176,512]{1,0:T(8,128)S(1)}, u32[]{:S(2)}, u32[]{:S(2)}) collective-permute-start(f32[176,512]{1,0:T(8,128)S(1)} %get-tuple-element.27), channel_id=1, source_target_pairs={{0,64},{64,128},{128,192},{1,65},{65,129},{129,193},{2,66},{66,130... | collective-permute-start | bytes 1081352 | tf_op jit(solution)/shard_map/ppermute | solution.py:481
  39.3 3.6 %collective-permute-start.3 = (f32[176,512]{1,0:T(8,128)S(1)}, f32[176,512]{1,0:T(8,128)S(1)}, u32[]{:S(2)}, u32[]{:S(2)}) collective-permute-start(f32[176,512]{1,0:T(8,128)S(1)} %get-tuple-element.28), channel_id=1, source_target_pairs={{64,0},{128,64},{192,128},{65,1},{129,65},{193,129},{66,2},{130,66... | collective-permute-start | bytes 1081352 | tf_op jit(solution)/shard_map/ppermute | solution.py:482
  43.0 0.0 copy-done.2
  43.0 0.0 copy-done.4
  43.0 2.5 %inner.1 = (f32[4,8,24,512]{3,2,1,0:T(8,128)S(1)}, f32[8,24,512]{2,1,0:T(8,128)S(1)}, f32[4,6,24,512]{3,2,1,0:T(8,128)S(1)}, f32[4,4,16,512]{3,2,1,0:T(8,128)S(1)}) custom-call(f32[512,512]{1,0:T(8,128)S(1)} %bitcast.18, f32[128,512]{1,0:T(8,128)S(1)} %bitcast.21, f32[72,512]{1,0:T(8,128)S(1)} %collective-permute-done.left, ...), custom_call_target="tpu_custom_call" | custom-call | flops 10000000 | bytes 4194304 | tf_op jit(solution)/shard_map/inner/pallas_call | solution.py:348
  45.6 3.2 %collective-permute-done.2.below = f32[176,512]{1,0:T(8,128)S(1)} collective-permute-done((f32[176,512]{1,0:T(8,128)S(1)}, f32[176,512]{1,0:T(8,128)S(1)}, u32[]{:S(2)}, u32[]{:S(2)}) %collective-permute-start.2) | collective-permute-done | bytes 360480 | tf_op jit(solution)/shard_map/ppermute | solution.py:481
  48.8 0.8 %collective-permute-done.3.above = f32[176,512]{1,0:T(8,128)S(1)} collective-permute-done((f32[176,512]{1,0:T(8,128)S(1)}, f32[176,512]{1,0:T(8,128)S(1)}, u32[]{:S(2)}, u32[]{:S(2)}) %collective-permute-start.3) | collective-permute-done | bytes 360480 | tf_op jit(solution)/shard_map/ppermute | solution.py:482
  49.5 1.9 %outer.1 = (f32[512,512]{1,0:T(8,128)S(1)}, f32[4,128]{1,0:T(4,128)S(1)}) custom-call(f32[4,8,24,512]{3,2,1,0:T(8,128)S(1)} %get-tuple-element.23.state, f32[8,24,512]{2,1,0:T(8,128)S(1)} %get-tuple-element.24.visc, f32[4,6,24,512]{3,2,1,0:T(8,128)S(1)} %get-tuple-element.25.first, f32[4,4,16,512]{3,2,1,0:T(8,128)S(1)} %get-tuple-element.26.second, ...), custom_call_target="tpu_custom_call" | custom-call | flops 10000000 | bytes 4194304 | tf_op jit(solution)/shard_map/outer/pallas_call | solution.py:421
  51.4 3.0 %all-to-all-done.arrived = f32[192,4,128]{2,1,0:T(4,128)S(1)} async-done(((f32[192,4,128]{2,1,0:T(4,128)}), f32[192,4,128]{2,1,0:T(4,128)S(1)}, u32[]{:S(2)}, u32[]{:S(2)}) %all-to-all-start) | async-done | bytes 393248 | tf_op jit(solution)/shard_map/all_to_all | solution.py:479
  54.4 7.5 %land.1 = (f32[512,512]{1,0:T(8,128)}, f32[4,64,128]{2,1,0:T(8,128)}) custom-call(s32[32]{0:T(128)S(1)} %copy-done.2, f32[512,512]{1,0:T(8,128)S(1)} %get-tuple-element.29.second, f32[4,128]{1,0:T(4,128)S(1)} %get-tuple-element.30.inlet_now, s32[2,128]{1,0:T(2,128)S(1)} %pad.4.inlet, s32[64,128]{1,0:T(8,128)S(1)} %bitcast.23, ...), custom_call_target="tpu_custom_call" | custom-call | flops 8589934592 | bytes 2097152 | tf_op jit(solution)/shard_map/land/pallas_call | solution.py:206
  (6 shorter events, 0.0 us)
Async XLA Ops:
  2.7 17.5 %collective-permute-start = (f32[72,512]{1,0:T(8,128)}, f32[72,512]{1,0:T(8,128)S(1)}, u32[]{:S(2)}, u32[]{:S(2)}) collective-permute-start(f32[72,512]{1,0:T(8,128)} %get-tuple-element.18), channel_id=1, source_target_pairs={{0,1},{1,2},{2,3},{3,4},{4,5},{5,6},{6,7},{7,8},{8,9},{9,10},{10,1... | collective-permute-start | bytes 442376 | tf_op jit(solution)/shard_map/ppermute | solution.py:466
  6.7 13.5 %collective-permute-start.1 = (f32[72,512]{1,0:T(8,128)}, f32[72,512]{1,0:T(8,128)S(1)}, u32[]{:S(2)}, u32[]{:S(2)}) collective-permute-start(f32[72,512]{1,0:T(8,128)} %get-tuple-element.19), channel_id=1, source_target_pairs={{1,0},{2,1},{3,2},{4,3},{5,4},{6,5},{7,6},{8,7},{9,8},{10,9},{11,1... | collective-permute-start | bytes 442376 | tf_op jit(solution)/shard_map/ppermute | solution.py:467
  13.9 23.5 %copy-start = (f32[4,8,16,512]{3,2,1,0:T(8,128)S(1)}, f32[4,8,16,512]{3,2,1,0:T(8,128)}, u32[]{:S(2)}) copy-start(f32[4,8,16,512]{3,2,1,0:T(8,128)} %param.11) | copy-start | bytes 3145732
  13.9 23.5 %copy-start.1 = (f32[8,16,512]{2,1,0:T(8,128)S(1)}, f32[8,16,512]{2,1,0:T(8,128)}, u32[]{:S(2)}) copy-start(f32[8,16,512]{2,1,0:T(8,128)} %param.12) | copy-start | bytes 786436
  20.2 22.8 %copy-start.2 = (s32[32]{0:T(128)S(1)}, s32[32]{0:T(128)}, u32[]{:S(2)}) copy-start(s32[32]{0:T(128)} %match.1) | copy-start | bytes 388
  20.2 22.8 %copy-start.4 = (s32[32]{0:T(128)S(1)}, s32[32]{0:T(128)}, u32[]{:S(2)}) copy-start(s32[32]{0:T(128)} %param.15) | copy-start | bytes 388
  20.3 34.1 %all-to-all-start = ((f32[192,4,128]{2,1,0:T(4,128)}), f32[192,4,128]{2,1,0:T(4,128)S(1)}, u32[]{:S(2)}, u32[]{:S(2)}) async-start(f32[192,4,128]{2,1,0:T(4,128)} %slip.1), calls=%async_computation | async-start | bytes 786432 | tf_op jit(solution)/shard_map/all_to_all | solution.py:479
  37.4 11.4 %collective-permute-start.2 = (f32[176,512]{1,0:T(8,128)S(1)}, f32[176,512]{1,0:T(8,128)S(1)}, u32[]{:S(2)}, u32[]{:S(2)}) collective-permute-start(f32[176,512]{1,0:T(8,128)S(1)} %get-tuple-element.27), channel_id=1, source_target_pairs={{0,64},{64,128},{128,192},{1,65},{65,129},{129,193},{2,66},{66,130... | collective-permute-start | bytes 1081352 | tf_op jit(solution)/shard_map/ppermute | solution.py:481
  39.3 10.2 %collective-permute-start.3 = (f32[176,512]{1,0:T(8,128)S(1)}, f32[176,512]{1,0:T(8,128)S(1)}, u32[]{:S(2)}, u32[]{:S(2)}) collective-permute-start(f32[176,512]{1,0:T(8,128)S(1)} %get-tuple-element.28), channel_id=1, source_target_pairs={{64,0},{128,64},{192,128},{65,1},{129,65},{193,129},{66,2},{130,66... | collective-permute-start | bytes 1081352 | tf_op jit(solution)/shard_map/ppermute | solution.py:482
  49.5 4.8 %copy-start.3 = (s32[1,1,64,128]{3,2,1,0:T(8,128)S(1)}, s32[1,1,64,128]{3,2,1,0:T(8,128)}, u32[]{:S(2)}) copy-start(s32[1,1,64,128]{3,2,1,0:T(8,128)} %param.21) | copy-start | bytes 98308

commit v5 on v4

v5 whole, which is shorter than its diff:
```python
import functools

import jax
import jax.numpy as jnp
from jax import lax
from jax.experimental import pallas as pl
from jax.experimental.pallas import tpu as pltpu
from jax.sharding import PartitionSpec as P

VM = pl.BlockSpec(memory_space=pltpu.VMEM)
SM = pl.BlockSpec(memory_space=pltpu.SMEM)
HB = pl.BlockSpec(memory_space=pltpu.HBM)


def halves(value):
    high = value.astype(jnp.bfloat16)
    low = (value - high.astype(jnp.float32)).astype(jnp.bfloat16)
    return high, low


def column_hot(cells, depth):
    at = lax.broadcasted_iota(jnp.int32, (depth, cells.shape[1]), 0)
    return jnp.where(at == (cells & (depth - 1)), 1.0, 0.0).astype(jnp.bfloat16)


def sample_kernel(GP, counts, flow, anchor, sampled, table, packed):
    partners, cap = anchor.shape
    total, depth = flow.shape
    comps = sampled.shape[1]
    rows = total // comps
    shift = depth.bit_length() - 1
    cap_shift = cap.bit_length() - 1
    lane = lax.broadcasted_iota(jnp.int32, (1, cap), 1)
    packed[...] = jnp.zeros_like(packed)

    def pack(p, base):
        begin = base & (cap - 1)
        spot = base >> cap_shift
        turned = pltpu.roll(anchor[pl.ds(p, 1), :], begin, 1)
        pltpu.store(packed.at[pl.ds(spot, 1), :], turned, mask=lane >= begin)
        pltpu.store(packed.at[pl.ds(spot + 1, 1), :], turned, mask=lane < begin)
        return base + counts[p]

    used = lax.fori_loop(0, partners, pack, 0, unroll=8)
    high, low = halves(flow[...])
    table[0:total] = high
    table[total:] = low

    def group(g, carry):
        first = g * GP
        cells = jnp.concatenate([packed[pl.ds(first + i, 1), :] for i in range(GP)], axis=1)
        hot = column_hot(cells, depth)
        picked = jnp.dot(table[...], hot, preferred_element_type=jnp.float32)
        row = lax.broadcasted_iota(jnp.int32, (rows, cells.shape[1]), 0) == (cells >> shift)
        parts = []
        for c in range(comps):
            both = picked[c * rows : (c + 1) * rows] + picked[total + c * rows : total + (c + 1) * rows]
            parts.append(jnp.sum(jnp.where(row, both, 0.0), axis=0, keepdims=True))
        found = jnp.concatenate(parts, axis=0)
        for i in range(GP):
            sampled[first + i] = found[:, i * cap : (i + 1) * cap]
        return carry

    lax.fori_loop(0, (used + GP * cap - 1) // (GP * cap), group, 0)


def sample(comps, counts, flow, anchor, GP=4):
    partners, cap = anchor.shape
    return pl.pallas_call(
        functools.partial(sample_kernel, GP),
        out_shape=jax.ShapeDtypeStruct((partners + 8, comps, cap), jnp.float32),
        in_specs=[SM, VM, VM],
        out_specs=VM,
        scratch_shapes=[
            pltpu.VMEM((2 * flow.shape[0], flow.shape[1]), jnp.bfloat16),
            pltpu.VMEM((partners + 8, cap), jnp.int32),
        ],
        compiler_params=pltpu.CompilerParams(vmem_limit_bytes=24 * 1024 * 1024),
        cost_estimate=pl.CostEstimate(flops=2 * 8192 * 512 * 1024, bytes_accessed=2**21, transcendentals=0),
        name="sample",
    )(counts, flow, anchor)


chunks = 4


def slip_kernel(counts, sampled, state, rate, mass, ports, above, across, below, far, out, whole, out_sems):
    comps, partners, cap = state.shape
    per = ports.shape[1]
    cap_shift = cap.bit_length() - 1
    last = above.shape[0] - 8
    lane = lax.broadcasted_iota(jnp.int32, (1, cap), 1)
    whole[:, 0:per] = ports[...]
    whole[:, per : 2 * per] = above[last : last + comps, 0:per]
    whole[:, 2 * per : 3 * per] = across[...]
    whole[:, 3 * per :] = below[last : last + comps, 0:per]

    def finish(p, base):
        n = counts[p]
        begin = base & (cap - 1)
        spot = base >> cap_shift
        both = jnp.where(lane >= begin, sampled[spot], sampled[spot + 1])
        value = pltpu.roll(both, (cap - begin) & (cap - 1), 1)
        own = jnp.concatenate([state[c, pl.ds(p, 1), :] for c in range(comps)], axis=0)
        r = rate[pl.ds(p, 1), :]
        drop = r * (own - value)
        live = lane < n
        out[3 * p] = jnp.where(live, own - drop, 0.0)
        out[3 * p + 1] = jnp.where(live, mass[pl.ds(p, 1), :] * drop, 0.0)
        out[3 * p + 2] = whole[...]
        return base + n

    block = partners // chunks
    base = 0
    copies = []
    for i in range(chunks):
        base = lax.fori_loop(i * block, (i + 1) * block, finish, base, unroll=8)
        part = pl.ds(3 * i * block, 3 * block)
        copies.append(pltpu.make_async_copy(out.at[part], far.at[part], out_sems.at[i]))
        copies[i].start()
    for copy in copies:
        copy.wait()


def slip(counts, sampled, state, rate, mass, ports, above, across, below):
    comps, partners, cap = state.shape
    return pl.pallas_call(
        slip_kernel,
        out_shape=jax.ShapeDtypeStruct((partners * 3, comps, cap), jnp.float32),
        in_specs=[SM] + [VM] * 8,
        out_specs=HB,
        scratch_shapes=[
            pltpu.VMEM((partners * 3, comps, cap), jnp.float32),
            pltpu.VMEM((comps, cap), jnp.float32),
            pltpu.SemaphoreType.DMA((chunks,)),
        ],
        compiler_params=pltpu.CompilerParams(vmem_limit_bytes=24 * 1024 * 1024),
        cost_estimate=pl.CostEstimate(flops=2 * 10**6, bytes_accessed=2**20, transcendentals=0),
        name="slip",
    )(counts, sampled, state, rate, mass, ports, above, across, below)


def land_kernel(GP, match, second, inlet_now, inlet, arrival, arrived, flow_out, state_out, last_ref, last, packed, sem):
    comps, partners, cap = state_out.shape
    total, depth = second.shape
    rows = total // comps
    shift = depth.bit_length() - 1
    cap_shift = cap.bit_length() - 1
    entries = match.shape[0]
    per = entries
    nt = (((1,), (1,)), ((), ()))
    slot = lax.broadcasted_iota(jnp.int32, (1, cap), 1)

    def ends(p, carry):
        moved = arrived[3 * p]
        gift = arrived[3 * p + 1]
        for c in range(comps):
            state_out[c, pl.ds(p, 1), :] = moved[c : c + 1]
        biggest = jnp.max(jnp.abs(gift), axis=0, keepdims=True)
        last_ref[pl.ds(p, 1), :] = jnp.where(biggest > 0.0, slot + 1, 0)
        return carry

    lax.fori_loop(0, partners, ends, 0, unroll=8)
    last_ref[partners:, :] = jnp.zeros_like(last_ref[partners:, :])
    top = jnp.max(last_ref[...].T, axis=0, keepdims=True)
    last_ref[0:1, :] = top
    fetch = pltpu.make_async_copy(last_ref.at[0:1, :], last, sem)
    fetch.start()

    def spread(cells, values):
        row = lax.broadcasted_iota(jnp.int32, (rows, cells.shape[1]), 0) == (cells >> shift)
        high, low = halves(values)
        parts = []
        for part in (high.astype(jnp.float32), low.astype(jnp.float32)):
            for c in range(comps):
                parts.append(jnp.where(row, part[c : c + 1], 0.0).astype(jnp.bfloat16))
        return jnp.concatenate(parts, axis=0)

    def product(cells, values):
        both = lax.dot_general(spread(cells, values), column_hot(cells, depth), nt, preferred_element_type=jnp.float32)
        return both[:total] + both[total:]

    section = lax.axis_index("sec")
    sections = cap // per
    target = jnp.zeros((comps, cap), jnp.float32)
    for k in range(entries):
        port = match[k]
        device = port // entries
        place = (device // partners + sections - section) % sections * per + port % entries
        turned = pltpu.roll(arrived[3 * (device % partners) + 2], (k + cap - place) % cap, 1)
        target = jnp.where(slot == k, turned, target)
    change = jnp.where(slot < entries, 0.5 * (target - inlet_now[...]), 0.0)
    flow_out[...] = second[...] + product(inlet[0:1, :], change)
    packed[...] = jnp.zeros_like(packed)
    fetch.wait()

    def pack(p, base):
        begin = base & (cap - 1)
        spot = base >> cap_shift
        cells = arrival[pl.ds(p, 1), :].astype(jnp.float32)
        both = jnp.concatenate([arrived[3 * p + 1], jnp.broadcast_to(cells, (8 - comps, cap))], axis=0)
        turned = pltpu.roll(both, begin, 1)
        wide = lax.broadcasted_iota(jnp.int32, (8, cap), 1)
        pltpu.store(packed.at[spot], turned, mask=wide >= begin)
        pltpu.store(packed.at[spot + 1], turned, mask=wide < begin)
        return base + last[0, p]

    used = lax.fori_loop(0, partners, pack, 0, unroll=8)

    def group(g, carry):
        first = g * GP
        both = jnp.concatenate([packed[first + i] for i in range(GP)], axis=1)
        flow_out[...] += product(both[comps : comps + 1].astype(jnp.int32), both[:comps])
        return carry

    lax.fori_loop(0, (used + GP * cap - 1) // (GP * cap), group, 0)


def land(match, second, inlet_now, inlet, arrival, arrived, GP=8):
    partners, cap = arrival.shape
    comps = arrived.shape[1]
    return pl.pallas_call(
        functools.partial(land_kernel, GP),
        out_shape=(
            jax.ShapeDtypeStruct(second.shape, jnp.float32),
            jax.ShapeDtypeStruct((comps, partners, cap), jnp.float32),
        ),
        in_specs=[SM] + [VM] * 5,
        out_specs=(VM, VM),
        scratch_shapes=[
            pltpu.VMEM((cap, cap), jnp.int32),
            pltpu.SMEM((1, cap), jnp.int32),
            pltpu.VMEM((partners + 8, 8, cap), jnp.float32),
            pltpu.SemaphoreType.DMA,
        ],
        compiler_params=pltpu.CompilerParams(vmem_limit_bytes=24 * 1024 * 1024),
        cost_estimate=pl.CostEstimate(flops=2 * 8192 * 512 * 1024, bytes_accessed=2**21, transcendentals=0),
        name="land",
    )(match, second, inlet_now, inlet, arrival, arrived)


def tendency(plane, upper, lower, viscosity, keep):
    place = lax.broadcasted_iota(jnp.int32, (1, viscosity.shape[1]), 1)
    depth = viscosity.shape[1]
    centers, laps, dz, dx, dy = [], [], [], [], []
    for c in range(len(plane)):
        whole = plane[c]
        center = whole[:keep]
        up_x = pltpu.roll(whole, whole.shape[0] - 1, 0)[:keep]
        low_x = pltpu.roll(whole, 1, 0)[:keep]
        up_y = jnp.where(place == depth - 1, 0.0, pltpu.roll(center, depth - 1, 1))
        low_y = jnp.where(place == 0, 0.0, pltpu.roll(center, 1, 1))
        centers.append(center)
        laps.append((upper[c] + lower[c]) + (up_x + low_x) + (up_y + low_y) - 6.0 * center)
        dz.append(upper[c] - lower[c])
        dx.append(up_x - low_x)
        dy.append(up_y - low_y)
    strain = sum(d[c] * d[c] for c in range(3) for d in (dz, dx, dy)) * 0.25
    eddy = viscosity * (1.0 + strain / (1.0 + strain))
    out = []
    for c in range(len(plane)):
        carried = centers[0] * dz[c] + centers[1] * dx[c] + centers[2] * dy[c]
        out.append(0.5 * (eddy * laps[c]) - 0.25 * carried)
    return centers, out


def cap_kernel(comps, depth_z, width, flow, viscosity, ports, low_out, high_out, tile, sems):
    tile[...] = jnp.zeros_like(tile)
    tile[0:comps, 0 : ports.shape[1]] = ports[...]
    copies = []

    def copy(source, target):
        copies.append(pltpu.make_async_copy(source, target, sems.at[len(copies)]))
        copies[-1].start()

    two = 2 * width
    last = (depth_z - 1) * width
    for c in range(comps):
        base = c * depth_z * width
        copy(flow.at[base : base + two, :], low_out.at[c * two : (c + 1) * two, :])
        copy(flow.at[base + last - width : base + last + width, :], high_out.at[c * two : (c + 1) * two, :])
    base = comps * two
    copy(viscosity.at[0:width, :], low_out.at[base : base + width, :])
    copy(viscosity.at[last : last + width, :], high_out.at[base : base + width, :])
    copy(tile, low_out.at[base + width :, :])
    copy(tile, high_out.at[base + width :, :])
    for started in copies:
        started.wait()


def caps(comps, depth_z, width, flow, viscosity, ports):
    shape = jax.ShapeDtypeStruct((2 * comps * width + width + 8, flow.shape[1]), jnp.float32)
    return pl.pallas_call(
        functools.partial(cap_kernel, comps, depth_z, width),
        out_shape=(shape, shape),
        in_specs=[HB, HB, VM],
        out_specs=(HB, HB),
        scratch_shapes=[pltpu.VMEM((8, flow.shape[1]), jnp.float32), pltpu.SemaphoreType.DMA((2 * comps + 4,))],
        compiler_params=pltpu.CompilerParams(vmem_limit_bytes=60 * 1024 * 1024),
        name="caps",
    )(flow, viscosity, ports)


def edge_kernel(comps, depth_z, width, flow, viscosity, below, above, low_out, high_out, bottom, top):
    section = lax.axis_index("sec")
    bottom[...] = jnp.where(section > 0, below[0 : bottom.shape[0], :], 0.0)
    top[...] = jnp.where(section < lax.axis_size("sec") - 1, above[0 : top.shape[0], :], 0.0)
    two = 2 * width
    for k in range(comps * depth_z):
        low_out[2 * k : 2 * k + 2, :] = flow[k * width : k * width + 2, :]
        high_out[2 * k : 2 * k + 2, :] = flow[(k + 1) * width - 2 : (k + 1) * width, :]
    base = 2 * comps * depth_z
    for c in range(comps):
        low_out[base + 2 * c : base + 2 * c + 1, :] = bottom[c * two + width : c * two + width + 1, :]
        low_out[base + 2 * c + 1 : base + 2 * c + 2, :] = top[c * two : c * two + 1, :]
        high_out[base + 2 * c : base + 2 * c + 1, :] = bottom[(c + 1) * two - 1 : (c + 1) * two, :]
        high_out[base + 2 * c + 1 : base + 2 * c + 2, :] = top[c * two + width - 1 : c * two + width, :]
    base += 2 * comps
    for z in range(depth_z):
        low_out[base + z : base + z + 1, :] = viscosity[z * width : z * width + 1, :]
        high_out[base + z : base + z + 1, :] = viscosity[(z + 1) * width - 1 : (z + 1) * width, :]


def edges(comps, depth_z, width, flow, viscosity, below, above):
    depth = flow.shape[1]
    shape = jax.ShapeDtypeStruct((2 * comps * (depth_z + 1) + depth_z, depth), jnp.float32)
    halo = jax.ShapeDtypeStruct(((2 * comps + 1) * width, depth), jnp.float32)
    return pl.pallas_call(
        functools.partial(edge_kernel, comps, depth_z, width),
        out_shape=(shape, shape, halo, halo),
        in_specs=[VM] * 4,
        out_specs=(VM,) * 4,
        compiler_params=pltpu.CompilerParams(vmem_limit_bytes=24 * 1024 * 1024),
        name="edges",
    )(flow, viscosity, below, above)


def inner_kernel(comps, depth_z, width, flow, viscosity, below, above, first):
    two = 2 * width

    def own(z):
        if z < 0:
            return [below[c * two + (2 + z) * width : c * two + (3 + z) * width, :] for c in range(comps)]
        if z >= depth_z:
            return [above[c * two + (z - depth_z) * width : c * two + (z - depth_z + 1) * width, :] for c in range(comps)]
        return [flow[(c * depth_z + z) * width : (c * depth_z + z + 1) * width, :] for c in range(comps)]

    for z in range(-1, depth_z + 1):
        if z < 0:
            visc = below[comps * two :, :]
        elif z == depth_z:
            visc = above[comps * two :, :]
        else:
            visc = viscosity[z * width : (z + 1) * width, :]
        centers, change = tendency(own(z), own(z + 1), own(z - 1), visc, width)
        for c in range(comps):
            first[c, z + 1, 0:width, :] = centers[c] + change[c]


def inner(comps, depth_z, width, flow, viscosity, below, above):
    depth = flow.shape[1]
    return pl.pallas_call(
        functools.partial(inner_kernel, comps, depth_z, width),
        out_shape=jax.ShapeDtypeStruct((comps, depth_z + 2, width, depth), jnp.float32),
        in_specs=[VM] * 4,
        out_specs=VM,
        compiler_params=pltpu.CompilerParams(vmem_limit_bytes=24 * 1024 * 1024),
        cost_estimate=pl.CostEstimate(flops=10**7, bytes_accessed=2**22, transcendentals=0),
        name="inner",
    )(flow, viscosity, below, above)


def outer_kernel(comps, depth_z, width, flow, viscosity, below, above, first, left, right, inlet, second_out, inlet_now, strip, visc, started, table):
    depth = flow.shape[1]
    two = 2 * width
    rows = depth_z * width
    total = comps * rows
    base = 2 * comps * depth_z
    strip[...] = jnp.zeros_like(strip)
    visc[...] = jnp.zeros_like(visc)
    for c in range(comps):
        for z in range(-2, depth_z + 2):
            if z < 0:
                ref, spot = below, c * two + (2 + z) * width
            elif z >= depth_z:
                ref, spot = above, c * two + (z - depth_z) * width
            else:
                ref, spot = flow, (c * depth_z + z) * width
            strip[c, z + 2, 2:4, :] = ref[spot : spot + 2, :]
            strip[c, z + 2, 4:6, :] = ref[spot + width - 2 : spot + width, :]
            if 0 <= z < depth_z:
                k = 2 * (c * depth_z + z)
                strip[c, z + 2, 0:2, :] = left[k : k + 2, :]
                strip[c, z + 2, 6:8, :] = right[k : k + 2, :]
            elif z in (-1, depth_z):
                k = base + 2 * c + (z == depth_z)
                strip[c, z + 2, 1:2, :] = left[k : k + 1, :]
                strip[c, z + 2, 6:7, :] = right[k : k + 1, :]
    side = base + 2 * comps
    for z in range(-1, depth_z + 1):
        if z < 0:
            ref, spot = below, comps * two
        elif z == depth_z:
            ref, spot = above, comps * two
        else:
            ref, spot = viscosity, z * width
            visc[z + 1, 1:2, :] = left[side + z : side + z + 1, :]
            visc[z + 1, 6:7, :] = right[side + z : side + z + 1, :]
        visc[z + 1, 2:4, :] = ref[spot : spot + 2, :]
        visc[z + 1, 4:6, :] = ref[spot + width - 2 : spot + width, :]

    place = lax.broadcasted_iota(jnp.int32, (width, 1), 0)
    blank = jnp.zeros((6, depth), jnp.float32)

    def one(z, carry):
        plane, upper, lower = ([strip[c, z + 1 + d] for c in range(comps)] for d in (0, 1, -1))
        centers, change = tendency(plane, upper, lower, visc[z], 8)
        for c in range(comps):
            edge = centers[c] + change[c]
            mine = first[c, z]
            mine = jnp.where(place == 0, edge[2:3], mine)
            mine = jnp.where(place == width - 1, edge[5:6], mine)
            started[c, z, 0:width, :] = mine
            started[c, z, width : width + 8, :] = jnp.concatenate([edge[6:7], blank, edge[1:2]], axis=0)
        return carry

    lax.fori_loop(0, depth_z + 2, one, 0)

    def second(z, carry):
        plane = [started[c, z + 1] for c in range(comps)]
        upper, lower = ([started[c, z + 1 + d, 0:width, :] for c in range(comps)] for d in (1, -1))
        at = pl.multiple_of(z * width, width)
        centers, change = tendency(plane, upper, lower, viscosity[pl.ds(at, width), :], width)
        for c in range(comps):
            spot = pl.multiple_of((c * depth_z + z) * width, width)
            value = 0.5 * flow[pl.ds(spot, width), :] + 0.5 * (centers[c] + change[c])
            second_out[pl.ds(spot, width), :] = value
            high, low = halves(value)
            table[pl.ds(spot, width), :] = high
            table[pl.ds(total + spot, width), :] = low
        return carry

    lax.fori_loop(0, depth_z, second, 0)

    cells = inlet[0:1, :]
    picked = jnp.dot(table[...], column_hot(cells, depth), preferred_element_type=jnp.float32)
    row = lax.broadcasted_iota(jnp.int32, (rows, cells.shape[1]), 0) == (cells >> (depth.bit_length() - 1))
    for c in range(comps):
        both = picked[c * rows : (c + 1) * rows] + picked[total + c * rows : total + (c + 1) * rows]
        inlet_now[c : c + 1, :] = jnp.sum(jnp.where(row, both, 0.0), axis=0, keepdims=True)


def outer(comps, depth_z, width, flow, viscosity, below, above, first, left, right, inlet):
    depth = flow.shape[1]
    return pl.pallas_call(
        functools.partial(outer_kernel, comps, depth_z, width),
        out_shape=(
            jax.ShapeDtypeStruct(flow.shape, jnp.float32),
            jax.ShapeDtypeStruct((comps, inlet.shape[1]), jnp.float32),
        ),
        in_specs=[VM] * 8,
        out_specs=(VM, VM),
        scratch_shapes=[
            pltpu.VMEM((comps, depth_z + 4, 8, depth), jnp.float32),
            pltpu.VMEM((depth_z + 2, 8, depth), jnp.float32),
            pltpu.VMEM((comps, depth_z + 2, width + 8, depth), jnp.float32),
            pltpu.VMEM((2 * flow.shape[0], depth), jnp.bfloat16),
        ],
        compiler_params=pltpu.CompilerParams(vmem_limit_bytes=24 * 1024 * 1024),
        cost_estimate=pl.CostEstimate(flops=10**7, bytes_accessed=2**22, transcendentals=0),
        name="outer",
    )(flow, viscosity, below, above, first, left, right, inlet)


def on_device(
    flow_field,
    viscosity,
    port_plane,
    port_match,
    inlet_cell,
    inclusion_state,
    response_rate,
    inclusion_mass,
    anchor_cell,
    live_counts,
    arrival_cell,
):
    comps, depth_z, width, depth = flow_field.shape
    partners, cap = anchor_cell.shape[2:]
    sizes = (comps, depth_z, width)
    flow = flow_field.reshape(-1, depth)
    visc = viscosity.reshape(-1, depth)
    count = lax.axis_size("tile")
    forth = [(i, i + 1) for i in range(count - 1)]
    back = [(i + 1, i) for i in range(count - 1)]
    levels = lax.axis_size("sec")
    up = [(i, (i + 1) % levels) for i in range(levels)]
    down = [((i + 1) % levels, i) for i in range(levels)]
    over = [(i, (i + levels // 2) % levels) for i in range(levels)]

    low_cap, high_cap = caps(*sizes, flow, visc, port_plane)
    below = lax.ppermute(high_cap, "sec", up)
    above = lax.ppermute(low_cap, "sec", down)
    across = lax.ppermute(port_plane, "sec", over)
    counts = live_counts.reshape(-1)
    counts, low_cap, high_cap = lax.optimization_barrier((counts, low_cap, high_cap))
    sampled = sample(comps, counts, flow, anchor_cell.reshape(partners, cap))
    outgoing = slip(
        counts,
        sampled,
        inclusion_state.reshape(comps, partners, cap),
        response_rate.reshape(partners, cap),
        inclusion_mass.reshape(partners, cap),
        port_plane,
        above,
        across,
        below,
    )
    below, above, outgoing = lax.optimization_barrier((below, above, outgoing))
    arrived = lax.all_to_all(outgoing, "tile", split_axis=0, concat_axis=0, tiled=True)
    low_edge, high_edge, bottom, top = edges(*sizes, flow, visc, below, above)
    left = lax.ppermute(high_edge, "tile", forth)
    right = lax.ppermute(low_edge, "tile", back)
    inlet = jnp.pad(jnp.stack([inlet_cell, port_match]), ((0, 0), (0, cap - inlet_cell.shape[0])))
    first = inner(*sizes, flow, visc, bottom, top)
    second, inlet_now = outer(*sizes, flow, visc, bottom, top, first, left, right, inlet)
    flow_next, arrived_state = land(
        port_match, second, inlet_now, inlet, arrival_cell.reshape(partners, cap), arrived
    )
    return flow_next.reshape(flow_field.shape), arrived_state.reshape(inclusion_state.shape)


def solution(mesh):
    return jax.shard_map(
        on_device,
        mesh=mesh,
        in_specs=(
            P(None, "sec", "tile", None),
            P("sec", "tile", None),
            P(None, ("sec", "tile")),
            P(("sec", "tile")),
            P(("sec", "tile")),
            P(None, "sec", "tile", None, None),
            P("sec", "tile", None, None),
            P("sec", "tile", None, None),
            P("sec", "tile", None, None),
            P("sec", "tile", None),
            P("sec", "tile", None, None),
        ),
        out_specs=(P(None, "sec", "tile", None), P(None, "sec", "tile", None, None)),
        check_vma=False,
    )
```

time: 62.7 us -> 77.4 us (1.23)
  the two profiles are of different devices: /device:TPU:2 before, /device:TPU:88 now
where the time goes in v5:
time: 77.4 us; the launch traced here: 76.8 us
  Pallas kernels  39.2 us (51%)
  starting transfers between devices  24.5 us (32%)
  waiting for transfers between devices  12.2 us (16%)
  between operations  0.87 us (1%)
    pallas_call x1, Pallas kernels, caps(): pl.pallas_call(functools.partial(cap_kernel, comps, depth_z, width), out_...  19.8 us
    all_to_all x1, starting transfers between devices, on_device(): lax.all_to_all(outgoing, 'tile', split_axis=0, concat_axis=0, tiled=True)  12.8 us
    pallas_call x1, Pallas kernels, land(): pl.pallas_call(functools.partial(land_kernel, GP), out_shape=(jax.ShapeDt...  7.72 us
    ppermute x1, waiting for transfers between devices, on_device(): right = lax.ppermute(low_edge, 'tile', back)  5.54 us
    ppermute x1, starting transfers between devices, on_device(): left = lax.ppermute(high_edge, 'tile', forth)  4.91 us
    pallas_call x1, Pallas kernels, sample(): pl.pallas_call(functools.partial(sample_kernel, GP), out_shape=jax.ShapeD...  4.18 us
    pallas_call x1, Pallas kernels, outer(): pl.pallas_call(functools.partial(outer_kernel, comps, depth_z, width), ou...  3.85 us
    ppermute x1, waiting for transfers between devices, on_device(): left = lax.ppermute(high_edge, 'tile', forth)  3.55 us
  transfers between devices with their start and end apart: 6, of which 3 were waited for; matrix products, arithmetic and copies ran while one was open for 0% of the time, Pallas kernels for 38%

profile of v5, /device:TPU:88, one launch (start us, length us, event | category | flops | bytes accessed | tf_op | source)
XLA Modules:
  0.0 76.8 jit_solution(8120104823636148171)
XLA Ops:
  0.7 1.6 %collective-permute-start.2 = (f32[4,32]{1,0:T(4,128)}, f32[4,32]{1,0:T(4,128)S(1)}, u32[]{:S(2)}, u32[]{:S(2)}) collective-permute-start(f32[4,32]{1,0:T(4,128)} %ports.3), channel_id=1, source_target_pairs={{0,128},{64,192},{128,0},{192,64},{1,129},{65,193},{129,1},{193,65... | collective-permute-start | bytes 1544 | tf_op jit(solution)/shard_map/ppermute | solution.py:504
  2.2 19.8 %caps.1 = (f32[152,512]{1,0:T(8,128)}, f32[152,512]{1,0:T(8,128)}) custom-call(f32[512,512]{1,0:T(8,128)} %bitcast.14, f32[128,512]{1,0:T(8,128)} %bitcast.19, f32[4,32]{1,0:T(4,128)} %ports.3), custom_call_target="tpu_custom_call" | custom-call | tf_op jit(solution)/shard_map/caps/pallas_call | solution.py:293
  22.0 0.1 collective-permute-start
  22.1 1.7 %collective-permute-start.1 = (f32[152,512]{1,0:T(8,128)}, f32[152,512]{1,0:T(8,128)S(1)}, u32[]{:S(2)}, u32[]{:S(2)}) collective-permute-start(f32[152,512]{1,0:T(8,128)} %get-tuple-element.17), channel_id=1, source_target_pairs={{64,0},{128,64},{192,128},{0,192},{65,1},{129,65},{193,129},{1,193... | collective-permute-start | bytes 933896 | tf_op jit(solution)/shard_map/ppermute | solution.py:503
  23.9 0.0 copy-start.3
  23.9 0.0 copy-start.4
  23.9 0.0 copy-start.5
  23.9 4.2 %sample.1.sampled = f32[72,4,128]{2,1,0:T(4,128)S(1)} custom-call(s32[64]{0:T(128)S(1)} %bitcast.26, f32[512,512]{1,0:T(8,128)S(1)} %bitcast.15, s32[64,128]{1,0:T(8,128)S(1)} %bitcast.29), custom_call_target="tpu_custom_call" | custom-call | flops 8589934592 | bytes 2097152 | tf_op jit(solution)/shard_map/sample/pallas_call | solution.py:69
  28.1 0.0 copy-start.1
  28.1 0.0 collective-permute-done.2.across
  28.1 3.1 %collective-permute-done.below = f32[152,512]{1,0:T(8,128)S(1)} collective-permute-done((f32[152,512]{1,0:T(8,128)}, f32[152,512]{1,0:T(8,128)S(1)}, u32[]{:S(2)}, u32[]{:S(2)}) %collective-permute-start) | collective-permute-done | bytes 311328 | tf_op jit(solution)/shard_map/ppermute | solution.py:502
  31.2 2.0 %slip.1 = f32[192,4,128]{2,1,0:T(4,128)} custom-call(s32[64]{0:T(128)S(1)} %bitcast.27, f32[72,4,128]{2,1,0:T(4,128)S(1)} %sample.1.sampled, f32[4,64,128]{2,1,0:T(8,128)S(1)} %bitcast.23, f32[64,128]{1,0:T(8,128)S(1)} %bitcast.24, f32[64,128]{1,0:T(8,128)S(1)} %bitcast.25, f32[4,32]{1,0:T(4,128)S(1)} %copy-done.5, ...), custom_call_target="tpu_custom_call" | custom-call | flops 2000000 | bytes 1048576 | tf_op jit(solution)/shard_map/slip/pallas_call | solution.py:127
  33.2 0.0 copy-start.7
  33.3 0.0 copy-start.10
  33.3 12.8 %all-to-all-start = ((f32[192,4,128]{2,1,0:T(4,128)}), f32[192,4,128]{2,1,0:T(4,128)S(1)}, u32[]{:S(2)}, u32[]{:S(2)}) async-start(f32[192,4,128]{2,1,0:T(4,128)} %slip.1), calls=%async_computation | async-start | bytes 786432 | tf_op jit(solution)/shard_map/all_to_all | solution.py:520
  46.1 0.2 edges.1
  46.3 4.9 %collective-permute-start.3 = (f32[80,512]{1,0:T(8,128)S(1)}, f32[80,512]{1,0:T(8,128)S(1)}, u32[]{:S(2)}, u32[]{:S(2)}) collective-permute-start(f32[80,512]{1,0:T(8,128)S(1)} %get-tuple-element.23), channel_id=1, source_target_pairs={{0,1},{1,2},{2,3},{3,4},{4,5},{5,6},{6,7},{7,8},{8,9},{9,10},{10,1... | collective-permute-start | bytes 491528 | tf_op jit(solution)/shard_map/ppermute | solution.py:522
  51.2 3.4 %collective-permute-start.4 = (f32[80,512]{1,0:T(8,128)S(1)}, f32[80,512]{1,0:T(8,128)S(1)}, u32[]{:S(2)}, u32[]{:S(2)}) collective-permute-start(f32[80,512]{1,0:T(8,128)S(1)} %get-tuple-element.24), channel_id=1, source_target_pairs={{1,0},{2,1},{3,2},{4,3},{5,4},{6,5},{7,6},{8,7},{9,8},{10,9},{11,1... | collective-permute-start | bytes 491528 | tf_op jit(solution)/shard_map/ppermute | solution.py:523
  54.7 1.5 %inner.1.first = f32[4,10,16,512]{3,2,1,0:T(8,128)S(1)} custom-call(f32[512,512]{1,0:T(8,128)S(1)} %bitcast.17, f32[128,512]{1,0:T(8,128)S(1)} %bitcast.21, f32[144,512]{1,0:T(8,128)S(1)} %get-tuple-element.21.below, f32[144,512]{1,0:T(8,128)S(1)} %get-tuple-element.22.above), custom_call_target="tpu_custom_call" | custom-call | flops 10000000 | bytes 4194304 | tf_op jit(solution)/shard_map/inner/pallas_call | solution.py:362
  56.1 0.0 copy-start.9
  56.1 3.6 %collective-permute-done.3.left = f32[80,512]{1,0:T(8,128)S(1)} collective-permute-done((f32[80,512]{1,0:T(8,128)S(1)}, f32[80,512]{1,0:T(8,128)S(1)}, u32[]{:S(2)}, u32[]{:S(2)}) %collective-permute-start.3) | collective-permute-done | bytes 163872 | tf_op jit(solution)/shard_map/ppermute | solution.py:522
  59.7 5.5 %collective-permute-done.4.right = f32[80,512]{1,0:T(8,128)S(1)} collective-permute-done((f32[80,512]{1,0:T(8,128)S(1)}, f32[80,512]{1,0:T(8,128)S(1)}, u32[]{:S(2)}, u32[]{:S(2)}) %collective-permute-start.4) | collective-permute-done | bytes 163872 | tf_op jit(solution)/shard_map/ppermute | solution.py:523
  65.2 3.8 %outer.1 = (f32[512,512]{1,0:T(8,128)S(1)}, f32[4,128]{1,0:T(4,128)S(1)}) custom-call(f32[512,512]{1,0:T(8,128)S(1)} %bitcast.18, f32[128,512]{1,0:T(8,128)S(1)} %bitcast.22, f32[144,512]{1,0:T(8,128)S(1)} %get-tuple-element.21.below, f32[144,512]{1,0:T(8,128)S(1)} %get-tuple-element.22.above, f32[4,10,16,512]{3,2,1,0:T(8,128)S(1)} %inner.1.first, ...), custom_call_target="tpu_custom_call" | custom-call | flops 10000000 | bytes 4194304 | tf_op jit(solution)/shard_map/outer/pallas_call | solution.py:455
  69.1 7.7 %land.1 = (f32[512,512]{1,0:T(8,128)}, f32[4,64,128]{2,1,0:T(8,128)}) custom-call(s32[32]{0:T(128)S(1)} %copy-done.7, f32[512,512]{1,0:T(8,128)S(1)} %get-tuple-element.25.second, f32[4,128]{1,0:T(4,128)S(1)} %get-tuple-element.26.inlet_now, s32[2,128]{1,0:T(2,128)S(1)} %pad.4.inlet, s32[64,128]{1,0:T(8,128)S(1)} %bitcast.30, ...), custom_call_target="tpu_custom_call" | custom-call | flops 8589934592 | bytes 2097152 | tf_op jit(solution)/shard_map/land/pallas_call | solution.py:222
  (19 shorter events, 0.1 us)
Async XLA Ops:
  0.6 23.2 %copy-start = (f32[4,8,16,512]{3,2,1,0:T(8,128)S(1)}, f32[4,8,16,512]{3,2,1,0:T(8,128)}, u32[]{:S(2)}) copy-start(f32[4,8,16,512]{3,2,1,0:T(8,128)} %param.11) | copy-start | bytes 3145732
  0.6 23.2 %copy-start.6 = (s32[1,1,64]{2,1,0:T(1,128)S(1)}, s32[1,1,64]{2,1,0:T(1,128)}, u32[]{:S(2)}) copy-start(s32[1,1,64]{2,1,0:T(1,128)} %param.20) | copy-start | bytes 772
  0.6 23.2 %copy-start.8 = (s32[1,1,64,128]{3,2,1,0:T(8,128)S(1)}, s32[1,1,64,128]{3,2,1,0:T(8,128)}, u32[]{:S(2)}) copy-start(s32[1,1,64,128]{3,2,1,0:T(8,128)} %param.19) | copy-start | bytes 98308
  0.7 27.5 %collective-permute-start.2 = (f32[4,32]{1,0:T(4,128)}, f32[4,32]{1,0:T(4,128)S(1)}, u32[]{:S(2)}, u32[]{:S(2)}) collective-permute-start(f32[4,32]{1,0:T(4,128)} %ports.3), channel_id=1, source_target_pairs={{0,128},{64,192},{128,0},{192,64},{1,129},{65,193},{129,1},{193,65... | collective-permute-start | bytes 1544 | tf_op jit(solution)/shard_map/ppermute | solution.py:504
  22.0 9.1 %collective-permute-start = (f32[152,512]{1,0:T(8,128)}, f32[152,512]{1,0:T(8,128)S(1)}, u32[]{:S(2)}, u32[]{:S(2)}) collective-permute-start(f32[152,512]{1,0:T(8,128)} %get-tuple-element.16), channel_id=1, source_target_pairs={{0,64},{64,128},{128,192},{192,0},{1,65},{65,129},{129,193},{193,1... | collective-permute-start | bytes 933896 | tf_op jit(solution)/shard_map/ppermute | solution.py:502
  22.1 9.1 %collective-permute-start.1 = (f32[152,512]{1,0:T(8,128)}, f32[152,512]{1,0:T(8,128)S(1)}, u32[]{:S(2)}, u32[]{:S(2)}) collective-permute-start(f32[152,512]{1,0:T(8,128)} %get-tuple-element.17), channel_id=1, source_target_pairs={{64,0},{128,64},{192,128},{0,192},{65,1},{129,65},{193,129},{1,193... | collective-permute-start | bytes 933896 | tf_op jit(solution)/shard_map/ppermute | solution.py:503
  23.9 7.3 %copy-start.2 = (f32[4,1,1,64,128]{4,3,2,1,0:T(8,128)S(1)}, f32[4,1,1,64,128]{4,3,2,1,0:T(8,128)}, u32[]{:S(2)}) copy-start(f32[4,1,1,64,128]{4,3,2,1,0:T(8,128)} %param.16) | copy-start | bytes 393220
  23.9 7.3 %copy-start.3 = (f32[1,1,64,128]{3,2,1,0:T(8,128)S(1)}, f32[1,1,64,128]{3,2,1,0:T(8,128)}, u32[]{:S(2)}) copy-start(f32[1,1,64,128]{3,2,1,0:T(8,128)} %param.17) | copy-start | bytes 98308
  23.9 7.3 %copy-start.4 = (f32[1,1,64,128]{3,2,1,0:T(8,128)S(1)}, f32[1,1,64,128]{3,2,1,0:T(8,128)}, u32[]{:S(2)}) copy-start(f32[1,1,64,128]{3,2,1,0:T(8,128)} %param.18) | copy-start | bytes 98308
  23.9 7.3 %copy-start.5 = (f32[4,32]{1,0:T(4,128)S(1)}, f32[4,32]{1,0:T(4,128)}, u32[]{:S(2)}) copy-start(f32[4,32]{1,0:T(4,128)} %ports.3) | copy-start | bytes 1540
  28.1 18.0 %copy-start.1 = (f32[8,16,512]{2,1,0:T(8,128)S(1)}, f32[8,16,512]{2,1,0:T(8,128)}, u32[]{:S(2)}) copy-start(f32[8,16,512]{2,1,0:T(8,128)} %param.12) | copy-start | bytes 786436
  33.2 21.4 %copy-start.7 = (s32[32]{0:T(128)S(1)}, s32[32]{0:T(128)}, u32[]{:S(2)}) copy-start(s32[32]{0:T(128)} %match.1) | copy-start | bytes 388
  33.3 21.4 %copy-start.10 = (s32[32]{0:T(128)S(1)}, s32[32]{0:T(128)}, u32[]{:S(2)}) copy-start(s32[32]{0:T(128)} %param.15) | copy-start | bytes 388
  33.3 35.8 %all-to-all-start = ((f32[192,4,128]{2,1,0:T(4,128)}), f32[192,4,128]{2,1,0:T(4,128)S(1)}, u32[]{:S(2)}, u32[]{:S(2)}) async-start(f32[192,4,128]{2,1,0:T(4,128)} %slip.1), calls=%async_computation | async-start | bytes 786432 | tf_op jit(solution)/shard_map/all_to_all | solution.py:520
  46.3 13.4 %collective-permute-start.3 = (f32[80,512]{1,0:T(8,128)S(1)}, f32[80,512]{1,0:T(8,128)S(1)}, u32[]{:S(2)}, u32[]{:S(2)}) collective-permute-start(f32[80,512]{1,0:T(8,128)S(1)} %get-tuple-element.23), channel_id=1, source_target_pairs={{0,1},{1,2},{2,3},{3,4},{4,5},{5,6},{6,7},{7,8},{8,9},{9,10},{10,1... | collective-permute-start | bytes 491528 | tf_op jit(solution)/shard_map/ppermute | solution.py:522
  51.2 14.0 %collective-permute-start.4 = (f32[80,512]{1,0:T(8,128)S(1)}, f32[80,512]{1,0:T(8,128)S(1)}, u32[]{:S(2)}, u32[]{:S(2)}) collective-permute-start(f32[80,512]{1,0:T(8,128)S(1)} %get-tuple-element.24), channel_id=1, source_target_pairs={{1,0},{2,1},{3,2},{4,3},{5,4},{6,5},{7,6},{8,7},{9,8},{10,9},{11,1... | collective-permute-start | bytes 491528 | tf_op jit(solution)/shard_map/ppermute | solution.py:523
  56.1 13.0 %copy-start.9 = (s32[1,1,64,128]{3,2,1,0:T(8,128)S(1)}, s32[1,1,64,128]{3,2,1,0:T(8,128)}, u32[]{:S(2)}) copy-start(s32[1,1,64,128]{3,2,1,0:T(8,128)} %param.21) | copy-start | bytes 98308

commit v6 on v5

--- a/solution.py
+++ b/solution.py
@@ -264,9 +264,7 @@
     return centers, out
 
 
-def cap_kernel(comps, depth_z, width, flow, viscosity, ports, low_out, high_out, tile, sems):
-    tile[...] = jnp.zeros_like(tile)
-    tile[0:comps, 0 : ports.shape[1]] = ports[...]
+def cap_kernel(comps, depth_z, width, flow, viscosity, ports, low_out, high_out, sems):
     copies = []
 
     def copy(source, target):
@@ -282,8 +280,9 @@
     base = comps * two
     copy(viscosity.at[0:width, :], low_out.at[base : base + width, :])
     copy(viscosity.at[last : last + width, :], high_out.at[base : base + width, :])
-    copy(tile, low_out.at[base + width :, :])
-    copy(tile, high_out.at[base + width :, :])
+    for out in (low_out, high_out):
+        out[base + width :, :] = jnp.zeros((8, out.shape[1]), jnp.float32)
+        out[base + width : base + width + comps, 0 : ports.shape[1]] = ports[...]
     for started in copies:
         started.wait()
 
@@ -294,8 +293,8 @@
         functools.partial(cap_kernel, comps, depth_z, width),
         out_shape=(shape, shape),
         in_specs=[HB, HB, VM],
-        out_specs=(HB, HB),
-        scratch_shapes=[pltpu.VMEM((8, flow.shape[1]), jnp.float32), pltpu.SemaphoreType.DMA((2 * comps + 4,))],
+        out_specs=(VM, VM),
+        scratch_shapes=[pltpu.SemaphoreType.DMA((2 * comps + 2,))],
         compiler_params=pltpu.CompilerParams(vmem_limit_bytes=60 * 1024 * 1024),
         name="caps",
     )(flow, viscosity, ports)

time: 77.4 us -> 60.4 us (0.78)
  the two profiles are of different devices: /device:TPU:88 before, /device:TPU:1 now
where the time goes in v6:
time: 60.4 us; the launch traced here: 59.8 us
  starting transfers between devices  24.5 us (41%)
  Pallas kernels  22.8 us (38%)
  waiting for transfers between devices  11.6 us (19%)
  between operations  0.87 us (1%)
    all_to_all x1, starting transfers between devices, on_device(): lax.all_to_all(outgoing, 'tile', split_axis=0, concat_axis=0, tiled=True)  13.7 us
    pallas_call x1, Pallas kernels, land(): pl.pallas_call(functools.partial(land_kernel, GP), out_shape=(jax.ShapeDt...  7.72 us
    ppermute x1, waiting for transfers between devices, on_device(): right = lax.ppermute(low_edge, 'tile', back)  6.18 us
    pallas_call x1, Pallas kernels, sample(): pl.pallas_call(functools.partial(sample_kernel, GP), out_shape=jax.ShapeD...  4.9 us
    ppermute x1, starting transfers between devices, on_device(): left = lax.ppermute(high_edge, 'tile', forth)  4.43 us
    pallas_call x1, Pallas kernels, outer(): pl.pallas_call(functools.partial(outer_kernel, comps, depth_z, width), ou...  3.85 us
    ppermute x1, starting transfers between devices, on_device(): below = lax.ppermute(high_cap, 'sec', up)  2.91 us
    ppermute x1, waiting for transfers between devices, on_device(): left = lax.ppermute(high_edge, 'tile', forth)  2.77 us
  transfers between devices with their start and end apart: 6, of which 4 were waited for; matrix products, arithmetic and copies ran while one was open for 0% of the time, Pallas kernels for 22%

profile of v6, /device:TPU:1, one launch (start us, length us, event | category | flops | bytes accessed | tf_op | source)
XLA Modules:
  0.0 59.8 jit_solution(8735561386561808232)
XLA Ops:
  0.7 2.1 %collective-permute-start.2 = (f32[4,32]{1,0:T(4,128)}, f32[4,32]{1,0:T(4,128)S(1)}, u32[]{:S(2)}, u32[]{:S(2)}) collective-permute-start(f32[4,32]{1,0:T(4,128)} %ports.3), channel_id=1, source_target_pairs={{0,128},{64,192},{128,0},{192,64},{1,129},{65,193},{129,1},{193,65... | collective-permute-start | bytes 1544 | tf_op jit(solution)/shard_map/ppermute | solution.py:503
  2.8 2.7 %caps.1 = (f32[152,512]{1,0:T(8,128)}, f32[152,512]{1,0:T(8,128)}) custom-call(f32[512,512]{1,0:T(8,128)} %bitcast.14, f32[128,512]{1,0:T(8,128)} %bitcast.19, f32[4,32]{1,0:T(4,128)} %ports.3), custom_call_target="tpu_custom_call" | custom-call | tf_op jit(solution)/shard_map/caps/pallas_call | solution.py:292
  5.5 2.9 %collective-permute-start = (f32[152,512]{1,0:T(8,128)}, f32[152,512]{1,0:T(8,128)S(1)}, u32[]{:S(2)}, u32[]{:S(2)}) collective-permute-start(f32[152,512]{1,0:T(8,128)} %get-tuple-element.16), channel_id=1, source_target_pairs={{0,64},{64,128},{128,192},{192,0},{1,65},{65,129},{129,193},{193,1... | collective-permute-start | bytes 933896 | tf_op jit(solution)/shard_map/ppermute | solution.py:501
  8.4 0.0 copy-start.2
  8.4 0.0 copy-start.3
  8.4 0.0 copy-start.4
  8.5 0.0 copy-start.5
  8.5 4.9 %sample.1.sampled = f32[72,4,128]{2,1,0:T(4,128)S(1)} custom-call(s32[64]{0:T(128)S(1)} %bitcast.26, f32[512,512]{1,0:T(8,128)S(1)} %bitcast.15, s32[64,128]{1,0:T(8,128)S(1)} %bitcast.29), custom_call_target="tpu_custom_call" | custom-call | flops 8589934592 | bytes 2097152 | tf_op jit(solution)/shard_map/sample/pallas_call | solution.py:69
  13.4 0.0 copy-start.1
  13.4 2.2 %collective-permute-done.below = f32[152,512]{1,0:T(8,128)S(1)} collective-permute-done((f32[152,512]{1,0:T(8,128)}, f32[152,512]{1,0:T(8,128)S(1)}, u32[]{:S(2)}, u32[]{:S(2)}) %collective-permute-start) | collective-permute-done | bytes 311328 | tf_op jit(solution)/shard_map/ppermute | solution.py:501
  15.6 0.4 collective-permute-done.1.above
  16.0 2.0 %slip.1 = f32[192,4,128]{2,1,0:T(4,128)} custom-call(s32[64]{0:T(128)S(1)} %bitcast.27, f32[72,4,128]{2,1,0:T(4,128)S(1)} %sample.1.sampled, f32[4,64,128]{2,1,0:T(8,128)S(1)} %bitcast.23, f32[64,128]{1,0:T(8,128)S(1)} %bitcast.24, f32[64,128]{1,0:T(8,128)S(1)} %bitcast.25, f32[4,32]{1,0:T(4,128)S(1)} %copy-done.5, ...), custom_call_target="tpu_custom_call" | custom-call | flops 2000000 | bytes 1048576 | tf_op jit(solution)/shard_map/slip/pallas_call | solution.py:127
  18.1 0.0 copy-start.7
  18.1 0.0 copy-start.10
  18.1 13.7 %all-to-all-start = ((f32[192,4,128]{2,1,0:T(4,128)}), f32[192,4,128]{2,1,0:T(4,128)S(1)}, u32[]{:S(2)}, u32[]{:S(2)}) async-start(f32[192,4,128]{2,1,0:T(4,128)} %slip.1), calls=%async_computation | async-start | bytes 786432 | tf_op jit(solution)/shard_map/all_to_all | solution.py:519
  31.8 0.2 edges.1
  32.0 4.4 %collective-permute-start.3 = (f32[80,512]{1,0:T(8,128)S(1)}, f32[80,512]{1,0:T(8,128)S(1)}, u32[]{:S(2)}, u32[]{:S(2)}) collective-permute-start(f32[80,512]{1,0:T(8,128)S(1)} %get-tuple-element.23), channel_id=1, source_target_pairs={{0,1},{1,2},{2,3},{3,4},{4,5},{5,6},{6,7},{7,8},{8,9},{9,10},{10,1... | collective-permute-start | bytes 491528 | tf_op jit(solution)/shard_map/ppermute | solution.py:521
  36.4 1.3 %collective-permute-start.4 = (f32[80,512]{1,0:T(8,128)S(1)}, f32[80,512]{1,0:T(8,128)S(1)}, u32[]{:S(2)}, u32[]{:S(2)}) collective-permute-start(f32[80,512]{1,0:T(8,128)S(1)} %get-tuple-element.24), channel_id=1, source_target_pairs={{1,0},{2,1},{3,2},{4,3},{5,4},{6,5},{7,6},{8,7},{9,8},{10,9},{11,1... | collective-permute-start | bytes 491528 | tf_op jit(solution)/shard_map/ppermute | solution.py:522
  37.8 1.5 %inner.1.first = f32[4,10,16,512]{3,2,1,0:T(8,128)S(1)} custom-call(f32[512,512]{1,0:T(8,128)S(1)} %bitcast.17, f32[128,512]{1,0:T(8,128)S(1)} %bitcast.21, f32[144,512]{1,0:T(8,128)S(1)} %get-tuple-element.21.below, f32[144,512]{1,0:T(8,128)S(1)} %get-tuple-element.22.above), custom_call_target="tpu_custom_call" | custom-call | flops 10000000 | bytes 4194304 | tf_op jit(solution)/shard_map/inner/pallas_call | solution.py:361
  39.3 0.0 copy-start.9
  39.3 2.8 %collective-permute-done.3.left = f32[80,512]{1,0:T(8,128)S(1)} collective-permute-done((f32[80,512]{1,0:T(8,128)S(1)}, f32[80,512]{1,0:T(8,128)S(1)}, u32[]{:S(2)}, u32[]{:S(2)}) %collective-permute-start.3) | collective-permute-done | bytes 163872 | tf_op jit(solution)/shard_map/ppermute | solution.py:521
  42.0 6.2 %collective-permute-done.4.right = f32[80,512]{1,0:T(8,128)S(1)} collective-permute-done((f32[80,512]{1,0:T(8,128)S(1)}, f32[80,512]{1,0:T(8,128)S(1)}, u32[]{:S(2)}, u32[]{:S(2)}) %collective-permute-start.4) | collective-permute-done | bytes 163872 | tf_op jit(solution)/shard_map/ppermute | solution.py:522
  48.2 3.8 %outer.1 = (f32[512,512]{1,0:T(8,128)S(1)}, f32[4,128]{1,0:T(4,128)S(1)}) custom-call(f32[512,512]{1,0:T(8,128)S(1)} %bitcast.18, f32[128,512]{1,0:T(8,128)S(1)} %bitcast.22, f32[144,512]{1,0:T(8,128)S(1)} %get-tuple-element.21.below, f32[144,512]{1,0:T(8,128)S(1)} %get-tuple-element.22.above, f32[4,10,16,512]{3,2,1,0:T(8,128)S(1)} %inner.1.first, ...), custom_call_target="tpu_custom_call" | custom-call | flops 10000000 | bytes 4194304 | tf_op jit(solution)/shard_map/outer/pallas_call | solution.py:454
  52.1 7.7 %land.1 = (f32[512,512]{1,0:T(8,128)}, f32[4,64,128]{2,1,0:T(8,128)}) custom-call(s32[32]{0:T(128)S(1)} %copy-done.7, f32[512,512]{1,0:T(8,128)S(1)} %get-tuple-element.25.second, f32[4,128]{1,0:T(4,128)S(1)} %get-tuple-element.26.inlet_now, s32[2,128]{1,0:T(2,128)S(1)} %pad.4.inlet, s32[64,128]{1,0:T(8,128)S(1)} %bitcast.30, ...), custom_call_target="tpu_custom_call" | custom-call | flops 8589934592 | bytes 2097152 | tf_op jit(solution)/shard_map/land/pallas_call | solution.py:222
  (19 shorter events, 0.1 us)
Async XLA Ops:
  0.6 7.8 %copy-start = (f32[4,8,16,512]{3,2,1,0:T(8,128)S(1)}, f32[4,8,16,512]{3,2,1,0:T(8,128)}, u32[]{:S(2)}) copy-start(f32[4,8,16,512]{3,2,1,0:T(8,128)} %param.11) | copy-start | bytes 3145732
  0.6 7.8 %copy-start.6 = (s32[1,1,64]{2,1,0:T(1,128)S(1)}, s32[1,1,64]{2,1,0:T(1,128)}, u32[]{:S(2)}) copy-start(s32[1,1,64]{2,1,0:T(1,128)} %param.20) | copy-start | bytes 772
  0.6 7.8 %copy-start.8 = (s32[1,1,64,128]{3,2,1,0:T(8,128)S(1)}, s32[1,1,64,128]{3,2,1,0:T(8,128)}, u32[]{:S(2)}) copy-start(s32[1,1,64,128]{3,2,1,0:T(8,128)} %param.19) | copy-start | bytes 98308
  0.7 12.7 %collective-permute-start.2 = (f32[4,32]{1,0:T(4,128)}, f32[4,32]{1,0:T(4,128)S(1)}, u32[]{:S(2)}, u32[]{:S(2)}) collective-permute-start(f32[4,32]{1,0:T(4,128)} %ports.3), channel_id=1, source_target_pairs={{0,128},{64,192},{128,0},{192,64},{1,129},{65,193},{129,1},{193,65... | collective-permute-start | bytes 1544 | tf_op jit(solution)/shard_map/ppermute | solution.py:503
  5.5 10.1 %collective-permute-start = (f32[152,512]{1,0:T(8,128)}, f32[152,512]{1,0:T(8,128)S(1)}, u32[]{:S(2)}, u32[]{:S(2)}) collective-permute-start(f32[152,512]{1,0:T(8,128)} %get-tuple-element.16), channel_id=1, source_target_pairs={{0,64},{64,128},{128,192},{192,0},{1,65},{65,129},{129,193},{193,1... | collective-permute-start | bytes 933896 | tf_op jit(solution)/shard_map/ppermute | solution.py:501
  8.4 7.6 %collective-permute-start.1 = (f32[152,512]{1,0:T(8,128)}, f32[152,512]{1,0:T(8,128)S(1)}, u32[]{:S(2)}, u32[]{:S(2)}) collective-permute-start(f32[152,512]{1,0:T(8,128)} %get-tuple-element.17), channel_id=1, source_target_pairs={{64,0},{128,64},{192,128},{0,192},{65,1},{129,65},{193,129},{1,193... | collective-permute-start | bytes 933896 | tf_op jit(solution)/shard_map/ppermute | solution.py:502
  8.4 7.6 %copy-start.2 = (f32[4,1,1,64,128]{4,3,2,1,0:T(8,128)S(1)}, f32[4,1,1,64,128]{4,3,2,1,0:T(8,128)}, u32[]{:S(2)}) copy-start(f32[4,1,1,64,128]{4,3,2,1,0:T(8,128)} %param.16) | copy-start | bytes 393220
  8.4 7.6 %copy-start.3 = (f32[1,1,64,128]{3,2,1,0:T(8,128)S(1)}, f32[1,1,64,128]{3,2,1,0:T(8,128)}, u32[]{:S(2)}) copy-start(f32[1,1,64,128]{3,2,1,0:T(8,128)} %param.17) | copy-start | bytes 98308
  8.4 7.6 %copy-start.4 = (f32[1,1,64,128]{3,2,1,0:T(8,128)S(1)}, f32[1,1,64,128]{3,2,1,0:T(8,128)}, u32[]{:S(2)}) copy-start(f32[1,1,64,128]{3,2,1,0:T(8,128)} %param.18) | copy-start | bytes 98308
  8.5 7.6 %copy-start.5 = (f32[4,32]{1,0:T(4,128)S(1)}, f32[4,32]{1,0:T(4,128)}, u32[]{:S(2)}) copy-start(f32[4,32]{1,0:T(4,128)} %ports.3) | copy-start | bytes 1540
  13.4 18.4 %copy-start.1 = (f32[8,16,512]{2,1,0:T(8,128)S(1)}, f32[8,16,512]{2,1,0:T(8,128)}, u32[]{:S(2)}) copy-start(f32[8,16,512]{2,1,0:T(8,128)} %param.12) | copy-start | bytes 786436
  18.1 19.7 %copy-start.7 = (s32[32]{0:T(128)S(1)}, s32[32]{0:T(128)}, u32[]{:S(2)}) copy-start(s32[32]{0:T(128)} %match.1) | copy-start | bytes 388
  18.1 19.7 %copy-start.10 = (s32[32]{0:T(128)S(1)}, s32[32]{0:T(128)}, u32[]{:S(2)}) copy-start(s32[32]{0:T(128)} %param.15) | copy-start | bytes 388
  18.1 34.0 %all-to-all-start = ((f32[192,4,128]{2,1,0:T(4,128)}), f32[192,4,128]{2,1,0:T(4,128)S(1)}, u32[]{:S(2)}, u32[]{:S(2)}) async-start(f32[192,4,128]{2,1,0:T(4,128)} %slip.1), calls=%async_computation | async-start | bytes 786432 | tf_op jit(solution)/shard_map/all_to_all | solution.py:519
  32.0 10.0 %collective-permute-start.3 = (f32[80,512]{1,0:T(8,128)S(1)}, f32[80,512]{1,0:T(8,128)S(1)}, u32[]{:S(2)}, u32[]{:S(2)}) collective-permute-start(f32[80,512]{1,0:T(8,128)S(1)} %get-tuple-element.23), channel_id=1, source_target_pairs={{0,1},{1,2},{2,3},{3,4},{4,5},{5,6},{6,7},{7,8},{8,9},{9,10},{10,1... | collective-permute-start | bytes 491528 | tf_op jit(solution)/shard_map/ppermute | solution.py:521
  36.4 11.8 %collective-permute-start.4 = (f32[80,512]{1,0:T(8,128)S(1)}, f32[80,512]{1,0:T(8,128)S(1)}, u32[]{:S(2)}, u32[]{:S(2)}) collective-permute-start(f32[80,512]{1,0:T(8,128)S(1)} %get-tuple-element.24), channel_id=1, source_target_pairs={{1,0},{2,1},{3,2},{4,3},{5,4},{6,5},{7,6},{8,7},{9,8},{10,9},{11,1... | collective-permute-start | bytes 491528 | tf_op jit(solution)/shard_map/ppermute | solution.py:522
  39.3 12.8 %copy-start.9 = (s32[1,1,64,128]{3,2,1,0:T(8,128)S(1)}, s32[1,1,64,128]{3,2,1,0:T(8,128)}, u32[]{:S(2)}) copy-start(s32[1,1,64,128]{3,2,1,0:T(8,128)} %param.21) | copy-start | bytes 98308

commit v7 on v6

--- a/solution.py
+++ b/solution.py
@@ -264,74 +264,64 @@
     return centers, out
 
 
-def cap_kernel(comps, depth_z, width, flow, viscosity, ports, low_out, high_out, sems):
-    copies = []
-
-    def copy(source, target):
-        copies.append(pltpu.make_async_copy(source, target, sems.at[len(copies)]))
-        copies[-1].start()
-
+def rim_kernel(comps, depth_z, width, flow, viscosity, ports, low_edge, high_edge, low_cap, high_cap):
+    for k in range(comps * depth_z):
+        low_edge[2 * k : 2 * k + 2, :] = flow[k * width : k * width + 2, :]
+        high_edge[2 * k : 2 * k + 2, :] = flow[(k + 1) * width - 2 : (k + 1) * width, :]
+    base = 2 * comps * depth_z
+    for z in range(depth_z):
+        low_edge[base + z : base + z + 1, :] = viscosity[z * width : z * width + 1, :]
+        high_edge[base + z : base + z + 1, :] = viscosity[(z + 1) * width - 1 : (z + 1) * width, :]
     two = 2 * width
-    last = (depth_z - 1) * width
+    last = depth_z * width
     for c in range(comps):
-        base = c * depth_z * width
-        copy(flow.at[base : base + two, :], low_out.at[c * two : (c + 1) * two, :])
-        copy(flow.at[base + last - width : base + last + width, :], high_out.at[c * two : (c + 1) * two, :])
+        low_cap[c * two : (c + 1) * two, :] = flow[c * last : c * last + two, :]
+        high_cap[c * two : (c + 1) * two, :] = flow[(c + 1) * last - two : (c + 1) * last, :]
     base = comps * two
-    copy(viscosity.at[0:width, :], low_out.at[base : base + width, :])
-    copy(viscosity.at[last : last + width, :], high_out.at[base : base + width, :])
-    for out in (low_out, high_out):
+    low_cap[base : base + width, :] = viscosity[0:width, :]
+    high_cap[base : base + width, :] = viscosity[last - width : last, :]
+    for out in (low_cap, high_cap):
         out[base + width :, :] = jnp.zeros((8, out.shape[1]), jnp.float32)
         out[base + width : base + width + comps, 0 : ports.shape[1]] = ports[...]
-    for started in copies:
-        started.wait()
-
-
-def caps(comps, depth_z, width, flow, viscosity, ports):
-    shape = jax.ShapeDtypeStruct((2 * comps * width + width + 8, flow.shape[1]), jnp.float32)
-    return pl.pallas_call(
-        functools.partial(cap_kernel, comps, depth_z, width),
-        out_shape=(shape, shape),
-        in_specs=[HB, HB, VM],
-        out_specs=(VM, VM),
-        scratch_shapes=[pltpu.SemaphoreType.DMA((2 * comps + 2,))],
+
+
+def rims(comps, depth_z, width, flow, viscosity, ports):
+    depth = flow.shape[1]
+    edge = jax.ShapeDtypeStruct(((2 * comps + 1) * depth_z, depth), jnp.float32)
+    cap = jax.ShapeDtypeStruct((2 * comps * width + width + 8, depth), jnp.float32)
+    return pl.pallas_call(
+        functools.partial(rim_kernel, comps, depth_z, width),
+        out_shape=(edge, edge, cap, cap),
+        in_specs=[VM] * 3,
+        out_specs=(VM,) * 4,
         compiler_params=pltpu.CompilerParams(vmem_limit_bytes=60 * 1024 * 1024),
-        name="caps",
+        name="rims",
     )(flow, viscosity, ports)
 
 
-def edge_kernel(comps, depth_z, width, flow, viscosity, below, above, low_out, high_out, bottom, top):
+def corner_kernel(comps, depth_z, below, above, left, right, low_out, high_out, bottom, top):
     section = lax.axis_index("sec")
     bottom[...] = jnp.where(section > 0, below[0 : bottom.shape[0], :], 0.0)
     top[...] = jnp.where(section < lax.axis_size("sec") - 1, above[0 : top.shape[0], :], 0.0)
-    two = 2 * width
-    for k in range(comps * depth_z):
-        low_out[2 * k : 2 * k + 2, :] = flow[k * width : k * width + 2, :]
-        high_out[2 * k : 2 * k + 2, :] = flow[(k + 1) * width - 2 : (k + 1) * width, :]
-    base = 2 * comps * depth_z
     for c in range(comps):
-        low_out[base + 2 * c : base + 2 * c + 1, :] = bottom[c * two + width : c * two + width + 1, :]
-        low_out[base + 2 * c + 1 : base + 2 * c + 2, :] = top[c * two : c * two + 1, :]
-        high_out[base + 2 * c : base + 2 * c + 1, :] = bottom[(c + 1) * two - 1 : (c + 1) * two, :]
-        high_out[base + 2 * c + 1 : base + 2 * c + 2, :] = top[c * two + width - 1 : c * two + width, :]
-    base += 2 * comps
-    for z in range(depth_z):
-        low_out[base + z : base + z + 1, :] = viscosity[z * width : z * width + 1, :]
-        high_out[base + z : base + z + 1, :] = viscosity[(z + 1) * width - 1 : (z + 1) * width, :]
-
-
-def edges(comps, depth_z, width, flow, viscosity, below, above):
-    depth = flow.shape[1]
-    shape = jax.ShapeDtypeStruct((2 * comps * (depth_z + 1) + depth_z, depth), jnp.float32)
+        for out, z in ((low_out, 0), (high_out, depth_z - 1)):
+            k = 2 * (c * depth_z + z)
+            out[c : c + 1, :] = left[k + 1 : k + 2, :]
+            out[comps + c : comps + c + 1, :] = right[k : k + 1, :]
+
+
+def corners(comps, depth_z, width, below, above, left, right):
+    depth = below.shape[1]
+    shape = jax.ShapeDtypeStruct((2 * comps, depth), jnp.float32)
     halo = jax.ShapeDtypeStruct(((2 * comps + 1) * width, depth), jnp.float32)
     return pl.pallas_call(
-        functools.partial(edge_kernel, comps, depth_z, width),
+        functools.partial(corner_kernel, comps, depth_z),
         out_shape=(shape, shape, halo, halo),
         in_specs=[VM] * 4,
         out_specs=(VM,) * 4,
         compiler_params=pltpu.CompilerParams(vmem_limit_bytes=24 * 1024 * 1024),
-        name="edges",
-    )(flow, viscosity, below, above)
+        name="corners",
+    )(below, above, left, right)
 
 
 def inner_kernel(comps, depth_z, width, flow, viscosity, below, above, first):
@@ -369,7 +359,7 @@
     )(flow, viscosity, below, above)
 
 
-def outer_kernel(comps, depth_z, width, flow, viscosity, below, above, first, left, right, inlet, second_out, inlet_now, strip, visc, started, table):
+def outer_kernel(comps, depth_z, width, flow, viscosity, below, above, first, left, right, low_corner, high_corner, inlet, second_out, inlet_now, strip, visc, started, table):
     depth = flow.shape[1]
     two = 2 * width
     rows = depth_z * width
@@ -392,10 +382,9 @@
                 strip[c, z + 2, 0:2, :] = left[k : k + 2, :]
                 strip[c, z + 2, 6:8, :] = right[k : k + 2, :]
             elif z in (-1, depth_z):
-                k = base + 2 * c + (z == depth_z)
-                strip[c, z + 2, 1:2, :] = left[k : k + 1, :]
-                strip[c, z + 2, 6:7, :] = right[k : k + 1, :]
-    side = base + 2 * comps
+                corner = low_corner if z < 0 else high_corner
+                strip[c, z + 2, 1:2, :] = corner[c : c + 1, :]
+                strip[c, z + 2, 6:7, :] = corner[comps + c : comps + c + 1, :]
     for z in range(-1, depth_z + 1):
         if z < 0:
             ref, spot = below, comps * two
@@ -403,8 +392,8 @@
             ref, spot = above, comps * two
         else:
             ref, spot = viscosity, z * width
-            visc[z + 1, 1:2, :] = left[side + z : side + z + 1, :]
-            visc[z + 1, 6:7, :] = right[side + z : side + z + 1, :]
+            visc[z + 1, 1:2, :] = left[base + z : base + z + 1, :]
+            visc[z + 1, 6:7, :] = right[base + z : base + z + 1, :]
         visc[z + 1, 2:4, :] = ref[spot : spot + 2, :]
         visc[z + 1, 4:6, :] = ref[spot + width - 2 : spot + width, :]
 
@@ -449,7 +438,7 @@
         inlet_now[c : c + 1, :] = jnp.sum(jnp.where(row, both, 0.0), axis=0, keepdims=True)
 
 
-def outer(comps, depth_z, width, flow, viscosity, below, above, first, left, right, inlet):
+def outer(comps, depth_z, width, flow, viscosity, below, above, first, left, right, low_corner, high_corner, inlet):
     depth = flow.shape[1]
     return pl.pallas_call(
         functools.partial(outer_kernel, comps, depth_z, width),
@@ -457,7 +446,7 @@
             jax.ShapeDtypeStruct(flow.shape, jnp.float32),
             jax.ShapeDtypeStruct((comps, inlet.shape[1]), jnp.float32),
         ),
-        in_specs=[VM] * 8,
+        in_specs=[VM] * 10,
         out_specs=(VM, VM),
         scratch_shapes=[
             pltpu.VMEM((comps, depth_z + 4, 8, depth), jnp.float32),
@@ -468,7 +457,7 @@
         compiler_params=pltpu.CompilerParams(vmem_limit_bytes=24 * 1024 * 1024),
         cost_estimate=pl.CostEstimate(flops=10**7, bytes_accessed=2**22, transcendentals=0),
         name="outer",
-    )(flow, viscosity, below, above, first, left, right, inlet)
+    )(flow, viscosity, below, above, first, left, right, low_corner, high_corner, inlet)
 
 
 def on_device(
@@ -497,7 +486,9 @@
     down = [((i + 1) % levels, i) for i in range(levels)]
     over = [(i, (i + levels // 2) % levels) for i in range(levels)]
 
-    low_cap, high_cap = caps(*sizes, flow, visc, port_plane)
+    low_edge, high_edge, low_cap, high_cap = rims(*sizes, flow, visc, port_plane)
+    left = lax.ppermute(high_edge, "tile", forth)
+    right = lax.ppermute(low_edge, "tile", back)
     below = lax.ppermute(high_cap, "sec", up)
     above = lax.ppermute(low_cap, "sec", down)
     across = lax.ppermute(port_plane, "sec", over)
@@ -515,14 +506,14 @@
         across,
         below,
     )
-    below, above, outgoing = lax.optimization_barrier((below, above, outgoing))
+    left, right, below, above, outgoing = lax.optimization_barrier((left, right, below, above, outgoing))
     arrived = lax.all_to_all(outgoing, "tile", split_axis=0, concat_axis=0, tiled=True)
-    low_edge, high_edge, bottom, top = edges(*sizes, flow, visc, below, above)
-    left = lax.ppermute(high_edge, "tile", forth)
-    right = lax.ppermute(low_edge, "tile", back)
-    inlet = jnp.pad(jnp.stack([inlet_cell, port_match]), ((0, 0), (0, cap - inlet_cell.shape[0])))
+    low_out, high_out, bottom, top = corners(*sizes, below, above, left, right)
+    low_corner = lax.ppermute(high_out, "sec", up[:-1])
+    high_corner = lax.ppermute(low_out, "sec", down[:-1])
+    inlet = jnp.pad(inlet_cell.reshape(1, -1), ((0, 0), (0, cap - inlet_cell.shape[0])))
     first = inner(*sizes, flow, visc, bottom, top)
-    second, inlet_now = outer(*sizes, flow, visc, bottom, top, first, left, right, inlet)
+    second, inlet_now = outer(*sizes, flow, visc, bottom, top, first, left, right, low_corner, high_corner, inlet)
     flow_next, arrived_state = land(
         port_match, second, inlet_now, inlet, arrival_cell.reshape(partners, cap), arrived
     )

time: 60.4 us -> 64.9 us (1.075)
  starting transfers between devices: 24.5 us -> 27.2 us
  local copies, waits for them, and re-layouts: 0.07 us -> 2.26 us
  Pallas kernels: 22.8 us -> 21.1 us
  waiting for transfers between devices: 11.6 us -> 12.3 us
    ppermute x1, waiting for transfers between devices: 6.18 us -> 0.01 us  [on_device(): right = lax.ppermute(low_edge, 'tile', back)]
    ppermute x0 -> x2, starting transfers between devices: none -> 4.32 us  [the longest x1 2.4 us: on_device(): high_corner = lax.ppermute(low_out, 'sec', down[:-1])]
    all_to_all x1, waiting for transfers between devices: 0.01 us -> 3.57 us  [on_device(): lax.all_to_all(outgoing, 'tile', split_axis=0, concat_axis=0, tiled=True)]
    ppermute x1, waiting for transfers between devices: 2.77 us -> 0.01 us  [on_device(): left = lax.ppermute(high_edge, 'tile', forth)]
    ppermute x1, waiting for transfers between devices: 2.24 us -> 4.65 us  [on_device(): below = lax.ppermute(high_cap, 'sec', up)]
    ppermute x1, waiting for transfers between devices: 0.36 us -> 2.64 us  [on_device(): above = lax.ppermute(low_cap, 'sec', down)]
    unnamed x22 -> x26, local copies, waits for them, and re-layouts: 0.06 us -> 2.25 us
    ppermute x1, starting transfers between devices: 2.91 us -> 1.14 us  [on_device(): below = lax.ppermute(high_cap, 'sec', up)]
  transfers between devices with their start and end apart: 6 -> 8, of which waited for: 4 -> 4; matrix products, arithmetic and copies ran while one was open for 0% -> 0% of each run, Pallas kernels for 22% -> 23%
where the time goes in v7:
time: 64.9 us; the launch traced here: 63.7 us
  starting transfers between devices  27.2 us (42%)
  Pallas kernels  21.1 us (33%)
  waiting for transfers between devices  12.3 us (19%)
  local copies, waits for them, and re-layouts  2.26 us (3%)
  between operations  0.87 us (1%)
    all_to_all x1, starting transfers between devices, on_device(): lax.all_to_all(outgoing, 'tile', split_axis=0, concat_axis=0, tiled=True)  13.7 us
    pallas_call x1, Pallas kernels, land(): pl.pallas_call(functools.partial(land_kernel, GP), out_shape=(jax.ShapeDt...  6.43 us
    pallas_call x1, Pallas kernels, sample(): pl.pallas_call(functools.partial(sample_kernel, GP), out_shape=jax.ShapeD...  4.9 us
    ppermute x1, waiting for transfers between devices, on_device(): below = lax.ppermute(high_cap, 'sec', up)  4.65 us
    ppermute x1, starting transfers between devices, on_device(): left = lax.ppermute(high_edge, 'tile', forth)  4.35 us
    pallas_call x1, Pallas kernels, outer(): pl.pallas_call(functools.partial(outer_kernel, comps, depth_z, width), ou...  3.85 us
    all_to_all x1, waiting for transfers between devices, on_device(): lax.all_to_all(outgoing, 'tile', split_axis=0, concat_axis=0, tiled=True)  3.57 us
    ppermute x1, waiting for transfers between devices, on_device(): above = lax.ppermute(low_cap, 'sec', down)  2.64 us
  transfers between devices with their start and end apart: 8, of which 4 were waited for; matrix products, arithmetic and copies ran while one was open for 0% of the time, Pallas kernels for 23%

profile of v7, /device:TPU:1, one launch (start us, length us, event | category | flops | bytes accessed | tf_op | source)
XLA Modules:
  0.0 63.7 jit_solution(2553940161702122135)
XLA Ops:
  0.7 2.1 %collective-permute-start.4 = (f32[4,32]{1,0:T(4,128)}, f32[4,32]{1,0:T(4,128)S(1)}, u32[]{:S(2)}, u32[]{:S(2)}) collective-permute-start(f32[4,32]{1,0:T(4,128)} %ports.3), channel_id=1, source_target_pairs={{0,128},{64,192},{128,0},{192,64},{1,129},{65,193},{129,1},{193,65... | collective-permute-start | bytes 1544 | tf_op jit(solution)/shard_map/ppermute | solution.py:494
  2.8 2.4 %rims.1 = (f32[72,512]{1,0:T(8,128)}, f32[72,512]{1,0:T(8,128)}, f32[152,512]{1,0:T(8,128)}, f32[152,512]{1,0:T(8,128)}) custom-call(f32[512,512]{1,0:T(8,128)} %bitcast.13, f32[128,512]{1,0:T(8,128)} %bitcast.17, f32[4,32]{1,0:T(4,128)} %ports.3), custom_call_target="tpu_custom_call" | custom-call | tf_op jit(solution)/shard_map/rims/pallas_call | solution.py:292
  5.1 4.3 %collective-permute-start = (f32[72,512]{1,0:T(8,128)}, f32[72,512]{1,0:T(8,128)S(1)}, u32[]{:S(2)}, u32[]{:S(2)}) collective-permute-start(f32[72,512]{1,0:T(8,128)} %get-tuple-element.20), channel_id=1, source_target_pairs={{0,1},{1,2},{2,3},{3,4},{4,5},{5,6},{6,7},{7,8},{8,9},{9,10},{10,1... | collective-permute-start | bytes 442376 | tf_op jit(solution)/shard_map/ppermute | solution.py:490
  9.5 1.3 %collective-permute-start.1 = (f32[72,512]{1,0:T(8,128)}, f32[72,512]{1,0:T(8,128)S(1)}, u32[]{:S(2)}, u32[]{:S(2)}) collective-permute-start(f32[72,512]{1,0:T(8,128)} %get-tuple-element.21), channel_id=1, source_target_pairs={{1,0},{2,1},{3,2},{4,3},{5,4},{6,5},{7,6},{8,7},{9,8},{10,9},{11,1... | collective-permute-start | bytes 442376 | tf_op jit(solution)/shard_map/ppermute | solution.py:491
  10.8 1.1 %collective-permute-start.2 = (f32[152,512]{1,0:T(8,128)}, f32[152,512]{1,0:T(8,128)S(1)}, u32[]{:S(2)}, u32[]{:S(2)}) collective-permute-start(f32[152,512]{1,0:T(8,128)} %get-tuple-element.22), channel_id=1, source_target_pairs={{0,64},{64,128},{128,192},{192,0},{1,65},{65,129},{129,193},{193,1... | collective-permute-start | bytes 933896 | tf_op jit(solution)/shard_map/ppermute | solution.py:492
  11.9 0.3 collective-permute-start.3
  12.2 0.0 copy-start.5
  12.3 4.9 %sample.1.sampled = f32[72,4,128]{2,1,0:T(4,128)S(1)} custom-call(s32[64]{0:T(128)S(1)} %bitcast.23, f32[512,512]{1,0:T(8,128)S(1)} %bitcast.14, s32[64,128]{1,0:T(8,128)S(1)} %bitcast.25), custom_call_target="tpu_custom_call" | custom-call | flops 8589934592 | bytes 2097152 | tf_op jit(solution)/shard_map/sample/pallas_call | solution.py:69
  17.2 4.6 %collective-permute-done.2.below = f32[152,512]{1,0:T(8,128)S(1)} collective-permute-done((f32[152,512]{1,0:T(8,128)}, f32[152,512]{1,0:T(8,128)S(1)}, u32[]{:S(2)}, u32[]{:S(2)}) %collective-permute-start.2) | collective-permute-done | bytes 311328 | tf_op jit(solution)/shard_map/ppermute | solution.py:492
  21.8 2.6 %collective-permute-done.3.above = f32[152,512]{1,0:T(8,128)S(1)} collective-permute-done((f32[152,512]{1,0:T(8,128)}, f32[152,512]{1,0:T(8,128)S(1)}, u32[]{:S(2)}, u32[]{:S(2)}) %collective-permute-start.3) | collective-permute-done | bytes 311328 | tf_op jit(solution)/shard_map/ppermute | solution.py:493
  24.5 0.0 copy-start.12
  24.5 2.0 %slip.1 = f32[192,4,128]{2,1,0:T(4,128)} custom-call(s32[64]{0:T(128)S(1)} %bitcast.24, f32[72,4,128]{2,1,0:T(4,128)S(1)} %sample.1.sampled, f32[4,64,128]{2,1,0:T(8,128)S(1)} %bitcast.20, f32[64,128]{1,0:T(8,128)S(1)} %bitcast.21, f32[64,128]{1,0:T(8,128)S(1)} %bitcast.22, f32[4,32]{1,0:T(4,128)S(1)} %copy-done.5, ...), custom_call_target="tpu_custom_call" | custom-call | flops 2000000 | bytes 1048576 | tf_op jit(solution)/shard_map/slip/pallas_call | solution.py:127
  26.5 13.7 %all-to-all-start = ((f32[192,4,128]{2,1,0:T(4,128)}), f32[192,4,128]{2,1,0:T(4,128)S(1)}, u32[]{:S(2)}, u32[]{:S(2)}) async-start(f32[192,4,128]{2,1,0:T(4,128)} %slip.1), calls=%async_computation | async-start | bytes 786432 | tf_op jit(solution)/shard_map/all_to_all | solution.py:510
  40.2 0.1 corners.1
  40.3 1.9 %collective-permute-start.5 = (f32[8,512]{1,0:T(8,128)S(1)}, f32[8,512]{1,0:T(8,128)S(1)}, u32[]{:S(2)}, u32[]{:S(2)}) collective-permute-start(f32[8,512]{1,0:T(8,128)S(1)} %get-tuple-element.31), channel_id=1, source_target_pairs={{0,64},{64,128},{128,192},{1,65},{65,129},{129,193},{2,66},{66,130... | collective-permute-start | bytes 49160 | tf_op jit(solution)/shard_map/ppermute | solution.py:512
  42.3 2.4 %collective-permute-start.6 = (f32[8,512]{1,0:T(8,128)S(1)}, f32[8,512]{1,0:T(8,128)S(1)}, u32[]{:S(2)}, u32[]{:S(2)}) collective-permute-start(f32[8,512]{1,0:T(8,128)S(1)} %get-tuple-element.32), channel_id=1, source_target_pairs={{64,0},{128,64},{192,128},{65,1},{129,65},{193,129},{66,2},{130,66... | collective-permute-start | bytes 49160 | tf_op jit(solution)/shard_map/ppermute | solution.py:513
  44.7 1.5 %inner.1.first = f32[4,10,16,512]{3,2,1,0:T(8,128)S(1)} custom-call(f32[512,512]{1,0:T(8,128)S(1)} %bitcast.15, f32[128,512]{1,0:T(8,128)S(1)} %bitcast.18, f32[144,512]{1,0:T(8,128)S(1)} %get-tuple-element.29.below, f32[144,512]{1,0:T(8,128)S(1)} %get-tuple-element.30.above), custom_call_target="tpu_custom_call" | custom-call | flops 10000000 | bytes 4194304 | tf_op jit(solution)/shard_map/inner/pallas_call | solution.py:351
  46.2 0.0 copy-start.10
  46.2 1.4 %collective-permute-done.6.high_corner = f32[8,512]{1,0:T(8,128)S(1)} collective-permute-done((f32[8,512]{1,0:T(8,128)S(1)}, f32[8,512]{1,0:T(8,128)S(1)}, u32[]{:S(2)}, u32[]{:S(2)}) %collective-permute-start.6) | collective-permute-done | bytes 16416 | tf_op jit(solution)/shard_map/ppermute | solution.py:513
  47.7 3.8 %outer.1 = (f32[512,512]{1,0:T(8,128)S(1)}, f32[4,128]{1,0:T(4,128)S(1)}) custom-call(f32[512,512]{1,0:T(8,128)S(1)} %bitcast.16, f32[128,512]{1,0:T(8,128)S(1)} %bitcast.19, f32[144,512]{1,0:T(8,128)S(1)} %get-tuple-element.29.below, f32[144,512]{1,0:T(8,128)S(1)} %get-tuple-element.30.above, f32[4,10,16,512]{3,2,1,0:T(8,128)S(1)} %inner.1.first, ...), custom_call_target="tpu_custom_call" | custom-call | flops 10000000 | bytes 4194304 | tf_op jit(solution)/shard_map/outer/pallas_call | solution.py:443
  51.5 1.0 %copy-done.7 = f32[512,512]{1,0:T(8,128)} copy-done((f32[512,512]{1,0:T(8,128)}, f32[512,512]{1,0:T(8,128)S(1)}, u32[]{:S(2)}) %copy-start.7) | copy-done | bytes 1048600
  52.5 3.6 %all-to-all-done.arrived = f32[192,4,128]{2,1,0:T(4,128)S(1)} async-done(((f32[192,4,128]{2,1,0:T(4,128)}), f32[192,4,128]{2,1,0:T(4,128)S(1)}, u32[]{:S(2)}, u32[]{:S(2)}) %all-to-all-start) | async-done | bytes 393248 | tf_op jit(solution)/shard_map/all_to_all | solution.py:510
  56.1 1.2 %copy-done.8 = f32[512,512]{1,0:T(8,128)S(1)} copy-done((f32[512,512]{1,0:T(8,128)S(1)}, f32[512,512]{1,0:T(8,128)}, u32[]{:S(2)}) %copy-start.8) | copy-done | bytes 1048600
  57.3 6.4 %land.1 = (f32[512,512]{1,0:T(8,128)}, f32[4,64,128]{2,1,0:T(8,128)}) custom-call(s32[32]{0:T(128)S(1)} %copy-done.11, f32[512,512]{1,0:T(8,128)S(1)} %copy-done.8, f32[4,128]{1,0:T(4,128)S(1)} %get-tuple-element.34.inlet_now, s32[1,128]{1,0:T(1,128)S(1)} %pad.4.inlet, s32[64,128]{1,0:T(8,128)S(1)} %bitcast.26, f32[192,4,128]{2,1,0:T(4,128)S(1)} %all-to-all-done.arrived), custom_call_target="tpu_custom_call" | custom-call | flops 8589934592 | bytes 2097152 | tf_op jit(solution)/shard_map/land/pallas_call | solution.py:222
  (26 shorter events, 0.1 us)
Async XLA Ops:
  0.6 11.6 %copy-start = (f32[4,8,16,512]{3,2,1,0:T(8,128)S(1)}, f32[4,8,16,512]{3,2,1,0:T(8,128)}, u32[]{:S(2)}) copy-start(f32[4,8,16,512]{3,2,1,0:T(8,128)} %param.11) | copy-start | bytes 3145732
  0.6 11.6 %copy-start.6 = (s32[1,1,64]{2,1,0:T(1,128)S(1)}, s32[1,1,64]{2,1,0:T(1,128)}, u32[]{:S(2)}) copy-start(s32[1,1,64]{2,1,0:T(1,128)} %param.20) | copy-start | bytes 772
  0.6 11.6 %copy-start.9 = (s32[1,1,64,128]{3,2,1,0:T(8,128)S(1)}, s32[1,1,64,128]{3,2,1,0:T(8,128)}, u32[]{:S(2)}) copy-start(s32[1,1,64,128]{3,2,1,0:T(8,128)} %param.19) | copy-start | bytes 98308
  0.7 16.5 %collective-permute-start.4 = (f32[4,32]{1,0:T(4,128)}, f32[4,32]{1,0:T(4,128)S(1)}, u32[]{:S(2)}, u32[]{:S(2)}) collective-permute-start(f32[4,32]{1,0:T(4,128)} %ports.3), channel_id=1, source_target_pairs={{0,128},{64,192},{128,0},{192,64},{1,129},{65,193},{129,1},{193,65... | collective-permute-start | bytes 1544 | tf_op jit(solution)/shard_map/ppermute | solution.py:494
  5.1 21.4 %collective-permute-start = (f32[72,512]{1,0:T(8,128)}, f32[72,512]{1,0:T(8,128)S(1)}, u32[]{:S(2)}, u32[]{:S(2)}) collective-permute-start(f32[72,512]{1,0:T(8,128)} %get-tuple-element.20), channel_id=1, source_target_pairs={{0,1},{1,2},{2,3},{3,4},{4,5},{5,6},{6,7},{7,8},{8,9},{9,10},{10,1... | collective-permute-start | bytes 442376 | tf_op jit(solution)/shard_map/ppermute | solution.py:490
  9.5 17.0 %collective-permute-start.1 = (f32[72,512]{1,0:T(8,128)}, f32[72,512]{1,0:T(8,128)S(1)}, u32[]{:S(2)}, u32[]{:S(2)}) collective-permute-start(f32[72,512]{1,0:T(8,128)} %get-tuple-element.21), channel_id=1, source_target_pairs={{1,0},{2,1},{3,2},{4,3},{5,4},{6,5},{7,6},{8,7},{9,8},{10,9},{11,1... | collective-permute-start | bytes 442376 | tf_op jit(solution)/shard_map/ppermute | solution.py:491
  10.8 11.0 %collective-permute-start.2 = (f32[152,512]{1,0:T(8,128)}, f32[152,512]{1,0:T(8,128)S(1)}, u32[]{:S(2)}, u32[]{:S(2)}) collective-permute-start(f32[152,512]{1,0:T(8,128)} %get-tuple-element.22), channel_id=1, source_target_pairs={{0,64},{64,128},{128,192},{192,0},{1,65},{65,129},{129,193},{193,1... | collective-permute-start | bytes 933896 | tf_op jit(solution)/shard_map/ppermute | solution.py:492
  11.9 12.5 %collective-permute-start.3 = (f32[152,512]{1,0:T(8,128)}, f32[152,512]{1,0:T(8,128)S(1)}, u32[]{:S(2)}, u32[]{:S(2)}) collective-permute-start(f32[152,512]{1,0:T(8,128)} %get-tuple-element.23), channel_id=1, source_target_pairs={{64,0},{128,64},{192,128},{0,192},{65,1},{129,65},{193,129},{1,193... | collective-permute-start | bytes 933896 | tf_op jit(solution)/shard_map/ppermute | solution.py:493
  12.2 12.2 %copy-start.2 = (f32[4,1,1,64,128]{4,3,2,1,0:T(8,128)S(1)}, f32[4,1,1,64,128]{4,3,2,1,0:T(8,128)}, u32[]{:S(2)}) copy-start(f32[4,1,1,64,128]{4,3,2,1,0:T(8,128)} %param.16) | copy-start | bytes 393220
  12.2 12.2 %copy-start.3 = (f32[1,1,64,128]{3,2,1,0:T(8,128)S(1)}, f32[1,1,64,128]{3,2,1,0:T(8,128)}, u32[]{:S(2)}) copy-start(f32[1,1,64,128]{3,2,1,0:T(8,128)} %param.17) | copy-start | bytes 98308
  12.2 12.2 %copy-start.4 = (f32[1,1,64,128]{3,2,1,0:T(8,128)S(1)}, f32[1,1,64,128]{3,2,1,0:T(8,128)}, u32[]{:S(2)}) copy-start(f32[1,1,64,128]{3,2,1,0:T(8,128)} %param.18) | copy-start | bytes 98308
  12.2 12.2 %copy-start.5 = (f32[4,32]{1,0:T(4,128)S(1)}, f32[4,32]{1,0:T(4,128)}, u32[]{:S(2)}) copy-start(f32[4,32]{1,0:T(4,128)} %ports.3) | copy-start | bytes 1540
  24.5 20.2 %copy-start.12 = (s32[32]{0:T(128)S(1)}, s32[32]{0:T(128)}, u32[]{:S(2)}) copy-start(s32[32]{0:T(128)} %param.15) | copy-start | bytes 388
  24.5 20.2 %copy-start.1 = (f32[8,16,512]{2,1,0:T(8,128)S(1)}, f32[8,16,512]{2,1,0:T(8,128)}, u32[]{:S(2)}) copy-start(f32[8,16,512]{2,1,0:T(8,128)} %param.12) | copy-start | bytes 786436
  26.5 29.5 %all-to-all-start = ((f32[192,4,128]{2,1,0:T(4,128)}), f32[192,4,128]{2,1,0:T(4,128)S(1)}, u32[]{:S(2)}, u32[]{:S(2)}) async-start(f32[192,4,128]{2,1,0:T(4,128)} %slip.1), calls=%async_computation | async-start | bytes 786432 | tf_op jit(solution)/shard_map/all_to_all | solution.py:510
  40.3 5.9 %collective-permute-start.5 = (f32[8,512]{1,0:T(8,128)S(1)}, f32[8,512]{1,0:T(8,128)S(1)}, u32[]{:S(2)}, u32[]{:S(2)}) collective-permute-start(f32[8,512]{1,0:T(8,128)S(1)} %get-tuple-element.31), channel_id=1, source_target_pairs={{0,64},{64,128},{128,192},{1,65},{65,129},{129,193},{2,66},{66,130... | collective-permute-start | bytes 49160 | tf_op jit(solution)/shard_map/ppermute | solution.py:512
  42.3 5.4 %collective-permute-start.6 = (f32[8,512]{1,0:T(8,128)S(1)}, f32[8,512]{1,0:T(8,128)S(1)}, u32[]{:S(2)}, u32[]{:S(2)}) collective-permute-start(f32[8,512]{1,0:T(8,128)S(1)} %get-tuple-element.32), channel_id=1, source_target_pairs={{64,0},{128,64},{192,128},{65,1},{129,65},{193,129},{66,2},{130,66... | collective-permute-start | bytes 49160 | tf_op jit(solution)/shard_map/ppermute | solution.py:513
  46.2 9.9 %copy-start.10 = (s32[1,1,64,128]{3,2,1,0:T(8,128)S(1)}, s32[1,1,64,128]{3,2,1,0:T(8,128)}, u32[]{:S(2)}) copy-start(s32[1,1,64,128]{3,2,1,0:T(8,128)} %param.21) | copy-start | bytes 98308
  46.2 9.9 %copy-start.11 = (s32[32]{0:T(128)S(1)}, s32[32]{0:T(128)}, u32[]{:S(2)}) copy-start(s32[32]{0:T(128)} %match.1) | copy-start | bytes 388
  51.5 1.0 %copy-start.7 = (f32[512,512]{1,0:T(8,128)}, f32[512,512]{1,0:T(8,128)S(1)}, u32[]{:S(2)}) copy-start(f32[512,512]{1,0:T(8,128)S(1)} %get-tuple-element.33.second) | copy-start | bytes 3145732
  56.1 1.2 %copy-start.8 = (f32[512,512]{1,0:T(8,128)S(1)}, f32[512,512]{1,0:T(8,128)}, u32[]{:S(2)}) copy-start(f32[512,512]{1,0:T(8,128)} %copy-done.7) | copy-start | bytes 3145732

commit v8 on v6

--- a/solution.py
+++ b/solution.py
@@ -140,7 +140,7 @@
     )(counts, sampled, state, rate, mass, ports, above, across, below)
 
 
-def land_kernel(GP, match, second, inlet_now, inlet, arrival, arrived, flow_out, state_out, last_ref, last, packed, sem):
+def land_kernel(GP, match, second, inlet_now, inlet, arrival, arrived, flow_far, state_far, flow_out, state_out, last_ref, last, packed, sem, out_sems):
     comps, partners, cap = state_out.shape
     total, depth = second.shape
     rows = total // comps
@@ -166,19 +166,22 @@
     last_ref[0:1, :] = top
     fetch = pltpu.make_async_copy(last_ref.at[0:1, :], last, sem)
     fetch.start()
-
-    def spread(cells, values):
+    state_copy = pltpu.make_async_copy(state_out, state_far, out_sems.at[2])
+    state_copy.start()
+    flow_out[...] = second[...]
+
+    def add(cells, values, spot):
         row = lax.broadcasted_iota(jnp.int32, (rows, cells.shape[1]), 0) == (cells >> shift)
         high, low = halves(values)
         parts = []
         for part in (high.astype(jnp.float32), low.astype(jnp.float32)):
-            for c in range(comps):
+            for c in range(values.shape[0]):
                 parts.append(jnp.where(row, part[c : c + 1], 0.0).astype(jnp.bfloat16))
-        return jnp.concatenate(parts, axis=0)
-
-    def product(cells, values):
-        both = lax.dot_general(spread(cells, values), column_hot(cells, depth), nt, preferred_element_type=jnp.float32)
-        return both[:total] + both[total:]
+        both = lax.dot_general(
+            jnp.concatenate(parts, axis=0), column_hot(cells, depth), nt, preferred_element_type=jnp.float32
+        )
+        half = values.shape[0] * rows
+        flow_out[spot : spot + half, :] += both[:half] + both[half:]
 
     section = lax.axis_index("sec")
     sections = cap // per
@@ -190,7 +193,6 @@
         turned = pltpu.roll(arrived[3 * (device % partners) + 2], (k + cap - place) % cap, 1)
         target = jnp.where(slot == k, turned, target)
     change = jnp.where(slot < entries, 0.5 * (target - inlet_now[...]), 0.0)
-    flow_out[...] = second[...] + product(inlet[0:1, :], change)
     packed[...] = jnp.zeros_like(packed)
     fetch.wait()
 
@@ -207,16 +209,35 @@
 
     used = lax.fori_loop(0, partners, pack, 0, unroll=8)
 
+    spare = (used + cap - 1) >> cap_shift
+    cells = jnp.broadcast_to(inlet[0:1, :].astype(jnp.float32), (8 - comps, cap))
+    packed[spare] = jnp.concatenate([change, cells], axis=0)
+
+    def load(g):
+        both = jnp.concatenate([packed[g * GP + i] for i in range(GP)], axis=1)
+        return both[comps : comps + 1].astype(jnp.int32), both[:comps]
+
     def group(g, carry):
-        first = g * GP
-        both = jnp.concatenate([packed[first + i] for i in range(GP)], axis=1)
-        flow_out[...] += product(both[comps : comps + 1].astype(jnp.int32), both[:comps])
+        cells, values = load(g)
+        add(cells, values, 0)
         return carry
 
-    lax.fori_loop(0, (used + GP * cap - 1) // (GP * cap), group, 0)
-
-
-def land(match, second, inlet_now, inlet, arrival, arrived, GP=8):
+    final = spare // GP
+    lax.fori_loop(0, final, group, 0)
+    cells, values = load(final)
+    half = comps // 2
+    copies = []
+    for i in range(2):
+        part = pl.ds(i * half * rows, half * rows)
+        add(cells, values[i * half : (i + 1) * half], i * half * rows)
+        copies.append(pltpu.make_async_copy(flow_out.at[part, :], flow_far.at[part, :], out_sems.at[i]))
+        copies[i].start()
+    for copy in copies:
+        copy.wait()
+    state_copy.wait()
+
+
+def land(match, second, inlet_now, inlet, arrival, arrived, GP=4):
     partners, cap = arrival.shape
     comps = arrived.shape[1]
     return pl.pallas_call(
@@ -226,12 +247,15 @@
             jax.ShapeDtypeStruct((comps, partners, cap), jnp.float32),
         ),
         in_specs=[SM] + [VM] * 5,
-        out_specs=(VM, VM),
+        out_specs=(HB, HB),
         scratch_shapes=[
+            pltpu.VMEM(second.shape, jnp.float32),
+            pltpu.VMEM((comps, partners, cap), jnp.float32),
             pltpu.VMEM((cap, cap), jnp.int32),
             pltpu.SMEM((1, cap), jnp.int32),
             pltpu.VMEM((partners + 8, 8, cap), jnp.float32),
             pltpu.SemaphoreType.DMA,
+            pltpu.SemaphoreType.DMA((3,)),
         ],
         compiler_params=pltpu.CompilerParams(vmem_limit_bytes=24 * 1024 * 1024),
         cost_estimate=pl.CostEstimate(flops=2 * 8192 * 512 * 1024, bytes_accessed=2**21, transcendentals=0),
@@ -334,7 +358,7 @@
     )(flow, viscosity, below, above)
 
 
-def inner_kernel(comps, depth_z, width, flow, viscosity, below, above, first):
+def inner_kernel(comps, depth_z, width, flow, viscosity, below, above, first, middle):
     two = 2 * width
 
     def own(z):
@@ -355,21 +379,35 @@
         for c in range(comps):
             first[c, z + 1, 0:width, :] = centers[c] + change[c]
 
+    def second(z, carry):
+        plane, upper, lower = ([first[c, z + 1 + d] for c in range(comps)] for d in (0, 1, -1))
+        at = pl.multiple_of(z * width, width)
+        centers, change = tendency(plane, upper, lower, viscosity[pl.ds(at, width), :], width)
+        for c in range(comps):
+            spot = pl.multiple_of((c * depth_z + z) * width, width)
+            middle[pl.ds(spot, width), :] = 0.5 * flow[pl.ds(spot, width), :] + 0.5 * (centers[c] + change[c])
+        return carry
+
+    lax.fori_loop(0, depth_z, second, 0)
+
 
 def inner(comps, depth_z, width, flow, viscosity, below, above):
     depth = flow.shape[1]
     return pl.pallas_call(
         functools.partial(inner_kernel, comps, depth_z, width),
-        out_shape=jax.ShapeDtypeStruct((comps, depth_z + 2, width, depth), jnp.float32),
+        out_shape=(
+            jax.ShapeDtypeStruct((comps, depth_z + 2, width, depth), jnp.float32),
+            jax.ShapeDtypeStruct(flow.shape, jnp.float32),
+        ),
         in_specs=[VM] * 4,
-        out_specs=VM,
+        out_specs=(VM, VM),
         compiler_params=pltpu.CompilerParams(vmem_limit_bytes=24 * 1024 * 1024),
         cost_estimate=pl.CostEstimate(flops=10**7, bytes_accessed=2**22, transcendentals=0),
         name="inner",
     )(flow, viscosity, below, above)
 
 
-def outer_kernel(comps, depth_z, width, flow, viscosity, below, above, first, left, right, inlet, second_out, inlet_now, strip, visc, started, table):
+def outer_kernel(comps, depth_z, width, flow, viscosity, below, above, first, middle, left, right, inlet, second_out, inlet_now, strip, visc, started, table):
     depth = flow.shape[1]
     two = 2 * width
     rows = depth_z * width
@@ -408,38 +446,39 @@
         visc[z + 1, 2:4, :] = ref[spot : spot + 2, :]
         visc[z + 1, 4:6, :] = ref[spot + width - 2 : spot + width, :]
 
-    place = lax.broadcasted_iota(jnp.int32, (width, 1), 0)
-    blank = jnp.zeros((6, depth), jnp.float32)
+    place = lax.broadcasted_iota(jnp.int32, (8, 1), 0)
+
+    def apart(value):
+        return jnp.where(place < 4, pltpu.roll(value, 7, 0), pltpu.roll(value, 1, 0))
 
     def one(z, carry):
         plane, upper, lower = ([strip[c, z + 1 + d] for c in range(comps)] for d in (0, 1, -1))
         centers, change = tendency(plane, upper, lower, visc[z], 8)
         for c in range(comps):
-            edge = centers[c] + change[c]
-            mine = first[c, z]
-            mine = jnp.where(place == 0, edge[2:3], mine)
-            mine = jnp.where(place == width - 1, edge[5:6], mine)
-            started[c, z, 0:width, :] = mine
-            started[c, z, width : width + 8, :] = jnp.concatenate([edge[6:7], blank, edge[1:2]], axis=0)
+            ends = apart(centers[c] + change[c])
+            near = jnp.where(place < 4, pltpu.roll(first[c, z, 0:8, :], 1, 0), pltpu.roll(first[c, z, width - 8 : width, :], 7, 0))
+            started[c, z] = jnp.where((place < 2) | (place > 5), ends, near)
         return carry
 
-    lax.fori_loop(0, depth_z + 2, one, 0)
+    lax.fori_loop(0, depth_z + 2, one, 0, unroll=2)
 
     def second(z, carry):
-        plane = [started[c, z + 1] for c in range(comps)]
-        upper, lower = ([started[c, z + 1 + d, 0:width, :] for c in range(comps)] for d in (1, -1))
-        at = pl.multiple_of(z * width, width)
-        centers, change = tendency(plane, upper, lower, viscosity[pl.ds(at, width), :], width)
+        plane, upper, lower = ([started[c, z + 1 + d] for c in range(comps)] for d in (0, 1, -1))
+        centers, change = tendency(plane, upper, lower, apart(visc[z + 1]), 8)
         for c in range(comps):
             spot = pl.multiple_of((c * depth_z + z) * width, width)
-            value = 0.5 * flow[pl.ds(spot, width), :] + 0.5 * (centers[c] + change[c])
+            edge = 0.5 * apart(strip[c, z + 2]) + 0.5 * (centers[c] + change[c])
+            mine = middle[pl.ds(spot, width), :]
+            top = jnp.where(place < 2, pltpu.roll(edge, 7, 0), mine[0:8])
+            end = jnp.where(place > 5, pltpu.roll(edge, 1, 0), mine[width - 8 :])
+            value = jnp.concatenate([top, mine[8 : width - 8], end] if width > 16 else [top, end], axis=0)
             second_out[pl.ds(spot, width), :] = value
             high, low = halves(value)
             table[pl.ds(spot, width), :] = high
             table[pl.ds(total + spot, width), :] = low
         return carry
 
-    lax.fori_loop(0, depth_z, second, 0)
+    lax.fori_loop(0, depth_z, second, 0, unroll=2)
 
     cells = inlet[0:1, :]
     picked = jnp.dot(table[...], column_hot(cells, depth), preferred_element_type=jnp.float32)
@@ -449,7 +488,7 @@
         inlet_now[c : c + 1, :] = jnp.sum(jnp.where(row, both, 0.0), axis=0, keepdims=True)
 
 
-def outer(comps, depth_z, width, flow, viscosity, below, above, first, left, right, inlet):
+def outer(comps, depth_z, width, flow, viscosity, below, above, first, middle, left, right, inlet):
     depth = flow.shape[1]
     return pl.pallas_call(
         functools.partial(outer_kernel, comps, depth_z, width),
@@ -457,18 +496,18 @@
             jax.ShapeDtypeStruct(flow.shape, jnp.float32),
             jax.ShapeDtypeStruct((comps, inlet.shape[1]), jnp.float32),
         ),
-        in_specs=[VM] * 8,
+        in_specs=[VM] * 9,
         out_specs=(VM, VM),
         scratch_shapes=[
             pltpu.VMEM((comps, depth_z + 4, 8, depth), jnp.float32),
             pltpu.VMEM((depth_z + 2, 8, depth), jnp.float32),
-            pltpu.VMEM((comps, depth_z + 2, width + 8, depth), jnp.float32),
+            pltpu.VMEM((comps, depth_z + 2, 8, depth), jnp.float32),
             pltpu.VMEM((2 * flow.shape[0], depth), jnp.bfloat16),
         ],
         compiler_params=pltpu.CompilerParams(vmem_limit_bytes=24 * 1024 * 1024),
         cost_estimate=pl.CostEstimate(flops=10**7, bytes_accessed=2**22, transcendentals=0),
         name="outer",
-    )(flow, viscosity, below, above, first, left, right, inlet)
+    )(flow, viscosity, below, above, first, middle, left, right, inlet)
 
 
 def on_device(
@@ -520,9 +559,9 @@
     low_edge, high_edge, bottom, top = edges(*sizes, flow, visc, below, above)
     left = lax.ppermute(high_edge, "tile", forth)
     right = lax.ppermute(low_edge, "tile", back)
-    inlet = jnp.pad(jnp.stack([inlet_cell, port_match]), ((0, 0), (0, cap - inlet_cell.shape[0])))
-    first = inner(*sizes, flow, visc, bottom, top)
-    second, inlet_now = outer(*sizes, flow, visc, bottom, top, first, left, right, inlet)
+    inlet = jnp.pad(inlet_cell.reshape(1, -1), ((0, 0), (0, cap - inlet_cell.shape[0])))
+    first, middle = inner(*sizes, flow, visc, bottom, top)
+    second, inlet_now = outer(*sizes, flow, visc, bottom, top, first, middle, left, right, inlet)
     flow_next, arrived_state = land(
         port_match, second, inlet_now, inlet, arrival_cell.reshape(partners, cap), arrived
     )

time: 60.4 us -> 58.9 us (0.975)
  the two profiles are of different devices: /device:TPU:1 before, /device:TPU:88 now
where the time goes in v8:
time: 58.9 us; the launch traced here: 58.7 us
  starting transfers between devices  24.5 us (42%)
  Pallas kernels  22.6 us (38%)
  waiting for transfers between devices  10.7 us (18%)
  between operations  0.85 us (1%)
    all_to_all x1, starting transfers between devices, on_device(): lax.all_to_all(outgoing, 'tile', split_axis=0, concat_axis=0, tiled=True)  12.8 us
    pallas_call x1, Pallas kernels, land(): pl.pallas_call(functools.partial(land_kernel, GP), out_shape=(jax.ShapeDt...  7.79 us
    ppermute x1, waiting for transfers between devices, on_device(): right = lax.ppermute(low_edge, 'tile', back)  5.54 us
    ppermute x1, starting transfers between devices, on_device(): left = lax.ppermute(high_edge, 'tile', forth)  4.91 us
    pallas_call x1, Pallas kernels, sample(): pl.pallas_call(functools.partial(sample_kernel, GP), out_shape=jax.ShapeD...  4.18 us
    ppermute x1, starting transfers between devices, on_device(): right = lax.ppermute(low_edge, 'tile', back)  3.36 us
    ppermute x1, waiting for transfers between devices, on_device(): below = lax.ppermute(high_cap, 'sec', up)  3.06 us
    pallas_call x1, Pallas kernels, inner(): pl.pallas_call(functools.partial(inner_kernel, comps, depth_z, width), ou...  3 us
  transfers between devices with their start and end apart: 6, of which 3 were waited for; matrix products, arithmetic and copies ran while one was open for 0% of the time, Pallas kernels for 22%

profile of v8, /device:TPU:88, one launch (start us, length us, event | category | flops | bytes accessed | tf_op | source)
XLA Modules:
  0.0 58.7 jit_solution(1692210251494872202)
XLA Ops:
  0.7 1.6 %collective-permute-start.2 = (f32[4,32]{1,0:T(4,128)}, f32[4,32]{1,0:T(4,128)S(1)}, u32[]{:S(2)}, u32[]{:S(2)}) collective-permute-start(f32[4,32]{1,0:T(4,128)} %ports.3), channel_id=1, source_target_pairs={{0,128},{64,192},{128,0},{192,64},{1,129},{65,193},{129,1},{193,65... | collective-permute-start | bytes 1544 | tf_op jit(solution)/shard_map/ppermute | solution.py:542
  2.2 2.7 %caps.1 = (f32[152,512]{1,0:T(8,128)}, f32[152,512]{1,0:T(8,128)}) custom-call(f32[512,512]{1,0:T(8,128)} %bitcast.13, f32[128,512]{1,0:T(8,128)} %bitcast.18, f32[4,32]{1,0:T(4,128)} %ports.3), custom_call_target="tpu_custom_call" | custom-call | tf_op jit(solution)/shard_map/caps/pallas_call | solution.py:316
  4.9 0.1 collective-permute-start
  5.0 1.7 %collective-permute-start.1 = (f32[152,512]{1,0:T(8,128)}, f32[152,512]{1,0:T(8,128)S(1)}, u32[]{:S(2)}, u32[]{:S(2)}) collective-permute-start(f32[152,512]{1,0:T(8,128)} %get-tuple-element.19), channel_id=1, source_target_pairs={{64,0},{128,64},{192,128},{0,192},{65,1},{129,65},{193,129},{1,193... | collective-permute-start | bytes 933896 | tf_op jit(solution)/shard_map/ppermute | solution.py:541
  6.8 0.0 copy-start.3
  6.8 0.0 copy-start.4
  6.8 0.0 copy-start.5
  6.8 4.2 %sample.1.sampled = f32[72,4,128]{2,1,0:T(4,128)S(1)} custom-call(s32[64]{0:T(128)S(1)} %bitcast.25, f32[512,512]{1,0:T(8,128)S(1)} %bitcast.14, s32[64,128]{1,0:T(8,128)S(1)} %bitcast.27), custom_call_target="tpu_custom_call" | custom-call | flops 8589934592 | bytes 2097152 | tf_op jit(solution)/shard_map/sample/pallas_call | solution.py:69
  11.0 0.0 copy-start.1
  11.0 0.0 collective-permute-done.2.across
  11.0 3.1 %collective-permute-done.below = f32[152,512]{1,0:T(8,128)S(1)} collective-permute-done((f32[152,512]{1,0:T(8,128)}, f32[152,512]{1,0:T(8,128)S(1)}, u32[]{:S(2)}, u32[]{:S(2)}) %collective-permute-start) | collective-permute-done | bytes 311328 | tf_op jit(solution)/shard_map/ppermute | solution.py:540
  14.1 0.0 collective-permute-done.1.above
  14.1 2.0 %slip.1 = f32[192,4,128]{2,1,0:T(4,128)} custom-call(s32[64]{0:T(128)S(1)} %bitcast.26, f32[72,4,128]{2,1,0:T(4,128)S(1)} %sample.1.sampled, f32[4,64,128]{2,1,0:T(8,128)S(1)} %bitcast.22, f32[64,128]{1,0:T(8,128)S(1)} %bitcast.23, f32[64,128]{1,0:T(8,128)S(1)} %bitcast.24, f32[4,32]{1,0:T(4,128)S(1)} %copy-done.5, ...), custom_call_target="tpu_custom_call" | custom-call | flops 2000000 | bytes 1048576 | tf_op jit(solution)/shard_map/slip/pallas_call | solution.py:127
  16.1 0.0 copy-start.10
  16.1 12.8 %all-to-all-start = ((f32[192,4,128]{2,1,0:T(4,128)}), f32[192,4,128]{2,1,0:T(4,128)S(1)}, u32[]{:S(2)}, u32[]{:S(2)}) async-start(f32[192,4,128]{2,1,0:T(4,128)} %slip.1), calls=%async_computation | async-start | bytes 786432 | tf_op jit(solution)/shard_map/all_to_all | solution.py:558
  29.0 0.2 edges.1
  29.2 4.9 %collective-permute-start.3 = (f32[80,512]{1,0:T(8,128)S(1)}, f32[80,512]{1,0:T(8,128)S(1)}, u32[]{:S(2)}, u32[]{:S(2)}) collective-permute-start(f32[80,512]{1,0:T(8,128)S(1)} %get-tuple-element.27), channel_id=1, source_target_pairs={{0,1},{1,2},{2,3},{3,4},{4,5},{5,6},{6,7},{7,8},{8,9},{9,10},{10,1... | collective-permute-start | bytes 491528 | tf_op jit(solution)/shard_map/ppermute | solution.py:560
  34.1 3.4 %collective-permute-start.4 = (f32[80,512]{1,0:T(8,128)S(1)}, f32[80,512]{1,0:T(8,128)S(1)}, u32[]{:S(2)}, u32[]{:S(2)}) collective-permute-start(f32[80,512]{1,0:T(8,128)S(1)} %get-tuple-element.28), channel_id=1, source_target_pairs={{1,0},{2,1},{3,2},{4,3},{5,4},{6,5},{7,6},{8,7},{9,8},{10,9},{11,1... | collective-permute-start | bytes 491528 | tf_op jit(solution)/shard_map/ppermute | solution.py:561
  37.5 3.0 %inner.1 = (f32[4,10,16,512]{3,2,1,0:T(8,128)S(1)}, f32[512,512]{1,0:T(8,128)S(1)}) custom-call(f32[512,512]{1,0:T(8,128)S(1)} %bitcast.16, f32[128,512]{1,0:T(8,128)S(1)} %bitcast.20, f32[144,512]{1,0:T(8,128)S(1)} %get-tuple-element.23.below, f32[144,512]{1,0:T(8,128)S(1)} %get-tuple-element.24.above), custom_call_target="tpu_custom_call" | custom-call | flops 10000000 | bytes 4194304 | tf_op jit(solution)/shard_map/inner/pallas_call | solution.py:396
  40.5 2.1 %collective-permute-done.3.left = f32[80,512]{1,0:T(8,128)S(1)} collective-permute-done((f32[80,512]{1,0:T(8,128)S(1)}, f32[80,512]{1,0:T(8,128)S(1)}, u32[]{:S(2)}, u32[]{:S(2)}) %collective-permute-start.3) | collective-permute-done | bytes 163872 | tf_op jit(solution)/shard_map/ppermute | solution.py:560
  42.6 5.5 %collective-permute-done.4.right = f32[80,512]{1,0:T(8,128)S(1)} collective-permute-done((f32[80,512]{1,0:T(8,128)S(1)}, f32[80,512]{1,0:T(8,128)S(1)}, u32[]{:S(2)}, u32[]{:S(2)}) %collective-permute-start.4) | collective-permute-done | bytes 163872 | tf_op jit(solution)/shard_map/ppermute | solution.py:561
  48.1 2.8 %outer.1 = (f32[512,512]{1,0:T(8,128)S(1)}, f32[4,128]{1,0:T(4,128)S(1)}) custom-call(f32[512,512]{1,0:T(8,128)S(1)} %bitcast.17, f32[128,512]{1,0:T(8,128)S(1)} %bitcast.21, f32[144,512]{1,0:T(8,128)S(1)} %get-tuple-element.23.below, f32[144,512]{1,0:T(8,128)S(1)} %get-tuple-element.24.above, f32[4,10,16,512]{3,2,1,0:T(8,128)S(1)} %get-tuple-element.25.first, ...), custom_call_target="tpu_custom_call" | custom-call | flops 10000000 | bytes 4194304 | tf_op jit(solution)/shard_map/outer/pallas_call | solution.py:493
  50.9 0.0 all-to-all-done.arrived
  50.9 7.8 %land.1 = (f32[512,512]{1,0:T(8,128)}, f32[4,64,128]{2,1,0:T(8,128)}) custom-call(s32[32]{0:T(128)S(1)} %copy-done.9, f32[512,512]{1,0:T(8,128)S(1)} %get-tuple-element.29.second, f32[4,128]{1,0:T(4,128)S(1)} %get-tuple-element.30.inlet_now, s32[1,128]{1,0:T(1,128)S(1)} %pad.4.inlet, s32[64,128]{1,0:T(8,128)S(1)} %bitcast.28, ...), custom_call_target="tpu_custom_call" | custom-call | flops 8589934592 | bytes 2097152 | tf_op jit(solution)/shard_map/land/pallas_call | solution.py:243
  (18 shorter events, 0.0 us)
Async XLA Ops:
  0.6 6.1 %copy-start = (f32[4,8,16,512]{3,2,1,0:T(8,128)S(1)}, f32[4,8,16,512]{3,2,1,0:T(8,128)}, u32[]{:S(2)}) copy-start(f32[4,8,16,512]{3,2,1,0:T(8,128)} %param.11) | copy-start | bytes 3145732
  0.6 6.1 %copy-start.6 = (s32[1,1,64]{2,1,0:T(1,128)S(1)}, s32[1,1,64]{2,1,0:T(1,128)}, u32[]{:S(2)}) copy-start(s32[1,1,64]{2,1,0:T(1,128)} %param.20) | copy-start | bytes 772
  0.6 6.1 %copy-start.7 = (s32[1,1,64,128]{3,2,1,0:T(8,128)S(1)}, s32[1,1,64,128]{3,2,1,0:T(8,128)}, u32[]{:S(2)}) copy-start(s32[1,1,64,128]{3,2,1,0:T(8,128)} %param.19) | copy-start | bytes 98308
  0.7 10.3 %collective-permute-start.2 = (f32[4,32]{1,0:T(4,128)}, f32[4,32]{1,0:T(4,128)S(1)}, u32[]{:S(2)}, u32[]{:S(2)}) collective-permute-start(f32[4,32]{1,0:T(4,128)} %ports.3), channel_id=1, source_target_pairs={{0,128},{64,192},{128,0},{192,64},{1,129},{65,193},{129,1},{193,65... | collective-permute-start | bytes 1544 | tf_op jit(solution)/shard_map/ppermute | solution.py:542
  4.9 9.1 %collective-permute-start = (f32[152,512]{1,0:T(8,128)}, f32[152,512]{1,0:T(8,128)S(1)}, u32[]{:S(2)}, u32[]{:S(2)}) collective-permute-start(f32[152,512]{1,0:T(8,128)} %get-tuple-element.18), channel_id=1, source_target_pairs={{0,64},{64,128},{128,192},{192,0},{1,65},{65,129},{129,193},{193,1... | collective-permute-start | bytes 933896 | tf_op jit(solution)/shard_map/ppermute | solution.py:540
  5.0 9.1 %collective-permute-start.1 = (f32[152,512]{1,0:T(8,128)}, f32[152,512]{1,0:T(8,128)S(1)}, u32[]{:S(2)}, u32[]{:S(2)}) collective-permute-start(f32[152,512]{1,0:T(8,128)} %get-tuple-element.19), channel_id=1, source_target_pairs={{64,0},{128,64},{192,128},{0,192},{65,1},{129,65},{193,129},{1,193... | collective-permute-start | bytes 933896 | tf_op jit(solution)/shard_map/ppermute | solution.py:541
  6.8 7.3 %copy-start.2 = (f32[4,1,1,64,128]{4,3,2,1,0:T(8,128)S(1)}, f32[4,1,1,64,128]{4,3,2,1,0:T(8,128)}, u32[]{:S(2)}) copy-start(f32[4,1,1,64,128]{4,3,2,1,0:T(8,128)} %param.16) | copy-start | bytes 393220
  6.8 7.3 %copy-start.3 = (f32[1,1,64,128]{3,2,1,0:T(8,128)S(1)}, f32[1,1,64,128]{3,2,1,0:T(8,128)}, u32[]{:S(2)}) copy-start(f32[1,1,64,128]{3,2,1,0:T(8,128)} %param.17) | copy-start | bytes 98308
  6.8 7.3 %copy-start.4 = (f32[1,1,64,128]{3,2,1,0:T(8,128)S(1)}, f32[1,1,64,128]{3,2,1,0:T(8,128)}, u32[]{:S(2)}) copy-start(f32[1,1,64,128]{3,2,1,0:T(8,128)} %param.18) | copy-start | bytes 98308
  6.8 7.3 %copy-start.5 = (f32[4,32]{1,0:T(4,128)S(1)}, f32[4,32]{1,0:T(4,128)}, u32[]{:S(2)}) copy-start(f32[4,32]{1,0:T(4,128)} %ports.3) | copy-start | bytes 1540
  11.0 18.0 %copy-start.1 = (f32[8,16,512]{2,1,0:T(8,128)S(1)}, f32[8,16,512]{2,1,0:T(8,128)}, u32[]{:S(2)}) copy-start(f32[8,16,512]{2,1,0:T(8,128)} %param.12) | copy-start | bytes 786436
  16.1 21.4 %copy-start.10 = (s32[32]{0:T(128)S(1)}, s32[32]{0:T(128)}, u32[]{:S(2)}) copy-start(s32[32]{0:T(128)} %param.15) | copy-start | bytes 388
  16.1 34.8 %all-to-all-start = ((f32[192,4,128]{2,1,0:T(4,128)}), f32[192,4,128]{2,1,0:T(4,128)S(1)}, u32[]{:S(2)}, u32[]{:S(2)}) async-start(f32[192,4,128]{2,1,0:T(4,128)} %slip.1), calls=%async_computation | async-start | bytes 786432 | tf_op jit(solution)/shard_map/all_to_all | solution.py:558
  29.2 13.4 %collective-permute-start.3 = (f32[80,512]{1,0:T(8,128)S(1)}, f32[80,512]{1,0:T(8,128)S(1)}, u32[]{:S(2)}, u32[]{:S(2)}) collective-permute-start(f32[80,512]{1,0:T(8,128)S(1)} %get-tuple-element.27), channel_id=1, source_target_pairs={{0,1},{1,2},{2,3},{3,4},{4,5},{5,6},{6,7},{7,8},{8,9},{9,10},{10,1... | collective-permute-start | bytes 491528 | tf_op jit(solution)/shard_map/ppermute | solution.py:560
  34.1 14.0 %collective-permute-start.4 = (f32[80,512]{1,0:T(8,128)S(1)}, f32[80,512]{1,0:T(8,128)S(1)}, u32[]{:S(2)}, u32[]{:S(2)}) collective-permute-start(f32[80,512]{1,0:T(8,128)S(1)} %get-tuple-element.28), channel_id=1, source_target_pairs={{1,0},{2,1},{3,2},{4,3},{5,4},{6,5},{7,6},{8,7},{9,8},{10,9},{11,1... | collective-permute-start | bytes 491528 | tf_op jit(solution)/shard_map/ppermute | solution.py:561
  48.1 2.8 %copy-start.8 = (s32[1,1,64,128]{3,2,1,0:T(8,128)S(1)}, s32[1,1,64,128]{3,2,1,0:T(8,128)}, u32[]{:S(2)}) copy-start(s32[1,1,64,128]{3,2,1,0:T(8,128)} %param.21) | copy-start | bytes 98308
  48.1 2.8 %copy-start.9 = (s32[32]{0:T(128)S(1)}, s32[32]{0:T(128)}, u32[]{:S(2)}) copy-start(s32[32]{0:T(128)} %match.1) | copy-start | bytes 388

commit v9 on v8

--- a/solution.py
+++ b/solution.py
@@ -288,69 +288,65 @@
     return centers, out
 
 
-def cap_kernel(comps, depth_z, width, flow, viscosity, ports, low_out, high_out, sems):
-    copies = []
-
-    def copy(source, target):
-        copies.append(pltpu.make_async_copy(source, target, sems.at[len(copies)]))
-        copies[-1].start()
-
+def rim_kernel(comps, depth_z, width, flow, viscosity, ports, high_edge, low_cap, high_cap):
+    for k in range(comps * depth_z):
+        high_edge[2 * k : 2 * k + 2, :] = flow[(k + 1) * width - 2 : (k + 1) * width, :]
+    base = 2 * comps * depth_z
+    for z in range(depth_z):
+        high_edge[base + z : base + z + 1, :] = viscosity[(z + 1) * width - 1 : (z + 1) * width, :]
     two = 2 * width
-    last = (depth_z - 1) * width
+    last = depth_z * width
     for c in range(comps):
-        base = c * depth_z * width
-        copy(flow.at[base : base + two, :], low_out.at[c * two : (c + 1) * two, :])
-        copy(flow.at[base + last - width : base + last + width, :], high_out.at[c * two : (c + 1) * two, :])
+        low_cap[c * two : (c + 1) * two, :] = flow[c * last : c * last + two, :]
+        high_cap[c * two : (c + 1) * two, :] = flow[(c + 1) * last - two : (c + 1) * last, :]
     base = comps * two
-    copy(viscosity.at[0:width, :], low_out.at[base : base + width, :])
-    copy(viscosity.at[last : last + width, :], high_out.at[base : base + width, :])
-    for out in (low_out, high_out):
+    low_cap[base : base + width, :] = viscosity[0:width, :]
+    high_cap[base : base + width, :] = viscosity[last - width : last, :]
+    for out in (low_cap, high_cap):
         out[base + width :, :] = jnp.zeros((8, out.shape[1]), jnp.float32)
         out[base + width : base + width + comps, 0 : ports.shape[1]] = ports[...]
-    for started in copies:
-        started.wait()
-
-
-def caps(comps, depth_z, width, flow, viscosity, ports):
-    shape = jax.ShapeDtypeStruct((2 * comps * width + width + 8, flow.shape[1]), jnp.float32)
-    return pl.pallas_call(
-        functools.partial(cap_kernel, comps, depth_z, width),
-        out_shape=(shape, shape),
-        in_specs=[HB, HB, VM],
-        out_specs=(VM, VM),
-        scratch_shapes=[pltpu.SemaphoreType.DMA((2 * comps + 2,))],
+
+
+def rims(comps, depth_z, width, flow, viscosity, ports):
+    depth = flow.shape[1]
+    edge = jax.ShapeDtypeStruct(((2 * comps + 1) * depth_z, depth), jnp.float32)
+    cap = jax.ShapeDtypeStruct((2 * comps * width + width + 8, depth), jnp.float32)
+    return pl.pallas_call(
+        functools.partial(rim_kernel, comps, depth_z, width),
+        out_shape=(edge, cap, cap),
+        in_specs=[VM] * 3,
+        out_specs=(VM,) * 3,
         compiler_params=pltpu.CompilerParams(vmem_limit_bytes=60 * 1024 * 1024),
-        name="caps",
+        name="rims",
     )(flow, viscosity, ports)
 
 
-def edge_kernel(comps, depth_z, width, flow, viscosity, below, above, low_out, high_out, bottom, top):
+def edge_kernel(comps, depth_z, width, flow, viscosity, below, above, low_out, corner, bottom, top):
     section = lax.axis_index("sec")
     bottom[...] = jnp.where(section > 0, below[0 : bottom.shape[0], :], 0.0)
     top[...] = jnp.where(section < lax.axis_size("sec") - 1, above[0 : top.shape[0], :], 0.0)
     two = 2 * width
     for k in range(comps * depth_z):
         low_out[2 * k : 2 * k + 2, :] = flow[k * width : k * width + 2, :]
-        high_out[2 * k : 2 * k + 2, :] = flow[(k + 1) * width - 2 : (k + 1) * width, :]
     base = 2 * comps * depth_z
     for c in range(comps):
         low_out[base + 2 * c : base + 2 * c + 1, :] = bottom[c * two + width : c * two + width + 1, :]
         low_out[base + 2 * c + 1 : base + 2 * c + 2, :] = top[c * two : c * two + 1, :]
-        high_out[base + 2 * c : base + 2 * c + 1, :] = bottom[(c + 1) * two - 1 : (c + 1) * two, :]
-        high_out[base + 2 * c + 1 : base + 2 * c + 2, :] = top[c * two + width - 1 : c * two + width, :]
+        corner[2 * c : 2 * c + 1, :] = bottom[(c + 1) * two - 1 : (c + 1) * two, :]
+        corner[2 * c + 1 : 2 * c + 2, :] = top[c * two + width - 1 : c * two + width, :]
     base += 2 * comps
     for z in range(depth_z):
         low_out[base + z : base + z + 1, :] = viscosity[z * width : z * width + 1, :]
-        high_out[base + z : base + z + 1, :] = viscosity[(z + 1) * width - 1 : (z + 1) * width, :]
 
 
 def edges(comps, depth_z, width, flow, viscosity, below, above):
     depth = flow.shape[1]
     shape = jax.ShapeDtypeStruct((2 * comps * (depth_z + 1) + depth_z, depth), jnp.float32)
+    small = jax.ShapeDtypeStruct((2 * comps, depth), jnp.float32)
     halo = jax.ShapeDtypeStruct(((2 * comps + 1) * width, depth), jnp.float32)
     return pl.pallas_call(
         functools.partial(edge_kernel, comps, depth_z, width),
-        out_shape=(shape, shape, halo, halo),
+        out_shape=(shape, small, halo, halo),
         in_specs=[VM] * 4,
         out_specs=(VM,) * 4,
         compiler_params=pltpu.CompilerParams(vmem_limit_bytes=24 * 1024 * 1024),
@@ -407,7 +403,7 @@
     )(flow, viscosity, below, above)
 
 
-def outer_kernel(comps, depth_z, width, flow, viscosity, below, above, first, middle, left, right, inlet, second_out, inlet_now, strip, visc, started, table):
+def outer_kernel(comps, depth_z, width, flow, viscosity, below, above, first, middle, left, corner, right, inlet, second_out, inlet_now, strip, visc, started, table):
     depth = flow.shape[1]
     two = 2 * width
     rows = depth_z * width
@@ -431,7 +427,8 @@
                 strip[c, z + 2, 6:8, :] = right[k : k + 2, :]
             elif z in (-1, depth_z):
                 k = base + 2 * c + (z == depth_z)
-                strip[c, z + 2, 1:2, :] = left[k : k + 1, :]
+                j = k - base
+                strip[c, z + 2, 1:2, :] = corner[j : j + 1, :]
                 strip[c, z + 2, 6:7, :] = right[k : k + 1, :]
     side = base + 2 * comps
     for z in range(-1, depth_z + 1):
@@ -441,7 +438,7 @@
             ref, spot = above, comps * two
         else:
             ref, spot = viscosity, z * width
-            visc[z + 1, 1:2, :] = left[side + z : side + z + 1, :]
+            visc[z + 1, 1:2, :] = left[base + z : base + z + 1, :]
             visc[z + 1, 6:7, :] = right[side + z : side + z + 1, :]
         visc[z + 1, 2:4, :] = ref[spot : spot + 2, :]
         visc[z + 1, 4:6, :] = ref[spot + width - 2 : spot + width, :]
@@ -488,7 +485,7 @@
         inlet_now[c : c + 1, :] = jnp.sum(jnp.where(row, both, 0.0), axis=0, keepdims=True)
 
 
-def outer(comps, depth_z, width, flow, viscosity, below, above, first, middle, left, right, inlet):
+def outer(comps, depth_z, width, flow, viscosity, below, above, first, middle, left, corner, right, inlet):
     depth = flow.shape[1]
     return pl.pallas_call(
         functools.partial(outer_kernel, comps, depth_z, width),
@@ -496,7 +493,7 @@
             jax.ShapeDtypeStruct(flow.shape, jnp.float32),
             jax.ShapeDtypeStruct((comps, inlet.shape[1]), jnp.float32),
         ),
-        in_specs=[VM] * 9,
+        in_specs=[VM] * 10,
         out_specs=(VM, VM),
         scratch_shapes=[
             pltpu.VMEM((comps, depth_z + 4, 8, depth), jnp.float32),
@@ -507,7 +504,7 @@
         compiler_params=pltpu.CompilerParams(vmem_limit_bytes=24 * 1024 * 1024),
         cost_estimate=pl.CostEstimate(flops=10**7, bytes_accessed=2**22, transcendentals=0),
         name="outer",
-    )(flow, viscosity, below, above, first, middle, left, right, inlet)
+    )(flow, viscosity, below, above, first, middle, left, corner, right, inlet)
 
 
 def on_device(
@@ -536,7 +533,8 @@
     down = [((i + 1) % levels, i) for i in range(levels)]
     over = [(i, (i + levels // 2) % levels) for i in range(levels)]
 
-    low_cap, high_cap = caps(*sizes, flow, visc, port_plane)
+    high_edge, low_cap, high_cap = rims(*sizes, flow, visc, port_plane)
+    left = lax.ppermute(high_edge, "tile", forth)
     below = lax.ppermute(high_cap, "sec", up)
     above = lax.ppermute(low_cap, "sec", down)
     across = lax.ppermute(port_plane, "sec", over)
@@ -554,14 +552,14 @@
         across,
         below,
     )
-    below, above, outgoing = lax.optimization_barrier((below, above, outgoing))
+    left, below, above, outgoing = lax.optimization_barrier((left, below, above, outgoing))
     arrived = lax.all_to_all(outgoing, "tile", split_axis=0, concat_axis=0, tiled=True)
-    low_edge, high_edge, bottom, top = edges(*sizes, flow, visc, below, above)
-    left = lax.ppermute(high_edge, "tile", forth)
+    low_edge, corner, bottom, top = edges(*sizes, flow, visc, below, above)
     right = lax.ppermute(low_edge, "tile", back)
+    corner = lax.ppermute(corner, "tile", forth)
     inlet = jnp.pad(inlet_cell.reshape(1, -1), ((0, 0), (0, cap - inlet_cell.shape[0])))
     first, middle = inner(*sizes, flow, visc, bottom, top)
-    second, inlet_now = outer(*sizes, flow, visc, bottom, top, first, middle, left, right, inlet)
+    second, inlet_now = outer(*sizes, flow, visc, bottom, top, first, middle, left, corner, right, inlet)
     flow_next, arrived_state = land(
         port_match, second, inlet_now, inlet, arrival_cell.reshape(partners, cap), arrived
     )

time: 58.9 us -> 63.4 us (1.076)
  the two profiles are of different devices: /device:TPU:88 before, /device:TPU:32 now
where the time goes in v9:
time: 63.4 us; the launch traced here: 63.2 us
  starting transfers between devices  31.7 us (50%)
  Pallas kernels  22.1 us (35%)
  waiting for transfers between devices  8.39 us (13%)
  between operations  0.86 us (1%)
    all_to_all x1, starting transfers between devices, on_device(): lax.all_to_all(outgoing, 'tile', split_axis=0, concat_axis=0, tiled=True)  14.8 us
    pallas_call x1, Pallas kernels, land(): pl.pallas_call(functools.partial(land_kernel, GP), out_shape=(jax.ShapeDt...  7.05 us
    ppermute x1, starting transfers between devices, on_device(): right = lax.ppermute(low_edge, 'tile', back)  6.98 us
    ppermute x1, waiting for transfers between devices, on_device(): corner = lax.ppermute(corner, 'tile', forth)  5.19 us
    pallas_call x1, Pallas kernels, sample(): pl.pallas_call(functools.partial(sample_kernel, GP), out_shape=jax.ShapeD...  4.9 us
    ppermute x1, starting transfers between devices, on_device(): left = lax.ppermute(high_edge, 'tile', forth)  4.63 us
    ppermute x1, waiting for transfers between devices, on_device(): below = lax.ppermute(high_cap, 'sec', up)  3.19 us
    pallas_call x1, Pallas kernels, inner(): pl.pallas_call(functools.partial(inner_kernel, comps, depth_z, width), ou...  3 us
  transfers between devices with their start and end apart: 7, of which 2 were waited for; matrix products, arithmetic and copies ran while one was open for 0% of the time, Pallas kernels for 24%

profile of v9, /device:TPU:32, one launch (start us, length us, event | category | flops | bytes accessed | tf_op | source)
XLA Modules:
  0.0 63.2 jit_solution(8896919452518658053)
XLA Ops:
  0.7 1.6 %collective-permute-start.3 = (f32[4,32]{1,0:T(4,128)}, f32[4,32]{1,0:T(4,128)S(1)}, u32[]{:S(2)}, u32[]{:S(2)}) collective-permute-start(f32[4,32]{1,0:T(4,128)} %ports.3), channel_id=1, source_target_pairs={{0,128},{64,192},{128,0},{192,64},{1,129},{65,193},{129,1},{193,65... | collective-permute-start | bytes 1544 | tf_op jit(solution)/shard_map/ppermute | solution.py:540
  2.2 2.3 %rims.1 = (f32[72,512]{1,0:T(8,128)}, f32[152,512]{1,0:T(8,128)}, f32[152,512]{1,0:T(8,128)}) custom-call(f32[512,512]{1,0:T(8,128)} %bitcast.13, f32[128,512]{1,0:T(8,128)} %bitcast.18, f32[4,32]{1,0:T(4,128)} %ports.3), custom_call_target="tpu_custom_call" | custom-call | tf_op jit(solution)/shard_map/rims/pallas_call | solution.py:314
  4.5 4.6 %collective-permute-start = (f32[72,512]{1,0:T(8,128)}, f32[72,512]{1,0:T(8,128)S(1)}, u32[]{:S(2)}, u32[]{:S(2)}) collective-permute-start(f32[72,512]{1,0:T(8,128)} %get-tuple-element.20), channel_id=1, source_target_pairs={{0,1},{1,2},{2,3},{3,4},{4,5},{5,6},{6,7},{7,8},{8,9},{9,10},{10,1... | collective-permute-start | bytes 442376 | tf_op jit(solution)/shard_map/ppermute | solution.py:537
  9.1 0.1 collective-permute-start.1
  9.2 1.7 %collective-permute-start.2 = (f32[152,512]{1,0:T(8,128)}, f32[152,512]{1,0:T(8,128)S(1)}, u32[]{:S(2)}, u32[]{:S(2)}) collective-permute-start(f32[152,512]{1,0:T(8,128)} %get-tuple-element.22), channel_id=1, source_target_pairs={{64,0},{128,64},{192,128},{0,192},{65,1},{129,65},{193,129},{1,193... | collective-permute-start | bytes 933896 | tf_op jit(solution)/shard_map/ppermute | solution.py:539
  11.0 0.0 copy-start.3
  11.0 0.0 copy-start.4
  11.0 0.0 copy-start.5
  11.0 4.9 %sample.1.sampled = f32[72,4,128]{2,1,0:T(4,128)S(1)} custom-call(s32[64]{0:T(128)S(1)} %bitcast.25, f32[512,512]{1,0:T(8,128)S(1)} %bitcast.14, s32[64,128]{1,0:T(8,128)S(1)} %bitcast.27), custom_call_target="tpu_custom_call" | custom-call | flops 8589934592 | bytes 2097152 | tf_op jit(solution)/shard_map/sample/pallas_call | solution.py:69
  15.9 0.0 copy-start.1
  15.9 3.2 %collective-permute-done.1.below = f32[152,512]{1,0:T(8,128)S(1)} collective-permute-done((f32[152,512]{1,0:T(8,128)}, f32[152,512]{1,0:T(8,128)S(1)}, u32[]{:S(2)}, u32[]{:S(2)}) %collective-permute-start.1) | collective-permute-done | bytes 311328 | tf_op jit(solution)/shard_map/ppermute | solution.py:538
  19.1 0.0 collective-permute-done.2.above
  19.2 2.0 %slip.1 = f32[192,4,128]{2,1,0:T(4,128)} custom-call(s32[64]{0:T(128)S(1)} %bitcast.26, f32[72,4,128]{2,1,0:T(4,128)S(1)} %sample.1.sampled, f32[4,64,128]{2,1,0:T(8,128)S(1)} %bitcast.22, f32[64,128]{1,0:T(8,128)S(1)} %bitcast.23, f32[64,128]{1,0:T(8,128)S(1)} %bitcast.24, f32[4,32]{1,0:T(4,128)S(1)} %copy-done.5, ...), custom_call_target="tpu_custom_call" | custom-call | flops 2000000 | bytes 1048576 | tf_op jit(solution)/shard_map/slip/pallas_call | solution.py:127
  21.2 0.0 copy-start.10
  21.2 14.8 %all-to-all-start = ((f32[192,4,128]{2,1,0:T(4,128)}), f32[192,4,128]{2,1,0:T(4,128)S(1)}, u32[]{:S(2)}, u32[]{:S(2)}) async-start(f32[192,4,128]{2,1,0:T(4,128)} %slip.1), calls=%async_computation | async-start | bytes 786432 | tf_op jit(solution)/shard_map/all_to_all | solution.py:556
  36.0 0.1 edges.1
  36.2 7.0 %collective-permute-start.5 = (f32[80,512]{1,0:T(8,128)S(1)}, f32[80,512]{1,0:T(8,128)S(1)}, u32[]{:S(2)}, u32[]{:S(2)}) collective-permute-start(f32[80,512]{1,0:T(8,128)S(1)} %get-tuple-element.32), channel_id=1, source_target_pairs={{1,0},{2,1},{3,2},{4,3},{5,4},{6,5},{7,6},{8,7},{9,8},{10,9},{11,1... | collective-permute-start | bytes 491528 | tf_op jit(solution)/shard_map/ppermute | solution.py:558
  43.1 1.9 %collective-permute-start.4 = (f32[8,512]{1,0:T(8,128)S(1)}, f32[8,512]{1,0:T(8,128)S(1)}, u32[]{:S(2)}, u32[]{:S(2)}) collective-permute-start(f32[8,512]{1,0:T(8,128)S(1)} %get-tuple-element.31), channel_id=1, source_target_pairs={{0,1},{1,2},{2,3},{3,4},{4,5},{5,6},{6,7},{7,8},{8,9},{9,10},{10,1... | collective-permute-start | bytes 49160 | tf_op jit(solution)/shard_map/ppermute | solution.py:559
  45.1 3.0 %inner.1 = (f32[4,10,16,512]{3,2,1,0:T(8,128)S(1)}, f32[512,512]{1,0:T(8,128)S(1)}) custom-call(f32[512,512]{1,0:T(8,128)S(1)} %bitcast.16, f32[128,512]{1,0:T(8,128)S(1)} %bitcast.20, f32[144,512]{1,0:T(8,128)S(1)} %get-tuple-element.26.below, f32[144,512]{1,0:T(8,128)S(1)} %get-tuple-element.27.above), custom_call_target="tpu_custom_call" | custom-call | flops 10000000 | bytes 4194304 | tf_op jit(solution)/shard_map/inner/pallas_call | solution.py:392
  48.1 5.2 %collective-permute-done.4.corner = f32[8,512]{1,0:T(8,128)S(1)} collective-permute-done((f32[8,512]{1,0:T(8,128)S(1)}, f32[8,512]{1,0:T(8,128)S(1)}, u32[]{:S(2)}, u32[]{:S(2)}) %collective-permute-start.4) | collective-permute-done | bytes 16416 | tf_op jit(solution)/shard_map/ppermute | solution.py:559
  53.3 0.0 collective-permute-done.5.right
  53.3 2.8 %outer.1 = (f32[512,512]{1,0:T(8,128)S(1)}, f32[4,128]{1,0:T(4,128)S(1)}) custom-call(f32[512,512]{1,0:T(8,128)S(1)} %bitcast.17, f32[128,512]{1,0:T(8,128)S(1)} %bitcast.21, f32[144,512]{1,0:T(8,128)S(1)} %get-tuple-element.26.below, f32[144,512]{1,0:T(8,128)S(1)} %get-tuple-element.27.above, f32[4,10,16,512]{3,2,1,0:T(8,128)S(1)} %get-tuple-element.28.first, ...), custom_call_target="tpu_custom_call" | custom-call | flops 10000000 | bytes 4194304 | tf_op jit(solution)/shard_map/outer/pallas_call | solution.py:490
  56.1 0.0 all-to-all-done.arrived
  56.1 7.0 %land.1 = (f32[512,512]{1,0:T(8,128)}, f32[4,64,128]{2,1,0:T(8,128)}) custom-call(s32[32]{0:T(128)S(1)} %copy-done.9, f32[512,512]{1,0:T(8,128)S(1)} %get-tuple-element.33.second, f32[4,128]{1,0:T(4,128)S(1)} %get-tuple-element.34.inlet_now, s32[1,128]{1,0:T(1,128)S(1)} %pad.4.inlet, s32[64,128]{1,0:T(8,128)S(1)} %bitcast.28, ...), custom_call_target="tpu_custom_call" | custom-call | flops 8589934592 | bytes 2097152 | tf_op jit(solution)/shard_map/land/pallas_call | solution.py:243
  (20 shorter events, 0.0 us)
Async XLA Ops:
  0.6 10.3 %copy-start = (f32[4,8,16,512]{3,2,1,0:T(8,128)S(1)}, f32[4,8,16,512]{3,2,1,0:T(8,128)}, u32[]{:S(2)}) copy-start(f32[4,8,16,512]{3,2,1,0:T(8,128)} %param.11) | copy-start | bytes 3145732
  0.6 10.3 %copy-start.6 = (s32[1,1,64]{2,1,0:T(1,128)S(1)}, s32[1,1,64]{2,1,0:T(1,128)}, u32[]{:S(2)}) copy-start(s32[1,1,64]{2,1,0:T(1,128)} %param.20) | copy-start | bytes 772
  0.6 10.3 %copy-start.7 = (s32[1,1,64,128]{3,2,1,0:T(8,128)S(1)}, s32[1,1,64,128]{3,2,1,0:T(8,128)}, u32[]{:S(2)}) copy-start(s32[1,1,64,128]{3,2,1,0:T(8,128)} %param.19) | copy-start | bytes 98308
  0.7 15.3 %collective-permute-start.3 = (f32[4,32]{1,0:T(4,128)}, f32[4,32]{1,0:T(4,128)S(1)}, u32[]{:S(2)}, u32[]{:S(2)}) collective-permute-start(f32[4,32]{1,0:T(4,128)} %ports.3), channel_id=1, source_target_pairs={{0,128},{64,192},{128,0},{192,64},{1,129},{65,193},{129,1},{193,65... | collective-permute-start | bytes 1544 | tf_op jit(solution)/shard_map/ppermute | solution.py:540
  4.5 16.7 %collective-permute-start = (f32[72,512]{1,0:T(8,128)}, f32[72,512]{1,0:T(8,128)S(1)}, u32[]{:S(2)}, u32[]{:S(2)}) collective-permute-start(f32[72,512]{1,0:T(8,128)} %get-tuple-element.20), channel_id=1, source_target_pairs={{0,1},{1,2},{2,3},{3,4},{4,5},{5,6},{6,7},{7,8},{8,9},{9,10},{10,1... | collective-permute-start | bytes 442376 | tf_op jit(solution)/shard_map/ppermute | solution.py:537
  9.1 10.0 %collective-permute-start.1 = (f32[152,512]{1,0:T(8,128)}, f32[152,512]{1,0:T(8,128)S(1)}, u32[]{:S(2)}, u32[]{:S(2)}) collective-permute-start(f32[152,512]{1,0:T(8,128)} %get-tuple-element.21), channel_id=1, source_target_pairs={{0,64},{64,128},{128,192},{192,0},{1,65},{65,129},{129,193},{193,1... | collective-permute-start | bytes 933896 | tf_op jit(solution)/shard_map/ppermute | solution.py:538
  9.2 9.9 %collective-permute-start.2 = (f32[152,512]{1,0:T(8,128)}, f32[152,512]{1,0:T(8,128)S(1)}, u32[]{:S(2)}, u32[]{:S(2)}) collective-permute-start(f32[152,512]{1,0:T(8,128)} %get-tuple-element.22), channel_id=1, source_target_pairs={{64,0},{128,64},{192,128},{0,192},{65,1},{129,65},{193,129},{1,193... | collective-permute-start | bytes 933896 | tf_op jit(solution)/shard_map/ppermute | solution.py:539
  11.0 8.2 %copy-start.2 = (f32[4,1,1,64,128]{4,3,2,1,0:T(8,128)S(1)}, f32[4,1,1,64,128]{4,3,2,1,0:T(8,128)}, u32[]{:S(2)}) copy-start(f32[4,1,1,64,128]{4,3,2,1,0:T(8,128)} %param.16) | copy-start | bytes 393220
  11.0 8.2 %copy-start.3 = (f32[1,1,64,128]{3,2,1,0:T(8,128)S(1)}, f32[1,1,64,128]{3,2,1,0:T(8,128)}, u32[]{:S(2)}) copy-start(f32[1,1,64,128]{3,2,1,0:T(8,128)} %param.17) | copy-start | bytes 98308
  11.0 8.2 %copy-start.4 = (f32[1,1,64,128]{3,2,1,0:T(8,128)S(1)}, f32[1,1,64,128]{3,2,1,0:T(8,128)}, u32[]{:S(2)}) copy-start(f32[1,1,64,128]{3,2,1,0:T(8,128)} %param.18) | copy-start | bytes 98308
  11.0 8.2 %copy-start.5 = (f32[4,32]{1,0:T(4,128)S(1)}, f32[4,32]{1,0:T(4,128)}, u32[]{:S(2)}) copy-start(f32[4,32]{1,0:T(4,128)} %ports.3) | copy-start | bytes 1540
  15.9 20.1 %copy-start.1 = (f32[8,16,512]{2,1,0:T(8,128)S(1)}, f32[8,16,512]{2,1,0:T(8,128)}, u32[]{:S(2)}) copy-start(f32[8,16,512]{2,1,0:T(8,128)} %param.12) | copy-start | bytes 786436
  21.2 23.9 %copy-start.10 = (s32[32]{0:T(128)S(1)}, s32[32]{0:T(128)}, u32[]{:S(2)}) copy-start(s32[32]{0:T(128)} %param.15) | copy-start | bytes 388
  21.2 34.9 %all-to-all-start = ((f32[192,4,128]{2,1,0:T(4,128)}), f32[192,4,128]{2,1,0:T(4,128)S(1)}, u32[]{:S(2)}, u32[]{:S(2)}) async-start(f32[192,4,128]{2,1,0:T(4,128)} %slip.1), calls=%async_computation | async-start | bytes 786432 | tf_op jit(solution)/shard_map/all_to_all | solution.py:556
  36.2 17.1 %collective-permute-start.5 = (f32[80,512]{1,0:T(8,128)S(1)}, f32[80,512]{1,0:T(8,128)S(1)}, u32[]{:S(2)}, u32[]{:S(2)}) collective-permute-start(f32[80,512]{1,0:T(8,128)S(1)} %get-tuple-element.32), channel_id=1, source_target_pairs={{1,0},{2,1},{3,2},{4,3},{5,4},{6,5},{7,6},{8,7},{9,8},{10,9},{11,1... | collective-permute-start | bytes 491528 | tf_op jit(solution)/shard_map/ppermute | solution.py:558
  43.1 10.1 %collective-permute-start.4 = (f32[8,512]{1,0:T(8,128)S(1)}, f32[8,512]{1,0:T(8,128)S(1)}, u32[]{:S(2)}, u32[]{:S(2)}) collective-permute-start(f32[8,512]{1,0:T(8,128)S(1)} %get-tuple-element.31), channel_id=1, source_target_pairs={{0,1},{1,2},{2,3},{3,4},{4,5},{5,6},{6,7},{7,8},{8,9},{9,10},{10,1... | collective-permute-start | bytes 49160 | tf_op jit(solution)/shard_map/ppermute | solution.py:559
  53.3 2.8 %copy-start.8 = (s32[1,1,64,128]{3,2,1,0:T(8,128)S(1)}, s32[1,1,64,128]{3,2,1,0:T(8,128)}, u32[]{:S(2)}) copy-start(s32[1,1,64,128]{3,2,1,0:T(8,128)} %param.21) | copy-start | bytes 98308
  53.3 2.8 %copy-start.9 = (s32[32]{0:T(128)S(1)}, s32[32]{0:T(128)}, u32[]{:S(2)}) copy-start(s32[32]{0:T(128)} %match.1) | copy-start | bytes 388

commit v10 on v8

--- a/solution.py
+++ b/solution.py
@@ -84,16 +84,18 @@
 chunks = 4
 
 
-def slip_kernel(counts, sampled, state, rate, mass, ports, above, across, below, far, out, whole, out_sems):
+def slip_kernel(counts, sampled, state, rate, mass, ports, above, across, below, wrapped, far, out, whole, out_sems):
     comps, partners, cap = state.shape
     per = ports.shape[1]
     cap_shift = cap.bit_length() - 1
     last = above.shape[0] - 8
     lane = lax.broadcasted_iota(jnp.int32, (1, cap), 1)
     whole[:, 0:per] = ports[...]
-    whole[:, per : 2 * per] = above[last : last + comps, 0:per]
+    section = lax.axis_index("sec")
+    top = lax.axis_size("sec") - 1
+    whole[:, per : 2 * per] = jnp.where(section < top, above[last : last + comps, 0:per], wrapped[...])
     whole[:, 2 * per : 3 * per] = across[...]
-    whole[:, 3 * per :] = below[last : last + comps, 0:per]
+    whole[:, 3 * per :] = jnp.where(section > 0, below[last : last + comps, 0:per], wrapped[...])
 
     def finish(p, base):
         n = counts[p]
@@ -122,12 +124,12 @@
         copy.wait()
 
 
-def slip(counts, sampled, state, rate, mass, ports, above, across, below):
+def slip(counts, sampled, state, rate, mass, ports, above, across, below, wrapped):
     comps, partners, cap = state.shape
     return pl.pallas_call(
         slip_kernel,
         out_shape=jax.ShapeDtypeStruct((partners * 3, comps, cap), jnp.float32),
-        in_specs=[SM] + [VM] * 8,
+        in_specs=[SM] + [VM] * 9,
         out_specs=HB,
         scratch_shapes=[
             pltpu.VMEM((partners * 3, comps, cap), jnp.float32),
@@ -137,7 +139,7 @@
         compiler_params=pltpu.CompilerParams(vmem_limit_bytes=24 * 1024 * 1024),
         cost_estimate=pl.CostEstimate(flops=2 * 10**6, bytes_accessed=2**20, transcendentals=0),
         name="slip",
-    )(counts, sampled, state, rate, mass, ports, above, across, below)
+    )(counts, sampled, state, rate, mass, ports, above, across, below, wrapped)
 
 
 def land_kernel(GP, match, second, inlet_now, inlet, arrival, arrived, flow_far, state_far, flow_out, state_out, last_ref, last, packed, sem, out_sems):
@@ -288,56 +290,44 @@
     return centers, out
 
 
-def cap_kernel(comps, depth_z, width, flow, viscosity, ports, low_out, high_out, sems):
-    copies = []
-
-    def copy(source, target):
-        copies.append(pltpu.make_async_copy(source, target, sems.at[len(copies)]))
-        copies[-1].start()
-
+def cap_kernel(comps, depth_z, width, flow, viscosity, ports, low_cap, high_cap):
     two = 2 * width
-    last = (depth_z - 1) * width
+    last = depth_z * width
     for c in range(comps):
-        base = c * depth_z * width
-        copy(flow.at[base : base + two, :], low_out.at[c * two : (c + 1) * two, :])
-        copy(flow.at[base + last - width : base + last + width, :], high_out.at[c * two : (c + 1) * two, :])
+        low_cap[c * two : (c + 1) * two, :] = flow[c * last : c * last + two, :]
+        high_cap[c * two : (c + 1) * two, :] = flow[(c + 1) * last - two : (c + 1) * last, :]
     base = comps * two
-    copy(viscosity.at[0:width, :], low_out.at[base : base + width, :])
-    copy(viscosity.at[last : last + width, :], high_out.at[base : base + width, :])
-    for out in (low_out, high_out):
+    low_cap[base : base + width, :] = viscosity[0:width, :]
+    high_cap[base : base + width, :] = viscosity[last - width : last, :]
+    for out in (low_cap, high_cap):
         out[base + width :, :] = jnp.zeros((8, out.shape[1]), jnp.float32)
         out[base + width : base + width + comps, 0 : ports.shape[1]] = ports[...]
-    for started in copies:
-        started.wait()
 
 
 def caps(comps, depth_z, width, flow, viscosity, ports):
-    shape = jax.ShapeDtypeStruct((2 * comps * width + width + 8, flow.shape[1]), jnp.float32)
+    depth = flow.shape[1]
+    cap = jax.ShapeDtypeStruct((2 * comps * width + width + 8, depth), jnp.float32)
     return pl.pallas_call(
         functools.partial(cap_kernel, comps, depth_z, width),
-        out_shape=(shape, shape),
-        in_specs=[HB, HB, VM],
+        out_shape=(cap, cap),
+        in_specs=[VM] * 3,
         out_specs=(VM, VM),
-        scratch_shapes=[pltpu.SemaphoreType.DMA((2 * comps + 2,))],
         compiler_params=pltpu.CompilerParams(vmem_limit_bytes=60 * 1024 * 1024),
         name="caps",
     )(flow, viscosity, ports)
 
 
-def edge_kernel(comps, depth_z, width, flow, viscosity, below, above, low_out, high_out, bottom, top):
-    section = lax.axis_index("sec")
-    bottom[...] = jnp.where(section > 0, below[0 : bottom.shape[0], :], 0.0)
-    top[...] = jnp.where(section < lax.axis_size("sec") - 1, above[0 : top.shape[0], :], 0.0)
+def edge_kernel(comps, depth_z, width, flow, viscosity, below, above, low_out, high_out):
     two = 2 * width
     for k in range(comps * depth_z):
         low_out[2 * k : 2 * k + 2, :] = flow[k * width : k * width + 2, :]
         high_out[2 * k : 2 * k + 2, :] = flow[(k + 1) * width - 2 : (k + 1) * width, :]
     base = 2 * comps * depth_z
     for c in range(comps):
-        low_out[base + 2 * c : base + 2 * c + 1, :] = bottom[c * two + width : c * two + width + 1, :]
-        low_out[base + 2 * c + 1 : base + 2 * c + 2, :] = top[c * two : c * two + 1, :]
-        high_out[base + 2 * c : base + 2 * c + 1, :] = bottom[(c + 1) * two - 1 : (c + 1) * two, :]
-        high_out[base + 2 * c + 1 : base + 2 * c + 2, :] = top[c * two + width - 1 : c * two + width, :]
+        low_out[base + 2 * c : base + 2 * c + 1, :] = below[c * two + width : c * two + width + 1, :]
+        low_out[base + 2 * c + 1 : base + 2 * c + 2, :] = above[c * two : c * two + 1, :]
+        high_out[base + 2 * c : base + 2 * c + 1, :] = below[(c + 1) * two - 1 : (c + 1) * two, :]
+        high_out[base + 2 * c + 1 : base + 2 * c + 2, :] = above[c * two + width - 1 : c * two + width, :]
     base += 2 * comps
     for z in range(depth_z):
         low_out[base + z : base + z + 1, :] = viscosity[z * width : z * width + 1, :]
@@ -347,12 +337,11 @@
 def edges(comps, depth_z, width, flow, viscosity, below, above):
     depth = flow.shape[1]
     shape = jax.ShapeDtypeStruct((2 * comps * (depth_z + 1) + depth_z, depth), jnp.float32)
-    halo = jax.ShapeDtypeStruct(((2 * comps + 1) * width, depth), jnp.float32)
     return pl.pallas_call(
         functools.partial(edge_kernel, comps, depth_z, width),
-        out_shape=(shape, shape, halo, halo),
+        out_shape=(shape, shape),
         in_specs=[VM] * 4,
-        out_specs=(VM,) * 4,
+        out_specs=(VM, VM),
         compiler_params=pltpu.CompilerParams(vmem_limit_bytes=24 * 1024 * 1024),
         name="edges",
     )(flow, viscosity, below, above)
@@ -370,9 +359,9 @@
 
     for z in range(-1, depth_z + 1):
         if z < 0:
-            visc = below[comps * two :, :]
+            visc = below[comps * two : comps * two + width, :]
         elif z == depth_z:
-            visc = above[comps * two :, :]
+            visc = above[comps * two : comps * two + width, :]
         else:
             visc = viscosity[z * width : (z + 1) * width, :]
         centers, change = tendency(own(z), own(z + 1), own(z - 1), visc, width)
@@ -532,14 +521,15 @@
     forth = [(i, i + 1) for i in range(count - 1)]
     back = [(i + 1, i) for i in range(count - 1)]
     levels = lax.axis_size("sec")
-    up = [(i, (i + 1) % levels) for i in range(levels)]
-    down = [((i + 1) % levels, i) for i in range(levels)]
+    up = [(i, i + 1) for i in range(levels - 1)]
+    down = [(i + 1, i) for i in range(levels - 1)]
     over = [(i, (i + levels // 2) % levels) for i in range(levels)]
 
     low_cap, high_cap = caps(*sizes, flow, visc, port_plane)
     below = lax.ppermute(high_cap, "sec", up)
     above = lax.ppermute(low_cap, "sec", down)
     across = lax.ppermute(port_plane, "sec", over)
+    wrapped = lax.ppermute(port_plane, "sec", [(0, levels - 1), (levels - 1, 0)])
     counts = live_counts.reshape(-1)
     counts, low_cap, high_cap = lax.optimization_barrier((counts, low_cap, high_cap))
     sampled = sample(comps, counts, flow, anchor_cell.reshape(partners, cap))
@@ -553,15 +543,16 @@
         above,
         across,
         below,
+        wrapped,
     )
     below, above, outgoing = lax.optimization_barrier((below, above, outgoing))
     arrived = lax.all_to_all(outgoing, "tile", split_axis=0, concat_axis=0, tiled=True)
-    low_edge, high_edge, bottom, top = edges(*sizes, flow, visc, below, above)
+    low_edge, high_edge = edges(*sizes, flow, visc, below, above)
     left = lax.ppermute(high_edge, "tile", forth)
     right = lax.ppermute(low_edge, "tile", back)
     inlet = jnp.pad(inlet_cell.reshape(1, -1), ((0, 0), (0, cap - inlet_cell.shape[0])))
-    first, middle = inner(*sizes, flow, visc, bottom, top)
-    second, inlet_now = outer(*sizes, flow, visc, bottom, top, first, middle, left, right, inlet)
+    first, middle = inner(*sizes, flow, visc, below, above)
+    second, inlet_now = outer(*sizes, flow, visc, below, above, first, middle, left, right, inlet)
     flow_next, arrived_state = land(
         port_match, second, inlet_now, inlet, arrival_cell.reshape(partners, cap), arrived
     )

time: 58.9 us -> 59.8 us (1.015)
  the two profiles are of different devices: /device:TPU:88 before, /device:TPU:6 now
where the time goes in v10:
time: 59.8 us; the launch traced here: 59.6 us
  starting transfers between devices  29.9 us (50%)
  Pallas kernels  22.8 us (38%)
  waiting for transfers between devices  5.88 us (10%)
  between operations  0.92 us (2%)
    all_to_all x1, starting transfers between devices, on_device(): lax.all_to_all(outgoing, 'tile', split_axis=0, concat_axis=0, tiled=True)  14.6 us
    pallas_call x1, Pallas kernels, land(): pl.pallas_call(functools.partial(land_kernel, GP), out_shape=(jax.ShapeDt...  7.8 us
    pallas_call x1, Pallas kernels, sample(): pl.pallas_call(functools.partial(sample_kernel, GP), out_shape=jax.ShapeD...  4.9 us
    ppermute x1, waiting for transfers between devices, on_device(): right = lax.ppermute(low_edge, 'tile', back)  4.6 us
    ppermute x1, starting transfers between devices, on_device(): below = lax.ppermute(high_cap, 'sec', up)  4.46 us
    ppermute x1, starting transfers between devices, on_device(): right = lax.ppermute(low_edge, 'tile', back)  3.98 us
    ppermute x1, starting transfers between devices, on_device(): left = lax.ppermute(high_edge, 'tile', forth)  3.37 us
    pallas_call x1, Pallas kernels, inner(): pl.pallas_call(functools.partial(inner_kernel, comps, depth_z, width), ou...  3 us
  transfers between devices with their start and end apart: 7, of which 2 were waited for; matrix products, arithmetic and copies ran while one was open for 0% of the time, Pallas kernels for 22%

profile of v10, /device:TPU:6, one launch (start us, length us, event | category | flops | bytes accessed | tf_op | source)
XLA Modules:
  0.0 59.6 jit_solution(2691699387246084964)
XLA Ops:
  0.7 0.9 %collective-permute-start.2 = (f32[4,32]{1,0:T(4,128)}, f32[4,32]{1,0:T(4,128)S(1)}, u32[]{:S(2)}, u32[]{:S(2)}) collective-permute-start(f32[4,32]{1,0:T(4,128)} %ports.3), channel_id=1, source_target_pairs={{0,128},{64,192},{128,0},{192,64},{1,129},{65,193},{129,1},{193,65... | collective-permute-start | bytes 1544 | tf_op jit(solution)/shard_map/ppermute | solution.py:531
  1.6 0.6 %collective-permute-start.3 = (f32[4,32]{1,0:T(4,128)}, f32[4,32]{1,0:T(4,128)S(1)}, u32[]{:S(2)}, u32[]{:S(2)}) collective-permute-start(f32[4,32]{1,0:T(4,128)} %ports.3), channel_id=1, source_target_pairs={{0,192},{192,0},{1,193},{193,1},{2,194},{194,2},{3,195},{195,3},{4... | collective-permute-start | bytes 1544 | tf_op jit(solution)/shard_map/ppermute | solution.py:532
  2.2 2.2 %caps.1 = (f32[152,512]{1,0:T(8,128)}, f32[152,512]{1,0:T(8,128)}) custom-call(f32[512,512]{1,0:T(8,128)} %bitcast.13, f32[128,512]{1,0:T(8,128)} %bitcast.18, f32[4,32]{1,0:T(4,128)} %ports.3), custom_call_target="tpu_custom_call" | custom-call | tf_op jit(solution)/shard_map/caps/pallas_call | solution.py:310
  4.4 4.5 %collective-permute-start = (f32[152,512]{1,0:T(8,128)}, f32[152,512]{1,0:T(8,128)S(1)}, u32[]{:S(2)}, u32[]{:S(2)}) collective-permute-start(f32[152,512]{1,0:T(8,128)} %get-tuple-element.16), channel_id=1, source_target_pairs={{0,64},{64,128},{128,192},{1,65},{65,129},{129,193},{2,66},{66,130... | collective-permute-start | bytes 933896 | tf_op jit(solution)/shard_map/ppermute | solution.py:529
  8.9 1.9 %collective-permute-start.1 = (f32[152,512]{1,0:T(8,128)}, f32[152,512]{1,0:T(8,128)S(1)}, u32[]{:S(2)}, u32[]{:S(2)}) collective-permute-start(f32[152,512]{1,0:T(8,128)} %get-tuple-element.17), channel_id=1, source_target_pairs={{64,0},{128,64},{192,128},{65,1},{129,65},{193,129},{66,2},{130,66... | collective-permute-start | bytes 933896 | tf_op jit(solution)/shard_map/ppermute | solution.py:530
  10.8 0.0 copy-start.2
  10.8 0.0 copy-start.3
  10.9 0.0 copy-start.4
  10.9 0.0 copy-start.5
  10.9 4.9 %sample.1.sampled = f32[72,4,128]{2,1,0:T(4,128)S(1)} custom-call(s32[64]{0:T(128)S(1)} %bitcast.25, f32[512,512]{1,0:T(8,128)S(1)} %bitcast.14, s32[64,128]{1,0:T(8,128)S(1)} %bitcast.27), custom_call_target="tpu_custom_call" | custom-call | flops 8589934592 | bytes 2097152 | tf_op jit(solution)/shard_map/sample/pallas_call | solution.py:69
  15.8 0.0 copy-start.1
  15.8 0.0 collective-permute-done.below
  15.9 2.0 %slip.1 = f32[192,4,128]{2,1,0:T(4,128)} custom-call(s32[64]{0:T(128)S(1)} %bitcast.26, f32[72,4,128]{2,1,0:T(4,128)S(1)} %sample.1.sampled, f32[4,64,128]{2,1,0:T(8,128)S(1)} %bitcast.22, f32[64,128]{1,0:T(8,128)S(1)} %bitcast.23, f32[64,128]{1,0:T(8,128)S(1)} %bitcast.24, f32[4,32]{1,0:T(4,128)S(1)} %copy-done.5, ...), custom_call_target="tpu_custom_call" | custom-call | flops 2000000 | bytes 1048576 | tf_op jit(solution)/shard_map/slip/pallas_call | solution.py:129
  17.9 0.0 copy-start.10
  17.9 14.6 %all-to-all-start = ((f32[192,4,128]{2,1,0:T(4,128)}), f32[192,4,128]{2,1,0:T(4,128)S(1)}, u32[]{:S(2)}, u32[]{:S(2)}) async-start(f32[192,4,128]{2,1,0:T(4,128)} %slip.1), calls=%async_computation | async-start | bytes 786432 | tf_op jit(solution)/shard_map/all_to_all | solution.py:549
  32.6 0.1 edges.1
  32.7 3.4 %collective-permute-start.4 = (f32[80,512]{1,0:T(8,128)S(1)}, f32[80,512]{1,0:T(8,128)S(1)}, u32[]{:S(2)}, u32[]{:S(2)}) collective-permute-start(f32[80,512]{1,0:T(8,128)S(1)} %get-tuple-element.23), channel_id=1, source_target_pairs={{0,1},{1,2},{2,3},{3,4},{4,5},{5,6},{6,7},{7,8},{8,9},{9,10},{10,1... | collective-permute-start | bytes 491528 | tf_op jit(solution)/shard_map/ppermute | solution.py:551
  36.1 4.0 %collective-permute-start.5 = (f32[80,512]{1,0:T(8,128)S(1)}, f32[80,512]{1,0:T(8,128)S(1)}, u32[]{:S(2)}, u32[]{:S(2)}) collective-permute-start(f32[80,512]{1,0:T(8,128)S(1)} %get-tuple-element.24), channel_id=1, source_target_pairs={{1,0},{2,1},{3,2},{4,3},{5,4},{6,5},{7,6},{8,7},{9,8},{10,9},{11,1... | collective-permute-start | bytes 491528 | tf_op jit(solution)/shard_map/ppermute | solution.py:552
  40.1 3.0 %inner.1 = (f32[4,10,16,512]{3,2,1,0:T(8,128)S(1)}, f32[512,512]{1,0:T(8,128)S(1)}) custom-call(f32[512,512]{1,0:T(8,128)S(1)} %bitcast.16, f32[128,512]{1,0:T(8,128)S(1)} %bitcast.20, f32[152,512]{1,0:T(8,128)S(1)} %collective-permute-done.below, f32[152,512]{1,0:T(8,128)S(1)} %collective-permute-done.1.above), custom_call_target="tpu_custom_call" | custom-call | flops 10000000 | bytes 4194304 | tf_op jit(solution)/shard_map/inner/pallas_call | solution.py:385
  43.1 1.3 %collective-permute-done.4.left = f32[80,512]{1,0:T(8,128)S(1)} collective-permute-done((f32[80,512]{1,0:T(8,128)S(1)}, f32[80,512]{1,0:T(8,128)S(1)}, u32[]{:S(2)}, u32[]{:S(2)}) %collective-permute-start.4) | collective-permute-done | bytes 163872 | tf_op jit(solution)/shard_map/ppermute | solution.py:551
  44.4 4.6 %collective-permute-done.5.right = f32[80,512]{1,0:T(8,128)S(1)} collective-permute-done((f32[80,512]{1,0:T(8,128)S(1)}, f32[80,512]{1,0:T(8,128)S(1)}, u32[]{:S(2)}, u32[]{:S(2)}) %collective-permute-start.5) | collective-permute-done | bytes 163872 | tf_op jit(solution)/shard_map/ppermute | solution.py:552
  49.0 2.8 %outer.1 = (f32[512,512]{1,0:T(8,128)S(1)}, f32[4,128]{1,0:T(4,128)S(1)}) custom-call(f32[512,512]{1,0:T(8,128)S(1)} %bitcast.17, f32[128,512]{1,0:T(8,128)S(1)} %bitcast.21, f32[152,512]{1,0:T(8,128)S(1)} %collective-permute-done.below, f32[152,512]{1,0:T(8,128)S(1)} %collective-permute-done.1.above, f32[4,10,16,512]{3,2,1,0:T(8,128)S(1)} %get-tuple-element.21.first, ...), custom_call_target="tpu_custom_call" | custom-call | flops 10000000 | bytes 4194304 | tf_op jit(solution)/shard_map/outer/pallas_call | solution.py:482
  51.8 0.0 all-to-all-done.arrived
  51.8 7.8 %land.1 = (f32[512,512]{1,0:T(8,128)}, f32[4,64,128]{2,1,0:T(8,128)}) custom-call(s32[32]{0:T(128)S(1)} %copy-done.9, f32[512,512]{1,0:T(8,128)S(1)} %get-tuple-element.25.second, f32[4,128]{1,0:T(4,128)S(1)} %get-tuple-element.26.inlet_now, s32[1,128]{1,0:T(1,128)S(1)} %pad.4.inlet, s32[64,128]{1,0:T(8,128)S(1)} %bitcast.28, ...), custom_call_target="tpu_custom_call" | custom-call | flops 8589934592 | bytes 2097152 | tf_op jit(solution)/shard_map/land/pallas_call | solution.py:245
  (20 shorter events, 0.0 us)
Async XLA Ops:
  0.6 10.2 %copy-start = (f32[4,8,16,512]{3,2,1,0:T(8,128)S(1)}, f32[4,8,16,512]{3,2,1,0:T(8,128)}, u32[]{:S(2)}) copy-start(f32[4,8,16,512]{3,2,1,0:T(8,128)} %param.11) | copy-start | bytes 3145732
  0.6 10.2 %copy-start.6 = (s32[1,1,64]{2,1,0:T(1,128)S(1)}, s32[1,1,64]{2,1,0:T(1,128)}, u32[]{:S(2)}) copy-start(s32[1,1,64]{2,1,0:T(1,128)} %param.20) | copy-start | bytes 772
  0.6 10.2 %copy-start.7 = (s32[1,1,64,128]{3,2,1,0:T(8,128)S(1)}, s32[1,1,64,128]{3,2,1,0:T(8,128)}, u32[]{:S(2)}) copy-start(s32[1,1,64,128]{3,2,1,0:T(8,128)} %param.19) | copy-start | bytes 98308
  0.7 15.1 %collective-permute-start.2 = (f32[4,32]{1,0:T(4,128)}, f32[4,32]{1,0:T(4,128)S(1)}, u32[]{:S(2)}, u32[]{:S(2)}) collective-permute-start(f32[4,32]{1,0:T(4,128)} %ports.3), channel_id=1, source_target_pairs={{0,128},{64,192},{128,0},{192,64},{1,129},{65,193},{129,1},{193,65... | collective-permute-start | bytes 1544 | tf_op jit(solution)/shard_map/ppermute | solution.py:531
  1.6 14.2 %collective-permute-start.3 = (f32[4,32]{1,0:T(4,128)}, f32[4,32]{1,0:T(4,128)S(1)}, u32[]{:S(2)}, u32[]{:S(2)}) collective-permute-start(f32[4,32]{1,0:T(4,128)} %ports.3), channel_id=1, source_target_pairs={{0,192},{192,0},{1,193},{193,1},{2,194},{194,2},{3,195},{195,3},{4... | collective-permute-start | bytes 1544 | tf_op jit(solution)/shard_map/ppermute | solution.py:532
  4.4 11.4 %collective-permute-start = (f32[152,512]{1,0:T(8,128)}, f32[152,512]{1,0:T(8,128)S(1)}, u32[]{:S(2)}, u32[]{:S(2)}) collective-permute-start(f32[152,512]{1,0:T(8,128)} %get-tuple-element.16), channel_id=1, source_target_pairs={{0,64},{64,128},{128,192},{1,65},{65,129},{129,193},{2,66},{66,130... | collective-permute-start | bytes 933896 | tf_op jit(solution)/shard_map/ppermute | solution.py:529
  8.9 7.0 %collective-permute-start.1 = (f32[152,512]{1,0:T(8,128)}, f32[152,512]{1,0:T(8,128)S(1)}, u32[]{:S(2)}, u32[]{:S(2)}) collective-permute-start(f32[152,512]{1,0:T(8,128)} %get-tuple-element.17), channel_id=1, source_target_pairs={{64,0},{128,64},{192,128},{65,1},{129,65},{193,129},{66,2},{130,66... | collective-permute-start | bytes 933896 | tf_op jit(solution)/shard_map/ppermute | solution.py:530
  10.8 5.0 %copy-start.2 = (f32[4,1,1,64,128]{4,3,2,1,0:T(8,128)S(1)}, f32[4,1,1,64,128]{4,3,2,1,0:T(8,128)}, u32[]{:S(2)}) copy-start(f32[4,1,1,64,128]{4,3,2,1,0:T(8,128)} %param.16) | copy-start | bytes 393220
  10.8 5.0 %copy-start.3 = (f32[1,1,64,128]{3,2,1,0:T(8,128)S(1)}, f32[1,1,64,128]{3,2,1,0:T(8,128)}, u32[]{:S(2)}) copy-start(f32[1,1,64,128]{3,2,1,0:T(8,128)} %param.17) | copy-start | bytes 98308
  10.9 5.0 %copy-start.4 = (f32[1,1,64,128]{3,2,1,0:T(8,128)S(1)}, f32[1,1,64,128]{3,2,1,0:T(8,128)}, u32[]{:S(2)}) copy-start(f32[1,1,64,128]{3,2,1,0:T(8,128)} %param.18) | copy-start | bytes 98308
  10.9 5.0 %copy-start.5 = (f32[4,32]{1,0:T(4,128)S(1)}, f32[4,32]{1,0:T(4,128)}, u32[]{:S(2)}) copy-start(f32[4,32]{1,0:T(4,128)} %ports.3) | copy-start | bytes 1540
  15.8 16.8 %copy-start.1 = (f32[8,16,512]{2,1,0:T(8,128)S(1)}, f32[8,16,512]{2,1,0:T(8,128)}, u32[]{:S(2)}) copy-start(f32[8,16,512]{2,1,0:T(8,128)} %param.12) | copy-start | bytes 786436
  17.9 22.2 %copy-start.10 = (s32[32]{0:T(128)S(1)}, s32[32]{0:T(128)}, u32[]{:S(2)}) copy-start(s32[32]{0:T(128)} %param.15) | copy-start | bytes 388
  17.9 33.8 %all-to-all-start = ((f32[192,4,128]{2,1,0:T(4,128)}), f32[192,4,128]{2,1,0:T(4,128)S(1)}, u32[]{:S(2)}, u32[]{:S(2)}) async-start(f32[192,4,128]{2,1,0:T(4,128)} %slip.1), calls=%async_computation | async-start | bytes 786432 | tf_op jit(solution)/shard_map/all_to_all | solution.py:549
  32.7 11.7 %collective-permute-start.4 = (f32[80,512]{1,0:T(8,128)S(1)}, f32[80,512]{1,0:T(8,128)S(1)}, u32[]{:S(2)}, u32[]{:S(2)}) collective-permute-start(f32[80,512]{1,0:T(8,128)S(1)} %get-tuple-element.23), channel_id=1, source_target_pairs={{0,1},{1,2},{2,3},{3,4},{4,5},{5,6},{6,7},{7,8},{8,9},{9,10},{10,1... | collective-permute-start | bytes 491528 | tf_op jit(solution)/shard_map/ppermute | solution.py:551
  36.1 12.9 %collective-permute-start.5 = (f32[80,512]{1,0:T(8,128)S(1)}, f32[80,512]{1,0:T(8,128)S(1)}, u32[]{:S(2)}, u32[]{:S(2)}) collective-permute-start(f32[80,512]{1,0:T(8,128)S(1)} %get-tuple-element.24), channel_id=1, source_target_pairs={{1,0},{2,1},{3,2},{4,3},{5,4},{6,5},{7,6},{8,7},{9,8},{10,9},{11,1... | collective-permute-start | bytes 491528 | tf_op jit(solution)/shard_map/ppermute | solution.py:552
  49.0 2.8 %copy-start.8 = (s32[1,1,64,128]{3,2,1,0:T(8,128)S(1)}, s32[1,1,64,128]{3,2,1,0:T(8,128)}, u32[]{:S(2)}) copy-start(s32[1,1,64,128]{3,2,1,0:T(8,128)} %param.21) | copy-start | bytes 98308
  49.0 2.8 %copy-start.9 = (s32[32]{0:T(128)S(1)}, s32[32]{0:T(128)}, u32[]{:S(2)}) copy-start(s32[32]{0:T(128)} %match.1) | copy-start | bytes 388

commit v11 on v8

--- a/solution.py
+++ b/solution.py
@@ -288,37 +288,28 @@
     return centers, out
 
 
-def cap_kernel(comps, depth_z, width, flow, viscosity, ports, low_out, high_out, sems):
-    copies = []
-
-    def copy(source, target):
-        copies.append(pltpu.make_async_copy(source, target, sems.at[len(copies)]))
-        copies[-1].start()
-
+def cap_kernel(comps, depth_z, width, flow, viscosity, ports, low_cap, high_cap):
     two = 2 * width
-    last = (depth_z - 1) * width
+    last = depth_z * width
     for c in range(comps):
-        base = c * depth_z * width
-        copy(flow.at[base : base + two, :], low_out.at[c * two : (c + 1) * two, :])
-        copy(flow.at[base + last - width : base + last + width, :], high_out.at[c * two : (c + 1) * two, :])
+        low_cap[c * two : (c + 1) * two, :] = flow[c * last : c * last + two, :]
+        high_cap[c * two : (c + 1) * two, :] = flow[(c + 1) * last - two : (c + 1) * last, :]
     base = comps * two
-    copy(viscosity.at[0:width, :], low_out.at[base : base + width, :])
-    copy(viscosity.at[last : last + width, :], high_out.at[base : base + width, :])
-    for out in (low_out, high_out):
+    low_cap[base : base + width, :] = viscosity[0:width, :]
+    high_cap[base : base + width, :] = viscosity[last - width : last, :]
+    for out in (low_cap, high_cap):
         out[base + width :, :] = jnp.zeros((8, out.shape[1]), jnp.float32)
         out[base + width : base + width + comps, 0 : ports.shape[1]] = ports[...]
-    for started in copies:
-        started.wait()
 
 
 def caps(comps, depth_z, width, flow, viscosity, ports):
-    shape = jax.ShapeDtypeStruct((2 * comps * width + width + 8, flow.shape[1]), jnp.float32)
+    depth = flow.shape[1]
+    cap = jax.ShapeDtypeStruct((2 * comps * width + width + 8, depth), jnp.float32)
     return pl.pallas_call(
         functools.partial(cap_kernel, comps, depth_z, width),
-        out_shape=(shape, shape),
-        in_specs=[HB, HB, VM],
+        out_shape=(cap, cap),
+        in_specs=[VM] * 3,
         out_specs=(VM, VM),
-        scratch_shapes=[pltpu.SemaphoreType.DMA((2 * comps + 2,))],
         compiler_params=pltpu.CompilerParams(vmem_limit_bytes=60 * 1024 * 1024),
         name="caps",
     )(flow, viscosity, ports)
@@ -413,6 +404,14 @@
     rows = depth_z * width
     total = comps * rows
     base = 2 * comps * depth_z
+    tile = lax.axis_index("tile")
+
+    def from_left(spot, count):
+        return jnp.where(tile > 0, left[spot : spot + count, :], 0.0)
+
+    def from_right(spot, count):
+        return jnp.where(tile < lax.axis_size("tile") - 1, right[spot : spot + count, :], 0.0)
+
     strip[...] = jnp.zeros_like(strip)
     visc[...] = jnp.zeros_like(visc)
     for c in range(comps):
@@ -427,12 +426,12 @@
             strip[c, z + 2, 4:6, :] = ref[spot + width - 2 : spot + width, :]
             if 0 <= z < depth_z:
                 k = 2 * (c * depth_z + z)
-                strip[c, z + 2, 0:2, :] = left[k : k + 2, :]
-                strip[c, z + 2, 6:8, :] = right[k : k + 2, :]
+                strip[c, z + 2, 0:2, :] = from_left(k, 2)
+                strip[c, z + 2, 6:8, :] = from_right(k, 2)
             elif z in (-1, depth_z):
                 k = base + 2 * c + (z == depth_z)
-                strip[c, z + 2, 1:2, :] = left[k : k + 1, :]
-                strip[c, z + 2, 6:7, :] = right[k : k + 1, :]
+                strip[c, z + 2, 1:2, :] = from_left(k, 1)
+                strip[c, z + 2, 6:7, :] = from_right(k, 1)
     side = base + 2 * comps
     for z in range(-1, depth_z + 1):
         if z < 0:
@@ -441,8 +440,8 @@
             ref, spot = above, comps * two
         else:
             ref, spot = viscosity, z * width
-            visc[z + 1, 1:2, :] = left[side + z : side + z + 1, :]
-            visc[z + 1, 6:7, :] = right[side + z : side + z + 1, :]
+            visc[z + 1, 1:2, :] = from_left(side + z, 1)
+            visc[z + 1, 6:7, :] = from_right(side + z, 1)
         visc[z + 1, 2:4, :] = ref[spot : spot + 2, :]
         visc[z + 1, 4:6, :] = ref[spot + width - 2 : spot + width, :]
 
@@ -529,8 +528,8 @@
     flow = flow_field.reshape(-1, depth)
     visc = viscosity.reshape(-1, depth)
     count = lax.axis_size("tile")
-    forth = [(i, i + 1) for i in range(count - 1)]
-    back = [(i + 1, i) for i in range(count - 1)]
+    forth = [(i, (i + 1) % count) for i in range(count)]
+    back = [((i + 1) % count, i) for i in range(count)]
     levels = lax.axis_size("sec")
     up = [(i, (i + 1) % levels) for i in range(levels)]
     down = [((i + 1) % levels, i) for i in range(levels)]

time: 58.9 us -> 61 us (1.036)
  the two profiles are of different devices: /device:TPU:88 before, /device:TPU:1 now
where the time goes in v11:
time: 61 us; the launch traced here: 60.9 us
  starting transfers between devices  25.9 us (42%)
  Pallas kernels  22.1 us (36%)
  waiting for transfers between devices  11.9 us (20%)
  between operations  0.81 us (1%)
    all_to_all x1, starting transfers between devices, on_device(): lax.all_to_all(outgoing, 'tile', split_axis=0, concat_axis=0, tiled=True)  13.7 us
    ppermute x1, waiting for transfers between devices, on_device(): left = lax.ppermute(high_edge, 'tile', forth)  9.29 us
    pallas_call x1, Pallas kernels, land(): pl.pallas_call(functools.partial(land_kernel, GP), out_shape=(jax.ShapeDt...  7.05 us
    pallas_call x1, Pallas kernels, sample(): pl.pallas_call(functools.partial(sample_kernel, GP), out_shape=jax.ShapeD...  4.9 us
    ppermute x1, starting transfers between devices, on_device(): right = lax.ppermute(low_edge, 'tile', back)  4.67 us
    pallas_call x1, Pallas kernels, inner(): pl.pallas_call(functools.partial(inner_kernel, comps, depth_z, width), ou...  2.99 us
    ppermute x1, starting transfers between devices, on_device(): below = lax.ppermute(high_cap, 'sec', up)  2.83 us
    pallas_call x1, Pallas kernels, outer(): pl.pallas_call(functools.partial(outer_kernel, comps, depth_z, width), ou...  2.82 us
  transfers between devices with their start and end apart: 6, of which 3 were waited for; matrix products, arithmetic and copies ran while one was open for 0% of the time, Pallas kernels for 21%

profile of v11, /device:TPU:1, one launch (start us, length us, event | category | flops | bytes accessed | tf_op | source)
XLA Modules:
  0.0 60.9 jit_solution(10360146662195520706)
XLA Ops:
  0.7 2.1 %collective-permute-start.2 = (f32[4,32]{1,0:T(4,128)}, f32[4,32]{1,0:T(4,128)S(1)}, u32[]{:S(2)}, u32[]{:S(2)}) collective-permute-start(f32[4,32]{1,0:T(4,128)} %ports.3), channel_id=1, source_target_pairs={{0,128},{64,192},{128,0},{192,64},{1,129},{65,193},{129,1},{193,65... | collective-permute-start | bytes 1544 | tf_op jit(solution)/shard_map/ppermute | solution.py:541
  2.8 2.2 %caps.1 = (f32[152,512]{1,0:T(8,128)}, f32[152,512]{1,0:T(8,128)}) custom-call(f32[512,512]{1,0:T(8,128)} %bitcast.13, f32[128,512]{1,0:T(8,128)} %bitcast.18, f32[4,32]{1,0:T(4,128)} %ports.3), custom_call_target="tpu_custom_call" | custom-call | tf_op jit(solution)/shard_map/caps/pallas_call | solution.py:308
  5.0 2.8 %collective-permute-start = (f32[152,512]{1,0:T(8,128)}, f32[152,512]{1,0:T(8,128)S(1)}, u32[]{:S(2)}, u32[]{:S(2)}) collective-permute-start(f32[152,512]{1,0:T(8,128)} %get-tuple-element.18), channel_id=1, source_target_pairs={{0,64},{64,128},{128,192},{192,0},{1,65},{65,129},{129,193},{193,1... | collective-permute-start | bytes 933896 | tf_op jit(solution)/shard_map/ppermute | solution.py:539
  7.8 0.0 collective-permute-start.1
  7.8 0.0 copy-start.2
  7.8 0.0 copy-start.3
  7.8 0.0 copy-start.4
  7.9 0.0 copy-start.5
  7.9 4.9 %sample.1.sampled = f32[72,4,128]{2,1,0:T(4,128)S(1)} custom-call(s32[64]{0:T(128)S(1)} %bitcast.25, f32[512,512]{1,0:T(8,128)S(1)} %bitcast.14, s32[64,128]{1,0:T(8,128)S(1)} %bitcast.27), custom_call_target="tpu_custom_call" | custom-call | flops 8589934592 | bytes 2097152 | tf_op jit(solution)/shard_map/sample/pallas_call | solution.py:69
  12.8 0.0 copy-start.1
  12.8 0.0 collective-permute-done.2.across
  12.8 2.2 %collective-permute-done.below = f32[152,512]{1,0:T(8,128)S(1)} collective-permute-done((f32[152,512]{1,0:T(8,128)}, f32[152,512]{1,0:T(8,128)S(1)}, u32[]{:S(2)}, u32[]{:S(2)}) %collective-permute-start) | collective-permute-done | bytes 311328 | tf_op jit(solution)/shard_map/ppermute | solution.py:539
  15.0 0.4 collective-permute-done.1.above
  15.4 2.0 %slip.1 = f32[192,4,128]{2,1,0:T(4,128)} custom-call(s32[64]{0:T(128)S(1)} %bitcast.26, f32[72,4,128]{2,1,0:T(4,128)S(1)} %sample.1.sampled, f32[4,64,128]{2,1,0:T(8,128)S(1)} %bitcast.22, f32[64,128]{1,0:T(8,128)S(1)} %bitcast.23, f32[64,128]{1,0:T(8,128)S(1)} %bitcast.24, f32[4,32]{1,0:T(4,128)S(1)} %copy-done.5, ...), custom_call_target="tpu_custom_call" | custom-call | flops 2000000 | bytes 1048576 | tf_op jit(solution)/shard_map/slip/pallas_call | solution.py:127
  17.5 0.0 copy-start.10
  17.5 13.7 %all-to-all-start = ((f32[192,4,128]{2,1,0:T(4,128)}), f32[192,4,128]{2,1,0:T(4,128)S(1)}, u32[]{:S(2)}, u32[]{:S(2)}) async-start(f32[192,4,128]{2,1,0:T(4,128)} %slip.1), calls=%async_computation | async-start | bytes 786432 | tf_op jit(solution)/shard_map/all_to_all | solution.py:557
  31.2 0.2 edges.1
  31.4 2.6 %collective-permute-start.3 = (f32[80,512]{1,0:T(8,128)S(1)}, f32[80,512]{1,0:T(8,128)S(1)}, u32[]{:S(2)}, u32[]{:S(2)}) collective-permute-start(f32[80,512]{1,0:T(8,128)S(1)} %get-tuple-element.27), channel_id=1, source_target_pairs={{0,1},{1,2},{2,3},{3,4},{4,5},{5,6},{6,7},{7,8},{8,9},{9,10},{10,1... | collective-permute-start | bytes 491528 | tf_op jit(solution)/shard_map/ppermute | solution.py:559
  34.0 4.7 %collective-permute-start.4 = (f32[80,512]{1,0:T(8,128)S(1)}, f32[80,512]{1,0:T(8,128)S(1)}, u32[]{:S(2)}, u32[]{:S(2)}) collective-permute-start(f32[80,512]{1,0:T(8,128)S(1)} %get-tuple-element.28), channel_id=1, source_target_pairs={{1,0},{2,1},{3,2},{4,3},{5,4},{6,5},{7,6},{8,7},{9,8},{10,9},{11,1... | collective-permute-start | bytes 491528 | tf_op jit(solution)/shard_map/ppermute | solution.py:560
  38.7 3.0 %inner.1 = (f32[4,10,16,512]{3,2,1,0:T(8,128)S(1)}, f32[512,512]{1,0:T(8,128)S(1)}) custom-call(f32[512,512]{1,0:T(8,128)S(1)} %bitcast.16, f32[128,512]{1,0:T(8,128)S(1)} %bitcast.20, f32[144,512]{1,0:T(8,128)S(1)} %get-tuple-element.23.below, f32[144,512]{1,0:T(8,128)S(1)} %get-tuple-element.24.above), custom_call_target="tpu_custom_call" | custom-call | flops 10000000 | bytes 4194304 | tf_op jit(solution)/shard_map/inner/pallas_call | solution.py:387
  41.7 9.3 %collective-permute-done.3.left = f32[80,512]{1,0:T(8,128)S(1)} collective-permute-done((f32[80,512]{1,0:T(8,128)S(1)}, f32[80,512]{1,0:T(8,128)S(1)}, u32[]{:S(2)}, u32[]{:S(2)}) %collective-permute-start.3) | collective-permute-done | bytes 163872 | tf_op jit(solution)/shard_map/ppermute | solution.py:559
  51.0 0.0 collective-permute-done.4.right
  51.0 2.8 %outer.1 = (f32[512,512]{1,0:T(8,128)S(1)}, f32[4,128]{1,0:T(4,128)S(1)}) custom-call(f32[512,512]{1,0:T(8,128)S(1)} %bitcast.17, f32[128,512]{1,0:T(8,128)S(1)} %bitcast.21, f32[144,512]{1,0:T(8,128)S(1)} %get-tuple-element.23.below, f32[144,512]{1,0:T(8,128)S(1)} %get-tuple-element.24.above, f32[4,10,16,512]{3,2,1,0:T(8,128)S(1)} %get-tuple-element.25.first, ...), custom_call_target="tpu_custom_call" | custom-call | flops 10000000 | bytes 4194304 | tf_op jit(solution)/shard_map/outer/pallas_call | solution.py:492
  53.8 7.0 %land.1 = (f32[512,512]{1,0:T(8,128)}, f32[4,64,128]{2,1,0:T(8,128)}) custom-call(s32[32]{0:T(128)S(1)} %copy-done.9, f32[512,512]{1,0:T(8,128)S(1)} %get-tuple-element.29.second, f32[4,128]{1,0:T(4,128)S(1)} %get-tuple-element.30.inlet_now, s32[1,128]{1,0:T(1,128)S(1)} %pad.4.inlet, s32[64,128]{1,0:T(8,128)S(1)} %bitcast.28, ...), custom_call_target="tpu_custom_call" | custom-call | flops 8589934592 | bytes 2097152 | tf_op jit(solution)/shard_map/land/pallas_call | solution.py:243
  (18 shorter events, 0.0 us)
Async XLA Ops:
  0.6 7.2 %copy-start = (f32[4,8,16,512]{3,2,1,0:T(8,128)S(1)}, f32[4,8,16,512]{3,2,1,0:T(8,128)}, u32[]{:S(2)}) copy-start(f32[4,8,16,512]{3,2,1,0:T(8,128)} %param.11) | copy-start | bytes 3145732
  0.6 7.2 %copy-start.6 = (s32[1,1,64]{2,1,0:T(1,128)S(1)}, s32[1,1,64]{2,1,0:T(1,128)}, u32[]{:S(2)}) copy-start(s32[1,1,64]{2,1,0:T(1,128)} %param.20) | copy-start | bytes 772
  0.6 7.2 %copy-start.7 = (s32[1,1,64,128]{3,2,1,0:T(8,128)S(1)}, s32[1,1,64,128]{3,2,1,0:T(8,128)}, u32[]{:S(2)}) copy-start(s32[1,1,64,128]{3,2,1,0:T(8,128)} %param.19) | copy-start | bytes 98308
  0.7 12.1 %collective-permute-start.2 = (f32[4,32]{1,0:T(4,128)}, f32[4,32]{1,0:T(4,128)S(1)}, u32[]{:S(2)}, u32[]{:S(2)}) collective-permute-start(f32[4,32]{1,0:T(4,128)} %ports.3), channel_id=1, source_target_pairs={{0,128},{64,192},{128,0},{192,64},{1,129},{65,193},{129,1},{193,65... | collective-permute-start | bytes 1544 | tf_op jit(solution)/shard_map/ppermute | solution.py:541
  5.0 10.0 %collective-permute-start = (f32[152,512]{1,0:T(8,128)}, f32[152,512]{1,0:T(8,128)S(1)}, u32[]{:S(2)}, u32[]{:S(2)}) collective-permute-start(f32[152,512]{1,0:T(8,128)} %get-tuple-element.18), channel_id=1, source_target_pairs={{0,64},{64,128},{128,192},{192,0},{1,65},{65,129},{129,193},{193,1... | collective-permute-start | bytes 933896 | tf_op jit(solution)/shard_map/ppermute | solution.py:539
  7.8 7.6 %collective-permute-start.1 = (f32[152,512]{1,0:T(8,128)}, f32[152,512]{1,0:T(8,128)S(1)}, u32[]{:S(2)}, u32[]{:S(2)}) collective-permute-start(f32[152,512]{1,0:T(8,128)} %get-tuple-element.19), channel_id=1, source_target_pairs={{64,0},{128,64},{192,128},{0,192},{65,1},{129,65},{193,129},{1,193... | collective-permute-start | bytes 933896 | tf_op jit(solution)/shard_map/ppermute | solution.py:540
  7.8 7.6 %copy-start.2 = (f32[4,1,1,64,128]{4,3,2,1,0:T(8,128)S(1)}, f32[4,1,1,64,128]{4,3,2,1,0:T(8,128)}, u32[]{:S(2)}) copy-start(f32[4,1,1,64,128]{4,3,2,1,0:T(8,128)} %param.16) | copy-start | bytes 393220
  7.8 7.6 %copy-start.3 = (f32[1,1,64,128]{3,2,1,0:T(8,128)S(1)}, f32[1,1,64,128]{3,2,1,0:T(8,128)}, u32[]{:S(2)}) copy-start(f32[1,1,64,128]{3,2,1,0:T(8,128)} %param.17) | copy-start | bytes 98308
  7.8 7.6 %copy-start.4 = (f32[1,1,64,128]{3,2,1,0:T(8,128)S(1)}, f32[1,1,64,128]{3,2,1,0:T(8,128)}, u32[]{:S(2)}) copy-start(f32[1,1,64,128]{3,2,1,0:T(8,128)} %param.18) | copy-start | bytes 98308
  7.9 7.6 %copy-start.5 = (f32[4,32]{1,0:T(4,128)S(1)}, f32[4,32]{1,0:T(4,128)}, u32[]{:S(2)}) copy-start(f32[4,32]{1,0:T(4,128)} %ports.3) | copy-start | bytes 1540
  12.8 18.4 %copy-start.1 = (f32[8,16,512]{2,1,0:T(8,128)S(1)}, f32[8,16,512]{2,1,0:T(8,128)}, u32[]{:S(2)}) copy-start(f32[8,16,512]{2,1,0:T(8,128)} %param.12) | copy-start | bytes 786436
  17.5 21.2 %copy-start.10 = (s32[32]{0:T(128)S(1)}, s32[32]{0:T(128)}, u32[]{:S(2)}) copy-start(s32[32]{0:T(128)} %param.15) | copy-start | bytes 388
  17.5 36.3 %all-to-all-start = ((f32[192,4,128]{2,1,0:T(4,128)}), f32[192,4,128]{2,1,0:T(4,128)S(1)}, u32[]{:S(2)}, u32[]{:S(2)}) async-start(f32[192,4,128]{2,1,0:T(4,128)} %slip.1), calls=%async_computation | async-start | bytes 786432 | tf_op jit(solution)/shard_map/all_to_all | solution.py:557
  31.4 19.6 %collective-permute-start.3 = (f32[80,512]{1,0:T(8,128)S(1)}, f32[80,512]{1,0:T(8,128)S(1)}, u32[]{:S(2)}, u32[]{:S(2)}) collective-permute-start(f32[80,512]{1,0:T(8,128)S(1)} %get-tuple-element.27), channel_id=1, source_target_pairs={{0,1},{1,2},{2,3},{3,4},{4,5},{5,6},{6,7},{7,8},{8,9},{9,10},{10,1... | collective-permute-start | bytes 491528 | tf_op jit(solution)/shard_map/ppermute | solution.py:559
  34.0 17.0 %collective-permute-start.4 = (f32[80,512]{1,0:T(8,128)S(1)}, f32[80,512]{1,0:T(8,128)S(1)}, u32[]{:S(2)}, u32[]{:S(2)}) collective-permute-start(f32[80,512]{1,0:T(8,128)S(1)} %get-tuple-element.28), channel_id=1, source_target_pairs={{1,0},{2,1},{3,2},{4,3},{5,4},{6,5},{7,6},{8,7},{9,8},{10,9},{11,1... | collective-permute-start | bytes 491528 | tf_op jit(solution)/shard_map/ppermute | solution.py:560
  51.0 2.8 %copy-start.8 = (s32[1,1,64,128]{3,2,1,0:T(8,128)S(1)}, s32[1,1,64,128]{3,2,1,0:T(8,128)}, u32[]{:S(2)}) copy-start(s32[1,1,64,128]{3,2,1,0:T(8,128)} %param.21) | copy-start | bytes 98308
  51.0 2.8 %copy-start.9 = (s32[32]{0:T(128)S(1)}, s32[32]{0:T(128)}, u32[]{:S(2)}) copy-start(s32[32]{0:T(128)} %match.1) | copy-start | bytes 388

commit v12 on v11

--- a/solution.py
+++ b/solution.py
@@ -315,7 +315,7 @@
     )(flow, viscosity, ports)
 
 
-def edge_kernel(comps, depth_z, width, flow, viscosity, below, above, low_out, high_out, bottom, top):
+def edge_kernel(comps, depth_z, width, flow, viscosity, below, above, even_out, odd_out, bottom, top, low_out, high_out):
     section = lax.axis_index("sec")
     bottom[...] = jnp.where(section > 0, below[0 : bottom.shape[0], :], 0.0)
     top[...] = jnp.where(section < lax.axis_size("sec") - 1, above[0 : top.shape[0], :], 0.0)
@@ -333,6 +333,9 @@
     for z in range(depth_z):
         low_out[base + z : base + z + 1, :] = viscosity[z * width : z * width + 1, :]
         high_out[base + z : base + z + 1, :] = viscosity[(z + 1) * width - 1 : (z + 1) * width, :]
+    even = lax.axis_index("tile") % 2 == 0
+    even_out[...] = jnp.where(even, high_out[...], low_out[...])
+    odd_out[...] = jnp.where(even, low_out[...], high_out[...])
 
 
 def edges(comps, depth_z, width, flow, viscosity, below, above):
@@ -344,6 +347,7 @@
         out_shape=(shape, shape, halo, halo),
         in_specs=[VM] * 4,
         out_specs=(VM,) * 4,
+        scratch_shapes=[pltpu.VMEM(shape.shape, jnp.float32)] * 2,
         compiler_params=pltpu.CompilerParams(vmem_limit_bytes=24 * 1024 * 1024),
         name="edges",
     )(flow, viscosity, below, above)
@@ -398,7 +402,7 @@
     )(flow, viscosity, below, above)
 
 
-def outer_kernel(comps, depth_z, width, flow, viscosity, below, above, first, middle, left, right, inlet, second_out, inlet_now, strip, visc, started, table):
+def outer_kernel(comps, depth_z, width, flow, viscosity, below, above, first, middle, by_even, by_odd, inlet, second_out, inlet_now, strip, visc, started, table):
     depth = flow.shape[1]
     two = 2 * width
     rows = depth_z * width
@@ -406,11 +410,15 @@
     base = 2 * comps * depth_z
     tile = lax.axis_index("tile")
 
+    even = tile % 2 == 0
+
     def from_left(spot, count):
-        return jnp.where(tile > 0, left[spot : spot + count, :], 0.0)
+        side = pl.ds(spot, count)
+        return jnp.where(tile > 0, jnp.where(even, by_odd[side, :], by_even[side, :]), 0.0)
 
     def from_right(spot, count):
-        return jnp.where(tile < lax.axis_size("tile") - 1, right[spot : spot + count, :], 0.0)
+        side = pl.ds(spot, count)
+        return jnp.where(tile < lax.axis_size("tile") - 1, jnp.where(even, by_even[side, :], by_odd[side, :]), 0.0)
 
     strip[...] = jnp.zeros_like(strip)
     visc[...] = jnp.zeros_like(visc)
@@ -528,8 +536,8 @@
     flow = flow_field.reshape(-1, depth)
     visc = viscosity.reshape(-1, depth)
     count = lax.axis_size("tile")
-    forth = [(i, (i + 1) % count) for i in range(count)]
-    back = [((i + 1) % count, i) for i in range(count)]
+    even_pairs = [(i, i ^ 1) for i in range(count)]
+    odd_pairs = [(0, 0), (count - 1, count - 1)] + [(i, ((i + 1) ^ 1) - 1) for i in range(1, count - 1)]
     levels = lax.axis_size("sec")
     up = [(i, (i + 1) % levels) for i in range(levels)]
     down = [((i + 1) % levels, i) for i in range(levels)]
@@ -555,12 +563,12 @@
     )
     below, above, outgoing = lax.optimization_barrier((below, above, outgoing))
     arrived = lax.all_to_all(outgoing, "tile", split_axis=0, concat_axis=0, tiled=True)
-    low_edge, high_edge, bottom, top = edges(*sizes, flow, visc, below, above)
-    left = lax.ppermute(high_edge, "tile", forth)
-    right = lax.ppermute(low_edge, "tile", back)
+    even_edge, odd_edge, bottom, top = edges(*sizes, flow, visc, below, above)
+    by_even = lax.ppermute(even_edge, "tile", even_pairs)
+    by_odd = lax.ppermute(odd_edge, "tile", odd_pairs)
     inlet = jnp.pad(inlet_cell.reshape(1, -1), ((0, 0), (0, cap - inlet_cell.shape[0])))
     first, middle = inner(*sizes, flow, visc, bottom, top)
-    second, inlet_now = outer(*sizes, flow, visc, bottom, top, first, middle, left, right, inlet)
+    second, inlet_now = outer(*sizes, flow, visc, bottom, top, first, middle, by_even, by_odd, inlet)
     flow_next, arrived_state = land(
         port_match, second, inlet_now, inlet, arrival_cell.reshape(partners, cap), arrived
     )

time: 61 us -> 57.8 us (0.948)
  the two profiles are of different devices: /device:TPU:1 before, /device:TPU:97 now
where the time goes in v12:
time: 57.8 us; the launch traced here: 56.9 us
  Pallas kernels  22.1 us (38%)
  starting transfers between devices  22 us (38%)
  waiting for transfers between devices  11.9 us (21%)
  between operations  0.84 us (1%)
    all_to_all x1, starting transfers between devices, on_device(): lax.all_to_all(outgoing, 'tile', split_axis=0, concat_axis=0, tiled=True)  12.5 us
    ppermute x1, waiting for transfers between devices, on_device(): by_odd = lax.ppermute(odd_edge, 'tile', odd_pairs)  7.83 us
    pallas_call x1, Pallas kernels, land(): pl.pallas_call(functools.partial(land_kernel, GP), out_shape=(jax.ShapeDt...  7.05 us
    pallas_call x1, Pallas kernels, sample(): pl.pallas_call(functools.partial(sample_kernel, GP), out_shape=jax.ShapeD...  4.9 us
    ppermute x1, starting transfers between devices, on_device(): by_odd = lax.ppermute(odd_edge, 'tile', odd_pairs)  4.27 us
    ppermute x1, waiting for transfers between devices, on_device(): above = lax.ppermute(low_cap, 'sec', down)  3.4 us
    pallas_call x1, Pallas kernels, inner(): pl.pallas_call(functools.partial(inner_kernel, comps, depth_z, width), ou...  3 us
    pallas_call x1, Pallas kernels, outer(): pl.pallas_call(functools.partial(outer_kernel, comps, depth_z, width), ou...  2.81 us
  transfers between devices with their start and end apart: 6, of which 3 were waited for; matrix products, arithmetic and copies ran while one was open for 0% of the time, Pallas kernels for 23%

profile of v12, /device:TPU:97, one launch (start us, length us, event | category | flops | bytes accessed | tf_op | source)
XLA Modules:
  0.0 56.9 jit_solution(14880411773832282851)
XLA Ops:
  0.7 1.3 %collective-permute-start.2 = (f32[4,32]{1,0:T(4,128)}, f32[4,32]{1,0:T(4,128)S(1)}, u32[]{:S(2)}, u32[]{:S(2)}) collective-permute-start(f32[4,32]{1,0:T(4,128)} %ports.3), channel_id=1, source_target_pairs={{0,128},{64,192},{128,0},{192,64},{1,129},{65,193},{129,1},{193,65... | collective-permute-start | bytes 1544 | tf_op jit(solution)/shard_map/ppermute | solution.py:549
  2.0 2.2 %caps.1 = (f32[152,512]{1,0:T(8,128)}, f32[152,512]{1,0:T(8,128)}) custom-call(f32[512,512]{1,0:T(8,128)} %bitcast.13, f32[128,512]{1,0:T(8,128)} %bitcast.18, f32[4,32]{1,0:T(4,128)} %ports.3), custom_call_target="tpu_custom_call" | custom-call | tf_op jit(solution)/shard_map/caps/pallas_call | solution.py:308
  4.1 1.1 %collective-permute-start = (f32[152,512]{1,0:T(8,128)}, f32[152,512]{1,0:T(8,128)S(1)}, u32[]{:S(2)}, u32[]{:S(2)}) collective-permute-start(f32[152,512]{1,0:T(8,128)} %get-tuple-element.18), channel_id=1, source_target_pairs={{0,64},{64,128},{128,192},{192,0},{1,65},{65,129},{129,193},{193,1... | collective-permute-start | bytes 933896 | tf_op jit(solution)/shard_map/ppermute | solution.py:547
  5.2 0.0 collective-permute-start.1
  5.3 0.0 copy-start.2
  5.3 0.0 copy-start.3
  5.3 0.0 copy-start.4
  5.3 0.0 copy-start.5
  5.3 4.9 %sample.1.sampled = f32[72,4,128]{2,1,0:T(4,128)S(1)} custom-call(s32[64]{0:T(128)S(1)} %bitcast.25, f32[512,512]{1,0:T(8,128)S(1)} %bitcast.14, s32[64,128]{1,0:T(8,128)S(1)} %bitcast.27), custom_call_target="tpu_custom_call" | custom-call | flops 8589934592 | bytes 2097152 | tf_op jit(solution)/shard_map/sample/pallas_call | solution.py:69
  10.2 0.0 copy-start.1
  10.2 0.0 collective-permute-done.2.across
  10.2 0.6 %collective-permute-done.below = f32[152,512]{1,0:T(8,128)S(1)} collective-permute-done((f32[152,512]{1,0:T(8,128)}, f32[152,512]{1,0:T(8,128)S(1)}, u32[]{:S(2)}, u32[]{:S(2)}) %collective-permute-start) | collective-permute-done | bytes 311328 | tf_op jit(solution)/shard_map/ppermute | solution.py:547
  10.9 3.4 %collective-permute-done.1.above = f32[152,512]{1,0:T(8,128)S(1)} collective-permute-done((f32[152,512]{1,0:T(8,128)}, f32[152,512]{1,0:T(8,128)S(1)}, u32[]{:S(2)}, u32[]{:S(2)}) %collective-permute-start.1) | collective-permute-done | bytes 311328 | tf_op jit(solution)/shard_map/ppermute | solution.py:548
  14.3 2.0 %slip.1 = f32[192,4,128]{2,1,0:T(4,128)} custom-call(s32[64]{0:T(128)S(1)} %bitcast.26, f32[72,4,128]{2,1,0:T(4,128)S(1)} %sample.1.sampled, f32[4,64,128]{2,1,0:T(8,128)S(1)} %bitcast.22, f32[64,128]{1,0:T(8,128)S(1)} %bitcast.23, f32[64,128]{1,0:T(8,128)S(1)} %bitcast.24, f32[4,32]{1,0:T(4,128)S(1)} %copy-done.5, ...), custom_call_target="tpu_custom_call" | custom-call | flops 2000000 | bytes 1048576 | tf_op jit(solution)/shard_map/slip/pallas_call | solution.py:127
  16.3 0.0 copy-start.10
  16.3 12.5 %all-to-all-start = ((f32[192,4,128]{2,1,0:T(4,128)}), f32[192,4,128]{2,1,0:T(4,128)S(1)}, u32[]{:S(2)}, u32[]{:S(2)}) async-start(f32[192,4,128]{2,1,0:T(4,128)} %slip.1), calls=%async_computation | async-start | bytes 786432 | tf_op jit(solution)/shard_map/all_to_all | solution.py:565
  28.9 0.2 edges.1
  29.1 2.8 %collective-permute-start.3 = (f32[80,512]{1,0:T(8,128)S(1)}, f32[80,512]{1,0:T(8,128)S(1)}, u32[]{:S(2)}, u32[]{:S(2)}) collective-permute-start(f32[80,512]{1,0:T(8,128)S(1)} %get-tuple-element.27), channel_id=1, source_target_pairs={{0,1},{1,0},{2,3},{3,2},{4,5},{5,4},{6,7},{7,6},{8,9},{9,8},{10,11... | collective-permute-start | bytes 491528 | tf_op jit(solution)/shard_map/ppermute | solution.py:567
  31.9 4.3 %collective-permute-start.4 = (f32[80,512]{1,0:T(8,128)S(1)}, f32[80,512]{1,0:T(8,128)S(1)}, u32[]{:S(2)}, u32[]{:S(2)}) collective-permute-start(f32[80,512]{1,0:T(8,128)S(1)} %get-tuple-element.28), channel_id=1, source_target_pairs={{0,0},{63,63},{1,2},{2,1},{3,4},{4,3},{5,6},{6,5},{7,8},{8,7},{9,1... | collective-permute-start | bytes 491528 | tf_op jit(solution)/shard_map/ppermute | solution.py:568
  36.1 3.0 %inner.1 = (f32[4,10,16,512]{3,2,1,0:T(8,128)S(1)}, f32[512,512]{1,0:T(8,128)S(1)}) custom-call(f32[512,512]{1,0:T(8,128)S(1)} %bitcast.16, f32[128,512]{1,0:T(8,128)S(1)} %bitcast.20, f32[144,512]{1,0:T(8,128)S(1)} %get-tuple-element.23.below, f32[144,512]{1,0:T(8,128)S(1)} %get-tuple-element.24.above), custom_call_target="tpu_custom_call" | custom-call | flops 10000000 | bytes 4194304 | tf_op jit(solution)/shard_map/inner/pallas_call | solution.py:391
  39.2 7.8 %collective-permute-done.4.by_odd = f32[80,512]{1,0:T(8,128)S(1)} collective-permute-done((f32[80,512]{1,0:T(8,128)S(1)}, f32[80,512]{1,0:T(8,128)S(1)}, u32[]{:S(2)}, u32[]{:S(2)}) %collective-permute-start.4) | collective-permute-done | bytes 163872 | tf_op jit(solution)/shard_map/ppermute | solution.py:568
  47.0 2.8 %outer.1 = (f32[512,512]{1,0:T(8,128)S(1)}, f32[4,128]{1,0:T(4,128)S(1)}) custom-call(f32[512,512]{1,0:T(8,128)S(1)} %bitcast.17, f32[128,512]{1,0:T(8,128)S(1)} %bitcast.21, f32[144,512]{1,0:T(8,128)S(1)} %get-tuple-element.23.below, f32[144,512]{1,0:T(8,128)S(1)} %get-tuple-element.24.above, f32[4,10,16,512]{3,2,1,0:T(8,128)S(1)} %get-tuple-element.25.first, ...), custom_call_target="tpu_custom_call" | custom-call | flops 10000000 | bytes 4194304 | tf_op jit(solution)/shard_map/outer/pallas_call | solution.py:500
  49.8 0.0 all-to-all-done.arrived
  49.8 7.0 %land.1 = (f32[512,512]{1,0:T(8,128)}, f32[4,64,128]{2,1,0:T(8,128)}) custom-call(s32[32]{0:T(128)S(1)} %copy-done.9, f32[512,512]{1,0:T(8,128)S(1)} %get-tuple-element.29.second, f32[4,128]{1,0:T(4,128)S(1)} %get-tuple-element.30.inlet_now, s32[1,128]{1,0:T(1,128)S(1)} %pad.4.inlet, s32[64,128]{1,0:T(8,128)S(1)} %bitcast.28, ...), custom_call_target="tpu_custom_call" | custom-call | flops 8589934592 | bytes 2097152 | tf_op jit(solution)/shard_map/land/pallas_call | solution.py:243
  (18 shorter events, 0.0 us)
Async XLA Ops:
  0.6 4.6 %copy-start = (f32[4,8,16,512]{3,2,1,0:T(8,128)S(1)}, f32[4,8,16,512]{3,2,1,0:T(8,128)}, u32[]{:S(2)}) copy-start(f32[4,8,16,512]{3,2,1,0:T(8,128)} %param.11) | copy-start | bytes 3145732
  0.6 4.6 %copy-start.6 = (s32[1,1,64]{2,1,0:T(1,128)S(1)}, s32[1,1,64]{2,1,0:T(1,128)}, u32[]{:S(2)}) copy-start(s32[1,1,64]{2,1,0:T(1,128)} %param.20) | copy-start | bytes 772
  0.6 4.6 %copy-start.7 = (s32[1,1,64,128]{3,2,1,0:T(8,128)S(1)}, s32[1,1,64,128]{3,2,1,0:T(8,128)}, u32[]{:S(2)}) copy-start(s32[1,1,64,128]{3,2,1,0:T(8,128)} %param.19) | copy-start | bytes 98308
  0.7 9.6 %collective-permute-start.2 = (f32[4,32]{1,0:T(4,128)}, f32[4,32]{1,0:T(4,128)S(1)}, u32[]{:S(2)}, u32[]{:S(2)}) collective-permute-start(f32[4,32]{1,0:T(4,128)} %ports.3), channel_id=1, source_target_pairs={{0,128},{64,192},{128,0},{192,64},{1,129},{65,193},{129,1},{193,65... | collective-permute-start | bytes 1544 | tf_op jit(solution)/shard_map/ppermute | solution.py:549
  4.1 6.7 %collective-permute-start = (f32[152,512]{1,0:T(8,128)}, f32[152,512]{1,0:T(8,128)S(1)}, u32[]{:S(2)}, u32[]{:S(2)}) collective-permute-start(f32[152,512]{1,0:T(8,128)} %get-tuple-element.18), channel_id=1, source_target_pairs={{0,64},{64,128},{128,192},{192,0},{1,65},{65,129},{129,193},{193,1... | collective-permute-start | bytes 933896 | tf_op jit(solution)/shard_map/ppermute | solution.py:547
  5.2 9.0 %collective-permute-start.1 = (f32[152,512]{1,0:T(8,128)}, f32[152,512]{1,0:T(8,128)S(1)}, u32[]{:S(2)}, u32[]{:S(2)}) collective-permute-start(f32[152,512]{1,0:T(8,128)} %get-tuple-element.19), channel_id=1, source_target_pairs={{64,0},{128,64},{192,128},{0,192},{65,1},{129,65},{193,129},{1,193... | collective-permute-start | bytes 933896 | tf_op jit(solution)/shard_map/ppermute | solution.py:548
  5.3 9.0 %copy-start.2 = (f32[4,1,1,64,128]{4,3,2,1,0:T(8,128)S(1)}, f32[4,1,1,64,128]{4,3,2,1,0:T(8,128)}, u32[]{:S(2)}) copy-start(f32[4,1,1,64,128]{4,3,2,1,0:T(8,128)} %param.16) | copy-start | bytes 393220
  5.3 9.0 %copy-start.3 = (f32[1,1,64,128]{3,2,1,0:T(8,128)S(1)}, f32[1,1,64,128]{3,2,1,0:T(8,128)}, u32[]{:S(2)}) copy-start(f32[1,1,64,128]{3,2,1,0:T(8,128)} %param.17) | copy-start | bytes 98308
  5.3 9.0 %copy-start.4 = (f32[1,1,64,128]{3,2,1,0:T(8,128)S(1)}, f32[1,1,64,128]{3,2,1,0:T(8,128)}, u32[]{:S(2)}) copy-start(f32[1,1,64,128]{3,2,1,0:T(8,128)} %param.18) | copy-start | bytes 98308
  5.3 9.0 %copy-start.5 = (f32[4,32]{1,0:T(4,128)S(1)}, f32[4,32]{1,0:T(4,128)}, u32[]{:S(2)}) copy-start(f32[4,32]{1,0:T(4,128)} %ports.3) | copy-start | bytes 1540
  10.2 18.7 %copy-start.1 = (f32[8,16,512]{2,1,0:T(8,128)S(1)}, f32[8,16,512]{2,1,0:T(8,128)}, u32[]{:S(2)}) copy-start(f32[8,16,512]{2,1,0:T(8,128)} %param.12) | copy-start | bytes 786436
  16.3 19.8 %copy-start.10 = (s32[32]{0:T(128)S(1)}, s32[32]{0:T(128)}, u32[]{:S(2)}) copy-start(s32[32]{0:T(128)} %param.15) | copy-start | bytes 388
  16.3 33.5 %all-to-all-start = ((f32[192,4,128]{2,1,0:T(4,128)}), f32[192,4,128]{2,1,0:T(4,128)S(1)}, u32[]{:S(2)}, u32[]{:S(2)}) async-start(f32[192,4,128]{2,1,0:T(4,128)} %slip.1), calls=%async_computation | async-start | bytes 786432 | tf_op jit(solution)/shard_map/all_to_all | solution.py:565
  29.1 10.1 %collective-permute-start.3 = (f32[80,512]{1,0:T(8,128)S(1)}, f32[80,512]{1,0:T(8,128)S(1)}, u32[]{:S(2)}, u32[]{:S(2)}) collective-permute-start(f32[80,512]{1,0:T(8,128)S(1)} %get-tuple-element.27), channel_id=1, source_target_pairs={{0,1},{1,0},{2,3},{3,2},{4,5},{5,4},{6,7},{7,6},{8,9},{9,8},{10,11... | collective-permute-start | bytes 491528 | tf_op jit(solution)/shard_map/ppermute | solution.py:567
  31.9 15.1 %collective-permute-start.4 = (f32[80,512]{1,0:T(8,128)S(1)}, f32[80,512]{1,0:T(8,128)S(1)}, u32[]{:S(2)}, u32[]{:S(2)}) collective-permute-start(f32[80,512]{1,0:T(8,128)S(1)} %get-tuple-element.28), channel_id=1, source_target_pairs={{0,0},{63,63},{1,2},{2,1},{3,4},{4,3},{5,6},{6,5},{7,8},{8,7},{9,1... | collective-permute-start | bytes 491528 | tf_op jit(solution)/shard_map/ppermute | solution.py:568
  47.0 2.8 %copy-start.8 = (s32[1,1,64,128]{3,2,1,0:T(8,128)S(1)}, s32[1,1,64,128]{3,2,1,0:T(8,128)}, u32[]{:S(2)}) copy-start(s32[1,1,64,128]{3,2,1,0:T(8,128)} %param.21) | copy-start | bytes 98308
  47.0 2.8 %copy-start.9 = (s32[32]{0:T(128)S(1)}, s32[32]{0:T(128)}, u32[]{:S(2)}) copy-start(s32[32]{0:T(128)} %match.1) | copy-start | bytes 388

commit v13 on v12

--- a/solution.py
+++ b/solution.py
@@ -84,16 +84,18 @@
 chunks = 4
 
 
-def slip_kernel(counts, sampled, state, rate, mass, ports, above, across, below, far, out, whole, out_sems):
+def slip_kernel(counts, sampled, state, rate, mass, ports, near, across, opposite, far, out, whole, out_sems):
     comps, partners, cap = state.shape
     per = ports.shape[1]
     cap_shift = cap.bit_length() - 1
-    last = above.shape[0] - 8
+    last = near.shape[0] - 8
     lane = lax.broadcasted_iota(jnp.int32, (1, cap), 1)
     whole[:, 0:per] = ports[...]
-    whole[:, per : 2 * per] = above[last : last + comps, 0:per]
+    even = lax.axis_index("sec") % 2 == 0
+    close = near[last : last + comps, 0:per]
+    whole[:, per : 2 * per] = jnp.where(even, close, opposite[...])
     whole[:, 2 * per : 3 * per] = across[...]
-    whole[:, 3 * per :] = below[last : last + comps, 0:per]
+    whole[:, 3 * per :] = jnp.where(even, opposite[...], close)
 
     def finish(p, base):
         n = counts[p]
@@ -122,7 +124,7 @@
         copy.wait()
 
 
-def slip(counts, sampled, state, rate, mass, ports, above, across, below):
+def slip(counts, sampled, state, rate, mass, ports, near, across, opposite):
     comps, partners, cap = state.shape
     return pl.pallas_call(
         slip_kernel,
@@ -137,7 +139,7 @@
         compiler_params=pltpu.CompilerParams(vmem_limit_bytes=24 * 1024 * 1024),
         cost_estimate=pl.CostEstimate(flops=2 * 10**6, bytes_accessed=2**20, transcendentals=0),
         name="slip",
-    )(counts, sampled, state, rate, mass, ports, above, across, below)
+    )(counts, sampled, state, rate, mass, ports, near, across, opposite)
 
 
 def land_kernel(GP, match, second, inlet_now, inlet, arrival, arrived, flow_far, state_far, flow_out, state_out, last_ref, last, packed, sem, out_sems):
@@ -288,16 +290,20 @@
     return centers, out
 
 
-def cap_kernel(comps, depth_z, width, flow, viscosity, ports, low_cap, high_cap):
+def cap_kernel(comps, depth_z, width, flow, viscosity, ports, near_out, next_out):
+    even = lax.axis_index("sec") % 2 == 0
     two = 2 * width
     last = depth_z * width
+
+    def put(spot, count, low, high):
+        near_out[spot : spot + count, :] = jnp.where(even, high, low)
+        next_out[spot : spot + count, :] = jnp.where(even, low, high)
+
     for c in range(comps):
-        low_cap[c * two : (c + 1) * two, :] = flow[c * last : c * last + two, :]
-        high_cap[c * two : (c + 1) * two, :] = flow[(c + 1) * last - two : (c + 1) * last, :]
+        put(c * two, two, flow[c * last : c * last + two, :], flow[(c + 1) * last - two : (c + 1) * last, :])
     base = comps * two
-    low_cap[base : base + width, :] = viscosity[0:width, :]
-    high_cap[base : base + width, :] = viscosity[last - width : last, :]
-    for out in (low_cap, high_cap):
+    put(base, width, viscosity[0:width, :], viscosity[last - width : last, :])
+    for out in (near_out, next_out):
         out[base + width :, :] = jnp.zeros((8, out.shape[1]), jnp.float32)
         out[base + width : base + width + comps, 0 : ports.shape[1]] = ports[...]
 
@@ -315,10 +321,13 @@
     )(flow, viscosity, ports)
 
 
-def edge_kernel(comps, depth_z, width, flow, viscosity, below, above, even_out, odd_out, bottom, top, low_out, high_out):
+def edge_kernel(comps, depth_z, width, flow, viscosity, by_near, by_next, even_out, odd_out, bottom, top, low_out, high_out):
     section = lax.axis_index("sec")
-    bottom[...] = jnp.where(section > 0, below[0 : bottom.shape[0], :], 0.0)
-    top[...] = jnp.where(section < lax.axis_size("sec") - 1, above[0 : top.shape[0], :], 0.0)
+    upper = section % 2 == 0
+    near = by_near[0 : bottom.shape[0], :]
+    beyond = by_next[0 : bottom.shape[0], :]
+    bottom[...] = jnp.where(section > 0, jnp.where(upper, beyond, near), 0.0)
+    top[...] = jnp.where(section < lax.axis_size("sec") - 1, jnp.where(upper, near, beyond), 0.0)
     two = 2 * width
     for k in range(comps * depth_z):
         low_out[2 * k : 2 * k + 2, :] = flow[k * width : k * width + 2, :]
@@ -539,16 +548,16 @@
     even_pairs = [(i, i ^ 1) for i in range(count)]
     odd_pairs = [(0, 0), (count - 1, count - 1)] + [(i, ((i + 1) ^ 1) - 1) for i in range(1, count - 1)]
     levels = lax.axis_size("sec")
-    up = [(i, (i + 1) % levels) for i in range(levels)]
-    down = [((i + 1) % levels, i) for i in range(levels)]
-    over = [(i, (i + levels // 2) % levels) for i in range(levels)]
-
-    low_cap, high_cap = caps(*sizes, flow, visc, port_plane)
-    below = lax.ppermute(high_cap, "sec", up)
-    above = lax.ppermute(low_cap, "sec", down)
-    across = lax.ppermute(port_plane, "sec", over)
+    near_pairs = [(i, i ^ 1) for i in range(levels)]
+    next_pairs = [(0, 0), (levels - 1, levels - 1)] + [(i, ((i + 1) ^ 1) - 1) for i in range(1, levels - 1)]
+
+    near_cap, next_cap = caps(*sizes, flow, visc, port_plane)
+    by_near = lax.ppermute(near_cap, "sec", near_pairs)
+    by_next = lax.ppermute(next_cap, "sec", next_pairs)
+    across = lax.ppermute(port_plane, "sec", [(i, (i + levels // 2) % levels) for i in range(levels)])
+    opposite = lax.ppermute(port_plane, "sec", [(i, levels - 1 - i) for i in range(levels)])
     counts = live_counts.reshape(-1)
-    counts, low_cap, high_cap = lax.optimization_barrier((counts, low_cap, high_cap))
+    counts, near_cap, next_cap = lax.optimization_barrier((counts, near_cap, next_cap))
     sampled = sample(comps, counts, flow, anchor_cell.reshape(partners, cap))
     outgoing = slip(
         counts,
@@ -557,13 +566,13 @@
         response_rate.reshape(partners, cap),
         inclusion_mass.reshape(partners, cap),
         port_plane,
-        above,
+        by_near,
         across,
-        below,
+        opposite,
     )
-    below, above, outgoing = lax.optimization_barrier((below, above, outgoing))
+    by_near, by_next, outgoing = lax.optimization_barrier((by_near, by_next, outgoing))
     arrived = lax.all_to_all(outgoing, "tile", split_axis=0, concat_axis=0, tiled=True)
-    even_edge, odd_edge, bottom, top = edges(*sizes, flow, visc, below, above)
+    even_edge, odd_edge, bottom, top = edges(*sizes, flow, visc, by_near, by_next)
     by_even = lax.ppermute(even_edge, "tile", even_pairs)
     by_odd = lax.ppermute(odd_edge, "tile", odd_pairs)
     inlet = jnp.pad(inlet_cell.reshape(1, -1), ((0, 0), (0, cap - inlet_cell.shape[0])))

time: 57.8 us -> 57.2 us (0.990)
  the two profiles are of different devices: /device:TPU:97 before, /device:TPU:33 now
where the time goes in v13:
time: 57.2 us; the launch traced here: 56.6 us
  starting transfers between devices  26.4 us (46%)
  Pallas kernels  22.2 us (39%)
  waiting for transfers between devices  7.08 us (12%)
  between operations  0.91 us (2%)
    all_to_all x1, starting transfers between devices, on_device(): lax.all_to_all(outgoing, 'tile', split_axis=0, concat_axis=0, tiled=True)  13.4 us
    ppermute x1, waiting for transfers between devices, on_device(): by_odd = lax.ppermute(odd_edge, 'tile', odd_pairs)  7.06 us
    pallas_call x1, Pallas kernels, land(): pl.pallas_call(functools.partial(land_kernel, GP), out_shape=(jax.ShapeDt...  7.05 us
    pallas_call x1, Pallas kernels, sample(): pl.pallas_call(functools.partial(sample_kernel, GP), out_shape=jax.ShapeD...  4.9 us
    ppermute x1, starting transfers between devices, on_device(): by_odd = lax.ppermute(odd_edge, 'tile', odd_pairs)  4.29 us
    ppermute x1, starting transfers between devices, on_device(): by_next = lax.ppermute(next_cap, 'sec', next_pairs)  3.5 us
    pallas_call x1, Pallas kernels, inner(): pl.pallas_call(functools.partial(inner_kernel, comps, depth_z, width), ou...  3 us
    pallas_call x1, Pallas kernels, outer(): pl.pallas_call(functools.partial(outer_kernel, comps, depth_z, width), ou...  2.81 us
  transfers between devices with their start and end apart: 7, of which 1 were waited for; matrix products, arithmetic and copies ran while one was open for 0% of the time, Pallas kernels for 27%

profile of v13, /device:TPU:33, one launch (start us, length us, event | category | flops | bytes accessed | tf_op | source)
XLA Modules:
  0.0 56.6 jit_solution(7805308316689240982)
XLA Ops:
  0.7 1.3 %collective-permute-start.2 = (f32[4,32]{1,0:T(4,128)}, f32[4,32]{1,0:T(4,128)S(1)}, u32[]{:S(2)}, u32[]{:S(2)}) collective-permute-start(f32[4,32]{1,0:T(4,128)} %ports.3), channel_id=1, source_target_pairs={{0,128},{64,192},{128,0},{192,64},{1,129},{65,193},{129,1},{193,65... | collective-permute-start | bytes 1544 | tf_op jit(solution)/shard_map/ppermute | solution.py:557
  2.0 1.1 %collective-permute-start.3 = (f32[4,32]{1,0:T(4,128)}, f32[4,32]{1,0:T(4,128)S(1)}, u32[]{:S(2)}, u32[]{:S(2)}) collective-permute-start(f32[4,32]{1,0:T(4,128)} %ports.3), channel_id=1, source_target_pairs={{0,192},{64,128},{128,64},{192,0},{1,193},{65,129},{129,65},{193,1... | collective-permute-start | bytes 1544 | tf_op jit(solution)/shard_map/ppermute | solution.py:558
  3.1 2.2 %caps.1 = (f32[152,512]{1,0:T(8,128)}, f32[152,512]{1,0:T(8,128)}) custom-call(f32[512,512]{1,0:T(8,128)} %bitcast.13, f32[128,512]{1,0:T(8,128)} %bitcast.18, f32[4,32]{1,0:T(4,128)} %ports.3), custom_call_target="tpu_custom_call" | custom-call | tf_op jit(solution)/shard_map/caps/pallas_call | solution.py:314
  5.2 0.0 collective-permute-start
  5.2 3.5 %collective-permute-start.1 = (f32[152,512]{1,0:T(8,128)}, f32[152,512]{1,0:T(8,128)S(1)}, u32[]{:S(2)}, u32[]{:S(2)}) collective-permute-start(f32[152,512]{1,0:T(8,128)} %get-tuple-element.19), channel_id=1, source_target_pairs={{0,0},{192,192},{64,128},{128,64},{1,1},{193,193},{65,129},{129,65... | collective-permute-start | bytes 933896 | tf_op jit(solution)/shard_map/ppermute | solution.py:556
  8.8 0.0 copy-start.2
  8.8 0.0 copy-start.3
  8.8 0.0 copy-start.4
  8.8 0.0 copy-start.5
  8.8 4.9 %sample.1.sampled = f32[72,4,128]{2,1,0:T(4,128)S(1)} custom-call(s32[64]{0:T(128)S(1)} %bitcast.25, f32[512,512]{1,0:T(8,128)S(1)} %bitcast.14, s32[64,128]{1,0:T(8,128)S(1)} %bitcast.27), custom_call_target="tpu_custom_call" | custom-call | flops 8589934592 | bytes 2097152 | tf_op jit(solution)/shard_map/sample/pallas_call | solution.py:69
  13.7 0.0 copy-start.1
  13.7 0.0 collective-permute-done.2.across
  13.8 0.0 collective-permute-done.3.opposite
  13.8 0.0 collective-permute-done.near.by_near
  13.8 2.0 %slip.1 = f32[192,4,128]{2,1,0:T(4,128)} custom-call(s32[64]{0:T(128)S(1)} %bitcast.26, f32[72,4,128]{2,1,0:T(4,128)S(1)} %sample.1.sampled, f32[4,64,128]{2,1,0:T(8,128)S(1)} %bitcast.22, f32[64,128]{1,0:T(8,128)S(1)} %bitcast.23, f32[64,128]{1,0:T(8,128)S(1)} %bitcast.24, f32[4,32]{1,0:T(4,128)S(1)} %copy-done.5, ...), custom_call_target="tpu_custom_call" | custom-call | flops 2000000 | bytes 1048576 | tf_op jit(solution)/shard_map/slip/pallas_call | solution.py:129
  15.9 0.0 copy-start.10
  15.9 13.4 %all-to-all-start = ((f32[192,4,128]{2,1,0:T(4,128)}), f32[192,4,128]{2,1,0:T(4,128)S(1)}, u32[]{:S(2)}, u32[]{:S(2)}) async-start(f32[192,4,128]{2,1,0:T(4,128)} %slip.1), calls=%async_computation | async-start | bytes 786432 | tf_op jit(solution)/shard_map/all_to_all | solution.py:574
  29.3 0.2 edges.1
  29.6 2.8 %collective-permute-start.4 = (f32[80,512]{1,0:T(8,128)S(1)}, f32[80,512]{1,0:T(8,128)S(1)}, u32[]{:S(2)}, u32[]{:S(2)}) collective-permute-start(f32[80,512]{1,0:T(8,128)S(1)} %get-tuple-element.27), channel_id=1, source_target_pairs={{0,1},{1,0},{2,3},{3,2},{4,5},{5,4},{6,7},{7,6},{8,9},{9,8},{10,11... | collective-permute-start | bytes 491528 | tf_op jit(solution)/shard_map/ppermute | solution.py:576
  32.3 4.3 %collective-permute-start.5 = (f32[80,512]{1,0:T(8,128)S(1)}, f32[80,512]{1,0:T(8,128)S(1)}, u32[]{:S(2)}, u32[]{:S(2)}) collective-permute-start(f32[80,512]{1,0:T(8,128)S(1)} %get-tuple-element.28), channel_id=1, source_target_pairs={{0,0},{63,63},{1,2},{2,1},{3,4},{4,3},{5,6},{6,5},{7,8},{8,7},{9,1... | collective-permute-start | bytes 491528 | tf_op jit(solution)/shard_map/ppermute | solution.py:577
  36.6 3.0 %inner.1 = (f32[4,10,16,512]{3,2,1,0:T(8,128)S(1)}, f32[512,512]{1,0:T(8,128)S(1)}) custom-call(f32[512,512]{1,0:T(8,128)S(1)} %bitcast.16, f32[128,512]{1,0:T(8,128)S(1)} %bitcast.20, f32[144,512]{1,0:T(8,128)S(1)} %get-tuple-element.23.below, f32[144,512]{1,0:T(8,128)S(1)} %get-tuple-element.24.above), custom_call_target="tpu_custom_call" | custom-call | flops 10000000 | bytes 4194304 | tf_op jit(solution)/shard_map/inner/pallas_call | solution.py:400
  39.7 7.1 %collective-permute-done.5.by_odd = f32[80,512]{1,0:T(8,128)S(1)} collective-permute-done((f32[80,512]{1,0:T(8,128)S(1)}, f32[80,512]{1,0:T(8,128)S(1)}, u32[]{:S(2)}, u32[]{:S(2)}) %collective-permute-start.5) | collective-permute-done | bytes 163872 | tf_op jit(solution)/shard_map/ppermute | solution.py:577
  46.7 2.8 %outer.1 = (f32[512,512]{1,0:T(8,128)S(1)}, f32[4,128]{1,0:T(4,128)S(1)}) custom-call(f32[512,512]{1,0:T(8,128)S(1)} %bitcast.17, f32[128,512]{1,0:T(8,128)S(1)} %bitcast.21, f32[144,512]{1,0:T(8,128)S(1)} %get-tuple-element.23.below, f32[144,512]{1,0:T(8,128)S(1)} %get-tuple-element.24.above, f32[4,10,16,512]{3,2,1,0:T(8,128)S(1)} %get-tuple-element.25.first, ...), custom_call_target="tpu_custom_call" | custom-call | flops 10000000 | bytes 4194304 | tf_op jit(solution)/shard_map/outer/pallas_call | solution.py:509
  49.6 7.0 %land.1 = (f32[512,512]{1,0:T(8,128)}, f32[4,64,128]{2,1,0:T(8,128)}) custom-call(s32[32]{0:T(128)S(1)} %copy-done.9, f32[512,512]{1,0:T(8,128)S(1)} %get-tuple-element.29.second, f32[4,128]{1,0:T(4,128)S(1)} %get-tuple-element.30.inlet_now, s32[1,128]{1,0:T(1,128)S(1)} %pad.4.inlet, s32[64,128]{1,0:T(8,128)S(1)} %bitcast.28, ...), custom_call_target="tpu_custom_call" | custom-call | flops 8589934592 | bytes 2097152 | tf_op jit(solution)/shard_map/land/pallas_call | solution.py:245
  (20 shorter events, 0.0 us)
Async XLA Ops:
  0.6 8.1 %copy-start = (f32[4,8,16,512]{3,2,1,0:T(8,128)S(1)}, f32[4,8,16,512]{3,2,1,0:T(8,128)}, u32[]{:S(2)}) copy-start(f32[4,8,16,512]{3,2,1,0:T(8,128)} %param.11) | copy-start | bytes 3145732
  0.6 8.1 %copy-start.6 = (s32[1,1,64]{2,1,0:T(1,128)S(1)}, s32[1,1,64]{2,1,0:T(1,128)}, u32[]{:S(2)}) copy-start(s32[1,1,64]{2,1,0:T(1,128)} %param.20) | copy-start | bytes 772
  0.6 8.1 %copy-start.7 = (s32[1,1,64,128]{3,2,1,0:T(8,128)S(1)}, s32[1,1,64,128]{3,2,1,0:T(8,128)}, u32[]{:S(2)}) copy-start(s32[1,1,64,128]{3,2,1,0:T(8,128)} %param.19) | copy-start | bytes 98308
  0.7 13.1 %collective-permute-start.2 = (f32[4,32]{1,0:T(4,128)}, f32[4,32]{1,0:T(4,128)S(1)}, u32[]{:S(2)}, u32[]{:S(2)}) collective-permute-start(f32[4,32]{1,0:T(4,128)} %ports.3), channel_id=1, source_target_pairs={{0,128},{64,192},{128,0},{192,64},{1,129},{65,193},{129,1},{193,65... | collective-permute-start | bytes 1544 | tf_op jit(solution)/shard_map/ppermute | solution.py:557
  2.0 11.8 %collective-permute-start.3 = (f32[4,32]{1,0:T(4,128)}, f32[4,32]{1,0:T(4,128)S(1)}, u32[]{:S(2)}, u32[]{:S(2)}) collective-permute-start(f32[4,32]{1,0:T(4,128)} %ports.3), channel_id=1, source_target_pairs={{0,192},{64,128},{128,64},{192,0},{1,193},{65,129},{129,65},{193,1... | collective-permute-start | bytes 1544 | tf_op jit(solution)/shard_map/ppermute | solution.py:558
  5.2 8.5 %collective-permute-start = (f32[152,512]{1,0:T(8,128)}, f32[152,512]{1,0:T(8,128)S(1)}, u32[]{:S(2)}, u32[]{:S(2)}) collective-permute-start(f32[152,512]{1,0:T(8,128)} %get-tuple-element.18), channel_id=1, source_target_pairs={{0,64},{64,0},{128,192},{192,128},{1,65},{65,1},{129,193},{193,129... | collective-permute-start | bytes 933896 | tf_op jit(solution)/shard_map/ppermute | solution.py:555
  5.2 10.6 %collective-permute-start.1 = (f32[152,512]{1,0:T(8,128)}, f32[152,512]{1,0:T(8,128)S(1)}, u32[]{:S(2)}, u32[]{:S(2)}) collective-permute-start(f32[152,512]{1,0:T(8,128)} %get-tuple-element.19), channel_id=1, source_target_pairs={{0,0},{192,192},{64,128},{128,64},{1,1},{193,193},{65,129},{129,65... | collective-permute-start | bytes 933896 | tf_op jit(solution)/shard_map/ppermute | solution.py:556
  8.8 5.0 %copy-start.2 = (f32[4,1,1,64,128]{4,3,2,1,0:T(8,128)S(1)}, f32[4,1,1,64,128]{4,3,2,1,0:T(8,128)}, u32[]{:S(2)}) copy-start(f32[4,1,1,64,128]{4,3,2,1,0:T(8,128)} %param.16) | copy-start | bytes 393220
  8.8 5.0 %copy-start.3 = (f32[1,1,64,128]{3,2,1,0:T(8,128)S(1)}, f32[1,1,64,128]{3,2,1,0:T(8,128)}, u32[]{:S(2)}) copy-start(f32[1,1,64,128]{3,2,1,0:T(8,128)} %param.17) | copy-start | bytes 98308
  8.8 5.0 %copy-start.4 = (f32[1,1,64,128]{3,2,1,0:T(8,128)S(1)}, f32[1,1,64,128]{3,2,1,0:T(8,128)}, u32[]{:S(2)}) copy-start(f32[1,1,64,128]{3,2,1,0:T(8,128)} %param.18) | copy-start | bytes 98308
  8.8 5.0 %copy-start.5 = (f32[4,32]{1,0:T(4,128)S(1)}, f32[4,32]{1,0:T(4,128)}, u32[]{:S(2)}) copy-start(f32[4,32]{1,0:T(4,128)} %ports.3) | copy-start | bytes 1540
  13.7 15.6 %copy-start.1 = (f32[8,16,512]{2,1,0:T(8,128)S(1)}, f32[8,16,512]{2,1,0:T(8,128)}, u32[]{:S(2)}) copy-start(f32[8,16,512]{2,1,0:T(8,128)} %param.12) | copy-start | bytes 786436
  15.9 20.8 %copy-start.10 = (s32[32]{0:T(128)S(1)}, s32[32]{0:T(128)}, u32[]{:S(2)}) copy-start(s32[32]{0:T(128)} %param.15) | copy-start | bytes 388
  15.9 33.7 %all-to-all-start = ((f32[192,4,128]{2,1,0:T(4,128)}), f32[192,4,128]{2,1,0:T(4,128)S(1)}, u32[]{:S(2)}, u32[]{:S(2)}) async-start(f32[192,4,128]{2,1,0:T(4,128)} %slip.1), calls=%async_computation | async-start | bytes 786432 | tf_op jit(solution)/shard_map/all_to_all | solution.py:574
  29.6 10.1 %collective-permute-start.4 = (f32[80,512]{1,0:T(8,128)S(1)}, f32[80,512]{1,0:T(8,128)S(1)}, u32[]{:S(2)}, u32[]{:S(2)}) collective-permute-start(f32[80,512]{1,0:T(8,128)S(1)} %get-tuple-element.27), channel_id=1, source_target_pairs={{0,1},{1,0},{2,3},{3,2},{4,5},{5,4},{6,7},{7,6},{8,9},{9,8},{10,11... | collective-permute-start | bytes 491528 | tf_op jit(solution)/shard_map/ppermute | solution.py:576
  32.3 14.4 %collective-permute-start.5 = (f32[80,512]{1,0:T(8,128)S(1)}, f32[80,512]{1,0:T(8,128)S(1)}, u32[]{:S(2)}, u32[]{:S(2)}) collective-permute-start(f32[80,512]{1,0:T(8,128)S(1)} %get-tuple-element.28), channel_id=1, source_target_pairs={{0,0},{63,63},{1,2},{2,1},{3,4},{4,3},{5,6},{6,5},{7,8},{8,7},{9,1... | collective-permute-start | bytes 491528 | tf_op jit(solution)/shard_map/ppermute | solution.py:577
  46.7 2.8 %copy-start.8 = (s32[1,1,64,128]{3,2,1,0:T(8,128)S(1)}, s32[1,1,64,128]{3,2,1,0:T(8,128)}, u32[]{:S(2)}) copy-start(s32[1,1,64,128]{3,2,1,0:T(8,128)} %param.21) | copy-start | bytes 98308
  46.7 2.8 %copy-start.9 = (s32[32]{0:T(128)S(1)}, s32[32]{0:T(128)}, u32[]{:S(2)}) copy-start(s32[32]{0:T(128)} %match.1) | copy-start | bytes 388

commit v14 on v13

--- a/solution.py
+++ b/solution.py
@@ -411,7 +411,7 @@
     )(flow, viscosity, below, above)
 
 
-def outer_kernel(comps, depth_z, width, flow, viscosity, below, above, first, middle, by_even, by_odd, inlet, second_out, inlet_now, strip, visc, started, table):
+def outer_kernel(comps, depth_z, width, flow, viscosity, below, above, first, middle, by_odd, by_even, inlet, second_out, inlet_now, strip, visc, started, table):
     depth = flow.shape[1]
     two = 2 * width
     rows = depth_z * width
@@ -573,11 +573,11 @@
     by_near, by_next, outgoing = lax.optimization_barrier((by_near, by_next, outgoing))
     arrived = lax.all_to_all(outgoing, "tile", split_axis=0, concat_axis=0, tiled=True)
     even_edge, odd_edge, bottom, top = edges(*sizes, flow, visc, by_near, by_next)
+    by_odd = lax.ppermute(odd_edge, "tile", odd_pairs)
     by_even = lax.ppermute(even_edge, "tile", even_pairs)
-    by_odd = lax.ppermute(odd_edge, "tile", odd_pairs)
     inlet = jnp.pad(inlet_cell.reshape(1, -1), ((0, 0), (0, cap - inlet_cell.shape[0])))
     first, middle = inner(*sizes, flow, visc, bottom, top)
-    second, inlet_now = outer(*sizes, flow, visc, bottom, top, first, middle, by_even, by_odd, inlet)
+    second, inlet_now = outer(*sizes, flow, visc, bottom, top, first, middle, by_odd, by_even, inlet)
     flow_next, arrived_state = land(
         port_match, second, inlet_now, inlet, arrival_cell.reshape(partners, cap), arrived
     )

time: 57.2 us -> 57.2 us (level)
  the two profiles are of different devices: /device:TPU:33 before, /device:TPU:1 now
where the time goes in v14:
time: 57.2 us; the launch traced here: 57 us
  starting transfers between devices  26.4 us (46%)
  Pallas kernels  22.2 us (39%)
  waiting for transfers between devices  7.43 us (13%)
  between operations  0.89 us (2%)
    all_to_all x1, starting transfers between devices, on_device(): lax.all_to_all(outgoing, 'tile', split_axis=0, concat_axis=0, tiled=True)  13.7 us
    ppermute x1, waiting for transfers between devices, on_device(): by_even = lax.ppermute(even_edge, 'tile', even_pairs)  7.41 us
    pallas_call x1, Pallas kernels, land(): pl.pallas_call(functools.partial(land_kernel, GP), out_shape=(jax.ShapeDt...  7.05 us
    ppermute x1, starting transfers between devices, on_device(): by_even = lax.ppermute(even_edge, 'tile', even_pairs)  5.02 us
    pallas_call x1, Pallas kernels, sample(): pl.pallas_call(functools.partial(sample_kernel, GP), out_shape=jax.ShapeD...  4.9 us
    pallas_call x1, Pallas kernels, inner(): pl.pallas_call(functools.partial(inner_kernel, comps, depth_z, width), ou...  2.99 us
    ppermute x1, starting transfers between devices, on_device(): lax.ppermute(port_plane, 'sec', [(i, levels - 1 - i) for i in range(level...  2.83 us
    pallas_call x1, Pallas kernels, outer(): pl.pallas_call(functools.partial(outer_kernel, comps, depth_z, width), ou...  2.82 us
  transfers between devices with their start and end apart: 7, of which 1 were waited for; matrix products, arithmetic and copies ran while one was open for 0% of the time, Pallas kernels for 27%

profile of v14, /device:TPU:1, one launch (start us, length us, event | category | flops | bytes accessed | tf_op | source)
XLA Modules:
  0.0 57.0 jit_solution(6084510496982481750)
XLA Ops:
  0.7 2.1 %collective-permute-start.2 = (f32[4,32]{1,0:T(4,128)}, f32[4,32]{1,0:T(4,128)S(1)}, u32[]{:S(2)}, u32[]{:S(2)}) collective-permute-start(f32[4,32]{1,0:T(4,128)} %ports.3), channel_id=1, source_target_pairs={{0,128},{64,192},{128,0},{192,64},{1,129},{65,193},{129,1},{193,65... | collective-permute-start | bytes 1544 | tf_op jit(solution)/shard_map/ppermute | solution.py:557
  2.8 2.8 %collective-permute-start.3 = (f32[4,32]{1,0:T(4,128)}, f32[4,32]{1,0:T(4,128)S(1)}, u32[]{:S(2)}, u32[]{:S(2)}) collective-permute-start(f32[4,32]{1,0:T(4,128)} %ports.3), channel_id=1, source_target_pairs={{0,192},{64,128},{128,64},{192,0},{1,193},{65,129},{129,65},{193,1... | collective-permute-start | bytes 1544 | tf_op jit(solution)/shard_map/ppermute | solution.py:558
  5.6 2.2 %caps.1 = (f32[152,512]{1,0:T(8,128)}, f32[152,512]{1,0:T(8,128)}) custom-call(f32[512,512]{1,0:T(8,128)} %bitcast.13, f32[128,512]{1,0:T(8,128)} %bitcast.18, f32[4,32]{1,0:T(4,128)} %ports.3), custom_call_target="tpu_custom_call" | custom-call | tf_op jit(solution)/shard_map/caps/pallas_call | solution.py:314
  7.8 2.1 %collective-permute-start.1 = (f32[152,512]{1,0:T(8,128)}, f32[152,512]{1,0:T(8,128)S(1)}, u32[]{:S(2)}, u32[]{:S(2)}) collective-permute-start(f32[152,512]{1,0:T(8,128)} %get-tuple-element.19), channel_id=1, source_target_pairs={{0,0},{192,192},{64,128},{128,64},{1,1},{193,193},{65,129},{129,65... | collective-permute-start | bytes 933896 | tf_op jit(solution)/shard_map/ppermute | solution.py:556
  10.0 0.0 copy-start.2
  10.0 0.0 copy-start.3
  10.0 0.0 copy-start.4
  10.0 0.0 copy-start.5
  10.0 4.9 %sample.1.sampled = f32[72,4,128]{2,1,0:T(4,128)S(1)} custom-call(s32[64]{0:T(128)S(1)} %bitcast.25, f32[512,512]{1,0:T(8,128)S(1)} %bitcast.14, s32[64,128]{1,0:T(8,128)S(1)} %bitcast.27), custom_call_target="tpu_custom_call" | custom-call | flops 8589934592 | bytes 2097152 | tf_op jit(solution)/shard_map/sample/pallas_call | solution.py:69
  14.9 0.0 copy-start.1
  14.9 0.0 collective-permute-done.3.opposite
  14.9 0.0 collective-permute-done.near.by_near
  15.0 2.0 %slip.1 = f32[192,4,128]{2,1,0:T(4,128)} custom-call(s32[64]{0:T(128)S(1)} %bitcast.26, f32[72,4,128]{2,1,0:T(4,128)S(1)} %sample.1.sampled, f32[4,64,128]{2,1,0:T(8,128)S(1)} %bitcast.22, f32[64,128]{1,0:T(8,128)S(1)} %bitcast.23, f32[64,128]{1,0:T(8,128)S(1)} %bitcast.24, f32[4,32]{1,0:T(4,128)S(1)} %copy-done.5, ...), custom_call_target="tpu_custom_call" | custom-call | flops 2000000 | bytes 1048576 | tf_op jit(solution)/shard_map/slip/pallas_call | solution.py:129
  17.0 0.0 copy-start.10
  17.1 0.0 collective-permute-done.1.by_next
  17.1 13.7 %all-to-all-start = ((f32[192,4,128]{2,1,0:T(4,128)}), f32[192,4,128]{2,1,0:T(4,128)S(1)}, u32[]{:S(2)}, u32[]{:S(2)}) async-start(f32[192,4,128]{2,1,0:T(4,128)} %slip.1), calls=%async_computation | async-start | bytes 786432 | tf_op jit(solution)/shard_map/all_to_all | solution.py:574
  30.8 0.2 edges.1
  31.0 0.7 %collective-permute-start.4 = (f32[80,512]{1,0:T(8,128)S(1)}, f32[80,512]{1,0:T(8,128)S(1)}, u32[]{:S(2)}, u32[]{:S(2)}) collective-permute-start(f32[80,512]{1,0:T(8,128)S(1)} %get-tuple-element.27), channel_id=1, source_target_pairs={{0,0},{63,63},{1,2},{2,1},{3,4},{4,3},{5,6},{6,5},{7,8},{8,7},{9,1... | collective-permute-start | bytes 491528 | tf_op jit(solution)/shard_map/ppermute | solution.py:576
  31.7 5.0 %collective-permute-start.5 = (f32[80,512]{1,0:T(8,128)S(1)}, f32[80,512]{1,0:T(8,128)S(1)}, u32[]{:S(2)}, u32[]{:S(2)}) collective-permute-start(f32[80,512]{1,0:T(8,128)S(1)} %get-tuple-element.28), channel_id=1, source_target_pairs={{0,1},{1,0},{2,3},{3,2},{4,5},{5,4},{6,7},{7,6},{8,9},{9,8},{10,11... | collective-permute-start | bytes 491528 | tf_op jit(solution)/shard_map/ppermute | solution.py:577
  36.7 3.0 %inner.1 = (f32[4,10,16,512]{3,2,1,0:T(8,128)S(1)}, f32[512,512]{1,0:T(8,128)S(1)}) custom-call(f32[512,512]{1,0:T(8,128)S(1)} %bitcast.16, f32[128,512]{1,0:T(8,128)S(1)} %bitcast.20, f32[144,512]{1,0:T(8,128)S(1)} %get-tuple-element.23.below, f32[144,512]{1,0:T(8,128)S(1)} %get-tuple-element.24.above), custom_call_target="tpu_custom_call" | custom-call | flops 10000000 | bytes 4194304 | tf_op jit(solution)/shard_map/inner/pallas_call | solution.py:400
  39.7 0.0 collective-permute-done.4.by_odd
  39.7 7.4 %collective-permute-done.5.by_even = f32[80,512]{1,0:T(8,128)S(1)} collective-permute-done((f32[80,512]{1,0:T(8,128)S(1)}, f32[80,512]{1,0:T(8,128)S(1)}, u32[]{:S(2)}, u32[]{:S(2)}) %collective-permute-start.5) | collective-permute-done | bytes 163872 | tf_op jit(solution)/shard_map/ppermute | solution.py:577
  47.1 2.8 %outer.1 = (f32[512,512]{1,0:T(8,128)S(1)}, f32[4,128]{1,0:T(4,128)S(1)}) custom-call(f32[512,512]{1,0:T(8,128)S(1)} %bitcast.17, f32[128,512]{1,0:T(8,128)S(1)} %bitcast.21, f32[144,512]{1,0:T(8,128)S(1)} %get-tuple-element.23.below, f32[144,512]{1,0:T(8,128)S(1)} %get-tuple-element.24.above, f32[4,10,16,512]{3,2,1,0:T(8,128)S(1)} %get-tuple-element.25.first, ...), custom_call_target="tpu_custom_call" | custom-call | flops 10000000 | bytes 4194304 | tf_op jit(solution)/shard_map/outer/pallas_call | solution.py:509
  50.0 7.0 %land.1 = (f32[512,512]{1,0:T(8,128)}, f32[4,64,128]{2,1,0:T(8,128)}) custom-call(s32[32]{0:T(128)S(1)} %copy-done.9, f32[512,512]{1,0:T(8,128)S(1)} %get-tuple-element.29.second, f32[4,128]{1,0:T(4,128)S(1)} %get-tuple-element.30.inlet_now, s32[1,128]{1,0:T(1,128)S(1)} %pad.4.inlet, s32[64,128]{1,0:T(8,128)S(1)} %bitcast.28, ...), custom_call_target="tpu_custom_call" | custom-call | flops 8589934592 | bytes 2097152 | tf_op jit(solution)/shard_map/land/pallas_call | solution.py:245
  (20 shorter events, 0.0 us)
Async XLA Ops:
  0.6 9.3 %copy-start = (f32[4,8,16,512]{3,2,1,0:T(8,128)S(1)}, f32[4,8,16,512]{3,2,1,0:T(8,128)}, u32[]{:S(2)}) copy-start(f32[4,8,16,512]{3,2,1,0:T(8,128)} %param.11) | copy-start | bytes 3145732
  0.6 9.3 %copy-start.6 = (s32[1,1,64]{2,1,0:T(1,128)S(1)}, s32[1,1,64]{2,1,0:T(1,128)}, u32[]{:S(2)}) copy-start(s32[1,1,64]{2,1,0:T(1,128)} %param.20) | copy-start | bytes 772
  0.6 9.3 %copy-start.7 = (s32[1,1,64,128]{3,2,1,0:T(8,128)S(1)}, s32[1,1,64,128]{3,2,1,0:T(8,128)}, u32[]{:S(2)}) copy-start(s32[1,1,64,128]{3,2,1,0:T(8,128)} %param.19) | copy-start | bytes 98308
  0.7 14.3 %collective-permute-start.2 = (f32[4,32]{1,0:T(4,128)}, f32[4,32]{1,0:T(4,128)S(1)}, u32[]{:S(2)}, u32[]{:S(2)}) collective-permute-start(f32[4,32]{1,0:T(4,128)} %ports.3), channel_id=1, source_target_pairs={{0,128},{64,192},{128,0},{192,64},{1,129},{65,193},{129,1},{193,65... | collective-permute-start | bytes 1544 | tf_op jit(solution)/shard_map/ppermute | solution.py:557
  2.8 12.1 %collective-permute-start.3 = (f32[4,32]{1,0:T(4,128)}, f32[4,32]{1,0:T(4,128)S(1)}, u32[]{:S(2)}, u32[]{:S(2)}) collective-permute-start(f32[4,32]{1,0:T(4,128)} %ports.3), channel_id=1, source_target_pairs={{0,192},{64,128},{128,64},{192,0},{1,193},{65,129},{129,65},{193,1... | collective-permute-start | bytes 1544 | tf_op jit(solution)/shard_map/ppermute | solution.py:558
  7.8 7.1 %collective-permute-start = (f32[152,512]{1,0:T(8,128)}, f32[152,512]{1,0:T(8,128)S(1)}, u32[]{:S(2)}, u32[]{:S(2)}) collective-permute-start(f32[152,512]{1,0:T(8,128)} %get-tuple-element.18), channel_id=1, source_target_pairs={{0,64},{64,0},{128,192},{192,128},{1,65},{65,1},{129,193},{193,129... | collective-permute-start | bytes 933896 | tf_op jit(solution)/shard_map/ppermute | solution.py:555
  7.8 9.2 %collective-permute-start.1 = (f32[152,512]{1,0:T(8,128)}, f32[152,512]{1,0:T(8,128)S(1)}, u32[]{:S(2)}, u32[]{:S(2)}) collective-permute-start(f32[152,512]{1,0:T(8,128)} %get-tuple-element.19), channel_id=1, source_target_pairs={{0,0},{192,192},{64,128},{128,64},{1,1},{193,193},{65,129},{129,65... | collective-permute-start | bytes 933896 | tf_op jit(solution)/shard_map/ppermute | solution.py:556
  10.0 5.0 %copy-start.2 = (f32[4,1,1,64,128]{4,3,2,1,0:T(8,128)S(1)}, f32[4,1,1,64,128]{4,3,2,1,0:T(8,128)}, u32[]{:S(2)}) copy-start(f32[4,1,1,64,128]{4,3,2,1,0:T(8,128)} %param.16) | copy-start | bytes 393220
  10.0 5.0 %copy-start.3 = (f32[1,1,64,128]{3,2,1,0:T(8,128)S(1)}, f32[1,1,64,128]{3,2,1,0:T(8,128)}, u32[]{:S(2)}) copy-start(f32[1,1,64,128]{3,2,1,0:T(8,128)} %param.17) | copy-start | bytes 98308
  10.0 5.0 %copy-start.4 = (f32[1,1,64,128]{3,2,1,0:T(8,128)S(1)}, f32[1,1,64,128]{3,2,1,0:T(8,128)}, u32[]{:S(2)}) copy-start(f32[1,1,64,128]{3,2,1,0:T(8,128)} %param.18) | copy-start | bytes 98308
  10.0 5.0 %copy-start.5 = (f32[4,32]{1,0:T(4,128)S(1)}, f32[4,32]{1,0:T(4,128)}, u32[]{:S(2)}) copy-start(f32[4,32]{1,0:T(4,128)} %ports.3) | copy-start | bytes 1540
  14.9 15.8 %copy-start.1 = (f32[8,16,512]{2,1,0:T(8,128)S(1)}, f32[8,16,512]{2,1,0:T(8,128)}, u32[]{:S(2)}) copy-start(f32[8,16,512]{2,1,0:T(8,128)} %param.12) | copy-start | bytes 786436
  17.0 19.7 %copy-start.10 = (s32[32]{0:T(128)S(1)}, s32[32]{0:T(128)}, u32[]{:S(2)}) copy-start(s32[32]{0:T(128)} %param.15) | copy-start | bytes 388
  17.1 32.9 %all-to-all-start = ((f32[192,4,128]{2,1,0:T(4,128)}), f32[192,4,128]{2,1,0:T(4,128)S(1)}, u32[]{:S(2)}, u32[]{:S(2)}) async-start(f32[192,4,128]{2,1,0:T(4,128)} %slip.1), calls=%async_computation | async-start | bytes 786432 | tf_op jit(solution)/shard_map/all_to_all | solution.py:574
  31.0 8.7 %collective-permute-start.4 = (f32[80,512]{1,0:T(8,128)S(1)}, f32[80,512]{1,0:T(8,128)S(1)}, u32[]{:S(2)}, u32[]{:S(2)}) collective-permute-start(f32[80,512]{1,0:T(8,128)S(1)} %get-tuple-element.27), channel_id=1, source_target_pairs={{0,0},{63,63},{1,2},{2,1},{3,4},{4,3},{5,6},{6,5},{7,8},{8,7},{9,1... | collective-permute-start | bytes 491528 | tf_op jit(solution)/shard_map/ppermute | solution.py:576
  31.7 15.5 %collective-permute-start.5 = (f32[80,512]{1,0:T(8,128)S(1)}, f32[80,512]{1,0:T(8,128)S(1)}, u32[]{:S(2)}, u32[]{:S(2)}) collective-permute-start(f32[80,512]{1,0:T(8,128)S(1)} %get-tuple-element.28), channel_id=1, source_target_pairs={{0,1},{1,0},{2,3},{3,2},{4,5},{5,4},{6,7},{7,6},{8,9},{9,8},{10,11... | collective-permute-start | bytes 491528 | tf_op jit(solution)/shard_map/ppermute | solution.py:577
  47.1 2.8 %copy-start.8 = (s32[1,1,64,128]{3,2,1,0:T(8,128)S(1)}, s32[1,1,64,128]{3,2,1,0:T(8,128)}, u32[]{:S(2)}) copy-start(s32[1,1,64,128]{3,2,1,0:T(8,128)} %param.21) | copy-start | bytes 98308
  47.1 2.8 %copy-start.9 = (s32[32]{0:T(128)S(1)}, s32[32]{0:T(128)}, u32[]{:S(2)}) copy-start(s32[32]{0:T(128)} %match.1) | copy-start | bytes 388

commit v15 on v13

--- a/solution.py
+++ b/solution.py
@@ -41,7 +41,7 @@
         pltpu.store(packed.at[pl.ds(spot + 1, 1), :], turned, mask=lane < begin)
         return base + counts[p]
 
-    used = lax.fori_loop(0, partners, pack, 0, unroll=8)
+    used = lax.fori_loop(0, partners, pack, 0, unroll=16)
     high, low = halves(flow[...])
     table[0:total] = high
     table[total:] = low
@@ -116,7 +116,7 @@
     base = 0
     copies = []
     for i in range(chunks):
-        base = lax.fori_loop(i * block, (i + 1) * block, finish, base, unroll=8)
+        base = lax.fori_loop(i * block, (i + 1) * block, finish, base, unroll=16)
         part = pl.ds(3 * i * block, 3 * block)
         copies.append(pltpu.make_async_copy(out.at[part], far.at[part], out_sems.at[i]))
         copies[i].start()
@@ -162,7 +162,7 @@
         last_ref[pl.ds(p, 1), :] = jnp.where(biggest > 0.0, slot + 1, 0)
         return carry
 
-    lax.fori_loop(0, partners, ends, 0, unroll=8)
+    lax.fori_loop(0, partners, ends, 0, unroll=16)
     last_ref[partners:, :] = jnp.zeros_like(last_ref[partners:, :])
     top = jnp.max(last_ref[...].T, axis=0, keepdims=True)
     last_ref[0:1, :] = top
@@ -209,7 +209,7 @@
         pltpu.store(packed.at[spot + 1], turned, mask=wide < begin)
         return base + last[0, p]
 
-    used = lax.fori_loop(0, partners, pack, 0, unroll=8)
+    used = lax.fori_loop(0, partners, pack, 0, unroll=16)
 
     spare = (used + cap - 1) >> cap_shift
     cells = jnp.broadcast_to(inlet[0:1, :].astype(jnp.float32), (8 - comps, cap))

time: 57.2 us -> 55.7 us (0.974)
  the two profiles are of different devices: /device:TPU:33 before, /device:TPU:65 now
where the time goes in v15:
time: 55.7 us; the launch traced here: 55.6 us
  starting transfers between devices  25.9 us (46%)
  Pallas kernels  21.8 us (39%)
  waiting for transfers between devices  6.9 us (12%)
  between operations  0.9 us (2%)
    all_to_all x1, starting transfers between devices, on_device(): lax.all_to_all(outgoing, 'tile', split_axis=0, concat_axis=0, tiled=True)  13 us
    pallas_call x1, Pallas kernels, land(): pl.pallas_call(functools.partial(land_kernel, GP), out_shape=(jax.ShapeDt...  7.5 us
    ppermute x1, waiting for transfers between devices, on_device(): by_odd = lax.ppermute(odd_edge, 'tile', odd_pairs)  6.56 us
    pallas_call x1, Pallas kernels, sample(): pl.pallas_call(functools.partial(sample_kernel, GP), out_shape=jax.ShapeD...  4.63 us
    ppermute x1, starting transfers between devices, on_device(): by_odd = lax.ppermute(odd_edge, 'tile', odd_pairs)  4.29 us
    ppermute x1, starting transfers between devices, on_device(): by_next = lax.ppermute(next_cap, 'sec', next_pairs)  3.5 us
    pallas_call x1, Pallas kernels, inner(): pl.pallas_call(functools.partial(inner_kernel, comps, depth_z, width), ou...  3 us
    pallas_call x1, Pallas kernels, outer(): pl.pallas_call(functools.partial(outer_kernel, comps, depth_z, width), ou...  2.81 us
  transfers between devices with their start and end apart: 7, of which 2 were waited for; matrix products, arithmetic and copies ran while one was open for 0% of the time, Pallas kernels for 26%

profile of v15, /device:TPU:65, one launch (start us, length us, event | category | flops | bytes accessed | tf_op | source)
XLA Modules:
  0.0 55.6 jit_solution(8891702983504489023)
XLA Ops:
  0.7 1.3 %collective-permute-start.2 = (f32[4,32]{1,0:T(4,128)}, f32[4,32]{1,0:T(4,128)S(1)}, u32[]{:S(2)}, u32[]{:S(2)}) collective-permute-start(f32[4,32]{1,0:T(4,128)} %ports.3), channel_id=1, source_target_pairs={{0,128},{64,192},{128,0},{192,64},{1,129},{65,193},{129,1},{193,65... | collective-permute-start | bytes 1544 | tf_op jit(solution)/shard_map/ppermute | solution.py:557
  2.0 1.1 %collective-permute-start.3 = (f32[4,32]{1,0:T(4,128)}, f32[4,32]{1,0:T(4,128)S(1)}, u32[]{:S(2)}, u32[]{:S(2)}) collective-permute-start(f32[4,32]{1,0:T(4,128)} %ports.3), channel_id=1, source_target_pairs={{0,192},{64,128},{128,64},{192,0},{1,193},{65,129},{129,65},{193,1... | collective-permute-start | bytes 1544 | tf_op jit(solution)/shard_map/ppermute | solution.py:558
  3.1 2.2 %caps.1 = (f32[152,512]{1,0:T(8,128)}, f32[152,512]{1,0:T(8,128)}) custom-call(f32[512,512]{1,0:T(8,128)} %bitcast.13, f32[128,512]{1,0:T(8,128)} %bitcast.18, f32[4,32]{1,0:T(4,128)} %ports.3), custom_call_target="tpu_custom_call" | custom-call | tf_op jit(solution)/shard_map/caps/pallas_call | solution.py:314
  5.2 0.0 collective-permute-start
  5.2 3.5 %collective-permute-start.1 = (f32[152,512]{1,0:T(8,128)}, f32[152,512]{1,0:T(8,128)S(1)}, u32[]{:S(2)}, u32[]{:S(2)}) collective-permute-start(f32[152,512]{1,0:T(8,128)} %get-tuple-element.19), channel_id=1, source_target_pairs={{0,0},{192,192},{64,128},{128,64},{1,1},{193,193},{65,129},{129,65... | collective-permute-start | bytes 933896 | tf_op jit(solution)/shard_map/ppermute | solution.py:556
  8.8 0.0 copy-start.2
  8.8 0.0 copy-start.3
  8.8 0.0 copy-start.4
  8.8 0.0 copy-start.5
  8.8 4.6 %sample.1.sampled = f32[72,4,128]{2,1,0:T(4,128)S(1)} custom-call(s32[64]{0:T(128)S(1)} %bitcast.25, f32[512,512]{1,0:T(8,128)S(1)} %bitcast.14, s32[64,128]{1,0:T(8,128)S(1)} %bitcast.27), custom_call_target="tpu_custom_call" | custom-call | flops 8589934592 | bytes 2097152 | tf_op jit(solution)/shard_map/sample/pallas_call | solution.py:69
  13.5 0.0 copy-start.1
  13.5 0.0 collective-permute-done.3.opposite
  13.5 0.0 collective-permute-done.near.by_near
  13.5 1.5 %slip.1 = f32[192,4,128]{2,1,0:T(4,128)} custom-call(s32[64]{0:T(128)S(1)} %bitcast.26, f32[72,4,128]{2,1,0:T(4,128)S(1)} %sample.1.sampled, f32[4,64,128]{2,1,0:T(8,128)S(1)} %bitcast.22, f32[64,128]{1,0:T(8,128)S(1)} %bitcast.23, f32[64,128]{1,0:T(8,128)S(1)} %bitcast.24, f32[4,32]{1,0:T(4,128)S(1)} %copy-done.5, ...), custom_call_target="tpu_custom_call" | custom-call | flops 2000000 | bytes 1048576 | tf_op jit(solution)/shard_map/slip/pallas_call | solution.py:129
  15.0 0.0 copy-start.10
  15.1 13.0 %all-to-all-start = ((f32[192,4,128]{2,1,0:T(4,128)}), f32[192,4,128]{2,1,0:T(4,128)S(1)}, u32[]{:S(2)}, u32[]{:S(2)}) async-start(f32[192,4,128]{2,1,0:T(4,128)} %slip.1), calls=%async_computation | async-start | bytes 786432 | tf_op jit(solution)/shard_map/all_to_all | solution.py:574
  28.0 0.2 edges.1
  28.3 2.8 %collective-permute-start.4 = (f32[80,512]{1,0:T(8,128)S(1)}, f32[80,512]{1,0:T(8,128)S(1)}, u32[]{:S(2)}, u32[]{:S(2)}) collective-permute-start(f32[80,512]{1,0:T(8,128)S(1)} %get-tuple-element.27), channel_id=1, source_target_pairs={{0,1},{1,0},{2,3},{3,2},{4,5},{5,4},{6,7},{7,6},{8,9},{9,8},{10,11... | collective-permute-start | bytes 491528 | tf_op jit(solution)/shard_map/ppermute | solution.py:576
  31.0 4.3 %collective-permute-start.5 = (f32[80,512]{1,0:T(8,128)S(1)}, f32[80,512]{1,0:T(8,128)S(1)}, u32[]{:S(2)}, u32[]{:S(2)}) collective-permute-start(f32[80,512]{1,0:T(8,128)S(1)} %get-tuple-element.28), channel_id=1, source_target_pairs={{0,0},{63,63},{1,2},{2,1},{3,4},{4,3},{5,6},{6,5},{7,8},{8,7},{9,1... | collective-permute-start | bytes 491528 | tf_op jit(solution)/shard_map/ppermute | solution.py:577
  35.4 3.0 %inner.1 = (f32[4,10,16,512]{3,2,1,0:T(8,128)S(1)}, f32[512,512]{1,0:T(8,128)S(1)}) custom-call(f32[512,512]{1,0:T(8,128)S(1)} %bitcast.16, f32[128,512]{1,0:T(8,128)S(1)} %bitcast.20, f32[144,512]{1,0:T(8,128)S(1)} %get-tuple-element.23.below, f32[144,512]{1,0:T(8,128)S(1)} %get-tuple-element.24.above), custom_call_target="tpu_custom_call" | custom-call | flops 10000000 | bytes 4194304 | tf_op jit(solution)/shard_map/inner/pallas_call | solution.py:400
  38.4 0.3 collective-permute-done.4.by_even
  38.7 6.6 %collective-permute-done.5.by_odd = f32[80,512]{1,0:T(8,128)S(1)} collective-permute-done((f32[80,512]{1,0:T(8,128)S(1)}, f32[80,512]{1,0:T(8,128)S(1)}, u32[]{:S(2)}, u32[]{:S(2)}) %collective-permute-start.5) | collective-permute-done | bytes 163872 | tf_op jit(solution)/shard_map/ppermute | solution.py:577
  45.3 2.8 %outer.1 = (f32[512,512]{1,0:T(8,128)S(1)}, f32[4,128]{1,0:T(4,128)S(1)}) custom-call(f32[512,512]{1,0:T(8,128)S(1)} %bitcast.17, f32[128,512]{1,0:T(8,128)S(1)} %bitcast.21, f32[144,512]{1,0:T(8,128)S(1)} %get-tuple-element.23.below, f32[144,512]{1,0:T(8,128)S(1)} %get-tuple-element.24.above, f32[4,10,16,512]{3,2,1,0:T(8,128)S(1)} %get-tuple-element.25.first, ...), custom_call_target="tpu_custom_call" | custom-call | flops 10000000 | bytes 4194304 | tf_op jit(solution)/shard_map/outer/pallas_call | solution.py:509
  48.1 7.5 %land.1 = (f32[512,512]{1,0:T(8,128)}, f32[4,64,128]{2,1,0:T(8,128)}) custom-call(s32[32]{0:T(128)S(1)} %copy-done.9, f32[512,512]{1,0:T(8,128)S(1)} %get-tuple-element.29.second, f32[4,128]{1,0:T(4,128)S(1)} %get-tuple-element.30.inlet_now, s32[1,128]{1,0:T(1,128)S(1)} %pad.4.inlet, s32[64,128]{1,0:T(8,128)S(1)} %bitcast.28, ...), custom_call_target="tpu_custom_call" | custom-call | flops 8589934592 | bytes 2097152 | tf_op jit(solution)/shard_map/land/pallas_call | solution.py:245
  (20 shorter events, 0.0 us)
Async XLA Ops:
  0.6 8.1 %copy-start = (f32[4,8,16,512]{3,2,1,0:T(8,128)S(1)}, f32[4,8,16,512]{3,2,1,0:T(8,128)}, u32[]{:S(2)}) copy-start(f32[4,8,16,512]{3,2,1,0:T(8,128)} %param.11) | copy-start | bytes 3145732
  0.6 8.1 %copy-start.6 = (s32[1,1,64]{2,1,0:T(1,128)S(1)}, s32[1,1,64]{2,1,0:T(1,128)}, u32[]{:S(2)}) copy-start(s32[1,1,64]{2,1,0:T(1,128)} %param.20) | copy-start | bytes 772
  0.6 8.1 %copy-start.7 = (s32[1,1,64,128]{3,2,1,0:T(8,128)S(1)}, s32[1,1,64,128]{3,2,1,0:T(8,128)}, u32[]{:S(2)}) copy-start(s32[1,1,64,128]{3,2,1,0:T(8,128)} %param.19) | copy-start | bytes 98308
  0.7 12.8 %collective-permute-start.2 = (f32[4,32]{1,0:T(4,128)}, f32[4,32]{1,0:T(4,128)S(1)}, u32[]{:S(2)}, u32[]{:S(2)}) collective-permute-start(f32[4,32]{1,0:T(4,128)} %ports.3), channel_id=1, source_target_pairs={{0,128},{64,192},{128,0},{192,64},{1,129},{65,193},{129,1},{193,65... | collective-permute-start | bytes 1544 | tf_op jit(solution)/shard_map/ppermute | solution.py:557
  2.0 11.5 %collective-permute-start.3 = (f32[4,32]{1,0:T(4,128)}, f32[4,32]{1,0:T(4,128)S(1)}, u32[]{:S(2)}, u32[]{:S(2)}) collective-permute-start(f32[4,32]{1,0:T(4,128)} %ports.3), channel_id=1, source_target_pairs={{0,192},{64,128},{128,64},{192,0},{1,193},{65,129},{129,65},{193,1... | collective-permute-start | bytes 1544 | tf_op jit(solution)/shard_map/ppermute | solution.py:558
  5.2 8.3 %collective-permute-start = (f32[152,512]{1,0:T(8,128)}, f32[152,512]{1,0:T(8,128)S(1)}, u32[]{:S(2)}, u32[]{:S(2)}) collective-permute-start(f32[152,512]{1,0:T(8,128)} %get-tuple-element.18), channel_id=1, source_target_pairs={{0,64},{64,0},{128,192},{192,128},{1,65},{65,1},{129,193},{193,129... | collective-permute-start | bytes 933896 | tf_op jit(solution)/shard_map/ppermute | solution.py:555
  5.2 9.8 %collective-permute-start.1 = (f32[152,512]{1,0:T(8,128)}, f32[152,512]{1,0:T(8,128)S(1)}, u32[]{:S(2)}, u32[]{:S(2)}) collective-permute-start(f32[152,512]{1,0:T(8,128)} %get-tuple-element.19), channel_id=1, source_target_pairs={{0,0},{192,192},{64,128},{128,64},{1,1},{193,193},{65,129},{129,65... | collective-permute-start | bytes 933896 | tf_op jit(solution)/shard_map/ppermute | solution.py:556
  8.8 4.7 %copy-start.2 = (f32[4,1,1,64,128]{4,3,2,1,0:T(8,128)S(1)}, f32[4,1,1,64,128]{4,3,2,1,0:T(8,128)}, u32[]{:S(2)}) copy-start(f32[4,1,1,64,128]{4,3,2,1,0:T(8,128)} %param.16) | copy-start | bytes 393220
  8.8 4.7 %copy-start.3 = (f32[1,1,64,128]{3,2,1,0:T(8,128)S(1)}, f32[1,1,64,128]{3,2,1,0:T(8,128)}, u32[]{:S(2)}) copy-start(f32[1,1,64,128]{3,2,1,0:T(8,128)} %param.17) | copy-start | bytes 98308
  8.8 4.7 %copy-start.4 = (f32[1,1,64,128]{3,2,1,0:T(8,128)S(1)}, f32[1,1,64,128]{3,2,1,0:T(8,128)}, u32[]{:S(2)}) copy-start(f32[1,1,64,128]{3,2,1,0:T(8,128)} %param.18) | copy-start | bytes 98308
  8.8 4.7 %copy-start.5 = (f32[4,32]{1,0:T(4,128)S(1)}, f32[4,32]{1,0:T(4,128)}, u32[]{:S(2)}) copy-start(f32[4,32]{1,0:T(4,128)} %ports.3) | copy-start | bytes 1540
  13.5 14.6 %copy-start.1 = (f32[8,16,512]{2,1,0:T(8,128)S(1)}, f32[8,16,512]{2,1,0:T(8,128)}, u32[]{:S(2)}) copy-start(f32[8,16,512]{2,1,0:T(8,128)} %param.12) | copy-start | bytes 786436
  15.0 20.3 %copy-start.10 = (s32[32]{0:T(128)S(1)}, s32[32]{0:T(128)}, u32[]{:S(2)}) copy-start(s32[32]{0:T(128)} %param.15) | copy-start | bytes 388
  15.1 33.0 %all-to-all-start = ((f32[192,4,128]{2,1,0:T(4,128)}), f32[192,4,128]{2,1,0:T(4,128)S(1)}, u32[]{:S(2)}, u32[]{:S(2)}) async-start(f32[192,4,128]{2,1,0:T(4,128)} %slip.1), calls=%async_computation | async-start | bytes 786432 | tf_op jit(solution)/shard_map/all_to_all | solution.py:574
  28.3 10.4 %collective-permute-start.4 = (f32[80,512]{1,0:T(8,128)S(1)}, f32[80,512]{1,0:T(8,128)S(1)}, u32[]{:S(2)}, u32[]{:S(2)}) collective-permute-start(f32[80,512]{1,0:T(8,128)S(1)} %get-tuple-element.27), channel_id=1, source_target_pairs={{0,1},{1,0},{2,3},{3,2},{4,5},{5,4},{6,7},{7,6},{8,9},{9,8},{10,11... | collective-permute-start | bytes 491528 | tf_op jit(solution)/shard_map/ppermute | solution.py:576
  31.0 14.2 %collective-permute-start.5 = (f32[80,512]{1,0:T(8,128)S(1)}, f32[80,512]{1,0:T(8,128)S(1)}, u32[]{:S(2)}, u32[]{:S(2)}) collective-permute-start(f32[80,512]{1,0:T(8,128)S(1)} %get-tuple-element.28), channel_id=1, source_target_pairs={{0,0},{63,63},{1,2},{2,1},{3,4},{4,3},{5,6},{6,5},{7,8},{8,7},{9,1... | collective-permute-start | bytes 491528 | tf_op jit(solution)/shard_map/ppermute | solution.py:577
  45.3 2.8 %copy-start.8 = (s32[1,1,64,128]{3,2,1,0:T(8,128)S(1)}, s32[1,1,64,128]{3,2,1,0:T(8,128)}, u32[]{:S(2)}) copy-start(s32[1,1,64,128]{3,2,1,0:T(8,128)} %param.21) | copy-start | bytes 98308
  45.3 2.8 %copy-start.9 = (s32[32]{0:T(128)S(1)}, s32[32]{0:T(128)}, u32[]{:S(2)}) copy-start(s32[32]{0:T(128)} %match.1) | copy-start | bytes 388
